TPU v7x, 32 devices: a whole 2x2x4 slice. The times are simulated.
32 devices in a mesh: grp: 2 (over y), scan: 4 (over z), chan: 4 (over x, core).
Axes of the slice: x: 2, y: 2, z: 4, core: 2. Of those that a mesh axis runs over, the one named last changes fastest.
Arguments:
- frames: bfloat16 [3072, 24576], P(('grp', 'scan'), 'chan'), parts along dimension 0, may hold values from -6 to 6
- counts: int32 [2048], P(('grp', 'scan')), parts along dimension 0, may hold values from 1 to 2, as said below
- point_ray: int32 [2048], P(('grp', 'scan')), parts along dimension 0, may hold values from 0 to 1023, as said below
- channel_pair_weights: bfloat16 [192, 128, 256], P('chan'), may hold values from 0 to 0.049804688
- tile_bin: int32 [192], P('chan'), may hold values from 0 to 14, as said below
- image: float32 [32768, 2048], P(('grp', 'scan'), 'chan'), parts along dimension 0, may hold values from -3 to 8
Outputs:
- corrected: float32 [32768, 2048], P(('grp', 'scan'), 'chan'), parts along dimension 0
There are 2 independent parts, one for each index of `grp`. A program takes and returns all parts, laid end to end along the dimension named above; an argument that names none is the same for every part. Nothing has to cross between parts.
Inputs may be any that keep to these rules, and one draw needn't show every extreme that they name: `counts`: each scan point has one or two frames; the frames of the 256 points of one scan index fill at most 384 slots, and one scan index fills all 384. `point_ray`: A permutation of the rays. Of the points of one scan index, at most 2 * 256 / 4 measure rays of one aligned block of 256 rays, and every block receives that many from some scan index. `tile_bin`: nondecreasing along the pixel blocks, from 0 at the first to 2048/128 - 2 at the last.
All inputs are finite; a program needn't handle non-finite values.
Results may differ from a plain program's by a relative error of at most 0.0045.
Values may be sent and summed in bfloat16 or wider, within the bound.
No kernel may reach another device: no remote copies, remote signals or barrier semaphores. Data moves between devices by JAX's collectives and lax.ppermute only.
A program may use at most 128 MiB of HBM per device.

v0:
```python
import math

import jax
import jax.numpy as jnp
from jax import lax
from jax.sharding import PartitionSpec as P

NIMG = 128


def hat_weights(ray_numbers, cell_ids, img_side, angles):
    half = (img_side - 1) / 2.0
    theta = (ray_numbers // img_side).astype(jnp.float32) * (math.pi / angles)
    offset = (ray_numbers % img_side).astype(jnp.float32) - half
    upos = (cell_ids // img_side).astype(jnp.float32) - half
    vpos = (cell_ids % img_side).astype(jnp.float32) - half
    along = jnp.cos(theta)[:, None] * upos[None, :] + jnp.sin(theta)[:, None] * vpos[None, :]
    return (jnp.maximum(0.0, 1.0 - jnp.abs(along - offset[:, None])) / img_side).astype(
        jnp.bfloat16
    )


def body(frames, counts, point_ray, channel_pair_weights, tile_bin, image):
    scan_count = lax.axis_size("scan")
    scan_me = lax.axis_index("scan")
    points = counts.shape[0]
    slots_dev = frames.shape[0]
    nblocks, tile_pix, paired_channel_blocks = channel_pair_weights.shape
    tile_bins = paired_channel_blocks // 2
    chans = image.shape[1]
    cells_dev = image.shape[0]
    rays_all = points * scan_count
    angles = rays_all // NIMG
    ends = jnp.cumsum(counts)
    slot_ids = jnp.arange(slots_dev, dtype=jnp.int32)
    owner = jnp.sum((ends[None, :] <= slot_ids[:, None]).astype(jnp.int32), axis=1)
    member = (owner[None, :] == jnp.arange(points, dtype=jnp.int32)[:, None]).astype(jnp.bfloat16)
    sums = jnp.dot(member, frames, preferred_element_type=jnp.float32)
    means = (sums / counts[:, None].astype(jnp.float32)).astype(jnp.bfloat16)
    pixel_grouped_weights = means.reshape(points, nblocks, tile_pix)
    partial_channel_value = jnp.einsum(
        "orj,rjm->rom",
        pixel_grouped_weights,
        channel_pair_weights,
        preferred_element_type=jnp.float32,
    )
    lower_part = partial_channel_value[:, :, :tile_bins]
    upper_part = partial_channel_value[:, :, tile_bins:]
    wanted = jnp.arange(chans * lax.axis_size("chan") // tile_bins, dtype=jnp.int32)
    lower_hot = (tile_bin[:, None] == wanted[None, :]).astype(jnp.float32)
    upper_hot = (tile_bin[:, None] + 1 == wanted[None, :]).astype(jnp.float32)
    placed = jnp.einsum("pk,pfb->kbf", lower_hot, lower_part, precision=lax.Precision.HIGHEST)
    placed = placed + jnp.einsum(
        "pk,pfb->kbf", upper_hot, upper_part, precision=lax.Precision.HIGHEST
    )
    pattern = lax.psum_scatter(
        placed.reshape(chans * lax.axis_size("chan"), points).astype(jnp.bfloat16),
        "chan",
        scatter_dimension=0,
        tiled=True,
    )
    pattern_rows = jnp.transpose(pattern)
    capacity = 2 * points // scan_count
    dest = point_ray // points
    dest_hot = (dest[:, None] == jnp.arange(scan_count, dtype=jnp.int32)[None, :]).astype(jnp.int32)
    position = jnp.sum((jnp.cumsum(dest_hot, axis=0) - 1) * dest_hot, axis=1)
    target = dest * capacity + position
    outgoing = jnp.zeros((scan_count * capacity, chans), jnp.bfloat16).at[target].set(pattern_rows)
    out_ids = (
        jnp.full((scan_count * capacity,), points, jnp.int32).at[target].set(point_ray % points)
    )
    incoming, in_ids = (
        lax.all_to_all(
            outgoing.reshape(scan_count, capacity, chans),
            "scan",
            split_axis=0,
            concat_axis=0,
            tiled=True,
        ),
        lax.all_to_all(
            out_ids.reshape(scan_count, capacity), "scan", split_axis=0, concat_axis=0, tiled=True
        ),
    )
    sinogram = (
        jnp.zeros((points, chans), jnp.bfloat16)
        .at[in_ids.reshape(-1)]
        .set(incoming.reshape(-1, chans), mode="drop")
    )
    row_ray = jnp.arange(rays_all, dtype=jnp.int32)
    image_low = image.astype(jnp.bfloat16)
    cell_ids = scan_me * cells_dev + jnp.arange(cells_dev, dtype=jnp.int32)
    local_weights = hat_weights(row_ray, cell_ids, NIMG, angles)
    col_total = jnp.sum(local_weights, axis=0, dtype=jnp.float32)
    forward_terms = jnp.dot(local_weights, image_low, preferred_element_type=jnp.float32)
    row_terms = jnp.sum(local_weights, axis=1, dtype=jnp.float32)
    projected, row_total = (
        lax.psum_scatter(forward_terms, "scan", scatter_dimension=0, tiled=True),
        lax.psum_scatter(row_terms, "scan", scatter_dimension=0, tiled=True),
    )
    residual = ((sinogram.astype(jnp.float32) - projected) / row_total[:, None]).astype(
        jnp.bfloat16
    )
    back = lax.dot_general(
        local_weights,
        lax.all_gather(residual, "scan", axis=0, tiled=True),
        (((0,), (0,)), ((), ())),
        preferred_element_type=jnp.float32,
    )
    return image + back / col_total[:, None]


def solution(mesh):
    in_specs = (
        P(("grp", "scan"), "chan"),
        P(("grp", "scan")),
        P(("grp", "scan")),
        P("chan", None, None),
        P("chan"),
        P(("grp", "scan"), "chan"),
    )
    out_specs = P(("grp", "scan"), "chan")
    return jax.shard_map(body, mesh=mesh, in_specs=in_specs, out_specs=out_specs, check_vma=False)
```

profile of v0, /device:TPU:0, one launch (start us, length us, event | category | flops | bytes accessed | tf_op | source)
XLA Modules:
  0.0 176.3 jit_solution(6974577594151923371)
XLA Ops:
  6.5 0.8 convert_element_type.83
  7.4 1.1 reduce-window.19
  8.9 4.2 %fusion.10 = bf16[32,48,8,128]{3,2,1,0:T(8,128)(2,1)S(1)} fusion(f32[256]{0:T(256)S(1)} %convert_element_type.83, bf16[384,6144]{1,0:T(8,128)(2,1)} %param.6, s32[384]{0:T(512)S(1)} %convert_reduce_fusion.2), kind=kOutput, calls=%fused_computation.19 | convolution fusion | flops 1211203584 | bytes 7866880 | tf_op jit(solution)/shard_map/dot_general | solution.py:38
  13.1 6.4 %fusion.7 = f32[48,256,256]{2,1,0:T(8,128)} fusion(bf16[48,128,256]{2,1,0:T(8,128)(2,1)S(1)} %copy-done, bf16[32,48,8,128]{3,2,1,0:T(8,128)(2,1)S(1)} %fusion.10), kind=kOutput, calls=%fused_computation.15 | convolution fusion | flops 805306368 | bytes 18874368 | tf_op jit(solution)/shard_map/orj,rjm->rom/dot_general | solution.py:41
  19.5 10.9 %fusion.57 = (f32[48,256,128]{2,1,0:T(8,128)}, f32[48,256,128]{2,1,0:T(8,128)}) fusion(f32[48,256,256]{2,1,0:T(8,128)} %fusion.7), kind=kLoop, calls=%fused_computation.96 | loop fusion | bytes 25165824 | tf_op jit(solution)/shard_map/slice | solution.py:47
  30.4 8.7 %fusion.1 = f32[256,128,16]{1,2,0:T(8,128)S(1)} fusion(f32[48,256,128]{2,1,0:T(8,128)} %get-tuple-element.8, s32[48]{0:T(128)S(1)} %broadcast_add_fusion), kind=kOutput, calls=%fused_computation.9 | convolution fusion | flops 301990656 | bytes 8388800 | tf_op jit(solution)/shard_map/pk,pfb->kbf/dot_general | solution.py:53
  39.1 5.8 %add_convert_fusion = bf16[256,128,16]{1,2,0:T(8,128)(2,1)S(1)} fusion(f32[256,128,16]{1,2,0:T(8,128)S(1)} %fusion.1, f32[48,256,128]{2,1,0:T(8,128)S(1)} %copy-done.1, s32[48]{0:T(128)S(1)} %copy-done.3), kind=kOutput, calls=%fused_computation.18 | convolution fusion | flops 303039232 | bytes 9437376 | tf_op jit(solution)/shard_map/pk,pfb->kbf/dot_general | solution.py:52
  44.9 1.3 copy.42
  46.6 9.6 %fusion.5 = f32[1024,512]{1,0:T(8,128)} fusion(f32[4096,512]{1,0:T(8,128)} %param.11, f32[1024]{0:T(1024)S(1)} %get-tuple-element.13, f32[4096]{0:T(1024)S(1)} %get-tuple-element.12, f32[1024]{0:T(1024)S(1)} %get-tuple-element.14, f32[4096]{0:T(1024)S(1)} %get-tuple-element.11, f32[1024]{0:T(1024)S(1)} %fusion.44), kind=kOutput, calls=%fused_computation.13 | convolution fusion | flops 4334813184 | bytes 10530816 | tf_op jit(solution)/shard_map/dot_general | solution.py:94
  56.3 1.2 reduce-window.15
  58.0 2.0 %scatter_custom_fusion = s32[512]{0:T(512)} fusion(s32[256]{0:T(256)S(1)} %compare_select_fusion.1, s32[256]{0:T(256)S(1)} %get-tuple-element.9, s32[]{:T(128)} %constant.114.clone.1), kind=kCustom, calls=%fused_computation.85 | custom fusion | bytes 2052 | tf_op jit(solution)/shard_map/scatter | solution.py:70
  59.9 6.3 %all-to-all-start = ((s32[4,1,128]{2,1,0:T(1,128)}), s32[4,1,128]{2,1,0:T(1,128)S(1)}, u32[]{:S(2)}, u32[]{:S(2)}) async-start(s32[4,1,128]{2,1,0:T(1,128)} %bitcast.3), calls=%async_computation | async-start | bytes 4096 | tf_op jit(solution)/shard_map/all_to_all | solution.py:80
  66.3 7.7 %reduce-scatter.3.cloned.1.call-done = bf16[512,256]{0,1:T(8,128)(2,1)} async-done(((bf16[2048,256]{0,1:T(8,128)(2,1)}), bf16[512,256]{0,1:T(8,128)(2,1)}) %reduce-scatter.3.cloned.1.call-update) | async-done | bytes 262160 | tf_op jit(solution)/shard_map/reduce_scatter | solution.py:56
  73.9 2.7 %scatter_custom_fusion.1 = bf16[512,512]{1,0:T(8,128)(2,1)} fusion(s32[256]{0:T(256)S(1)} %compare_select_fusion.1, bf16[512,256]{0,1:T(8,128)(2,1)} %reduce-scatter.3.cloned.1.call-done, bf16[]{:T(256)} %constant.113.clone.1), kind=kCustom, calls=%fused_computation.25 | custom fusion | bytes 786434 | tf_op jit(solution)/shard_map/scatter | solution.py:68
  76.6 4.6 %all-to-all-start.1 = ((bf16[4,128,512]{2,1,0:T(8,128)(2,1)}), bf16[4,128,512]{2,1,0:T(8,128)(2,1)}, u32[]{:S(2)}, u32[]{:S(2)}) async-start(bf16[4,128,512]{2,1,0:T(8,128)(2,1)} %bitcast.52), calls=%async_computation.2 | async-start | bytes 1048576 | tf_op jit(solution)/shard_map/all_to_all | solution.py:73
  81.2 8.3 %convert_reduce_fusion.1 = (f32[1024]{0:T(1024)S(1)}, f32[4096]{0:T(1024)S(1)}) fusion(f32[1024]{0:T(1024)S(1)} %get-tuple-element.13, f32[4096]{0:T(1024)S(1)} %get-tuple-element.12, f32[1024]{0:T(1024)S(1)} %get-tuple-element.14, f32[4096]{0:T(1024)S(1)} %get-tuple-element.11, f32[1024]{0:T(1024)S(1)} %fusion.44), kind=kLoop, calls=%fused_computation.4 | loop fusion | flops 50326528 | bytes 65536 | tf_op jit(solution)/shard_map/reduce_sum | solution.py:95
  89.6 0.6 dynamic-slice
  90.8 13.8 %all-reduce = f32[1024]{0:T(1024)S(1)} all-reduce(f32[1024]{0:T(1024)S(1)} %get-tuple-element.5), channel_id=4, replica_groups=mesh['grp'=2,'scan'=4,'chan'=4] {'scan'}, use_global_device_ids=true, to_apply=%region_12.13.clone | all-reduce | flops 1024 | bytes 8192
  104.7 5.4 %all-to-all-done.1 = bf16[4,128,512]{2,1,0:T(8,128)(2,1)} async-done(((bf16[4,128,512]{2,1,0:T(8,128)(2,1)}), bf16[4,128,512]{2,1,0:T(8,128)(2,1)}, u32[]{:S(2)}, u32[]{:S(2)}) %all-to-all-start.1) | async-done | bytes 524320 | tf_op jit(solution)/shard_map/all_to_all | solution.py:73
  110.1 3.2 %scatter_custom_fusion.2 = bf16[256,512]{1,0:T(8,128)(2,1)S(1)} fusion(s32[512]{0:T(512)S(1)} %bitcast.56, bf16[512,512]{1,0:T(8,128)(2,1)} %bitcast.13, bf16[]{:T(256)} %constant.113.clone.1), kind=kCustom, calls=%fused_computation.29 | custom fusion | bytes 262656 | tf_op jit(solution)/shard_map/scatter | solution.py:87
  113.3 14.7 %reduce-scatter.5.cloned.1.call-done = f32[256,512]{1,0:T(8,128)} async-done(((f32[1024,512]{1,0:T(8,128)}), f32[256,512]{1,0:T(8,128)}) %reduce-scatter.5.cloned.1.call-update) | async-done | bytes 524304 | tf_op jit(solution)/shard_map/reduce_scatter | solution.py:97
  127.9 1.9 %divide_convert_fusion = bf16[256,512]{1,0:T(8,128)(2,1)} fusion(f32[256,512]{1,0:T(8,128)} %reduce-scatter.5.cloned.1.call-done, bf16[256,512]{1,0:T(8,128)(2,1)S(1)} %scatter_custom_fusion.2, f32[256]{0:T(256)S(1)} %dynamic-slice.1), kind=kLoop, calls=%fused_computation.21 | loop fusion | flops 524288 | bytes 1049600 | tf_op jit(solution)/shard_map/convert_element_type | solution.py:100
  129.8 28.2 %all-gather.2.cloned.1.call-done = bf16[1024,512]{1,0:T(8,128)(2,1)} async-done(((bf16[256,512]{1,0:T(8,128)(2,1)}), bf16[1024,512]{1,0:T(8,128)(2,1)}) %all-gather.2.cloned.1.call-update) | async-done | bytes 1048592 | tf_op jit(solution)/shard_map/all_gather | solution.py:105
  158.0 11.8 %divide_add_fusion = f32[4096,512]{1,0:T(8,128)} fusion(f32[4096,512]{1,0:T(8,128)} %param.11, f32[4096]{0:T(1024)S(1)} %get-tuple-element.6, bf16[1024,512]{1,0:T(8,128)(2,1)} %all-gather.2.cloned.1.call-done, f32[1024]{0:T(1024)S(1)} %get-tuple-element.13, f32[4096]{0:T(1024)S(1)} %get-tuple-element.12, f32[1024]{0:T(1024)S(1)} %get-tuple-element.14, ...), kind=kOutput, calls=%fused_computation.6 | convolution fusion | flops 4336910336 | bytes 17887232 | tf_op jit(solution)/shard_map/dot_general | solution.py:103
  (38 shorter events, 1.4 us)
Async XLA Ops:
  6.5 6.6 %copy-start = (bf16[48,128,256]{2,1,0:T(8,128)(2,1)S(1)}, bf16[48,128,256]{2,1,0:T(8,128)(2,1)}, u32[]{:S(2)}) copy-start(bf16[48,128,256]{2,1,0:T(8,128)(2,1)} %param.9) | copy-start | bytes 9437188
  6.5 67.4 %reduce-scatter.3.cloned.1.call-start = ((), (), s32[]{:S(2)}) async-start(), calls=%async_computation.4 | async-start | bytes 1310720 | tf_op jit(solution)/shard_map/reduce_scatter | solution.py:56
  19.5 10.9 %copy-start.3 = (s32[48]{0:T(128)S(1)}, s32[48]{0:T(128)}, u32[]{:S(2)}) copy-start(s32[48]{0:T(128)} %param.10) | copy-start | bytes 580
  30.4 8.7 %copy-start.1 = (f32[48,256,128]{2,1,0:T(8,128)S(1)}, f32[48,256,128]{2,1,0:T(8,128)}, u32[]{:S(2)}) copy-start(f32[48,256,128]{2,1,0:T(8,128)} %get-tuple-element.7) | copy-start | bytes 18874372
  46.2 81.8 %reduce-scatter.5.cloned.1.call-start = ((), (), s32[]{:S(2)}) async-start(), calls=%async_computation.5 | async-start | bytes 2621440 | tf_op jit(solution)/shard_map/reduce_scatter | solution.py:97
  46.6 9.7 %copy-start.2 = (s32[256]{0:T(256)S(1)}, s32[256]{0:T(256)}, u32[]{:S(2)}) copy-start(s32[256]{0:T(256)} %param.8) | copy-start | bytes 3076
  46.6 43.0 %copy-start.4 = (u32[32]{0:T(128)S(1)}, u32[32]{0:T(128)}, u32[]{:S(2)}) copy-start(u32[32]{0:T(128)} %constant.120) | copy-start | bytes 388
  59.9 16.7 %all-to-all-start = ((s32[4,1,128]{2,1,0:T(1,128)}), s32[4,1,128]{2,1,0:T(1,128)S(1)}, u32[]{:S(2)}, u32[]{:S(2)}) async-start(s32[4,1,128]{2,1,0:T(1,128)} %bitcast.3), calls=%async_computation | async-start | bytes 4096 | tf_op jit(solution)/shard_map/all_to_all | solution.py:80
  76.6 33.5 %all-to-all-start.1 = ((bf16[4,128,512]{2,1,0:T(8,128)(2,1)}), bf16[4,128,512]{2,1,0:T(8,128)(2,1)}, u32[]{:S(2)}, u32[]{:S(2)}) async-start(bf16[4,128,512]{2,1,0:T(8,128)(2,1)} %bitcast.52), calls=%async_computation.2 | async-start | bytes 1048576 | tf_op jit(solution)/shard_map/all_to_all | solution.py:73
  81.2 76.8 %all-gather.2.cloned.1.call-start = ((), (), s32[]{:S(2)}) async-start(), calls=%async_computation.6 | async-start | bytes 1310720 | tf_op jit(solution)/shard_map/all_gather | solution.py:105
Sparse Core Ops, SparseCore 0:
  46.3 27.5 reduce-scatter.2
  76.3 51.5 reduce-scatter.4
  129.9 28.0 all-gather.1
where the time goes:
time: 177 us; the launch traced here: 176 us
  waiting for transfers between devices  56 us (32%)
  matrix products  46.5 us (26%)
  local copies, waits for them, and re-layouts  21.2 us (12%)
  other arithmetic  13.9 us (8%)
  between operations  13.9 us (8%)
  blocking collectives  13.8 us (8%)
  starting transfers between devices  11.2 us (6%)
    all_gather x1, waiting for transfers between devices, body(): lax.all_gather(residual, 'scan', axis=0, tiled=True)  28.2 us
    reduce_scatter x1, waiting for transfers between devices, body(): lax.psum_scatter(forward_terms, 'scan', scatter_dimension=0, tiled=True)  14.7 us
    unnamed x1, blocking collectives  13.8 us
    dot_general x1, matrix products, body(): lax.dot_general(local_weights, lax.all_gather(residual, 'scan', axis=0, t...  11.8 us
    slice x1, local copies, waits for them, and re-layouts, body(): lower_part = partial_channel_value[:, :, :tile_bins]  10.9 us
    dot_general x1, matrix products, body(): jnp.dot(local_weights, image_low, preferred_element_type=jnp.float32)  9.65 us
    dot_general x1, matrix products, body(): jnp.einsum('pk,pfb->kbf', upper_hot, upper_part, precision=lax.Precision....  8.66 us
    reduce_sum x1, other arithmetic, body(): row_terms = jnp.sum(local_weights, axis=1, dtype=jnp.float32)  8.33 us
  transfers between devices with their start and end apart: 5, of which 4 were waited for; matrix products, arithmetic and copies ran while one was open for 16% of the time, Pallas kernels for 0%

commit v1 on v0

v1 whole, which is shorter than its diff:
```python
import functools
import math

import jax
import jax.numpy as jnp
import numpy as np
from jax import lax
from jax.experimental import pallas as pl
from jax.experimental.pallas import tpu as pltpu
from jax.sharding import PartitionSpec as P

NIMG = 128
HALF = (NIMG - 1) / 2.0
LANES = 128
VMEM_BYTES = 50 * 1024 * 1024
F32 = jnp.float32
BF16 = jnp.bfloat16


def angle_tables(angles):
    theta = np.arange(angles, dtype=np.float32) * np.float32(math.pi / angles)
    return [float(c) for c in np.cos(theta)], [float(s) for s in np.sin(theta)]


def ray_geometry(rays, angles):
    cos_tab, sin_tab = angle_tables(angles)
    which = rays // NIMG
    offset = (rays - which * NIMG).astype(F32) - HALF
    cosine = jnp.zeros(rays.shape, F32)
    sine = jnp.zeros(rays.shape, F32)
    for a in range(angles):
        here = which == a
        cosine = jnp.where(here, cos_tab[a], cosine)
        sine = jnp.where(here, sin_tab[a], sine)
    return cosine, sine, offset


def hat(distance):
    return jnp.maximum(1.0 - jnp.abs(distance), 0.0).astype(BF16)


def integrate_kernel(
    nx, per_chunk, tile_bin, place, counts, frames, weights, send, keep_own, keep_rest, member, acc
):
    step = pl.program_id(0)
    points, slots = member.shape
    blocks = weights.shape[0]
    tile_bins = acc.shape[2]

    @pl.when(step == 0)
    def _():
        acc[...] = jnp.zeros_like(acc)
        count_row = counts[...].astype(F32)
        row = lax.broadcasted_iota(jnp.int32, (points, points), 0)
        col = lax.broadcasted_iota(jnp.int32, (points, points), 1)
        ends = jnp.sum(jnp.where(col <= row, count_row, 0.0), axis=1, keepdims=True)
        count = jnp.sum(jnp.where(col == row, count_row, 0.0), axis=1, keepdims=True)
        slot = lax.broadcasted_iota(jnp.int32, (points, slots), 1).astype(F32)
        inside = jnp.logical_and(slot >= ends - count, slot < ends)
        member[...] = jnp.where(inside, 1.0 / count, 0.0).astype(BF16)

    means = jnp.dot(member[...], frames[...], preferred_element_type=F32).astype(BF16)
    for b in range(blocks):
        value = jnp.dot(
            means[:, b * LANES : (b + 1) * LANES], weights[b], preferred_element_type=F32
        )
        k = tile_bin[step * blocks + b]
        acc[k] += value[:, :tile_bins]
        acc[k + 1] += value[:, tile_bins:]

    @pl.when(step == pl.num_programs(0) - 1)
    def _():
        for e in range(nx):
            other, mine = place[2 * e], place[2 * e + 1]
            for j in range(per_chunk):
                lanes = slice(j * tile_bins, (j + 1) * tile_bins)
                send[e, :, lanes] = acc[other * per_chunk + j].astype(BF16)
                if e == 0:
                    keep_own[:, lanes] = acc[mine * per_chunk + j]
                else:
                    keep_rest[e - 1, :, lanes] = acc[mine * per_chunk + j]


def integrate(frames, counts, weights, tile_bin, place, nx, chans):
    slots, pixels = frames.shape
    points = counts.shape[0]
    nblocks, tile_pix, pair = weights.shape
    tile_bins = pair // 2
    blocks = 8 if nblocks % 8 == 0 else 1
    channel_blocks = 2 * nx * chans // tile_bins
    whole = lambda shape: pl.BlockSpec(shape, lambda i, *_: (0,) * len(shape))
    return pl.pallas_call(
        functools.partial(integrate_kernel, nx, chans // tile_bins),
        grid_spec=pltpu.PrefetchScalarGridSpec(
            num_scalar_prefetch=2,
            grid=(nblocks // blocks,),
            in_specs=[
                whole((1, points)),
                pl.BlockSpec((slots, blocks * tile_pix), lambda i, *_: (0, i)),
                pl.BlockSpec((blocks, tile_pix, pair), lambda i, *_: (i, 0, 0)),
            ],
            out_specs=[
                whole((nx, points, chans)),
                whole((points, chans)),
                whole((nx - 1, points, chans)),
            ],
            scratch_shapes=[
                pltpu.VMEM((points, slots), BF16),
                pltpu.VMEM((channel_blocks, points, tile_bins), F32),
            ],
        ),
        out_shape=[
            jax.ShapeDtypeStruct((nx, points, chans), BF16),
            jax.ShapeDtypeStruct((points, chans), F32),
            jax.ShapeDtypeStruct((nx - 1, points, chans), F32),
        ],
        compiler_params=pltpu.CompilerParams(vmem_limit_bytes=VMEM_BYTES),
        cost_estimate=pl.CostEstimate(
            flops=2 * points * pixels * (slots + pair),
            bytes_accessed=2 * (slots * pixels + pixels * pair),
            transcendentals=0,
        ),
        name="integrate",
    )(tile_bin, place, counts.reshape(1, points), frames, weights)


def project_kernel(angles, parts, first_row, rays, image, *refs):
    outs, (cosine, base, tile, total) = refs[:parts], refs[parts:]
    step = pl.program_id(0)
    rows = tile.shape[1] // LANES
    points = total.shape[0] // parts

    @pl.when(step == 0)
    def _():
        total[...] = jnp.zeros_like(total)
        cos_c, sin_c, off_c = ray_geometry(rays[...], angles)
        vpos = lax.broadcasted_iota(jnp.int32, (LANES, LANES), 1).astype(F32) - HALF
        for k in range(rays.shape[0]):
            here = slice(k * LANES, (k + 1) * LANES)
            column = lambda x: jnp.transpose(jnp.broadcast_to(x[k : k + 1, :], (LANES, LANES)))
            cosine[here, :] = column(cos_c)
            base[here, :] = column(sin_c) * vpos - column(off_c)

    for i in range(rows):
        upos = (first_row[0] + step * rows + i).astype(F32) - HALF
        tile[:, i * LANES : (i + 1) * LANES] = hat(base[...] + cosine[...] * upos)
    total[...] += jnp.dot(tile[...], image[...].astype(BF16), preferred_element_type=F32)

    @pl.when(step == pl.num_programs(0) - 1)
    def _():
        for d in range(parts):
            outs[d][...] = total[d * points : (d + 1) * points, :].astype(outs[d].dtype)


def project(rays, image, first_row, angles, parts):
    cells, chans = image.shape
    all_points = rays.shape[0] * LANES
    points = all_points // parts
    rows = min(8, cells // LANES)
    out = pl.BlockSpec((points, chans), lambda i, *_: (0, 0))
    return pl.pallas_call(
        functools.partial(project_kernel, angles, parts),
        grid_spec=pltpu.PrefetchScalarGridSpec(
            num_scalar_prefetch=1,
            grid=(cells // (rows * LANES),),
            in_specs=[
                pl.BlockSpec(rays.shape, lambda i, *_: (0, 0)),
                pl.BlockSpec((rows * LANES, chans), lambda i, *_: (i, 0)),
            ],
            out_specs=[out] * parts,
            scratch_shapes=[
                pltpu.VMEM((all_points, LANES), F32),
                pltpu.VMEM((all_points, LANES), F32),
                pltpu.VMEM((all_points, rows * LANES), BF16),
                pltpu.VMEM((all_points, chans), F32),
            ],
        ),
        out_shape=[
            jax.ShapeDtypeStruct((points, chans), F32 if d == 0 else BF16) for d in range(parts)
        ],
        compiler_params=pltpu.CompilerParams(vmem_limit_bytes=VMEM_BYTES),
        cost_estimate=pl.CostEstimate(
            flops=2 * all_points * cells * chans, bytes_accessed=4 * cells * chans, transcendentals=0
        ),
        name="project",
    )(first_row, rays, image)


def totals_kernel(angles, first_row, rays, row_total, col_recip):
    cos_tab, sin_tab = angle_tables(angles)
    cos_r, sin_r, off_r = ray_geometry(rays[...], angles)
    lane = lax.broadcasted_iota(jnp.int32, (LANES, LANES), 1).astype(F32) - HALF
    vpos = lax.broadcasted_iota(jnp.int32, (LANES, LANES), 0).astype(F32) - HALF
    for k in range(rays.shape[0]):
        base = sin_r[k : k + 1, :] * vpos - off_r[k : k + 1, :]
        slope = cos_r[k : k + 1, :]

        def add_row(i, sums):
            upos = i.astype(F32) - HALF
            return sums + hat(base + slope * upos).astype(F32)

        sums = lax.fori_loop(0, NIMG, add_row, jnp.zeros((LANES, LANES), F32), unroll=4)
        total = jnp.sum(sums, axis=0, keepdims=True)
        row_total[k * LANES : (k + 1) * LANES, :] = jnp.transpose(
            jnp.broadcast_to(total, (LANES, LANES))
        )

    def column_row(i, carry):
        upos = (first_row[0] + i).astype(F32) - HALF
        sums = jnp.zeros((LANES, LANES), F32)
        for a in range(angles):
            sums += hat((sin_tab[a] * vpos - lane) + cos_tab[a] * upos).astype(F32)
        total = jnp.sum(sums, axis=1, keepdims=True)
        start = pl.multiple_of(i * LANES, LANES)
        col_recip[pl.ds(start, LANES), :] = jnp.broadcast_to(1.0 / total, (LANES, LANES))
        return carry

    lax.fori_loop(0, col_recip.shape[0] // LANES, column_row, 0)


def totals(rays, first_row, cells, angles):
    points = rays.shape[0] * LANES
    vmem = pl.BlockSpec(memory_space=pltpu.VMEM)
    return pl.pallas_call(
        functools.partial(totals_kernel, angles),
        in_specs=[pl.BlockSpec(memory_space=pltpu.SMEM), vmem],
        out_specs=[vmem, vmem],
        out_shape=[
            jax.ShapeDtypeStruct((points, LANES), F32),
            jax.ShapeDtypeStruct((cells, LANES), F32),
        ],
        compiler_params=pltpu.CompilerParams(vmem_limit_bytes=VMEM_BYTES),
        cost_estimate=pl.CostEstimate(
            flops=8 * points * NIMG * NIMG * 8, bytes_accessed=4 * cells * LANES, transcendentals=0
        ),
        name="totals",
    )(first_row, rays)


def back_kernel(angles, parts, first_row, rays, *refs):
    residuals, (image, recip, out, base, cosine, joined, tile) = refs[:parts], refs[parts:]
    step = pl.program_id(0)
    points, chans = residuals[0].shape
    rows = tile.shape[0] // LANES

    @pl.when(step == 0)
    def _():
        cos_c, sin_c, off_c = ray_geometry(rays[...], angles)
        cosine[...] = cos_c
        vpos = lax.broadcasted_iota(jnp.int32, (LANES, LANES), 0).astype(F32) - HALF
        for k in range(rays.shape[0]):
            base[:, k * LANES : (k + 1) * LANES] = sin_c[k : k + 1, :] * vpos - off_c[k : k + 1, :]
        for d in range(parts):
            joined[d * points : (d + 1) * points, :] = residuals[d][...]

    for i in range(rows):
        upos = (first_row[0] + step * rows + i).astype(F32) - HALF
        for k in range(rays.shape[0]):
            lanes = slice(k * LANES, (k + 1) * LANES)
            shift = cosine[k : k + 1, :] * upos
            tile[i * LANES : (i + 1) * LANES, lanes] = hat(base[:, lanes] + shift)
    back = jnp.dot(tile[...], joined[...], preferred_element_type=F32)
    for j in range(chans // LANES):
        lanes = slice(j * LANES, (j + 1) * LANES)
        out[:, lanes] = image[:, lanes] + back[:, lanes] * recip[...]


def back_project(rays, residuals, image, recip, first_row, angles):
    cells, chans = image.shape
    parts = len(residuals)
    points = residuals[0].shape[0]
    all_points = parts * points
    rows = min(4, cells // LANES)
    fixed = lambda shape: pl.BlockSpec(shape, lambda i, *_: (0, 0))
    sliding = lambda width: pl.BlockSpec((rows * LANES, width), lambda i, *_: (i, 0))
    return pl.pallas_call(
        functools.partial(back_kernel, angles, parts),
        grid_spec=pltpu.PrefetchScalarGridSpec(
            num_scalar_prefetch=1,
            grid=(cells // (rows * LANES),),
            in_specs=[fixed(rays.shape)]
            + [fixed((points, chans))] * parts
            + [sliding(chans), sliding(LANES)],
            out_specs=sliding(chans),
            scratch_shapes=[
                pltpu.VMEM((LANES, all_points), F32),
                pltpu.VMEM(rays.shape, F32),
                pltpu.VMEM((all_points, chans), BF16),
                pltpu.VMEM((rows * LANES, all_points), BF16),
            ],
        ),
        out_shape=jax.ShapeDtypeStruct((cells, chans), F32),
        compiler_params=pltpu.CompilerParams(vmem_limit_bytes=VMEM_BYTES),
        cost_estimate=pl.CostEstimate(
            flops=2 * all_points * cells * chans, bytes_accessed=8 * cells * chans, transcendentals=0
        ),
        name="back_project",
    )(first_row, rays, *residuals, image, recip)


def rotate(x, axis, shift, n):
    return lax.ppermute(x, axis, [(i, (i + shift) % n) for i in range(n)])


def body(frames, counts, point_ray, channel_pair_weights, tile_bin, image):
    n_scan = lax.axis_size("scan")
    n_chan = lax.axis_size("chan")
    nx = n_chan // 2
    points = counts.shape[0]
    cells, chans = image.shape
    angles = points * n_scan // NIMG
    chan_me = lax.axis_index("chan")
    x_me, core_me = chan_me // 2, chan_me % 2
    first_row = (lax.axis_index("scan") * (cells // NIMG)).astype(jnp.int32).reshape(1)

    own_rays = point_ray.reshape(points // LANES, LANES)
    rays = [own_rays] + [rotate(own_rays, "scan", -d, n_scan) for d in range(1, n_scan)]
    all_rays = jnp.concatenate(rays, axis=0)

    shares = project(all_rays, image, first_row, angles, n_scan)
    arrived = [rotate(shares[d], "scan", d, n_scan) for d in range(1, n_scan)]

    place = []
    for e in range(nx):
        xi = (x_me + e) % nx
        place += [2 * xi + 1 - core_me, 2 * xi + core_me]
    place = jnp.stack(place).astype(jnp.int32)
    send, keep_own, keep_rest = integrate(
        frames, counts, channel_pair_weights, tile_bin, place, nx, chans
    )
    partner = [(i, i ^ 1) for i in range(n_chan)]
    got = lax.ppermute(send, "chan", partner)
    pattern = keep_own + got[0].astype(F32)
    for e in range(1, nx):
        joined = (keep_rest[e - 1] + got[e].astype(F32)).astype(BF16)
        pattern = pattern + rotate(joined, "chan", 2 * e, n_chan).astype(F32)

    row_total, col_recip = totals(own_rays, first_row, cells, angles)
    projected = shares[0]
    for part in arrived:
        projected = projected + part.astype(F32)
    residual = ((pattern * float(NIMG) - projected) / row_total[:, :1]).astype(BF16)
    residuals = [residual] + [rotate(residual, "scan", -d, n_scan) for d in range(1, n_scan)]
    return back_project(all_rays, residuals, image, col_recip, first_row, angles)


def solution(mesh):
    in_specs = (
        P(("grp", "scan"), "chan"),
        P(("grp", "scan")),
        P(("grp", "scan")),
        P("chan", None, None),
        P("chan"),
        P(("grp", "scan"), "chan"),
    )
    out_specs = P(("grp", "scan"), "chan")
    return jax.shard_map(body, mesh=mesh, in_specs=in_specs, out_specs=out_specs, check_vma=False)
```

time: 177 us -> 90.9 us (0.51)
  the two profiles are of different devices: /device:TPU:0 before, /device:TPU:24 now
where the time goes in v1:
time: 90.9 us; the launch traced here: 90.3 us
  Pallas kernels  38.6 us (42%)
  waiting for transfers between devices  33.4 us (37%)
  starting transfers between devices  16.4 us (18%)
  local copies, waits for them, and re-layouts  1.47 us (2%)
    ppermute x10, waiting for transfers between devices, rotate(): return lax.ppermute(x, axis, [(i, (i + shift) % n) for i in range(n)])  33.4 us
    ppermute x10, starting transfers between devices, rotate(): return lax.ppermute(x, axis, [(i, (i + shift) % n) for i in range(n)])  16.3 us
    pallas_call x1, Pallas kernels, totals(): pl.pallas_call(functools.partial(totals_kernel, angles), in_specs=[pl.Blo...  11.6 us
    pallas_call x1, Pallas kernels, back_project(): pl.pallas_call(functools.partial(back_kernel, angles, parts), grid_spec=p...  11.2 us
    pallas_call x1, Pallas kernels, integrate(): pl.pallas_call(functools.partial(integrate_kernel, nx, chans // tile_bins...  8.03 us
    pallas_call x1, Pallas kernels, project(): pl.pallas_call(functools.partial(project_kernel, angles, parts), grid_spe...  7.76 us
  transfers between devices with their start and end apart: 11, of which 6 were waited for; matrix products, arithmetic and copies ran while one was open for 0% of the time, Pallas kernels for 21%

profile of v1, /device:TPU:24, one launch (start us, length us, event | category | flops | bytes accessed | tf_op | source)
XLA Modules:
  0.0 90.3 jit_solution(16940680014406950938)
XLA Ops:
  0.0 0.1 pad_add_fusion.1.place
  0.1 0.7 copy-done
  0.8 0.7 copy-done.2
  1.4 8.0 %integrate.1 = (bf16[2,256,512]{2,1,0:T(8,128)(2,1)S(1)}, f32[256,512]{1,0:T(8,128)S(1)}, f32[1,256,512]{2,1,0:T(8,128)S(1)}) custom-call(s32[48]{0:T(128)S(1)} %copy-done.2, s32[4]{0:T(128)S(1)} %pad_add_fusion.1.place, s32[1,256]{1,0:T(1,128)S(1)} %bitcast.14, bf16[384,6144]{1,0:T(8,128)(2,1)} %frames.1, bf16[48,128,256]{2,1,0:T(8,128)(2,1)} %weights.1), custom_call_target="tpu_custom_call" | custom-call | flops 2013265920 | bytes 7864320 | tf_op jit(solution)/shard_map/integrate/pallas_call | solution.py:92
  9.5 0.1 collective-permute-start.3
  9.6 1.9 %collective-permute-start.1 = (s32[2,128]{1,0:T(2,128)S(1)}, s32[2,128]{1,0:T(2,128)S(1)}, u32[]{:S(2)}, u32[]{:S(2)}) collective-permute-start(s32[2,128]{1,0:T(2,128)S(1)} %bitcast.16), channel_id=1, source_target_pairs={{0,8},{4,12},{8,0},{12,4},{1,9},{5,13},{9,1},{13,5},{2,10},{6,14},... | collective-permute-start | bytes 3080 | tf_op jit(solution)/shard_map/ppermute | solution.py:302
  11.5 0.4 collective-permute-start
  12.0 1.2 %collective-permute-done.2 = s32[2,128]{1,0:T(2,128)S(1)} collective-permute-done((s32[2,128]{1,0:T(2,128)S(1)}, s32[2,128]{1,0:T(2,128)S(1)}, u32[]{:S(2)}, u32[]{:S(2)}) %collective-permute-start.2) | collective-permute-done | bytes 1056 | tf_op jit(solution)/shard_map/ppermute | solution.py:302
  13.2 1.0 %collective-permute-done.1 = s32[2,128]{1,0:T(2,128)S(1)} collective-permute-done((s32[2,128]{1,0:T(2,128)S(1)}, s32[2,128]{1,0:T(2,128)S(1)}, u32[]{:S(2)}, u32[]{:S(2)}) %collective-permute-start.1) | collective-permute-done | bytes 1056 | tf_op jit(solution)/shard_map/ppermute | solution.py:302
  14.2 2.7 %collective-permute-done = s32[2,128]{1,0:T(2,128)S(1)} collective-permute-done((s32[2,128]{1,0:T(2,128)S(1)}, s32[2,128]{1,0:T(2,128)S(1)}, u32[]{:S(2)}, u32[]{:S(2)}) %collective-permute-start) | collective-permute-done | bytes 1056 | tf_op jit(solution)/shard_map/ppermute | solution.py:302
  16.9 7.8 %project.1 = (f32[256,512]{1,0:T(8,128)S(1)}, bf16[256,512]{1,0:T(8,128)(2,1)S(1)}, bf16[256,512]{1,0:T(8,128)(2,1)S(1)}, bf16[256,512]{1,0:T(8,128)(2,1)S(1)}) custom-call(s32[1]{0:T(128)} %bitcast.first_row, s32[8,128]{1,0:T(8,128)S(1)} %pad_add_fusion.rays, f32[4096,512]{1,0:T(8,128)} %refs_4_.1), custom_call_target="tpu_custom_call" | custom-call | flops 4294967296 | bytes 8388608 | tf_op jit(solution)/shard_map/project/pallas_call | solution.py:161
  24.7 0.7 collective-permute-start.5
  25.4 1.3 %collective-permute-start.7 = (bf16[256,512]{1,0:T(8,128)(2,1)S(1)}, bf16[256,512]{1,0:T(8,128)(2,1)S(1)}, u32[]{:S(2)}, u32[]{:S(2)}) collective-permute-start(bf16[256,512]{1,0:T(8,128)(2,1)S(1)} %get-tuple-element.20), channel_id=1, source_target_pairs={{0,12},{4,0},{8,4},{12,8},{1,13},{5,1},{9,5},{13,9},{2,14},{6,2},{... | collective-permute-start | bytes 786440 | tf_op jit(solution)/shard_map/ppermute | solution.py:302
  26.7 0.1 fusion.5
  26.8 1.6 %collective-permute-start.4 = (bf16[256,512]{1,0:T(8,128)(2,1)S(1)}, bf16[256,512]{1,0:T(8,128)(2,1)S(1)}, u32[]{:S(2)}, u32[]{:S(2)}) collective-permute-start(bf16[256,512]{1,0:T(8,128)(2,1)S(1)} %fusion.5), channel_id=1, source_target_pairs={{0,2},{1,3},{2,0},{3,1},{4,6},{5,7},{6,4},{7,5},{8,10},{9,11},{10,... | collective-permute-start | bytes 786440 | tf_op jit(solution)/shard_map/ppermute | solution.py:302
  28.4 11.6 %totals.1 = (f32[256,128]{1,0:T(8,128)S(1)}, f32[4096,128]{1,0:T(8,128)S(1)}) custom-call(s32[1]{0:T(128)} %bitcast.first_row, s32[2,128]{1,0:T(2,128)S(1)} %bitcast.19), custom_call_target="tpu_custom_call" | custom-call | flops 268435456 | bytes 2097152 | tf_op jit(solution)/shard_map/totals/pallas_call | solution.py:224
  40.0 0.1 slice_reduce_fusion
  40.2 7.3 %collective-permute-done.6 = bf16[256,512]{1,0:T(8,128)(2,1)S(1)} collective-permute-done((bf16[256,512]{1,0:T(8,128)(2,1)S(1)}, bf16[256,512]{1,0:T(8,128)(2,1)S(1)}, u32[]{:S(2)}, u32[]{:S(2)}) %collective-permute-start.6) | collective-permute-done | bytes 262176 | tf_op jit(solution)/shard_map/ppermute | solution.py:302
  47.4 0.3 fusion.4.refs_0_
  47.8 8.2 %collective-permute-start.9 = (bf16[256,512]{1,0:T(8,128)(2,1)S(1)}, bf16[256,512]{1,0:T(8,128)(2,1)S(1)}, u32[]{:S(2)}, u32[]{:S(2)}) collective-permute-start(bf16[256,512]{1,0:T(8,128)(2,1)S(1)} %fusion.4.refs_0_), channel_id=1, source_target_pairs={{0,8},{4,12},{8,0},{12,4},{1,9},{5,13},{9,1},{13,5},{2,10},{6,14},... | collective-permute-start | bytes 786440 | tf_op jit(solution)/shard_map/ppermute | solution.py:302
  56.0 1.9 %collective-permute-start.8 = (bf16[256,512]{1,0:T(8,128)(2,1)S(1)}, bf16[256,512]{1,0:T(8,128)(2,1)S(1)}, u32[]{:S(2)}, u32[]{:S(2)}) collective-permute-start(bf16[256,512]{1,0:T(8,128)(2,1)S(1)} %fusion.4.refs_0_), channel_id=1, source_target_pairs={{0,12},{4,0},{8,4},{12,8},{1,13},{5,1},{9,5},{13,9},{2,14},{6,2},{... | collective-permute-start | bytes 786440 | tf_op jit(solution)/shard_map/ppermute | solution.py:302
  58.0 0.4 collective-permute-done.10.refs_3_
  58.4 20.8 %collective-permute-done.9.refs_2_ = bf16[256,512]{1,0:T(8,128)(2,1)S(1)} collective-permute-done((bf16[256,512]{1,0:T(8,128)(2,1)S(1)}, bf16[256,512]{1,0:T(8,128)(2,1)S(1)}, u32[]{:S(2)}, u32[]{:S(2)}) %collective-permute-start.9) | collective-permute-done | bytes 262176 | tf_op jit(solution)/shard_map/ppermute | solution.py:302
  79.2 11.2 %back_project.1 = f32[4096,512]{1,0:T(8,128)} custom-call(s32[1]{0:T(128)} %bitcast.first_row, s32[8,128]{1,0:T(8,128)S(1)} %pad_add_fusion.rays, bf16[256,512]{1,0:T(8,128)(2,1)S(1)} %fusion.4.refs_0_, bf16[256,512]{1,0:T(8,128)(2,1)S(1)} %collective-permute-done.8.refs_1_, bf16[256,512]{1,0:T(8,128)(2,1)S(1)} %collective-permute-done.9.refs_2_, ...), custom_call_target="tpu_custom_call" | custom-call | flops 4294967296 | bytes 16777216 | tf_op jit(solution)/shard_map/back_project/pallas_call | solution.py:276
  (13 shorter events, 0.2 us)
Async XLA Ops:
  0.0 9.5 %copy-start.1 = (s32[256]{0:T(256)S(1)}, s32[256]{0:T(256)}, u32[]{:S(2)}) copy-start(s32[256]{0:T(256)} %param.8) | copy-start | bytes 3076
  0.1 0.7 copy-start
  0.8 0.7 copy-start.2
  9.5 17.3 %collective-permute-start.3 = (bf16[2,256,512]{2,1,0:T(8,128)(2,1)S(1)}, bf16[2,256,512]{2,1,0:T(8,128)(2,1)S(1)}, u32[]{:S(2)}, u32[]{:S(2)}) collective-permute-start(bf16[2,256,512]{2,1,0:T(8,128)(2,1)S(1)} %get-tuple-element.15), channel_id=1, source_target_pairs={{0,1},{1,0},{2,3},{3,2},{4,5},{5,4},{6,7},{7,6},{8,9},{9,8},{10,11... | collective-permute-start | bytes 1572872 | tf_op jit(solution)/shard_map/ppermute | solution.py:332
  9.5 3.6 %collective-permute-start.2 = (s32[2,128]{1,0:T(2,128)S(1)}, s32[2,128]{1,0:T(2,128)S(1)}, u32[]{:S(2)}, u32[]{:S(2)}) collective-permute-start(s32[2,128]{1,0:T(2,128)S(1)} %bitcast.15), channel_id=1, source_target_pairs={{0,4},{4,8},{8,12},{12,0},{1,5},{5,9},{9,13},{13,1},{2,6},{6,10},{... | collective-permute-start | bytes 3080 | tf_op jit(solution)/shard_map/ppermute | solution.py:302
  9.6 4.5 %collective-permute-start.1 = (s32[2,128]{1,0:T(2,128)S(1)}, s32[2,128]{1,0:T(2,128)S(1)}, u32[]{:S(2)}, u32[]{:S(2)}) collective-permute-start(s32[2,128]{1,0:T(2,128)S(1)} %bitcast.16), channel_id=1, source_target_pairs={{0,8},{4,12},{8,0},{12,4},{1,9},{5,13},{9,1},{13,5},{2,10},{6,14},... | collective-permute-start | bytes 3080 | tf_op jit(solution)/shard_map/ppermute | solution.py:302
  11.5 5.4 %collective-permute-start = (s32[2,128]{1,0:T(2,128)S(1)}, s32[2,128]{1,0:T(2,128)S(1)}, u32[]{:S(2)}, u32[]{:S(2)}) collective-permute-start(s32[2,128]{1,0:T(2,128)S(1)} %bitcast.17), channel_id=1, source_target_pairs={{0,12},{4,0},{8,4},{12,8},{1,13},{5,1},{9,5},{13,9},{2,14},{6,2},{... | collective-permute-start | bytes 3080 | tf_op jit(solution)/shard_map/ppermute | solution.py:302
  24.7 15.5 %collective-permute-start.5 = (bf16[256,512]{1,0:T(8,128)(2,1)S(1)}, bf16[256,512]{1,0:T(8,128)(2,1)S(1)}, u32[]{:S(2)}, u32[]{:S(2)}) collective-permute-start(bf16[256,512]{1,0:T(8,128)(2,1)S(1)} %get-tuple-element.18), channel_id=1, source_target_pairs={{0,4},{4,8},{8,12},{12,0},{1,5},{5,9},{9,13},{13,1},{2,6},{6,10},{... | collective-permute-start | bytes 786440 | tf_op jit(solution)/shard_map/ppermute | solution.py:302
  25.4 22.0 %collective-permute-start.6 = (bf16[256,512]{1,0:T(8,128)(2,1)S(1)}, bf16[256,512]{1,0:T(8,128)(2,1)S(1)}, u32[]{:S(2)}, u32[]{:S(2)}) collective-permute-start(bf16[256,512]{1,0:T(8,128)(2,1)S(1)} %get-tuple-element.19), channel_id=1, source_target_pairs={{0,8},{4,12},{8,0},{12,4},{1,9},{5,13},{9,1},{13,5},{2,10},{6,14},... | collective-permute-start | bytes 786440 | tf_op jit(solution)/shard_map/ppermute | solution.py:302
  25.4 22.0 %collective-permute-start.7 = (bf16[256,512]{1,0:T(8,128)(2,1)S(1)}, bf16[256,512]{1,0:T(8,128)(2,1)S(1)}, u32[]{:S(2)}, u32[]{:S(2)}) collective-permute-start(bf16[256,512]{1,0:T(8,128)(2,1)S(1)} %get-tuple-element.20), channel_id=1, source_target_pairs={{0,12},{4,0},{8,4},{12,8},{1,13},{5,1},{9,5},{13,9},{2,14},{6,2},{... | collective-permute-start | bytes 786440 | tf_op jit(solution)/shard_map/ppermute | solution.py:302
  26.8 20.6 %collective-permute-start.4 = (bf16[256,512]{1,0:T(8,128)(2,1)S(1)}, bf16[256,512]{1,0:T(8,128)(2,1)S(1)}, u32[]{:S(2)}, u32[]{:S(2)}) collective-permute-start(bf16[256,512]{1,0:T(8,128)(2,1)S(1)} %fusion.5), channel_id=1, source_target_pairs={{0,2},{1,3},{2,0},{3,1},{4,6},{5,7},{6,4},{7,5},{8,10},{9,11},{10,... | collective-permute-start | bytes 786440 | tf_op jit(solution)/shard_map/ppermute | solution.py:302
  47.7 10.7 %collective-permute-start.10 = (bf16[256,512]{1,0:T(8,128)(2,1)S(1)}, bf16[256,512]{1,0:T(8,128)(2,1)S(1)}, u32[]{:S(2)}, u32[]{:S(2)}) collective-permute-start(bf16[256,512]{1,0:T(8,128)(2,1)S(1)} %fusion.4.refs_0_), channel_id=1, source_target_pairs={{0,4},{4,8},{8,12},{12,0},{1,5},{5,9},{9,13},{13,1},{2,6},{6,10},{... | collective-permute-start | bytes 786440 | tf_op jit(solution)/shard_map/ppermute | solution.py:302
  47.8 31.4 %collective-permute-start.9 = (bf16[256,512]{1,0:T(8,128)(2,1)S(1)}, bf16[256,512]{1,0:T(8,128)(2,1)S(1)}, u32[]{:S(2)}, u32[]{:S(2)}) collective-permute-start(bf16[256,512]{1,0:T(8,128)(2,1)S(1)} %fusion.4.refs_0_), channel_id=1, source_target_pairs={{0,8},{4,12},{8,0},{12,4},{1,9},{5,13},{9,1},{13,5},{2,10},{6,14},... | collective-permute-start | bytes 786440 | tf_op jit(solution)/shard_map/ppermute | solution.py:302
  56.0 23.1 %collective-permute-start.8 = (bf16[256,512]{1,0:T(8,128)(2,1)S(1)}, bf16[256,512]{1,0:T(8,128)(2,1)S(1)}, u32[]{:S(2)}, u32[]{:S(2)}) collective-permute-start(bf16[256,512]{1,0:T(8,128)(2,1)S(1)} %fusion.4.refs_0_), channel_id=1, source_target_pairs={{0,12},{4,0},{8,4},{12,8},{1,13},{5,1},{9,5},{13,9},{2,14},{6,2},{... | collective-permute-start | bytes 786440 | tf_op jit(solution)/shard_map/ppermute | solution.py:302

commit v2 on v1

--- a/solution.py
+++ b/solution.py
@@ -12,7 +12,7 @@
 NIMG = 128
 HALF = (NIMG - 1) / 2.0
 LANES = 128
-VMEM_BYTES = 50 * 1024 * 1024
+MIB = 1024 * 1024
 F32 = jnp.float32
 BF16 = jnp.bfloat16
 
@@ -36,11 +36,11 @@
 
 
 def hat(distance):
-    return jnp.maximum(1.0 - jnp.abs(distance), 0.0).astype(BF16)
+    return jnp.maximum((1.0 - jnp.abs(distance)).astype(BF16), jnp.zeros((), BF16))
 
 
 def integrate_kernel(
-    nx, per_chunk, tile_bin, place, counts, frames, weights, send, keep_own, keep_rest, member, acc
+    nx, per_chunk, tile_bin, place, after, counts, frames, weights, send, keep_own, keep_rest, member, acc
 ):
     step = pl.program_id(0)
     points, slots = member.shape
@@ -81,12 +81,12 @@
                     keep_rest[e - 1, :, lanes] = acc[mine * per_chunk + j]
 
 
-def integrate(frames, counts, weights, tile_bin, place, nx, chans):
+def integrate(frames, counts, weights, tile_bin, place, after, nx, chans):
     slots, pixels = frames.shape
     points = counts.shape[0]
     nblocks, tile_pix, pair = weights.shape
     tile_bins = pair // 2
-    blocks = 8 if nblocks % 8 == 0 else 1
+    blocks = 16 if nblocks % 16 == 0 else 1
     channel_blocks = 2 * nx * chans // tile_bins
     whole = lambda shape: pl.BlockSpec(shape, lambda i, *_: (0,) * len(shape))
     return pl.pallas_call(
@@ -95,6 +95,7 @@
             num_scalar_prefetch=2,
             grid=(nblocks // blocks,),
             in_specs=[
+                pl.BlockSpec(memory_space=pl.ANY),
                 whole((1, points)),
                 pl.BlockSpec((slots, blocks * tile_pix), lambda i, *_: (0, i)),
                 pl.BlockSpec((blocks, tile_pix, pair), lambda i, *_: (i, 0, 0)),
@@ -114,21 +115,27 @@
             jax.ShapeDtypeStruct((points, chans), F32),
             jax.ShapeDtypeStruct((nx - 1, points, chans), F32),
         ],
-        compiler_params=pltpu.CompilerParams(vmem_limit_bytes=VMEM_BYTES),
+        compiler_params=pltpu.CompilerParams(vmem_limit_bytes=24 * MIB),
         cost_estimate=pl.CostEstimate(
             flops=2 * points * pixels * (slots + pair),
             bytes_accessed=2 * (slots * pixels + pixels * pair),
             transcendentals=0,
         ),
         name="integrate",
-    )(tile_bin, place, counts.reshape(1, points), frames, weights)
+    )(tile_bin, place, after, counts.reshape(1, points), frames, weights)
 
 
 def project_kernel(angles, parts, first_row, rays, image, *refs):
-    outs, (cosine, base, tile, total) = refs[:parts], refs[parts:]
+    outs, (cosine, base, tile_a, tile_b, total) = refs[:parts], refs[parts:]
     step = pl.program_id(0)
-    rows = tile.shape[1] // LANES
+    rows = tile_a.shape[1] // LANES
+    half = rows * LANES
     points = total.shape[0] // parts
+
+    def fill(tile, first):
+        for i in range(rows):
+            upos = (first + i).astype(F32) - HALF
+            tile[:, i * LANES : (i + 1) * LANES] = hat(base[...] + cosine[...] * upos)
 
     @pl.when(step == 0)
     def _():
@@ -140,11 +147,13 @@
             column = lambda x: jnp.transpose(jnp.broadcast_to(x[k : k + 1, :], (LANES, LANES)))
             cosine[here, :] = column(cos_c)
             base[here, :] = column(sin_c) * vpos - column(off_c)
-
-    for i in range(rows):
-        upos = (first_row[0] + step * rows + i).astype(F32) - HALF
-        tile[:, i * LANES : (i + 1) * LANES] = hat(base[...] + cosine[...] * upos)
-    total[...] += jnp.dot(tile[...], image[...].astype(BF16), preferred_element_type=F32)
+        fill(tile_a, first_row[0])
+
+    now = first_row[0] + step * (2 * rows)
+    fill(tile_b, now + rows)
+    total[...] += jnp.dot(tile_a[...], image[:half, :].astype(BF16), preferred_element_type=F32)
+    fill(tile_a, now + 2 * rows)
+    total[...] += jnp.dot(tile_b[...], image[half:, :].astype(BF16), preferred_element_type=F32)
 
     @pl.when(step == pl.num_programs(0) - 1)
     def _():
@@ -156,29 +165,30 @@
     cells, chans = image.shape
     all_points = rays.shape[0] * LANES
     points = all_points // parts
-    rows = min(8, cells // LANES)
+    rows = min(4, cells // LANES // 2)
     out = pl.BlockSpec((points, chans), lambda i, *_: (0, 0))
     return pl.pallas_call(
         functools.partial(project_kernel, angles, parts),
         grid_spec=pltpu.PrefetchScalarGridSpec(
             num_scalar_prefetch=1,
-            grid=(cells // (rows * LANES),),
+            grid=(cells // (2 * rows * LANES),),
             in_specs=[
                 pl.BlockSpec(rays.shape, lambda i, *_: (0, 0)),
-                pl.BlockSpec((rows * LANES, chans), lambda i, *_: (i, 0)),
+                pl.BlockSpec((2 * rows * LANES, chans), lambda i, *_: (i, 0)),
             ],
             out_specs=[out] * parts,
             scratch_shapes=[
                 pltpu.VMEM((all_points, LANES), F32),
                 pltpu.VMEM((all_points, LANES), F32),
                 pltpu.VMEM((all_points, rows * LANES), BF16),
+                pltpu.VMEM((all_points, rows * LANES), BF16),
                 pltpu.VMEM((all_points, chans), F32),
             ],
         ),
         out_shape=[
             jax.ShapeDtypeStruct((points, chans), F32 if d == 0 else BF16) for d in range(parts)
         ],
-        compiler_params=pltpu.CompilerParams(vmem_limit_bytes=VMEM_BYTES),
+        compiler_params=pltpu.CompilerParams(vmem_limit_bytes=32 * MIB),
         cost_estimate=pl.CostEstimate(
             flops=2 * all_points * cells * chans, bytes_accessed=4 * cells * chans, transcendentals=0
         ),
@@ -186,10 +196,8 @@
     )(first_row, rays, image)
 
 
-def totals_kernel(angles, first_row, rays, row_total, col_recip):
-    cos_tab, sin_tab = angle_tables(angles)
+def row_total_kernel(angles, after, rays, row_total):
     cos_r, sin_r, off_r = ray_geometry(rays[...], angles)
-    lane = lax.broadcasted_iota(jnp.int32, (LANES, LANES), 1).astype(F32) - HALF
     vpos = lax.broadcasted_iota(jnp.int32, (LANES, LANES), 0).astype(F32) - HALF
     for k in range(rays.shape[0]):
         base = sin_r[k : k + 1, :] * vpos - off_r[k : k + 1, :]
@@ -205,42 +213,27 @@
             jnp.broadcast_to(total, (LANES, LANES))
         )
 
-    def column_row(i, carry):
-        upos = (first_row[0] + i).astype(F32) - HALF
-        sums = jnp.zeros((LANES, LANES), F32)
-        for a in range(angles):
-            sums += hat((sin_tab[a] * vpos - lane) + cos_tab[a] * upos).astype(F32)
-        total = jnp.sum(sums, axis=1, keepdims=True)
-        start = pl.multiple_of(i * LANES, LANES)
-        col_recip[pl.ds(start, LANES), :] = jnp.broadcast_to(1.0 / total, (LANES, LANES))
-        return carry
-
-    lax.fori_loop(0, col_recip.shape[0] // LANES, column_row, 0)
-
-
-def totals(rays, first_row, cells, angles):
+
+def row_totals(rays, angles, after):
     points = rays.shape[0] * LANES
     vmem = pl.BlockSpec(memory_space=pltpu.VMEM)
     return pl.pallas_call(
-        functools.partial(totals_kernel, angles),
-        in_specs=[pl.BlockSpec(memory_space=pltpu.SMEM), vmem],
-        out_specs=[vmem, vmem],
-        out_shape=[
-            jax.ShapeDtypeStruct((points, LANES), F32),
-            jax.ShapeDtypeStruct((cells, LANES), F32),
-        ],
-        compiler_params=pltpu.CompilerParams(vmem_limit_bytes=VMEM_BYTES),
-        cost_estimate=pl.CostEstimate(
-            flops=8 * points * NIMG * NIMG * 8, bytes_accessed=4 * cells * LANES, transcendentals=0
-        ),
-        name="totals",
-    )(first_row, rays)
-
-
-def back_kernel(angles, parts, first_row, rays, *refs):
-    residuals, (image, recip, out, base, cosine, joined, tile) = refs[:parts], refs[parts:]
+        functools.partial(row_total_kernel, angles),
+        in_specs=[pl.BlockSpec(memory_space=pl.ANY), vmem],
+        out_specs=vmem,
+        out_shape=jax.ShapeDtypeStruct((points, LANES), F32),
+        compiler_params=pltpu.CompilerParams(vmem_limit_bytes=8 * MIB),
+        cost_estimate=pl.CostEstimate(
+            flops=8 * points * NIMG * NIMG, bytes_accessed=4 * points * LANES, transcendentals=0
+        ),
+        name="row_totals",
+    )(after, rays)
+
+
+def prepare_kernel(angles, first_row, rays, residual, image, tile, recip, partial, base, cosine):
     step = pl.program_id(0)
-    points, chans = residuals[0].shape
+    chunks = rays.shape[0]
+    points, chans = residual.shape
     rows = tile.shape[0] // LANES
 
     @pl.when(step == 0)
@@ -248,54 +241,94 @@
         cos_c, sin_c, off_c = ray_geometry(rays[...], angles)
         cosine[...] = cos_c
         vpos = lax.broadcasted_iota(jnp.int32, (LANES, LANES), 0).astype(F32) - HALF
-        for k in range(rays.shape[0]):
+        for k in range(chunks):
             base[:, k * LANES : (k + 1) * LANES] = sin_c[k : k + 1, :] * vpos - off_c[k : k + 1, :]
-        for d in range(parts):
-            joined[d * points : (d + 1) * points, :] = residuals[d][...]
 
     for i in range(rows):
+        here = slice(i * LANES, (i + 1) * LANES)
         upos = (first_row[0] + step * rows + i).astype(F32) - HALF
-        for k in range(rays.shape[0]):
+        sums = jnp.zeros((LANES, LANES), F32)
+        for k in range(chunks):
             lanes = slice(k * LANES, (k + 1) * LANES)
-            shift = cosine[k : k + 1, :] * upos
-            tile[i * LANES : (i + 1) * LANES, lanes] = hat(base[:, lanes] + shift)
-    back = jnp.dot(tile[...], joined[...], preferred_element_type=F32)
+            value = hat(base[:, lanes] + cosine[k : k + 1, :] * upos)
+            tile[here, lanes] = value
+            sums += value.astype(F32)
+        total = jnp.sum(sums, axis=1, keepdims=True)
+        recip[here, :] = jnp.broadcast_to(1.0 / total, (LANES, LANES))
+    back = jnp.dot(tile[:, :points], residual[...], preferred_element_type=F32)
     for j in range(chans // LANES):
         lanes = slice(j * LANES, (j + 1) * LANES)
-        out[:, lanes] = image[:, lanes] + back[:, lanes] * recip[...]
-
-
-def back_project(rays, residuals, image, recip, first_row, angles):
+        partial[:, lanes] = image[:, lanes] + back[:, lanes] * recip[...]
+
+
+def prepare(rays, residual, image, first_row, angles):
     cells, chans = image.shape
-    parts = len(residuals)
-    points = residuals[0].shape[0]
-    all_points = parts * points
+    all_points = rays.shape[0] * LANES
     rows = min(4, cells // LANES)
     fixed = lambda shape: pl.BlockSpec(shape, lambda i, *_: (0, 0))
     sliding = lambda width: pl.BlockSpec((rows * LANES, width), lambda i, *_: (i, 0))
     return pl.pallas_call(
-        functools.partial(back_kernel, angles, parts),
+        functools.partial(prepare_kernel, angles),
         grid_spec=pltpu.PrefetchScalarGridSpec(
             num_scalar_prefetch=1,
             grid=(cells // (rows * LANES),),
-            in_specs=[fixed(rays.shape)]
-            + [fixed((points, chans))] * parts
-            + [sliding(chans), sliding(LANES)],
-            out_specs=sliding(chans),
-            scratch_shapes=[
-                pltpu.VMEM((LANES, all_points), F32),
-                pltpu.VMEM(rays.shape, F32),
-                pltpu.VMEM((all_points, chans), BF16),
-                pltpu.VMEM((rows * LANES, all_points), BF16),
-            ],
-        ),
+            in_specs=[fixed(rays.shape), fixed(residual.shape), sliding(chans)],
+            out_specs=[sliding(all_points), sliding(LANES), sliding(chans)],
+            scratch_shapes=[pltpu.VMEM((LANES, all_points), F32), pltpu.VMEM(rays.shape, F32)],
+        ),
+        out_shape=[
+            jax.ShapeDtypeStruct((cells, all_points), BF16),
+            jax.ShapeDtypeStruct((cells, LANES), F32),
+            jax.ShapeDtypeStruct((cells, chans), F32),
+        ],
+        compiler_params=pltpu.CompilerParams(vmem_limit_bytes=16 * MIB),
+        cost_estimate=pl.CostEstimate(
+            flops=2 * all_points * cells * chans, bytes_accessed=8 * cells * chans, transcendentals=0
+        ),
+        name="prepare",
+    )(first_row, rays, residual, image)
+
+
+def back_kernel(parts, *refs):
+    residuals, (tile, recip, partial, out, joined) = refs[:parts], refs[parts:]
+    step = pl.program_id(0)
+    points, chans = residuals[0].shape
+    rows = out.shape[0]
+
+    @pl.when(step == 0)
+    def _():
+        for d in range(parts):
+            joined[d * points : (d + 1) * points, :] = residuals[d][...]
+
+    here = pl.ds(pl.multiple_of(step * rows, rows), rows)
+    back = jnp.dot(tile[here, points:], joined[...], preferred_element_type=F32)
+    scale = recip[here, :]
+    for j in range(chans // LANES):
+        lanes = slice(j * LANES, (j + 1) * LANES)
+        out[:, lanes] = partial[here, lanes] + back[:, lanes] * scale
+
+
+def back_project(residuals, tile, recip, partial):
+    cells, chans = partial.shape
+    parts = len(residuals)
+    points = residuals[0].shape[0]
+    rows = min(1024, cells)
+    vmem = pl.BlockSpec(memory_space=pltpu.VMEM)
+    return pl.pallas_call(
+        functools.partial(back_kernel, parts),
+        grid=(cells // rows,),
+        in_specs=[vmem] * (parts + 3),
+        out_specs=pl.BlockSpec((rows, chans), lambda i: (i, 0)),
+        scratch_shapes=[pltpu.VMEM((parts * points, chans), BF16)],
         out_shape=jax.ShapeDtypeStruct((cells, chans), F32),
-        compiler_params=pltpu.CompilerParams(vmem_limit_bytes=VMEM_BYTES),
-        cost_estimate=pl.CostEstimate(
-            flops=2 * all_points * cells * chans, bytes_accessed=8 * cells * chans, transcendentals=0
+        compiler_params=pltpu.CompilerParams(vmem_limit_bytes=32 * MIB),
+        cost_estimate=pl.CostEstimate(
+            flops=2 * parts * points * cells * chans,
+            bytes_accessed=4 * cells * chans,
+            transcendentals=0,
         ),
         name="back_project",
-    )(first_row, rays, *residuals, image, recip)
+    )(*residuals, tile, recip, partial)
 
 
 def rotate(x, axis, shift, n):
@@ -326,7 +359,7 @@
         place += [2 * xi + 1 - core_me, 2 * xi + core_me]
     place = jnp.stack(place).astype(jnp.int32)
     send, keep_own, keep_rest = integrate(
-        frames, counts, channel_pair_weights, tile_bin, place, nx, chans
+        frames, counts, channel_pair_weights, tile_bin, place, shares[0], nx, chans
     )
     partner = [(i, i ^ 1) for i in range(n_chan)]
     got = lax.ppermute(send, "chan", partner)
@@ -335,13 +368,14 @@
         joined = (keep_rest[e - 1] + got[e].astype(F32)).astype(BF16)
         pattern = pattern + rotate(joined, "chan", 2 * e, n_chan).astype(F32)
 
-    row_total, col_recip = totals(own_rays, first_row, cells, angles)
+    row_total = row_totals(own_rays, angles, keep_own)
     projected = shares[0]
     for part in arrived:
         projected = projected + part.astype(F32)
     residual = ((pattern * float(NIMG) - projected) / row_total[:, :1]).astype(BF16)
-    residuals = [residual] + [rotate(residual, "scan", -d, n_scan) for d in range(1, n_scan)]
-    return back_project(all_rays, residuals, image, col_recip, first_row, angles)
+    others = [rotate(residual, "scan", -d, n_scan) for d in range(1, n_scan)]
+    tile, col_recip, partial = prepare(all_rays, residual, image, first_row, angles)
+    return back_project(others, tile, col_recip, partial)
 
 
 def solution(mesh):

time: 90.9 us -> 79.7 us (0.88)
  Pallas kernels: 38.6 us -> 26.9 us
  local copies, waits for them, and re-layouts: 1.47 us -> 6.9 us
  starting transfers between devices: 16.4 us -> 11 us
    pallas_call x2 -> x3, Pallas kernels: 22.8 us -> 15.5 us  [the longest x1 5.77 us: prepare(): pl.pallas_call(functools.partial(prepare_kernel, angles), grid_spec=pltpu...]
    unnamed x6 -> x16, local copies, waits for them, and re-layouts: 1.34 us -> 6.79 us
    ppermute x10, starting transfers between devices: 16.3 us -> 11 us  [rotate(): return lax.ppermute(x, axis, [(i, (i + shift) % n) for i in range(n)])]
    pallas_call x1, Pallas kernels: 8.03 us -> 5.45 us  [integrate(): pl.pallas_call(functools.partial(integrate_kernel, nx, chans // tile_bins...]
    pallas_call x1, Pallas kernels: 7.76 us -> 6 us  [project(): pl.pallas_call(functools.partial(project_kernel, angles, parts), grid_spe...]
  transfers between devices with their start and end apart: 11 -> 11, of which waited for: 6 -> 6; matrix products, arithmetic and copies ran while one was open for 0% -> 0% of each run, Pallas kernels for 21% -> 12%
where the time goes in v2:
time: 79.7 us; the launch traced here: 79.5 us
  waiting for transfers between devices  33.4 us (42%)
  Pallas kernels  26.9 us (34%)
  starting transfers between devices  11 us (14%)
  local copies, waits for them, and re-layouts  6.9 us (9%)
  other arithmetic  1.11 us (1%)
    ppermute x10, waiting for transfers between devices, rotate(): return lax.ppermute(x, axis, [(i, (i + shift) % n) for i in range(n)])  33.4 us
    ppermute x10, starting transfers between devices, rotate(): return lax.ppermute(x, axis, [(i, (i + shift) % n) for i in range(n)])  11 us
    unnamed x16, local copies, waits for them, and re-layouts  6.79 us
    pallas_call x1, Pallas kernels, project(): pl.pallas_call(functools.partial(project_kernel, angles, parts), grid_spe...  6 us
    pallas_call x1, Pallas kernels, prepare(): pl.pallas_call(functools.partial(prepare_kernel, angles), grid_spec=pltpu...  5.77 us
    pallas_call x1, Pallas kernels, back_project(): pl.pallas_call(functools.partial(back_kernel, parts), grid=(cells // rows...  5.65 us
    pallas_call x1, Pallas kernels, integrate(): pl.pallas_call(functools.partial(integrate_kernel, nx, chans // tile_bins...  5.45 us
    pallas_call x1, Pallas kernels, row_totals(): pl.pallas_call(functools.partial(row_total_kernel, angles), in_specs=[pl....  4.06 us
  transfers between devices with their start and end apart: 11, of which 6 were waited for; matrix products, arithmetic and copies ran while one was open for 0% of the time, Pallas kernels for 12%

profile of v2, /device:TPU:24, one launch (start us, length us, event | category | flops | bytes accessed | tf_op | source)
XLA Modules:
  0.0 79.5 jit_solution(14991720298667022938)
XLA Ops:
  0.1 1.9 %collective-permute-start.1 = (s32[2,128]{1,0:T(2,128)}, s32[2,128]{1,0:T(2,128)S(1)}, u32[]{:S(2)}, u32[]{:S(2)}) collective-permute-start(s32[2,128]{1,0:T(2,128)} %bitcast.17), channel_id=1, source_target_pairs={{0,8},{4,12},{8,0},{12,4},{1,9},{5,13},{9,1},{13,5},{2,10},{6,14},... | collective-permute-start | bytes 3080 | tf_op jit(solution)/shard_map/ppermute | solution.py:335
  2.0 0.4 collective-permute-start
  2.5 1.3 %collective-permute-done.2 = s32[2,128]{1,0:T(2,128)S(1)} collective-permute-done((s32[2,128]{1,0:T(2,128)}, s32[2,128]{1,0:T(2,128)S(1)}, u32[]{:S(2)}, u32[]{:S(2)}) %collective-permute-start.2) | collective-permute-done | bytes 1056 | tf_op jit(solution)/shard_map/ppermute | solution.py:335
  3.8 1.0 %collective-permute-done.1 = s32[2,128]{1,0:T(2,128)S(1)} collective-permute-done((s32[2,128]{1,0:T(2,128)}, s32[2,128]{1,0:T(2,128)S(1)}, u32[]{:S(2)}, u32[]{:S(2)}) %collective-permute-start.1) | collective-permute-done | bytes 1056 | tf_op jit(solution)/shard_map/ppermute | solution.py:335
  4.8 2.7 %collective-permute-done = s32[2,128]{1,0:T(2,128)S(1)} collective-permute-done((s32[2,128]{1,0:T(2,128)}, s32[2,128]{1,0:T(2,128)S(1)}, u32[]{:S(2)}, u32[]{:S(2)}) %collective-permute-start) | collective-permute-done | bytes 1056 | tf_op jit(solution)/shard_map/ppermute | solution.py:335
  7.6 0.7 pad_add_fusion.rays
  8.2 3.4 %copy-done.4 = f32[4096,512]{1,0:T(8,128)S(1)} copy-done((f32[4096,512]{1,0:T(8,128)S(1)}, f32[4096,512]{1,0:T(8,128)}, u32[]{:S(2)}) %copy-start.4) | copy-done | bytes 8388632
  11.6 6.0 %project.1 = (f32[256,512]{1,0:T(8,128)S(1)}, bf16[256,512]{1,0:T(8,128)(2,1)S(1)}, bf16[256,512]{1,0:T(8,128)(2,1)S(1)}, bf16[256,512]{1,0:T(8,128)(2,1)S(1)}) custom-call(s32[1]{0:T(128)} %bitcast.4.first_row, s32[8,128]{1,0:T(8,128)S(1)} %pad_add_fusion.rays, f32[4096,512]{1,0:T(8,128)S(1)} %copy-done.4), custom_call_target="tpu_custom_call" | custom-call | flops 4294967296 | bytes 8388608 | tf_op jit(solution)/shard_map/project/pallas_call | solution.py:170
  17.7 5.4 %integrate.1 = (bf16[2,256,512]{2,1,0:T(8,128)(2,1)S(1)}, f32[256,512]{1,0:T(8,128)S(1)}, f32[1,256,512]{2,1,0:T(8,128)S(1)}) custom-call(s32[48]{0:T(128)S(1)} %copy-done.3, s32[4]{0:T(128)S(1)} %pad_add_fusion.1.place, f32[256,512]{1,0:T(8,128)S(1)} %get-tuple-element.15.after, s32[1,256]{1,0:T(1,128)S(1)} %bitcast.21, bf16[384,6144]{1,0:T(8,128)(2,1)S(1)} %bitcast.15, ...), custom_call_target="tpu_custom_call" | custom-call | flops 2013265920 | bytes 7864320 | tf_op jit(solution)/shard_map/integrate/pallas_call | solution.py:92
  23.2 0.7 collective-permute-start.5
  24.0 1.3 %collective-permute-start.7 = (bf16[256,512]{1,0:T(8,128)(2,1)S(1)}, bf16[256,512]{1,0:T(8,128)(2,1)S(1)}, u32[]{:S(2)}, u32[]{:S(2)}) collective-permute-start(bf16[256,512]{1,0:T(8,128)(2,1)S(1)} %get-tuple-element.21), channel_id=1, source_target_pairs={{0,12},{4,0},{8,4},{12,8},{1,13},{5,1},{9,5},{13,9},{2,14},{6,2},{... | collective-permute-start | bytes 786440 | tf_op jit(solution)/shard_map/ppermute | solution.py:335
  25.3 0.1 fusion.5
  25.4 1.5 %collective-permute-start.4 = (bf16[256,512]{1,0:T(8,128)(2,1)S(1)}, bf16[256,512]{1,0:T(8,128)(2,1)S(1)}, u32[]{:S(2)}, u32[]{:S(2)}) collective-permute-start(bf16[256,512]{1,0:T(8,128)(2,1)S(1)} %fusion.5), channel_id=1, source_target_pairs={{0,2},{1,3},{2,0},{3,1},{4,6},{5,7},{6,4},{7,5},{8,10},{9,11},{10,... | collective-permute-start | bytes 786440 | tf_op jit(solution)/shard_map/ppermute | solution.py:335
  27.0 4.1 %row_totals.1 = f32[256,128]{1,0:T(8,128)S(1)} custom-call(f32[256,512]{1,0:T(8,128)S(1)} %get-tuple-element.16.after, s32[2,128]{1,0:T(2,128)S(1)} %bitcast.20), custom_call_target="tpu_custom_call" | custom-call | flops 33554432 | bytes 131072 | tf_op jit(solution)/shard_map/row_totals/pallas_call | solution.py:220
  31.0 0.1 slice_reduce_fusion
  31.1 1.2 %collective-permute-done.5 = bf16[256,512]{1,0:T(8,128)(2,1)S(1)} collective-permute-done((bf16[256,512]{1,0:T(8,128)(2,1)S(1)}, bf16[256,512]{1,0:T(8,128)(2,1)S(1)}, u32[]{:S(2)}, u32[]{:S(2)}) %collective-permute-start.5) | collective-permute-done | bytes 262176 | tf_op jit(solution)/shard_map/ppermute | solution.py:335
  32.4 15.1 %collective-permute-done.6 = bf16[256,512]{1,0:T(8,128)(2,1)S(1)} collective-permute-done((bf16[256,512]{1,0:T(8,128)(2,1)S(1)}, bf16[256,512]{1,0:T(8,128)(2,1)S(1)}, u32[]{:S(2)}, u32[]{:S(2)}) %collective-permute-start.6) | collective-permute-done | bytes 262176 | tf_op jit(solution)/shard_map/ppermute | solution.py:335
  47.5 0.3 fusion.4.residual
  47.8 2.9 %collective-permute-start.9 = (bf16[256,512]{1,0:T(8,128)(2,1)S(1)}, bf16[256,512]{1,0:T(8,128)(2,1)S(1)}, u32[]{:S(2)}, u32[]{:S(2)}) collective-permute-start(bf16[256,512]{1,0:T(8,128)(2,1)S(1)} %fusion.4.residual), channel_id=1, source_target_pairs={{0,8},{4,12},{8,0},{12,4},{1,9},{5,13},{9,1},{13,5},{2,10},{6,14},... | collective-permute-start | bytes 786440 | tf_op jit(solution)/shard_map/ppermute | solution.py:335
  50.7 1.9 %collective-permute-start.8 = (bf16[256,512]{1,0:T(8,128)(2,1)S(1)}, bf16[256,512]{1,0:T(8,128)(2,1)S(1)}, u32[]{:S(2)}, u32[]{:S(2)}) collective-permute-start(bf16[256,512]{1,0:T(8,128)(2,1)S(1)} %fusion.4.residual), channel_id=1, source_target_pairs={{0,12},{4,0},{8,4},{12,8},{1,13},{5,1},{9,5},{13,9},{2,14},{6,2},{... | collective-permute-start | bytes 786440 | tf_op jit(solution)/shard_map/ppermute | solution.py:335
  52.7 3.4 %copy-done.5 = f32[4096,512]{1,0:T(8,128)S(1)} copy-done((f32[4096,512]{1,0:T(8,128)S(1)}, f32[4096,512]{1,0:T(8,128)}, u32[]{:S(2)}) %copy-start.5) | copy-done | bytes 8388632
  56.0 5.8 %prepare.1 = (bf16[4096,1024]{1,0:T(8,128)(2,1)S(1)}, f32[4096,128]{1,0:T(8,128)S(1)}, f32[4096,512]{1,0:T(8,128)S(1)}) custom-call(s32[1]{0:T(128)} %bitcast.4.first_row, s32[8,128]{1,0:T(8,128)S(1)} %pad_add_fusion.rays, bf16[256,512]{1,0:T(8,128)(2,1)S(1)} %fusion.4.residual, f32[4096,512]{1,0:T(8,128)S(1)} %copy-done.5), custom_call_target="tpu_custom_call" | custom-call | flops 4294967296 | bytes 16777216 | tf_op jit(solution)/shard_map/prepare/pallas_call | solution.py:270
  61.8 12.0 %collective-permute-done.9.refs_1_ = bf16[256,512]{1,0:T(8,128)(2,1)S(1)} collective-permute-done((bf16[256,512]{1,0:T(8,128)(2,1)S(1)}, bf16[256,512]{1,0:T(8,128)(2,1)S(1)}, u32[]{:S(2)}, u32[]{:S(2)}) %collective-permute-start.9) | collective-permute-done | bytes 262176 | tf_op jit(solution)/shard_map/ppermute | solution.py:335
  73.9 5.6 %back_project.1 = f32[4096,512]{1,0:T(8,128)} custom-call(bf16[256,512]{1,0:T(8,128)(2,1)S(1)} %collective-permute-done.8.refs_0_, bf16[256,512]{1,0:T(8,128)(2,1)S(1)} %collective-permute-done.9.refs_1_, bf16[256,512]{1,0:T(8,128)(2,1)S(1)} %collective-permute-done.10.refs_2_, bf16[4096,1024]{1,0:T(8,128)(2,1)S(1)} %get-tuple-element.22.refs_3_, ...), custom_call_target="tpu_custom_call" | custom-call | flops 3221225472 | bytes 8388608 | tf_op jit(solution)/shard_map/back_project/pallas_call | solution.py:317
  (25 shorter events, 0.3 us)
Async XLA Ops:
  0.0 17.6 %copy-start.3 = (s32[48]{0:T(128)S(1)}, s32[48]{0:T(128)}, u32[]{:S(2)}) copy-start(s32[48]{0:T(128)} %tile_bin.1) | copy-start | bytes 580
  0.0 17.7 %copy-start.2 = (s32[256]{0:T(256)S(1)}, s32[256]{0:T(256)}, u32[]{:S(2)}) copy-start(s32[256]{0:T(256)} %param.7) | copy-start | bytes 3076
  0.0 17.7 %slice-start = ((s8[4718592]{0:T(1024)(128)(4,1)}), s8[524288]{0:T(1024)(128)(4,1)S(1)}, s32[]{:S(2)}) async-start(s8[4718592]{0:T(1024)(128)(4,1)} %bitcast.14), calls=%async_computation | async-start | bytes 1048576
  0.0 3.8 %collective-permute-start.2 = (s32[2,128]{1,0:T(2,128)}, s32[2,128]{1,0:T(2,128)S(1)}, u32[]{:S(2)}, u32[]{:S(2)}) collective-permute-start(s32[2,128]{1,0:T(2,128)} %bitcast.16), channel_id=1, source_target_pairs={{0,4},{4,8},{8,12},{12,0},{1,5},{5,9},{9,13},{13,1},{2,6},{6,10},{... | collective-permute-start | bytes 3080 | tf_op jit(solution)/shard_map/ppermute | solution.py:335
  0.1 4.7 %collective-permute-start.1 = (s32[2,128]{1,0:T(2,128)}, s32[2,128]{1,0:T(2,128)S(1)}, u32[]{:S(2)}, u32[]{:S(2)}) collective-permute-start(s32[2,128]{1,0:T(2,128)} %bitcast.17), channel_id=1, source_target_pairs={{0,8},{4,12},{8,0},{12,4},{1,9},{5,13},{9,1},{13,5},{2,10},{6,14},... | collective-permute-start | bytes 3080 | tf_op jit(solution)/shard_map/ppermute | solution.py:335
  2.0 5.6 %collective-permute-start = (s32[2,128]{1,0:T(2,128)}, s32[2,128]{1,0:T(2,128)S(1)}, u32[]{:S(2)}, u32[]{:S(2)}) collective-permute-start(s32[2,128]{1,0:T(2,128)} %bitcast.18), channel_id=1, source_target_pairs={{0,12},{4,0},{8,4},{12,8},{1,13},{5,1},{9,5},{13,9},{2,14},{6,2},{... | collective-permute-start | bytes 3080 | tf_op jit(solution)/shard_map/ppermute | solution.py:335
  2.5 15.2 %copy-start = (bf16[48,128,256]{2,1,0:T(8,128)(2,1)S(1)}, bf16[48,128,256]{2,1,0:T(8,128)(2,1)}, u32[]{:S(2)}) copy-start(bf16[48,128,256]{2,1,0:T(8,128)(2,1)} %weights.1) | copy-start | bytes 9437188
  8.2 3.4 %copy-start.4 = (f32[4096,512]{1,0:T(8,128)S(1)}, f32[4096,512]{1,0:T(8,128)}, u32[]{:S(2)}) copy-start(f32[4096,512]{1,0:T(8,128)} %image.3) | copy-start | bytes 25165828
  11.6 6.1 %slice-start.1 = ((s8[4718592]{0:T(1024)(128)(4,1)}), s8[4194304]{0:T(1024)(128)(4,1)S(1)}, s32[]{:S(2)}) async-start(s8[4718592]{0:T(1024)(128)(4,1)} %bitcast.14), calls=%async_computation.1 | async-start | bytes 8388608
  17.6 9.3 %copy-start.1 = (s32[256]{0:T(256)S(1)}, s32[256]{0:T(256)}, u32[]{:S(2)}) copy-start(s32[256]{0:T(256)} %param.8) | copy-start | bytes 3076
  23.2 2.2 %collective-permute-start.3 = (bf16[2,256,512]{2,1,0:T(8,128)(2,1)S(1)}, bf16[2,256,512]{2,1,0:T(8,128)(2,1)S(1)}, u32[]{:S(2)}, u32[]{:S(2)}) collective-permute-start(bf16[2,256,512]{2,1,0:T(8,128)(2,1)S(1)} %get-tuple-element.17), channel_id=1, source_target_pairs={{0,1},{1,0},{2,3},{3,2},{4,5},{5,4},{6,7},{7,6},{8,9},{9,8},{10,11... | collective-permute-start | bytes 1572872 | tf_op jit(solution)/shard_map/ppermute | solution.py:365
  23.2 9.1 %collective-permute-start.5 = (bf16[256,512]{1,0:T(8,128)(2,1)S(1)}, bf16[256,512]{1,0:T(8,128)(2,1)S(1)}, u32[]{:S(2)}, u32[]{:S(2)}) collective-permute-start(bf16[256,512]{1,0:T(8,128)(2,1)S(1)} %get-tuple-element.19), channel_id=1, source_target_pairs={{0,4},{4,8},{8,12},{12,0},{1,5},{5,9},{9,13},{13,1},{2,6},{6,10},{... | collective-permute-start | bytes 786440 | tf_op jit(solution)/shard_map/ppermute | solution.py:335
  24.0 23.5 %collective-permute-start.6 = (bf16[256,512]{1,0:T(8,128)(2,1)S(1)}, bf16[256,512]{1,0:T(8,128)(2,1)S(1)}, u32[]{:S(2)}, u32[]{:S(2)}) collective-permute-start(bf16[256,512]{1,0:T(8,128)(2,1)S(1)} %get-tuple-element.20), channel_id=1, source_target_pairs={{0,8},{4,12},{8,0},{12,4},{1,9},{5,13},{9,1},{13,5},{2,10},{6,14},... | collective-permute-start | bytes 786440 | tf_op jit(solution)/shard_map/ppermute | solution.py:335
  24.0 23.5 %collective-permute-start.7 = (bf16[256,512]{1,0:T(8,128)(2,1)S(1)}, bf16[256,512]{1,0:T(8,128)(2,1)S(1)}, u32[]{:S(2)}, u32[]{:S(2)}) collective-permute-start(bf16[256,512]{1,0:T(8,128)(2,1)S(1)} %get-tuple-element.21), channel_id=1, source_target_pairs={{0,12},{4,0},{8,4},{12,8},{1,13},{5,1},{9,5},{13,9},{2,14},{6,2},{... | collective-permute-start | bytes 786440 | tf_op jit(solution)/shard_map/ppermute | solution.py:335
  25.4 22.1 %collective-permute-start.4 = (bf16[256,512]{1,0:T(8,128)(2,1)S(1)}, bf16[256,512]{1,0:T(8,128)(2,1)S(1)}, u32[]{:S(2)}, u32[]{:S(2)}) collective-permute-start(bf16[256,512]{1,0:T(8,128)(2,1)S(1)} %fusion.5), channel_id=1, source_target_pairs={{0,2},{1,3},{2,0},{3,1},{4,6},{5,7},{6,4},{7,5},{8,10},{9,11},{10,... | collective-permute-start | bytes 786440 | tf_op jit(solution)/shard_map/ppermute | solution.py:335
  47.7 14.1 %collective-permute-start.10 = (bf16[256,512]{1,0:T(8,128)(2,1)S(1)}, bf16[256,512]{1,0:T(8,128)(2,1)S(1)}, u32[]{:S(2)}, u32[]{:S(2)}) collective-permute-start(bf16[256,512]{1,0:T(8,128)(2,1)S(1)} %fusion.4.residual), channel_id=1, source_target_pairs={{0,4},{4,8},{8,12},{12,0},{1,5},{5,9},{9,13},{13,1},{2,6},{6,10},{... | collective-permute-start | bytes 786440 | tf_op jit(solution)/shard_map/ppermute | solution.py:335
  47.8 26.1 %collective-permute-start.9 = (bf16[256,512]{1,0:T(8,128)(2,1)S(1)}, bf16[256,512]{1,0:T(8,128)(2,1)S(1)}, u32[]{:S(2)}, u32[]{:S(2)}) collective-permute-start(bf16[256,512]{1,0:T(8,128)(2,1)S(1)} %fusion.4.residual), channel_id=1, source_target_pairs={{0,8},{4,12},{8,0},{12,4},{1,9},{5,13},{9,1},{13,5},{2,10},{6,14},... | collective-permute-start | bytes 786440 | tf_op jit(solution)/shard_map/ppermute | solution.py:335
  50.7 23.1 %collective-permute-start.8 = (bf16[256,512]{1,0:T(8,128)(2,1)S(1)}, bf16[256,512]{1,0:T(8,128)(2,1)S(1)}, u32[]{:S(2)}, u32[]{:S(2)}) collective-permute-start(bf16[256,512]{1,0:T(8,128)(2,1)S(1)} %fusion.4.residual), channel_id=1, source_target_pairs={{0,12},{4,0},{8,4},{12,8},{1,13},{5,1},{9,5},{13,9},{2,14},{6,2},{... | collective-permute-start | bytes 786440 | tf_op jit(solution)/shard_map/ppermute | solution.py:335
  52.7 3.4 %copy-start.5 = (f32[4096,512]{1,0:T(8,128)S(1)}, f32[4096,512]{1,0:T(8,128)}, u32[]{:S(2)}) copy-start(f32[4096,512]{1,0:T(8,128)} %image.3) | copy-start | bytes 25165828

commit v3 on v2

--- a/solution.py
+++ b/solution.py
@@ -15,6 +15,8 @@
 MIB = 1024 * 1024
 F32 = jnp.float32
 BF16 = jnp.bfloat16
+SMALL = pl.CostEstimate(flops=1, bytes_accessed=1, transcendentals=0)
+LARGE = pl.CostEstimate(flops=10**11, bytes_accessed=10**8, transcendentals=0)
 
 
 def angle_tables(angles):
@@ -116,82 +118,98 @@
             jax.ShapeDtypeStruct((nx - 1, points, chans), F32),
         ],
         compiler_params=pltpu.CompilerParams(vmem_limit_bytes=24 * MIB),
-        cost_estimate=pl.CostEstimate(
-            flops=2 * points * pixels * (slots + pair),
-            bytes_accessed=2 * (slots * pixels + pixels * pair),
-            transcendentals=0,
-        ),
+        cost_estimate=SMALL,
         name="integrate",
     )(tile_bin, place, after, counts.reshape(1, points), frames, weights)
 
 
-def project_kernel(angles, parts, first_row, rays, image, *refs):
-    outs, (cosine, base, tile_a, tile_b, total) = refs[:parts], refs[parts:]
-    step = pl.program_id(0)
-    rows = tile_a.shape[1] // LANES
-    half = rows * LANES
+def lower_kernel(image, low):
+    low[...] = image[...].astype(BF16)
+
+
+def lower(image):
+    cells, chans = image.shape
+    rows = min(1024, cells)
+    block = pl.BlockSpec((rows, chans), lambda i: (i, 0))
+    return pl.pallas_call(
+        lower_kernel,
+        grid=(cells // rows,),
+        in_specs=[block],
+        out_specs=block,
+        out_shape=jax.ShapeDtypeStruct((cells, chans), BF16),
+        compiler_params=pltpu.CompilerParams(vmem_limit_bytes=16 * MIB),
+        cost_estimate=SMALL,
+        name="lower",
+    )(image)
+
+
+def row_groups(rows):
+    sizes = [min(4, rows)]
+    while sum(sizes) < rows:
+        sizes.append(min(8, rows - sum(sizes)))
+    return sizes
+
+
+def project_kernel(angles, first_row, rays, image, *refs):
+    outs, (cosine, base, tile_a, tile_b, total) = refs[:-5], refs[-5:]
+    parts = len(outs)
     points = total.shape[0] // parts
-
-    def fill(tile, first):
-        for i in range(rows):
+    tiles = (tile_a, tile_b)
+    sizes = row_groups(image.shape[0] // LANES)
+
+    def fill(group):
+        first = first_row[0] + sum(sizes[:group])
+        for i in range(sizes[group]):
             upos = (first + i).astype(F32) - HALF
-            tile[:, i * LANES : (i + 1) * LANES] = hat(base[...] + cosine[...] * upos)
-
-    @pl.when(step == 0)
-    def _():
-        total[...] = jnp.zeros_like(total)
-        cos_c, sin_c, off_c = ray_geometry(rays[...], angles)
-        vpos = lax.broadcasted_iota(jnp.int32, (LANES, LANES), 1).astype(F32) - HALF
-        for k in range(rays.shape[0]):
-            here = slice(k * LANES, (k + 1) * LANES)
-            column = lambda x: jnp.transpose(jnp.broadcast_to(x[k : k + 1, :], (LANES, LANES)))
-            cosine[here, :] = column(cos_c)
-            base[here, :] = column(sin_c) * vpos - column(off_c)
-        fill(tile_a, first_row[0])
-
-    now = first_row[0] + step * (2 * rows)
-    fill(tile_b, now + rows)
-    total[...] += jnp.dot(tile_a[...], image[:half, :].astype(BF16), preferred_element_type=F32)
-    fill(tile_a, now + 2 * rows)
-    total[...] += jnp.dot(tile_b[...], image[half:, :].astype(BF16), preferred_element_type=F32)
-
-    @pl.when(step == pl.num_programs(0) - 1)
-    def _():
-        for d in range(parts):
-            outs[d][...] = total[d * points : (d + 1) * points, :].astype(outs[d].dtype)
-
-
-def project(rays, image, first_row, angles, parts):
+            tiles[group % 2][:, i * LANES : (i + 1) * LANES] = hat(base[...] + cosine[...] * upos)
+
+    cos_c, sin_c, off_c = ray_geometry(rays[...], angles)
+    vpos = lax.broadcasted_iota(jnp.int32, (LANES, LANES), 1).astype(F32) - HALF
+    for k in range(rays.shape[0]):
+        here = slice(k * LANES, (k + 1) * LANES)
+        column = lambda x: jnp.transpose(jnp.broadcast_to(x[k : k + 1, :], (LANES, LANES)))
+        cosine[here, :] = column(cos_c)
+        base[here, :] = column(sin_c) * vpos - column(off_c)
+    fill(0)
+    for group, size in enumerate(sizes):
+        if group + 1 < len(sizes):
+            fill(group + 1)
+        start = sum(sizes[:group]) * LANES
+        width = size * LANES
+        product = jnp.dot(
+            tiles[group % 2][:, :width], image[start : start + width, :], preferred_element_type=F32
+        )
+        if group == 0:
+            total[...] = product
+        elif group + 1 < len(sizes):
+            total[...] += product
+        else:
+            product += total[...]
+            for d in range(parts):
+                here = slice(d * points, (d + 1) * points)
+                outs[d][...] = product[here, :].astype(outs[d].dtype)
+
+
+def project(rays, image, first_row, angles, kinds):
     cells, chans = image.shape
     all_points = rays.shape[0] * LANES
-    points = all_points // parts
-    rows = min(4, cells // LANES // 2)
-    out = pl.BlockSpec((points, chans), lambda i, *_: (0, 0))
-    return pl.pallas_call(
-        functools.partial(project_kernel, angles, parts),
-        grid_spec=pltpu.PrefetchScalarGridSpec(
-            num_scalar_prefetch=1,
-            grid=(cells // (2 * rows * LANES),),
-            in_specs=[
-                pl.BlockSpec(rays.shape, lambda i, *_: (0, 0)),
-                pl.BlockSpec((2 * rows * LANES, chans), lambda i, *_: (i, 0)),
-            ],
-            out_specs=[out] * parts,
-            scratch_shapes=[
-                pltpu.VMEM((all_points, LANES), F32),
-                pltpu.VMEM((all_points, LANES), F32),
-                pltpu.VMEM((all_points, rows * LANES), BF16),
-                pltpu.VMEM((all_points, rows * LANES), BF16),
-                pltpu.VMEM((all_points, chans), F32),
-            ],
-        ),
-        out_shape=[
-            jax.ShapeDtypeStruct((points, chans), F32 if d == 0 else BF16) for d in range(parts)
+    points = all_points // len(kinds)
+    widest = max(row_groups(cells // LANES)) * LANES
+    vmem = pl.BlockSpec(memory_space=pltpu.VMEM)
+    return pl.pallas_call(
+        functools.partial(project_kernel, angles),
+        in_specs=[pl.BlockSpec(memory_space=pltpu.SMEM), vmem, vmem],
+        out_specs=[vmem] * len(kinds),
+        scratch_shapes=[
+            pltpu.VMEM((all_points, LANES), F32),
+            pltpu.VMEM((all_points, LANES), F32),
+            pltpu.VMEM((all_points, widest), BF16),
+            pltpu.VMEM((all_points, widest), BF16),
+            pltpu.VMEM((all_points, chans), F32),
         ],
-        compiler_params=pltpu.CompilerParams(vmem_limit_bytes=32 * MIB),
-        cost_estimate=pl.CostEstimate(
-            flops=2 * all_points * cells * chans, bytes_accessed=4 * cells * chans, transcendentals=0
-        ),
+        out_shape=[jax.ShapeDtypeStruct((points, chans), kind) for kind in kinds],
+        compiler_params=pltpu.CompilerParams(vmem_limit_bytes=40 * MIB),
+        cost_estimate=SMALL,
         name="project",
     )(first_row, rays, image)
 
@@ -223,11 +241,36 @@
         out_specs=vmem,
         out_shape=jax.ShapeDtypeStruct((points, LANES), F32),
         compiler_params=pltpu.CompilerParams(vmem_limit_bytes=8 * MIB),
-        cost_estimate=pl.CostEstimate(
-            flops=8 * points * NIMG * NIMG, bytes_accessed=4 * points * LANES, transcendentals=0
-        ),
+        cost_estimate=LARGE,
         name="row_totals",
     )(after, rays)
+
+
+def join_kernel(row_total, own, *refs):
+    arrived, (scaled, recip) = refs[:-2], refs[-2:]
+    total = own[...]
+    for part in arrived:
+        total += part[...].astype(F32)
+    recip[...] = 1.0 / row_total[...]
+    for j in range(own.shape[1] // LANES):
+        lanes = slice(j * LANES, (j + 1) * LANES)
+        scaled[:, lanes] = total[:, lanes] * recip[...]
+
+
+def join(row_total, own, arrived):
+    vmem = pl.BlockSpec(memory_space=pltpu.VMEM)
+    return pl.pallas_call(
+        join_kernel,
+        in_specs=[vmem] * (2 + len(arrived)),
+        out_specs=[vmem, vmem],
+        out_shape=[
+            jax.ShapeDtypeStruct(own.shape, F32),
+            jax.ShapeDtypeStruct(row_total.shape, F32),
+        ],
+        compiler_params=pltpu.CompilerParams(vmem_limit_bytes=8 * MIB),
+        cost_estimate=LARGE,
+        name="join",
+    )(row_total, own, *arrived)
 
 
 def prepare_kernel(angles, first_row, rays, residual, image, tile, recip, partial, base, cosine):
@@ -282,9 +325,7 @@
             jax.ShapeDtypeStruct((cells, chans), F32),
         ],
         compiler_params=pltpu.CompilerParams(vmem_limit_bytes=16 * MIB),
-        cost_estimate=pl.CostEstimate(
-            flops=2 * all_points * cells * chans, bytes_accessed=8 * cells * chans, transcendentals=0
-        ),
+        cost_estimate=SMALL,
         name="prepare",
     )(first_row, rays, residual, image)
 
@@ -321,12 +362,8 @@
         out_specs=pl.BlockSpec((rows, chans), lambda i: (i, 0)),
         scratch_shapes=[pltpu.VMEM((parts * points, chans), BF16)],
         out_shape=jax.ShapeDtypeStruct((cells, chans), F32),
-        compiler_params=pltpu.CompilerParams(vmem_limit_bytes=32 * MIB),
-        cost_estimate=pl.CostEstimate(
-            flops=2 * parts * points * cells * chans,
-            bytes_accessed=4 * cells * chans,
-            transcendentals=0,
-        ),
+        compiler_params=pltpu.CompilerParams(vmem_limit_bytes=12 * MIB),
+        cost_estimate=SMALL,
         name="back_project",
     )(*residuals, tile, recip, partial)
 
@@ -350,7 +387,7 @@
     rays = [own_rays] + [rotate(own_rays, "scan", -d, n_scan) for d in range(1, n_scan)]
     all_rays = jnp.concatenate(rays, axis=0)
 
-    shares = project(all_rays, image, first_row, angles, n_scan)
+    shares = project(all_rays, lower(image), first_row, angles, [F32] + [BF16] * (n_scan - 1))
     arrived = [rotate(shares[d], "scan", d, n_scan) for d in range(1, n_scan)]
 
     place = []
@@ -369,10 +406,8 @@
         pattern = pattern + rotate(joined, "chan", 2 * e, n_chan).astype(F32)
 
     row_total = row_totals(own_rays, angles, keep_own)
-    projected = shares[0]
-    for part in arrived:
-        projected = projected + part.astype(F32)
-    residual = ((pattern * float(NIMG) - projected) / row_total[:, :1]).astype(BF16)
+    scaled, recip = join(row_total, shares[0], arrived)
+    residual = (pattern * (float(NIMG) * recip[:, :1]) - scaled).astype(BF16)
     others = [rotate(residual, "scan", -d, n_scan) for d in range(1, n_scan)]
     tile, col_recip, partial = prepare(all_rays, residual, image, first_row, angles)
     return back_project(others, tile, col_recip, partial)

time: 79.7 us -> 76.6 us (0.961)
  the two profiles are of different devices: /device:TPU:24 before, /device:TPU:11 now
where the time goes in v3:
time: 76.6 us; the launch traced here: 76.3 us
  Pallas kernels  27.8 us (36%)
  waiting for transfers between devices  26.2 us (34%)
  starting transfers between devices  11.8 us (15%)
  local copies, waits for them, and re-layouts  9.94 us (13%)
    ppermute x10, waiting for transfers between devices, rotate(): return lax.ppermute(x, axis, [(i, (i + shift) % n) for i in range(n)])  26.2 us
    unnamed x24, local copies, waits for them, and re-layouts  9.94 us
    ppermute x10, starting transfers between devices, rotate(): return lax.ppermute(x, axis, [(i, (i + shift) % n) for i in range(n)])  9.68 us
    pallas_call x1, Pallas kernels, project(): pl.pallas_call(functools.partial(project_kernel, angles), in_specs=[pl.Bl...  6.39 us
    pallas_call x1, Pallas kernels, prepare(): pl.pallas_call(functools.partial(prepare_kernel, angles), grid_spec=pltpu...  5.68 us
    pallas_call x1, Pallas kernels, back_project(): pl.pallas_call(functools.partial(back_kernel, parts), grid=(cells // rows...  5.68 us
    pallas_call x1, Pallas kernels, integrate(): pl.pallas_call(functools.partial(integrate_kernel, nx, chans // tile_bins...  5.29 us
    pallas_call x1, Pallas kernels, row_totals(): pl.pallas_call(functools.partial(row_total_kernel, angles), in_specs=[pl....  4.06 us
  transfers between devices with their start and end apart: 11, of which 4 were waited for; matrix products, arithmetic and copies ran while one was open for 0% of the time, Pallas kernels for 21%

profile of v3, /device:TPU:11, one launch (start us, length us, event | category | flops | bytes accessed | tf_op | source)
XLA Modules:
  0.0 76.3 jit_solution(1665960442800843539)
XLA Ops:
  0.0 1.3 %collective-permute-start.2 = (s32[2,128]{1,0:T(2,128)}, s32[2,128]{1,0:T(2,128)S(1)}, u32[]{:S(2)}, u32[]{:S(2)}) collective-permute-start(s32[2,128]{1,0:T(2,128)} %bitcast.17), channel_id=1, source_target_pairs={{0,4},{4,8},{8,12},{12,0},{1,5},{5,9},{9,13},{13,1},{2,6},{6,10},{... | collective-permute-start | bytes 3080 | tf_op jit(solution)/shard_map/ppermute | solution.py:372
  1.3 1.1 %collective-permute-start.1 = (s32[2,128]{1,0:T(2,128)}, s32[2,128]{1,0:T(2,128)S(1)}, u32[]{:S(2)}, u32[]{:S(2)}) collective-permute-start(s32[2,128]{1,0:T(2,128)} %bitcast.18), channel_id=1, source_target_pairs={{0,8},{4,12},{8,0},{12,4},{1,9},{5,13},{9,1},{13,5},{2,10},{6,14},... | collective-permute-start | bytes 3080 | tf_op jit(solution)/shard_map/ppermute | solution.py:372
  2.4 1.4 %collective-permute-start = (s32[2,128]{1,0:T(2,128)}, s32[2,128]{1,0:T(2,128)S(1)}, u32[]{:S(2)}, u32[]{:S(2)}) collective-permute-start(s32[2,128]{1,0:T(2,128)} %bitcast.19), channel_id=1, source_target_pairs={{0,12},{4,0},{8,4},{12,8},{1,13},{5,1},{9,5},{13,9},{2,14},{6,2},{... | collective-permute-start | bytes 3080 | tf_op jit(solution)/shard_map/ppermute | solution.py:372
  3.9 3.4 %copy-done = f32[4096,512]{1,0:T(8,128)S(1)} copy-done((f32[4096,512]{1,0:T(8,128)S(1)}, f32[4096,512]{1,0:T(8,128)}, u32[]{:S(2)}) %copy-start) | copy-done | bytes 8388632
  7.2 0.5 lower.1.image
  7.7 2.0 %copy-done.1 = bf16[4096,512]{1,0:T(8,128)(2,1)} copy-done((bf16[4096,512]{1,0:T(8,128)(2,1)}, bf16[4096,512]{1,0:T(8,128)(2,1)S(1)}, u32[]{:S(2)}) %copy-start.1) | copy-done | bytes 4194328
  9.8 2.2 %copy-done.2 = bf16[4096,512]{1,0:T(8,128)(2,1)S(1)} copy-done((bf16[4096,512]{1,0:T(8,128)(2,1)S(1)}, bf16[4096,512]{1,0:T(8,128)(2,1)}, u32[]{:S(2)}) %copy-start.2) | copy-done | bytes 4194328
  12.0 6.4 %project.1 = (f32[256,512]{1,0:T(8,128)S(1)}, bf16[256,512]{1,0:T(8,128)(2,1)S(1)}, bf16[256,512]{1,0:T(8,128)(2,1)S(1)}, bf16[256,512]{1,0:T(8,128)(2,1)S(1)}) custom-call(s32[1]{0:T(128)} %bitcast.4.first_row, s32[8,128]{1,0:T(8,128)S(1)} %pad_add_fusion.rays, bf16[4096,512]{1,0:T(8,128)(2,1)S(1)} %copy-done.2), custom_call_target="tpu_custom_call" | custom-call | flops 1 | bytes 1 | tf_op jit(solution)/shard_map/project/pallas_call | solution.py:199
  18.5 3.1 %collective-permute-start.6 = (bf16[256,512]{1,0:T(8,128)(2,1)S(1)}, bf16[256,512]{1,0:T(8,128)(2,1)S(1)}, u32[]{:S(2)}, u32[]{:S(2)}) collective-permute-start(bf16[256,512]{1,0:T(8,128)(2,1)S(1)} %get-tuple-element.22), channel_id=1, source_target_pairs={{0,8},{4,12},{8,0},{12,4},{1,9},{5,13},{9,1},{13,5},{2,10},{6,14},... | collective-permute-start | bytes 786440 | tf_op jit(solution)/shard_map/ppermute | solution.py:372
  21.6 2.3 %copy-done.3 = bf16[384,6144]{1,0:T(8,128)(2,1)S(1)} copy-done((bf16[384,6144]{1,0:T(8,128)(2,1)S(1)}, bf16[384,6144]{1,0:T(8,128)(2,1)}, u32[]{:S(2)}) %copy-start.3) | copy-done | bytes 4718616
  23.9 5.3 %integrate.1 = (bf16[2,256,512]{2,1,0:T(8,128)(2,1)S(1)}, f32[256,512]{1,0:T(8,128)S(1)}, f32[1,256,512]{2,1,0:T(8,128)S(1)}) custom-call(s32[48]{0:T(128)S(1)} %copy-done.9, s32[4]{0:T(128)S(1)} %pad_add_fusion.1.place, f32[256,512]{1,0:T(8,128)S(1)} %get-tuple-element.17.after.own, s32[1,256]{1,0:T(1,128)S(1)} %bitcast.16, ...), custom_call_target="tpu_custom_call" | custom-call | flops 1 | bytes 1 | tf_op jit(solution)/shard_map/integrate/pallas_call | solution.py:94
  29.2 2.1 %collective-permute-start.3 = (bf16[2,256,512]{2,1,0:T(8,128)(2,1)S(1)}, bf16[2,256,512]{2,1,0:T(8,128)(2,1)S(1)}, u32[]{:S(2)}, u32[]{:S(2)}) collective-permute-start(bf16[2,256,512]{2,1,0:T(8,128)(2,1)S(1)} %get-tuple-element.19), channel_id=1, source_target_pairs={{0,1},{1,0},{2,3},{3,2},{4,5},{5,4},{6,7},{7,6},{8,9},{9,8},{10,11... | collective-permute-start | bytes 1572872 | tf_op jit(solution)/shard_map/ppermute | solution.py:402
  31.4 4.1 %row_totals.1.row_total = f32[256,128]{1,0:T(8,128)S(1)} custom-call(f32[256,512]{1,0:T(8,128)S(1)} %get-tuple-element.18.after, s32[2,128]{1,0:T(2,128)S(1)} %bitcast.21), custom_call_target="tpu_custom_call" | custom-call | flops 99999997952 | bytes 100000000 | tf_op jit(solution)/shard_map/row_totals/pallas_call | solution.py:238
  35.6 0.3 collective-permute-start.4
  35.9 3.6 %collective-permute-done.6.refs_1_ = bf16[256,512]{1,0:T(8,128)(2,1)S(1)} collective-permute-done((bf16[256,512]{1,0:T(8,128)(2,1)S(1)}, bf16[256,512]{1,0:T(8,128)(2,1)S(1)}, u32[]{:S(2)}, u32[]{:S(2)}) %collective-permute-start.6) | collective-permute-done | bytes 262176 | tf_op jit(solution)/shard_map/ppermute | solution.py:372
  39.5 4.6 %collective-permute-done.7.refs_2_ = bf16[256,512]{1,0:T(8,128)(2,1)S(1)} collective-permute-done((bf16[256,512]{1,0:T(8,128)(2,1)S(1)}, bf16[256,512]{1,0:T(8,128)(2,1)S(1)}, u32[]{:S(2)}, u32[]{:S(2)}) %collective-permute-start.7) | collective-permute-done | bytes 262176 | tf_op jit(solution)/shard_map/ppermute | solution.py:372
  44.1 0.2 join.1
  44.5 0.1 fusion.3.residual
  44.6 0.9 %collective-permute-start.10 = (bf16[256,512]{1,0:T(8,128)(2,1)S(1)}, bf16[256,512]{1,0:T(8,128)(2,1)S(1)}, u32[]{:S(2)}, u32[]{:S(2)}) collective-permute-start(bf16[256,512]{1,0:T(8,128)(2,1)S(1)} %fusion.3.residual), channel_id=1, source_target_pairs={{0,4},{4,8},{8,12},{12,0},{1,5},{5,9},{9,13},{13,1},{2,6},{6,10},{... | collective-permute-start | bytes 786440 | tf_op jit(solution)/shard_map/ppermute | solution.py:372
  45.5 1.5 %collective-permute-start.9 = (bf16[256,512]{1,0:T(8,128)(2,1)S(1)}, bf16[256,512]{1,0:T(8,128)(2,1)S(1)}, u32[]{:S(2)}, u32[]{:S(2)}) collective-permute-start(bf16[256,512]{1,0:T(8,128)(2,1)S(1)} %fusion.3.residual), channel_id=1, source_target_pairs={{0,8},{4,12},{8,0},{12,4},{1,9},{5,13},{9,1},{13,5},{2,10},{6,14},... | collective-permute-start | bytes 786440 | tf_op jit(solution)/shard_map/ppermute | solution.py:372
  47.0 5.7 %prepare.1 = (bf16[4096,1024]{1,0:T(8,128)(2,1)S(1)}, f32[4096,128]{1,0:T(8,128)S(1)}, f32[4096,512]{1,0:T(8,128)S(1)}) custom-call(s32[1]{0:T(128)} %bitcast.4.first_row, s32[8,128]{1,0:T(8,128)S(1)} %copy-done.6, bf16[256,512]{1,0:T(8,128)(2,1)S(1)} %fusion.3.residual, f32[4096,512]{1,0:T(8,128)S(1)} %bitcast.15), custom_call_target="tpu_custom_call" | custom-call | flops 1 | bytes 1 | tf_op jit(solution)/shard_map/prepare/pallas_call | solution.py:313
  52.7 14.4 %collective-permute-done.9.refs_1_ = bf16[256,512]{1,0:T(8,128)(2,1)S(1)} collective-permute-done((bf16[256,512]{1,0:T(8,128)(2,1)S(1)}, bf16[256,512]{1,0:T(8,128)(2,1)S(1)}, u32[]{:S(2)}, u32[]{:S(2)}) %collective-permute-start.9) | collective-permute-done | bytes 262176 | tf_op jit(solution)/shard_map/ppermute | solution.py:372
  67.2 3.5 %collective-permute-done.8.refs_0_ = bf16[256,512]{1,0:T(8,128)(2,1)S(1)} collective-permute-done((bf16[256,512]{1,0:T(8,128)(2,1)S(1)}, bf16[256,512]{1,0:T(8,128)(2,1)S(1)}, u32[]{:S(2)}, u32[]{:S(2)}) %collective-permute-start.8) | collective-permute-done | bytes 262176 | tf_op jit(solution)/shard_map/ppermute | solution.py:372
  70.7 5.7 %back_project.1 = f32[4096,512]{1,0:T(8,128)} custom-call(bf16[256,512]{1,0:T(8,128)(2,1)S(1)} %collective-permute-done.8.refs_0_, bf16[256,512]{1,0:T(8,128)(2,1)S(1)} %collective-permute-done.9.refs_1_, bf16[256,512]{1,0:T(8,128)(2,1)S(1)} %collective-permute-done.10.refs_2_, bf16[4096,1024]{1,0:T(8,128)(2,1)S(1)} %get-tuple-element.26.refs_3_, ...), custom_call_target="tpu_custom_call" | custom-call | flops 1 | bytes 1 | tf_op jit(solution)/shard_map/back_project/pallas_call | solution.py:358
  (35 shorter events, 0.5 us)
Async XLA Ops:
  0.0 9.7 %copy-start.8 = (s32[256]{0:T(256)S(1)}, s32[256]{0:T(256)}, u32[]{:S(2)}) copy-start(s32[256]{0:T(256)} %param.8) | copy-start | bytes 3076
  0.0 9.7 %collective-permute-start.2 = (s32[2,128]{1,0:T(2,128)}, s32[2,128]{1,0:T(2,128)S(1)}, u32[]{:S(2)}, u32[]{:S(2)}) collective-permute-start(s32[2,128]{1,0:T(2,128)} %bitcast.17), channel_id=1, source_target_pairs={{0,4},{4,8},{8,12},{12,0},{1,5},{5,9},{9,13},{13,1},{2,6},{6,10},{... | collective-permute-start | bytes 3080 | tf_op jit(solution)/shard_map/ppermute | solution.py:372
  1.3 8.4 %collective-permute-start.1 = (s32[2,128]{1,0:T(2,128)}, s32[2,128]{1,0:T(2,128)S(1)}, u32[]{:S(2)}, u32[]{:S(2)}) collective-permute-start(s32[2,128]{1,0:T(2,128)} %bitcast.18), channel_id=1, source_target_pairs={{0,8},{4,12},{8,0},{12,4},{1,9},{5,13},{9,1},{13,5},{2,10},{6,14},... | collective-permute-start | bytes 3080 | tf_op jit(solution)/shard_map/ppermute | solution.py:372
  2.4 7.4 %collective-permute-start = (s32[2,128]{1,0:T(2,128)}, s32[2,128]{1,0:T(2,128)S(1)}, u32[]{:S(2)}, u32[]{:S(2)}) collective-permute-start(s32[2,128]{1,0:T(2,128)} %bitcast.19), channel_id=1, source_target_pairs={{0,12},{4,0},{8,4},{12,8},{1,13},{5,1},{9,5},{13,9},{2,14},{6,2},{... | collective-permute-start | bytes 3080 | tf_op jit(solution)/shard_map/ppermute | solution.py:372
  3.9 3.4 %copy-start = (f32[4096,512]{1,0:T(8,128)S(1)}, f32[4096,512]{1,0:T(8,128)}, u32[]{:S(2)}) copy-start(f32[4096,512]{1,0:T(8,128)} %image.3) | copy-start | bytes 25165828
  7.2 14.3 %copy-start.4 = (bf16[48,128,256]{2,1,0:T(8,128)(2,1)S(1)}, bf16[48,128,256]{2,1,0:T(8,128)(2,1)}, u32[]{:S(2)}) copy-start(bf16[48,128,256]{2,1,0:T(8,128)(2,1)} %weights.1) | copy-start | bytes 9437188
  7.2 14.3 %copy-start.7 = (s32[256]{0:T(256)S(1)}, s32[256]{0:T(256)}, u32[]{:S(2)}) copy-start(s32[256]{0:T(256)} %param.7) | copy-start | bytes 3076
  7.2 14.3 %copy-start.9 = (s32[48]{0:T(128)S(1)}, s32[48]{0:T(128)}, u32[]{:S(2)}) copy-start(s32[48]{0:T(128)} %tile_bin.1) | copy-start | bytes 580
  7.7 2.0 %copy-start.1 = (bf16[4096,512]{1,0:T(8,128)(2,1)}, bf16[4096,512]{1,0:T(8,128)(2,1)S(1)}, u32[]{:S(2)}) copy-start(bf16[4096,512]{1,0:T(8,128)(2,1)S(1)} %lower.1.image) | copy-start | bytes 12582916
  9.8 25.7 %copy-start.5 = (s32[8,128]{1,0:T(8,128)}, s32[8,128]{1,0:T(8,128)S(1)}, u32[]{:S(2)}) copy-start(s32[8,128]{1,0:T(8,128)S(1)} %pad_add_fusion.rays) | copy-start | bytes 12292
  9.8 2.2 %copy-start.2 = (bf16[4096,512]{1,0:T(8,128)(2,1)S(1)}, bf16[4096,512]{1,0:T(8,128)(2,1)}, u32[]{:S(2)}) copy-start(bf16[4096,512]{1,0:T(8,128)(2,1)} %copy-done.1) | copy-start | bytes 12582916
  18.4 17.5 %collective-permute-start.5 = (bf16[256,512]{1,0:T(8,128)(2,1)S(1)}, bf16[256,512]{1,0:T(8,128)(2,1)S(1)}, u32[]{:S(2)}, u32[]{:S(2)}) collective-permute-start(bf16[256,512]{1,0:T(8,128)(2,1)S(1)} %get-tuple-element.21), channel_id=1, source_target_pairs={{0,4},{4,8},{8,12},{12,0},{1,5},{5,9},{9,13},{13,1},{2,6},{6,10},{... | collective-permute-start | bytes 786440 | tf_op jit(solution)/shard_map/ppermute | solution.py:372
  18.5 21.1 %collective-permute-start.6 = (bf16[256,512]{1,0:T(8,128)(2,1)S(1)}, bf16[256,512]{1,0:T(8,128)(2,1)S(1)}, u32[]{:S(2)}, u32[]{:S(2)}) collective-permute-start(bf16[256,512]{1,0:T(8,128)(2,1)S(1)} %get-tuple-element.22), channel_id=1, source_target_pairs={{0,8},{4,12},{8,0},{12,4},{1,9},{5,13},{9,1},{13,5},{2,10},{6,14},... | collective-permute-start | bytes 786440 | tf_op jit(solution)/shard_map/ppermute | solution.py:372
  21.6 22.6 %collective-permute-start.7 = (bf16[256,512]{1,0:T(8,128)(2,1)S(1)}, bf16[256,512]{1,0:T(8,128)(2,1)S(1)}, u32[]{:S(2)}, u32[]{:S(2)}) collective-permute-start(bf16[256,512]{1,0:T(8,128)(2,1)S(1)} %get-tuple-element.23), channel_id=1, source_target_pairs={{0,12},{4,0},{8,4},{12,8},{1,13},{5,1},{9,5},{13,9},{2,14},{6,2},{... | collective-permute-start | bytes 786440 | tf_op jit(solution)/shard_map/ppermute | solution.py:372
  21.6 2.3 %copy-start.3 = (bf16[384,6144]{1,0:T(8,128)(2,1)S(1)}, bf16[384,6144]{1,0:T(8,128)(2,1)}, u32[]{:S(2)}) copy-start(bf16[384,6144]{1,0:T(8,128)(2,1)} %frames.1) | copy-start | bytes 14155780
  29.2 6.2 %collective-permute-start.3 = (bf16[2,256,512]{2,1,0:T(8,128)(2,1)S(1)}, bf16[2,256,512]{2,1,0:T(8,128)(2,1)S(1)}, u32[]{:S(2)}, u32[]{:S(2)}) collective-permute-start(bf16[2,256,512]{2,1,0:T(8,128)(2,1)S(1)} %get-tuple-element.19), channel_id=1, source_target_pairs={{0,1},{1,0},{2,3},{3,2},{4,5},{5,4},{6,7},{7,6},{8,9},{9,8},{10,11... | collective-permute-start | bytes 1572872 | tf_op jit(solution)/shard_map/ppermute | solution.py:402
  35.5 11.6 %slice-start = ((s8[8388608]{0:T(1024)(128)(4,1)}), s8[4194304]{0:T(1024)(128)(4,1)S(1)}, s32[]{:S(2)}) async-start(s8[8388608]{0:T(1024)(128)(4,1)} %bitcast.14), calls=%async_computation | async-start | bytes 8388608
  35.6 11.5 %slice-start.1 = ((s8[8388608]{0:T(1024)(128)(4,1)}), s8[4194304]{0:T(1024)(128)(4,1)S(1)}, s32[]{:S(2)}) async-start(s8[8388608]{0:T(1024)(128)(4,1)} %bitcast.14), calls=%async_computation.1 | async-start | bytes 8388608
  35.6 11.5 %copy-start.6 = (s32[8,128]{1,0:T(8,128)S(1)}, s32[8,128]{1,0:T(8,128)}, u32[]{:S(2)}) copy-start(s32[8,128]{1,0:T(8,128)} %copy-done.5) | copy-start | bytes 12292
  35.6 8.9 %collective-permute-start.4 = (bf16[256,512]{1,0:T(8,128)(2,1)S(1)}, bf16[256,512]{1,0:T(8,128)(2,1)S(1)}, u32[]{:S(2)}, u32[]{:S(2)}) collective-permute-start(bf16[256,512]{1,0:T(8,128)(2,1)S(1)} %fusion.4), channel_id=1, source_target_pairs={{0,2},{1,3},{2,0},{3,1},{4,6},{5,7},{6,4},{7,5},{8,10},{9,11},{10,... | collective-permute-start | bytes 786440 | tf_op jit(solution)/shard_map/ppermute | solution.py:372
  44.6 8.1 %collective-permute-start.10 = (bf16[256,512]{1,0:T(8,128)(2,1)S(1)}, bf16[256,512]{1,0:T(8,128)(2,1)S(1)}, u32[]{:S(2)}, u32[]{:S(2)}) collective-permute-start(bf16[256,512]{1,0:T(8,128)(2,1)S(1)} %fusion.3.residual), channel_id=1, source_target_pairs={{0,4},{4,8},{8,12},{12,0},{1,5},{5,9},{9,13},{13,1},{2,6},{6,10},{... | collective-permute-start | bytes 786440 | tf_op jit(solution)/shard_map/ppermute | solution.py:372
  45.5 21.7 %collective-permute-start.9 = (bf16[256,512]{1,0:T(8,128)(2,1)S(1)}, bf16[256,512]{1,0:T(8,128)(2,1)S(1)}, u32[]{:S(2)}, u32[]{:S(2)}) collective-permute-start(bf16[256,512]{1,0:T(8,128)(2,1)S(1)} %fusion.3.residual), channel_id=1, source_target_pairs={{0,8},{4,12},{8,0},{12,4},{1,9},{5,13},{9,1},{13,5},{2,10},{6,14},... | collective-permute-start | bytes 786440 | tf_op jit(solution)/shard_map/ppermute | solution.py:372
  47.0 23.7 %collective-permute-start.8 = (bf16[256,512]{1,0:T(8,128)(2,1)S(1)}, bf16[256,512]{1,0:T(8,128)(2,1)S(1)}, u32[]{:S(2)}, u32[]{:S(2)}) collective-permute-start(bf16[256,512]{1,0:T(8,128)(2,1)S(1)} %fusion.3.residual), channel_id=1, source_target_pairs={{0,12},{4,0},{8,4},{12,8},{1,13},{5,1},{9,5},{13,9},{2,14},{6,2},{... | collective-permute-start | bytes 786440 | tf_op jit(solution)/shard_map/ppermute | solution.py:372

commit v4 on v3

--- a/solution.py
+++ b/solution.py
@@ -42,7 +42,7 @@
 
 
 def integrate_kernel(
-    nx, per_chunk, tile_bin, place, after, counts, frames, weights, send, keep_own, keep_rest, member, acc
+    nx, per_chunk, tile_bin, place, after, counts, frames, weights, send, acc, member
 ):
     step = pl.program_id(0)
     points, slots = member.shape
@@ -73,14 +73,9 @@
     @pl.when(step == pl.num_programs(0) - 1)
     def _():
         for e in range(nx):
-            other, mine = place[2 * e], place[2 * e + 1]
             for j in range(per_chunk):
                 lanes = slice(j * tile_bins, (j + 1) * tile_bins)
-                send[e, :, lanes] = acc[other * per_chunk + j].astype(BF16)
-                if e == 0:
-                    keep_own[:, lanes] = acc[mine * per_chunk + j]
-                else:
-                    keep_rest[e - 1, :, lanes] = acc[mine * per_chunk + j]
+                send[e, :, lanes] = acc[place[2 * e] * per_chunk + j].astype(BF16)
 
 
 def integrate(frames, counts, weights, tile_bin, place, after, nx, chans):
@@ -104,18 +99,13 @@
             ],
             out_specs=[
                 whole((nx, points, chans)),
-                whole((points, chans)),
-                whole((nx - 1, points, chans)),
+                whole((channel_blocks, points, tile_bins)),
             ],
-            scratch_shapes=[
-                pltpu.VMEM((points, slots), BF16),
-                pltpu.VMEM((channel_blocks, points, tile_bins), F32),
-            ],
+            scratch_shapes=[pltpu.VMEM((points, slots), BF16)],
         ),
         out_shape=[
             jax.ShapeDtypeStruct((nx, points, chans), BF16),
-            jax.ShapeDtypeStruct((points, chans), F32),
-            jax.ShapeDtypeStruct((nx - 1, points, chans), F32),
+            jax.ShapeDtypeStruct((channel_blocks, points, tile_bins), F32),
         ],
         compiler_params=pltpu.CompilerParams(vmem_limit_bytes=24 * MIB),
         cost_estimate=SMALL,
@@ -123,24 +113,27 @@
     )(tile_bin, place, after, counts.reshape(1, points), frames, weights)
 
 
-def lower_kernel(image, low):
-    low[...] = image[...].astype(BF16)
-
-
-def lower(image):
-    cells, chans = image.shape
-    rows = min(1024, cells)
-    block = pl.BlockSpec((rows, chans), lambda i: (i, 0))
-    return pl.pallas_call(
-        lower_kernel,
-        grid=(cells // rows,),
-        in_specs=[block],
-        out_specs=block,
-        out_shape=jax.ShapeDtypeStruct((cells, chans), BF16),
-        compiler_params=pltpu.CompilerParams(vmem_limit_bytes=16 * MIB),
-        cost_estimate=SMALL,
-        name="lower",
-    )(image)
+def select_kernel(place, acc, own, *rest):
+    _, points, tile_bins = acc.shape
+    per_chunk = own.shape[1] // tile_bins
+    for e, keep in enumerate((own,) + rest):
+        for j in range(per_chunk):
+            lanes = slice(j * tile_bins, (j + 1) * tile_bins)
+            keep[:, lanes] = acc[place[2 * e + 1] * per_chunk + j]
+
+
+def select(place, acc, nx, chans):
+    points = acc.shape[1]
+    vmem = pl.BlockSpec(memory_space=pltpu.VMEM)
+    return pl.pallas_call(
+        select_kernel,
+        in_specs=[pl.BlockSpec(memory_space=pltpu.SMEM), vmem],
+        out_specs=[vmem] * nx,
+        out_shape=[jax.ShapeDtypeStruct((points, chans), F32)] * nx,
+        compiler_params=pltpu.CompilerParams(vmem_limit_bytes=8 * MIB),
+        cost_estimate=LARGE,
+        name="select",
+    )(place, acc)
 
 
 def row_groups(rows):
@@ -150,7 +143,7 @@
     return sizes
 
 
-def project_kernel(angles, first_row, rays, image, *refs):
+def project_kernel(angles, first_row, after, rays, image, *refs):
     outs, (cosine, base, tile_a, tile_b, total) = refs[:-5], refs[-5:]
     parts = len(outs)
     points = total.shape[0] // parts
@@ -177,7 +170,9 @@
         start = sum(sizes[:group]) * LANES
         width = size * LANES
         product = jnp.dot(
-            tiles[group % 2][:, :width], image[start : start + width, :], preferred_element_type=F32
+            tiles[group % 2][:, :width],
+            image[start : start + width, :].astype(BF16),
+            preferred_element_type=F32,
         )
         if group == 0:
             total[...] = product
@@ -190,7 +185,7 @@
                 outs[d][...] = product[here, :].astype(outs[d].dtype)
 
 
-def project(rays, image, first_row, angles, kinds):
+def project(rays, image, first_row, after, angles, kinds):
     cells, chans = image.shape
     all_points = rays.shape[0] * LANES
     points = all_points // len(kinds)
@@ -198,7 +193,12 @@
     vmem = pl.BlockSpec(memory_space=pltpu.VMEM)
     return pl.pallas_call(
         functools.partial(project_kernel, angles),
-        in_specs=[pl.BlockSpec(memory_space=pltpu.SMEM), vmem, vmem],
+        in_specs=[
+            pl.BlockSpec(memory_space=pltpu.SMEM),
+            pl.BlockSpec(memory_space=pl.ANY),
+            vmem,
+            vmem,
+        ],
         out_specs=[vmem] * len(kinds),
         scratch_shapes=[
             pltpu.VMEM((all_points, LANES), F32),
@@ -209,12 +209,14 @@
         ],
         out_shape=[jax.ShapeDtypeStruct((points, chans), kind) for kind in kinds],
         compiler_params=pltpu.CompilerParams(vmem_limit_bytes=40 * MIB),
-        cost_estimate=SMALL,
+        cost_estimate=pl.CostEstimate(
+            flops=4 * all_points * cells * chans, bytes_accessed=4 * cells * chans, transcendentals=0
+        ),
         name="project",
-    )(first_row, rays, image)
-
-
-def row_total_kernel(angles, after, rays, row_total):
+    )(first_row, after, rays, image)
+
+
+def row_total_kernel(angles, rays, row_total):
     cos_r, sin_r, off_r = ray_geometry(rays[...], angles)
     vpos = lax.broadcasted_iota(jnp.int32, (LANES, LANES), 0).astype(F32) - HALF
     for k in range(rays.shape[0]):
@@ -232,18 +234,18 @@
         )
 
 
-def row_totals(rays, angles, after):
+def row_totals(rays, angles):
     points = rays.shape[0] * LANES
     vmem = pl.BlockSpec(memory_space=pltpu.VMEM)
     return pl.pallas_call(
         functools.partial(row_total_kernel, angles),
-        in_specs=[pl.BlockSpec(memory_space=pl.ANY), vmem],
+        in_specs=[vmem],
         out_specs=vmem,
         out_shape=jax.ShapeDtypeStruct((points, LANES), F32),
         compiler_params=pltpu.CompilerParams(vmem_limit_bytes=8 * MIB),
         cost_estimate=LARGE,
         name="row_totals",
-    )(after, rays)
+    )(rays)
 
 
 def join_kernel(row_total, own, *refs):
@@ -387,7 +389,9 @@
     rays = [own_rays] + [rotate(own_rays, "scan", -d, n_scan) for d in range(1, n_scan)]
     all_rays = jnp.concatenate(rays, axis=0)
 
-    shares = project(all_rays, lower(image), first_row, angles, [F32] + [BF16] * (n_scan - 1))
+    row_total = row_totals(own_rays, angles)
+    kinds = [F32] + [BF16] * (n_scan - 1)
+    shares = project(all_rays, image, first_row, row_total, angles, kinds)
     arrived = [rotate(shares[d], "scan", d, n_scan) for d in range(1, n_scan)]
 
     place = []
@@ -395,17 +399,17 @@
         xi = (x_me + e) % nx
         place += [2 * xi + 1 - core_me, 2 * xi + core_me]
     place = jnp.stack(place).astype(jnp.int32)
-    send, keep_own, keep_rest = integrate(
+    send, sums = integrate(
         frames, counts, channel_pair_weights, tile_bin, place, shares[0], nx, chans
     )
+    keep = select(place, sums, nx, chans)
     partner = [(i, i ^ 1) for i in range(n_chan)]
     got = lax.ppermute(send, "chan", partner)
-    pattern = keep_own + got[0].astype(F32)
+    pattern = keep[0] + got[0].astype(F32)
     for e in range(1, nx):
-        joined = (keep_rest[e - 1] + got[e].astype(F32)).astype(BF16)
+        joined = (keep[e] + got[e].astype(F32)).astype(BF16)
         pattern = pattern + rotate(joined, "chan", 2 * e, n_chan).astype(F32)
 
-    row_total = row_totals(own_rays, angles, keep_own)
     scaled, recip = join(row_total, shares[0], arrived)
     residual = (pattern * (float(NIMG) * recip[:, :1]) - scaled).astype(BF16)
     others = [rotate(residual, "scan", -d, n_scan) for d in range(1, n_scan)]

time: 76.6 us -> 74.4 us (0.971)
  the two profiles are of different devices: /device:TPU:11 before, /device:TPU:30 now
where the time goes in v4:
time: 74.4 us; the launch traced here: 74.2 us
  Pallas kernels  28.2 us (38%)
  starting transfers between devices  21.3 us (29%)
  waiting for transfers between devices  20 us (27%)
  local copies, waits for them, and re-layouts  4.13 us (6%)
    ppermute x10, starting transfers between devices, rotate(): return lax.ppermute(x, axis, [(i, (i + shift) % n) for i in range(n)])  21.2 us
    ppermute x10, waiting for transfers between devices, rotate(): return lax.ppermute(x, axis, [(i, (i + shift) % n) for i in range(n)])  18.8 us
    pallas_call x1, Pallas kernels, project(): pl.pallas_call(functools.partial(project_kernel, angles), in_specs=[pl.Bl...  6.52 us
    pallas_call x1, Pallas kernels, prepare(): pl.pallas_call(functools.partial(prepare_kernel, angles), grid_spec=pltpu...  5.76 us
    pallas_call x1, Pallas kernels, back_project(): pl.pallas_call(functools.partial(back_kernel, parts), grid=(cells // rows...  5.67 us
    pallas_call x1, Pallas kernels, integrate(): pl.pallas_call(functools.partial(integrate_kernel, nx, chans // tile_bins...  5.31 us
    unnamed x22, local copies, waits for them, and re-layouts  4.13 us
    pallas_call x1, Pallas kernels, row_totals(): pl.pallas_call(functools.partial(row_total_kernel, angles), in_specs=[vme...  4.06 us
  transfers between devices with their start and end apart: 11, of which 4 were waited for; matrix products, arithmetic and copies ran while one was open for 0% of the time, Pallas kernels for 22%

profile of v4, /device:TPU:30, one launch (start us, length us, event | category | flops | bytes accessed | tf_op | source)
XLA Modules:
  0.0 74.2 jit_solution(14289200917105397387)
XLA Ops:
  0.0 0.2 collective-permute-start.2
  0.2 1.7 %collective-permute-start.1 = (s32[2,128]{1,0:T(2,128)}, s32[2,128]{1,0:T(2,128)S(1)}, u32[]{:S(2)}, u32[]{:S(2)}) collective-permute-start(s32[2,128]{1,0:T(2,128)} %bitcast.21), channel_id=1, source_target_pairs={{0,8},{4,12},{8,0},{12,4},{1,9},{5,13},{9,1},{13,5},{2,10},{6,14},... | collective-permute-start | bytes 3080 | tf_op jit(solution)/shard_map/ppermute | solution.py:374
  1.9 0.4 collective-permute-start
  2.4 0.7 copy-done.6
  3.1 4.1 %row_totals.1.after.row_total = f32[256,128]{1,0:T(8,128)S(1)} custom-call(s32[2,128]{1,0:T(2,128)S(1)} %bitcast.23), custom_call_target="tpu_custom_call" | custom-call | flops 99999997952 | bytes 100000000 | tf_op jit(solution)/shard_map/row_totals/pallas_call | solution.py:240
  7.2 0.1 pad_add_fusion.1.place
  7.2 0.3 collective-permute-done
  7.5 3.4 %copy-done = f32[4096,512]{1,0:T(8,128)S(1)} copy-done((f32[4096,512]{1,0:T(8,128)S(1)}, f32[4096,512]{1,0:T(8,128)}, u32[]{:S(2)}) %copy-start) | copy-done | bytes 8388632
  10.9 6.5 %project.1 = (f32[256,512]{1,0:T(8,128)S(1)}, bf16[256,512]{1,0:T(8,128)(2,1)S(1)}, bf16[256,512]{1,0:T(8,128)(2,1)S(1)}, bf16[256,512]{1,0:T(8,128)(2,1)S(1)}) custom-call(s32[1]{0:T(128)} %bitcast.4.first_row, f32[256,128]{1,0:T(8,128)S(1)} %row_totals.1.after.row_total, s32[8,128]{1,0:T(8,128)S(1)} %pad_add_fusion.rays, f32[4096,512]{1,0:T(8,128)S(1)} %copy-done), custom_call_target="tpu_custom_call" | custom-call | flops 8589934592 | bytes 8388608 | tf_op jit(solution)/shard_map/project/pallas_call | solution.py:194
  17.5 3.2 %collective-permute-start.5 = (bf16[256,512]{1,0:T(8,128)(2,1)S(1)}, bf16[256,512]{1,0:T(8,128)(2,1)S(1)}, u32[]{:S(2)}, u32[]{:S(2)}) collective-permute-start(bf16[256,512]{1,0:T(8,128)(2,1)S(1)} %get-tuple-element.23), channel_id=1, source_target_pairs={{0,4},{4,8},{8,12},{12,0},{1,5},{5,9},{9,13},{13,1},{2,6},{6,10},{... | collective-permute-start | bytes 786440 | tf_op jit(solution)/shard_map/ppermute | solution.py:374
  20.6 1.2 %collective-permute-start.7 = (bf16[256,512]{1,0:T(8,128)(2,1)S(1)}, bf16[256,512]{1,0:T(8,128)(2,1)S(1)}, u32[]{:S(2)}, u32[]{:S(2)}) collective-permute-start(bf16[256,512]{1,0:T(8,128)(2,1)S(1)} %get-tuple-element.25), channel_id=1, source_target_pairs={{0,12},{4,0},{8,4},{12,8},{1,13},{5,1},{9,5},{13,9},{2,14},{6,2},{... | collective-permute-start | bytes 786440 | tf_op jit(solution)/shard_map/ppermute | solution.py:374
  21.9 5.3 %integrate.1 = (bf16[2,256,512]{2,1,0:T(8,128)(2,1)S(1)}, f32[16,256,128]{2,1,0:T(8,128)S(1)}) custom-call(s32[48]{0:T(128)S(1)} %copy-done.8, s32[4]{0:T(128)S(1)} %pad_add_fusion.1.place, f32[256,512]{1,0:T(8,128)S(1)} %get-tuple-element.18.after.own, s32[1,256]{1,0:T(1,128)S(1)} %bitcast.19, bf16[384,6144]{1,0:T(8,128)(2,1)S(1)} %copy-done.1, ...), custom_call_target="tpu_custom_call" | custom-call | flops 1 | bytes 1 | tf_op jit(solution)/shard_map/integrate/pallas_call | solution.py:89
  27.3 0.7 select.11
  28.0 1.2 %collective-permute-done.3 = bf16[2,256,512]{2,1,0:T(8,128)(2,1)S(1)} collective-permute-done((bf16[2,256,512]{2,1,0:T(8,128)(2,1)S(1)}, bf16[2,256,512]{2,1,0:T(8,128)(2,1)S(1)}, u32[]{:S(2)}, u32[]{:S(2)}) %collective-permute-start.3) | collective-permute-done | bytes 524320 | tf_op jit(solution)/shard_map/ppermute | solution.py:407
  29.3 0.6 collective-permute-start.4
  29.9 12.3 %collective-permute-done.6.refs_1_ = bf16[256,512]{1,0:T(8,128)(2,1)S(1)} collective-permute-done((bf16[256,512]{1,0:T(8,128)(2,1)S(1)}, bf16[256,512]{1,0:T(8,128)(2,1)S(1)}, u32[]{:S(2)}, u32[]{:S(2)}) %collective-permute-start.6) | collective-permute-done | bytes 262176 | tf_op jit(solution)/shard_map/ppermute | solution.py:374
  42.2 0.2 join.1
  42.4 0.1 multiply_reduce_fusion
  42.5 0.1 fusion.4.residual
  42.8 11.8 %collective-permute-start.9 = (bf16[256,512]{1,0:T(8,128)(2,1)S(1)}, bf16[256,512]{1,0:T(8,128)(2,1)S(1)}, u32[]{:S(2)}, u32[]{:S(2)}) collective-permute-start(bf16[256,512]{1,0:T(8,128)(2,1)S(1)} %fusion.4.residual), channel_id=1, source_target_pairs={{0,8},{4,12},{8,0},{12,4},{1,9},{5,13},{9,1},{13,5},{2,10},{6,14},... | collective-permute-start | bytes 786440 | tf_op jit(solution)/shard_map/ppermute | solution.py:374
  54.5 1.9 %collective-permute-start.8 = (bf16[256,512]{1,0:T(8,128)(2,1)S(1)}, bf16[256,512]{1,0:T(8,128)(2,1)S(1)}, u32[]{:S(2)}, u32[]{:S(2)}) collective-permute-start(bf16[256,512]{1,0:T(8,128)(2,1)S(1)} %fusion.4.residual), channel_id=1, source_target_pairs={{0,12},{4,0},{8,4},{12,8},{1,13},{5,1},{9,5},{13,9},{2,14},{6,2},{... | collective-permute-start | bytes 786440 | tf_op jit(solution)/shard_map/ppermute | solution.py:374
  56.5 5.8 %prepare.1 = (bf16[4096,1024]{1,0:T(8,128)(2,1)S(1)}, f32[4096,128]{1,0:T(8,128)S(1)}, f32[4096,512]{1,0:T(8,128)S(1)}) custom-call(s32[1]{0:T(128)} %bitcast.4.first_row, s32[8,128]{1,0:T(8,128)S(1)} %copy-done.4, bf16[256,512]{1,0:T(8,128)(2,1)S(1)} %fusion.4.residual, f32[4096,512]{1,0:T(8,128)S(1)} %bitcast.18), custom_call_target="tpu_custom_call" | custom-call | flops 1 | bytes 1 | tf_op jit(solution)/shard_map/prepare/pallas_call | solution.py:315
  62.3 6.2 %collective-permute-done.9.refs_1_ = bf16[256,512]{1,0:T(8,128)(2,1)S(1)} collective-permute-done((bf16[256,512]{1,0:T(8,128)(2,1)S(1)}, bf16[256,512]{1,0:T(8,128)(2,1)S(1)}, u32[]{:S(2)}, u32[]{:S(2)}) %collective-permute-start.9) | collective-permute-done | bytes 262176 | tf_op jit(solution)/shard_map/ppermute | solution.py:374
  68.5 5.7 %back_project.1 = f32[4096,512]{1,0:T(8,128)} custom-call(bf16[256,512]{1,0:T(8,128)(2,1)S(1)} %collective-permute-done.8.refs_0_, bf16[256,512]{1,0:T(8,128)(2,1)S(1)} %collective-permute-done.9.refs_1_, bf16[256,512]{1,0:T(8,128)(2,1)S(1)} %collective-permute-done.10.refs_2_, bf16[4096,1024]{1,0:T(8,128)(2,1)S(1)} %get-tuple-element.28.refs_3_, ...), custom_call_target="tpu_custom_call" | custom-call | flops 1 | bytes 1 | tf_op jit(solution)/shard_map/back_project/pallas_call | solution.py:360
  (33 shorter events, 0.3 us)
Async XLA Ops:
  0.0 7.2 %collective-permute-start.2 = (s32[2,128]{1,0:T(2,128)}, s32[2,128]{1,0:T(2,128)S(1)}, u32[]{:S(2)}, u32[]{:S(2)}) collective-permute-start(s32[2,128]{1,0:T(2,128)} %bitcast.20), channel_id=1, source_target_pairs={{0,4},{4,8},{8,12},{12,0},{1,5},{5,9},{9,13},{13,1},{2,6},{6,10},{... | collective-permute-start | bytes 3080 | tf_op jit(solution)/shard_map/ppermute | solution.py:374
  0.2 7.0 %collective-permute-start.1 = (s32[2,128]{1,0:T(2,128)}, s32[2,128]{1,0:T(2,128)S(1)}, u32[]{:S(2)}, u32[]{:S(2)}) collective-permute-start(s32[2,128]{1,0:T(2,128)} %bitcast.21), channel_id=1, source_target_pairs={{0,8},{4,12},{8,0},{12,4},{1,9},{5,13},{9,1},{13,5},{2,10},{6,14},... | collective-permute-start | bytes 3080 | tf_op jit(solution)/shard_map/ppermute | solution.py:374
  1.9 5.6 %collective-permute-start = (s32[2,128]{1,0:T(2,128)}, s32[2,128]{1,0:T(2,128)S(1)}, u32[]{:S(2)}, u32[]{:S(2)}) collective-permute-start(s32[2,128]{1,0:T(2,128)} %bitcast.22), channel_id=1, source_target_pairs={{0,12},{4,0},{8,4},{12,8},{1,13},{5,1},{9,5},{13,9},{2,14},{6,2},{... | collective-permute-start | bytes 3080 | tf_op jit(solution)/shard_map/ppermute | solution.py:374
  2.4 0.7 copy-start.6
  3.1 4.4 %copy-start.7 = (s32[256]{0:T(256)S(1)}, s32[256]{0:T(256)}, u32[]{:S(2)}) copy-start(s32[256]{0:T(256)} %param.8) | copy-start | bytes 3076
  7.5 9.9 %copy-start.3 = (s32[8,128]{1,0:T(8,128)}, s32[8,128]{1,0:T(8,128)S(1)}, u32[]{:S(2)}) copy-start(s32[8,128]{1,0:T(8,128)S(1)} %pad_add_fusion.rays) | copy-start | bytes 12292
  7.5 3.4 %copy-start = (f32[4096,512]{1,0:T(8,128)S(1)}, f32[4096,512]{1,0:T(8,128)}, u32[]{:S(2)}) copy-start(f32[4096,512]{1,0:T(8,128)} %image.3) | copy-start | bytes 25165828
  10.9 11.0 %copy-start.1 = (bf16[384,6144]{1,0:T(8,128)(2,1)S(1)}, bf16[384,6144]{1,0:T(8,128)(2,1)}, u32[]{:S(2)}) copy-start(bf16[384,6144]{1,0:T(8,128)(2,1)} %frames.1) | copy-start | bytes 14155780
  10.9 11.0 %copy-start.2 = (bf16[48,128,256]{2,1,0:T(8,128)(2,1)S(1)}, bf16[48,128,256]{2,1,0:T(8,128)(2,1)}, u32[]{:S(2)}) copy-start(bf16[48,128,256]{2,1,0:T(8,128)(2,1)} %weights.1) | copy-start | bytes 9437188
  10.9 11.0 %copy-start.5 = (s32[256]{0:T(256)S(1)}, s32[256]{0:T(256)}, u32[]{:S(2)}) copy-start(s32[256]{0:T(256)} %param.7) | copy-start | bytes 3076
  10.9 11.0 %copy-start.8 = (s32[48]{0:T(128)S(1)}, s32[48]{0:T(128)}, u32[]{:S(2)}) copy-start(s32[48]{0:T(128)} %tile_bin.1) | copy-start | bytes 580
  17.5 12.5 %collective-permute-start.5 = (bf16[256,512]{1,0:T(8,128)(2,1)S(1)}, bf16[256,512]{1,0:T(8,128)(2,1)S(1)}, u32[]{:S(2)}, u32[]{:S(2)}) collective-permute-start(bf16[256,512]{1,0:T(8,128)(2,1)S(1)} %get-tuple-element.23), channel_id=1, source_target_pairs={{0,4},{4,8},{8,12},{12,0},{1,5},{5,9},{9,13},{13,1},{2,6},{6,10},{... | collective-permute-start | bytes 786440 | tf_op jit(solution)/shard_map/ppermute | solution.py:374
  20.6 21.5 %collective-permute-start.6 = (bf16[256,512]{1,0:T(8,128)(2,1)S(1)}, bf16[256,512]{1,0:T(8,128)(2,1)S(1)}, u32[]{:S(2)}, u32[]{:S(2)}) collective-permute-start(bf16[256,512]{1,0:T(8,128)(2,1)S(1)} %get-tuple-element.24), channel_id=1, source_target_pairs={{0,8},{4,12},{8,0},{12,4},{1,9},{5,13},{9,1},{13,5},{2,10},{6,14},... | collective-permute-start | bytes 786440 | tf_op jit(solution)/shard_map/ppermute | solution.py:374
  20.6 21.5 %collective-permute-start.7 = (bf16[256,512]{1,0:T(8,128)(2,1)S(1)}, bf16[256,512]{1,0:T(8,128)(2,1)S(1)}, u32[]{:S(2)}, u32[]{:S(2)}) collective-permute-start(bf16[256,512]{1,0:T(8,128)(2,1)S(1)} %get-tuple-element.25), channel_id=1, source_target_pairs={{0,12},{4,0},{8,4},{12,8},{1,13},{5,1},{9,5},{13,9},{2,14},{6,2},{... | collective-permute-start | bytes 786440 | tf_op jit(solution)/shard_map/ppermute | solution.py:374
  27.2 2.0 %collective-permute-start.3 = (bf16[2,256,512]{2,1,0:T(8,128)(2,1)S(1)}, bf16[2,256,512]{2,1,0:T(8,128)(2,1)S(1)}, u32[]{:S(2)}, u32[]{:S(2)}) collective-permute-start(bf16[2,256,512]{2,1,0:T(8,128)(2,1)S(1)} %get-tuple-element.21), channel_id=1, source_target_pairs={{0,1},{1,0},{2,3},{3,2},{4,5},{5,4},{6,7},{7,6},{8,9},{9,8},{10,11... | collective-permute-start | bytes 1572872 | tf_op jit(solution)/shard_map/ppermute | solution.py:407
  29.2 27.3 %slice-start = ((s8[8388608]{0:T(1024)(128)(4,1)}), s8[4194304]{0:T(1024)(128)(4,1)S(1)}, s32[]{:S(2)}) async-start(s8[8388608]{0:T(1024)(128)(4,1)} %bitcast.17), calls=%async_computation | async-start | bytes 8388608
  29.3 27.2 %slice-start.1 = ((s8[8388608]{0:T(1024)(128)(4,1)}), s8[4194304]{0:T(1024)(128)(4,1)S(1)}, s32[]{:S(2)}) async-start(s8[8388608]{0:T(1024)(128)(4,1)} %bitcast.17), calls=%async_computation.1 | async-start | bytes 8388608
  29.3 27.2 %copy-start.4 = (s32[8,128]{1,0:T(8,128)S(1)}, s32[8,128]{1,0:T(8,128)}, u32[]{:S(2)}) copy-start(s32[8,128]{1,0:T(8,128)} %copy-done.3) | copy-start | bytes 12292
  29.3 13.2 %collective-permute-start.4 = (bf16[256,512]{1,0:T(8,128)(2,1)S(1)}, bf16[256,512]{1,0:T(8,128)(2,1)S(1)}, u32[]{:S(2)}, u32[]{:S(2)}) collective-permute-start(bf16[256,512]{1,0:T(8,128)(2,1)S(1)} %fusion), channel_id=1, source_target_pairs={{0,2},{1,3},{2,0},{3,1},{4,6},{5,7},{6,4},{7,5},{8,10},{9,11},{10,... | collective-permute-start | bytes 786440 | tf_op jit(solution)/shard_map/ppermute | solution.py:374
  42.7 19.6 %collective-permute-start.10 = (bf16[256,512]{1,0:T(8,128)(2,1)S(1)}, bf16[256,512]{1,0:T(8,128)(2,1)S(1)}, u32[]{:S(2)}, u32[]{:S(2)}) collective-permute-start(bf16[256,512]{1,0:T(8,128)(2,1)S(1)} %fusion.4.residual), channel_id=1, source_target_pairs={{0,4},{4,8},{8,12},{12,0},{1,5},{5,9},{9,13},{13,1},{2,6},{6,10},{... | collective-permute-start | bytes 786440 | tf_op jit(solution)/shard_map/ppermute | solution.py:374
  42.8 25.8 %collective-permute-start.9 = (bf16[256,512]{1,0:T(8,128)(2,1)S(1)}, bf16[256,512]{1,0:T(8,128)(2,1)S(1)}, u32[]{:S(2)}, u32[]{:S(2)}) collective-permute-start(bf16[256,512]{1,0:T(8,128)(2,1)S(1)} %fusion.4.residual), channel_id=1, source_target_pairs={{0,8},{4,12},{8,0},{12,4},{1,9},{5,13},{9,1},{13,5},{2,10},{6,14},... | collective-permute-start | bytes 786440 | tf_op jit(solution)/shard_map/ppermute | solution.py:374
  54.5 14.0 %collective-permute-start.8 = (bf16[256,512]{1,0:T(8,128)(2,1)S(1)}, bf16[256,512]{1,0:T(8,128)(2,1)S(1)}, u32[]{:S(2)}, u32[]{:S(2)}) collective-permute-start(bf16[256,512]{1,0:T(8,128)(2,1)S(1)} %fusion.4.residual), channel_id=1, source_target_pairs={{0,12},{4,0},{8,4},{12,8},{1,13},{5,1},{9,5},{13,9},{2,14},{6,2},{... | collective-permute-start | bytes 786440 | tf_op jit(solution)/shard_map/ppermute | solution.py:374

commit v5 on v4

--- a/solution.py
+++ b/solution.py
@@ -137,18 +137,27 @@
 
 
 def row_groups(rows):
-    sizes = [min(4, rows)]
+    sizes = [min(2, rows)]
     while sum(sizes) < rows:
-        sizes.append(min(8, rows - sum(sizes)))
+        sizes.append(min(6, rows - sum(sizes)))
     return sizes
 
 
 def project_kernel(angles, first_row, after, rays, image, *refs):
-    outs, (cosine, base, tile_a, tile_b, total) = refs[:-5], refs[-5:]
+    outs, (staged, cosine, base, tile_a, tile_b, total, arrived) = refs[:-7], refs[-7:]
     parts = len(outs)
     points = total.shape[0] // parts
     tiles = (tile_a, tile_b)
     sizes = row_groups(image.shape[0] // LANES)
+
+    def cells(group):
+        return slice(sum(sizes[:group]) * LANES, sum(sizes[: group + 1]) * LANES)
+
+    def load(group):
+        here = cells(group)
+        return pltpu.make_async_copy(
+            image.at[here, :], staged.at[here, :], arrived.at[group]
+        )
 
     def fill(group):
         first = first_row[0] + sum(sizes[:group])
@@ -156,6 +165,8 @@
             upos = (first + i).astype(F32) - HALF
             tiles[group % 2][:, i * LANES : (i + 1) * LANES] = hat(base[...] + cosine[...] * upos)
 
+    for group in range(min(2, len(sizes))):
+        load(group).start()
     cos_c, sin_c, off_c = ray_geometry(rays[...], angles)
     vpos = lax.broadcasted_iota(jnp.int32, (LANES, LANES), 1).astype(F32) - HALF
     for k in range(rays.shape[0]):
@@ -167,11 +178,12 @@
     for group, size in enumerate(sizes):
         if group + 1 < len(sizes):
             fill(group + 1)
-        start = sum(sizes[:group]) * LANES
-        width = size * LANES
+        load(group).wait()
+        if group + 2 < len(sizes):
+            load(group + 2).start()
         product = jnp.dot(
-            tiles[group % 2][:, :width],
-            image[start : start + width, :].astype(BF16),
+            tiles[group % 2][:, : size * LANES],
+            staged[cells(group), :].astype(BF16),
             preferred_element_type=F32,
         )
         if group == 0:
@@ -189,23 +201,22 @@
     cells, chans = image.shape
     all_points = rays.shape[0] * LANES
     points = all_points // len(kinds)
-    widest = max(row_groups(cells // LANES)) * LANES
+    sizes = row_groups(cells // LANES)
+    widest = max(sizes) * LANES
     vmem = pl.BlockSpec(memory_space=pltpu.VMEM)
+    anywhere = pl.BlockSpec(memory_space=pl.ANY)
     return pl.pallas_call(
         functools.partial(project_kernel, angles),
-        in_specs=[
-            pl.BlockSpec(memory_space=pltpu.SMEM),
-            pl.BlockSpec(memory_space=pl.ANY),
-            vmem,
-            vmem,
-        ],
+        in_specs=[pl.BlockSpec(memory_space=pltpu.SMEM), anywhere, vmem, anywhere],
         out_specs=[vmem] * len(kinds),
         scratch_shapes=[
+            pltpu.VMEM((cells, chans), F32),
             pltpu.VMEM((all_points, LANES), F32),
             pltpu.VMEM((all_points, LANES), F32),
             pltpu.VMEM((all_points, widest), BF16),
             pltpu.VMEM((all_points, widest), BF16),
             pltpu.VMEM((all_points, chans), F32),
+            pltpu.SemaphoreType.DMA((len(sizes),)),
         ],
         out_shape=[jax.ShapeDtypeStruct((points, chans), kind) for kind in kinds],
         compiler_params=pltpu.CompilerParams(vmem_limit_bytes=40 * MIB),
@@ -213,7 +224,7 @@
             flops=4 * all_points * cells * chans, bytes_accessed=4 * cells * chans, transcendentals=0
         ),
         name="project",
-    )(first_row, after, rays, image)
+    )(first_row, after, rays, pltpu.with_memory_space_constraint(image, pltpu.HBM))
 
 
 def row_total_kernel(angles, rays, row_total):
@@ -275,10 +286,11 @@
     )(row_total, own, *arrived)
 
 
-def prepare_kernel(angles, first_row, rays, residual, image, tile, recip, partial, base, cosine):
+def prepare_kernel(angles, early, first_row, rays, *refs):
+    residuals, (image, tile, recip, partial, base, cosine) = refs[:early], refs[early:]
     step = pl.program_id(0)
     chunks = rays.shape[0]
-    points, chans = residual.shape
+    points, chans = residuals[0].shape
     rows = tile.shape[0] // LANES
 
     @pl.when(step == 0)
@@ -300,24 +312,27 @@
             sums += value.astype(F32)
         total = jnp.sum(sums, axis=1, keepdims=True)
         recip[here, :] = jnp.broadcast_to(1.0 / total, (LANES, LANES))
-    back = jnp.dot(tile[:, :points], residual[...], preferred_element_type=F32)
+    joined = jnp.concatenate([r[...] for r in residuals], axis=0)
+    back = jnp.dot(tile[:, : early * points], joined, preferred_element_type=F32)
     for j in range(chans // LANES):
         lanes = slice(j * LANES, (j + 1) * LANES)
         partial[:, lanes] = image[:, lanes] + back[:, lanes] * recip[...]
 
 
-def prepare(rays, residual, image, first_row, angles):
+def prepare(rays, residuals, image, first_row, angles):
     cells, chans = image.shape
     all_points = rays.shape[0] * LANES
     rows = min(4, cells // LANES)
     fixed = lambda shape: pl.BlockSpec(shape, lambda i, *_: (0, 0))
     sliding = lambda width: pl.BlockSpec((rows * LANES, width), lambda i, *_: (i, 0))
     return pl.pallas_call(
-        functools.partial(prepare_kernel, angles),
+        functools.partial(prepare_kernel, angles, len(residuals)),
         grid_spec=pltpu.PrefetchScalarGridSpec(
             num_scalar_prefetch=1,
             grid=(cells // (rows * LANES),),
-            in_specs=[fixed(rays.shape), fixed(residual.shape), sliding(chans)],
+            in_specs=[fixed(rays.shape)]
+            + [fixed(r.shape) for r in residuals]
+            + [sliding(chans)],
             out_specs=[sliding(all_points), sliding(LANES), sliding(chans)],
             scratch_shapes=[pltpu.VMEM((LANES, all_points), F32), pltpu.VMEM(rays.shape, F32)],
         ),
@@ -329,42 +344,51 @@
         compiler_params=pltpu.CompilerParams(vmem_limit_bytes=16 * MIB),
         cost_estimate=SMALL,
         name="prepare",
-    )(first_row, rays, residual, image)
+    )(first_row, rays, *residuals, image)
 
 
 def back_kernel(parts, *refs):
-    residuals, (tile, recip, partial, out, joined) = refs[:parts], refs[parts:]
-    step = pl.program_id(0)
+    residuals, (tile, recip, partial, out, joined, staged, sent) = refs[:parts], refs[parts:]
     points, chans = residuals[0].shape
-    rows = out.shape[0]
-
-    @pl.when(step == 0)
-    def _():
-        for d in range(parts):
-            joined[d * points : (d + 1) * points, :] = residuals[d][...]
-
-    here = pl.ds(pl.multiple_of(step * rows, rows), rows)
-    back = jnp.dot(tile[here, points:], joined[...], preferred_element_type=F32)
-    scale = recip[here, :]
-    for j in range(chans // LANES):
-        lanes = slice(j * LANES, (j + 1) * LANES)
-        out[:, lanes] = partial[here, lanes] + back[:, lanes] * scale
+    skip = tile.shape[1] - parts * points
+    chunks = sent.shape[0]
+    rows = out.shape[0] // chunks
+
+    for d in range(parts):
+        joined[d * points : (d + 1) * points, :] = residuals[d][...]
+    copies = []
+    for chunk in range(chunks):
+        here = slice(chunk * rows, (chunk + 1) * rows)
+        back = jnp.dot(tile[here, skip:], joined[...], preferred_element_type=F32)
+        scale = recip[here, :]
+        for j in range(chans // LANES):
+            lanes = slice(j * LANES, (j + 1) * LANES)
+            staged[here, lanes] = partial[here, lanes] + back[:, lanes] * scale
+        copies.append(
+            pltpu.make_async_copy(staged.at[here, :], out.at[here, :], sent.at[chunk])
+        )
+        copies[-1].start()
+    for copy in copies:
+        copy.wait()
 
 
 def back_project(residuals, tile, recip, partial):
     cells, chans = partial.shape
     parts = len(residuals)
     points = residuals[0].shape[0]
-    rows = min(1024, cells)
+    chunks = max(1, cells // 512)
     vmem = pl.BlockSpec(memory_space=pltpu.VMEM)
     return pl.pallas_call(
         functools.partial(back_kernel, parts),
-        grid=(cells // rows,),
         in_specs=[vmem] * (parts + 3),
-        out_specs=pl.BlockSpec((rows, chans), lambda i: (i, 0)),
-        scratch_shapes=[pltpu.VMEM((parts * points, chans), BF16)],
+        out_specs=pl.BlockSpec(memory_space=pl.ANY),
+        scratch_shapes=[
+            pltpu.VMEM((parts * points, chans), BF16),
+            pltpu.VMEM((cells, chans), F32),
+            pltpu.SemaphoreType.DMA((chunks,)),
+        ],
         out_shape=jax.ShapeDtypeStruct((cells, chans), F32),
-        compiler_params=pltpu.CompilerParams(vmem_limit_bytes=12 * MIB),
+        compiler_params=pltpu.CompilerParams(vmem_limit_bytes=16 * MIB),
         cost_estimate=SMALL,
         name="back_project",
     )(*residuals, tile, recip, partial)
@@ -385,14 +409,15 @@
     x_me, core_me = chan_me // 2, chan_me % 2
     first_row = (lax.axis_index("scan") * (cells // NIMG)).astype(jnp.int32).reshape(1)
 
+    order = sorted(range(1, n_scan), key=lambda d: (2 * d != n_scan, d))
     own_rays = point_ray.reshape(points // LANES, LANES)
-    rays = [own_rays] + [rotate(own_rays, "scan", -d, n_scan) for d in range(1, n_scan)]
+    rays = [own_rays] + [rotate(own_rays, "scan", -d, n_scan) for d in order]
     all_rays = jnp.concatenate(rays, axis=0)
 
     row_total = row_totals(own_rays, angles)
     kinds = [F32] + [BF16] * (n_scan - 1)
-    shares = project(all_rays, image, first_row, row_total, angles, kinds)
-    arrived = [rotate(shares[d], "scan", d, n_scan) for d in range(1, n_scan)]
+    own_share, *shares = project(all_rays, image, first_row, row_total, angles, kinds)
+    arrived = [rotate(share, "scan", d, n_scan) for d, share in zip(order, shares)]
 
     place = []
     for e in range(nx):
@@ -400,7 +425,7 @@
         place += [2 * xi + 1 - core_me, 2 * xi + core_me]
     place = jnp.stack(place).astype(jnp.int32)
     send, sums = integrate(
-        frames, counts, channel_pair_weights, tile_bin, place, shares[0], nx, chans
+        frames, counts, channel_pair_weights, tile_bin, place, own_share, nx, chans
     )
     keep = select(place, sums, nx, chans)
     partner = [(i, i ^ 1) for i in range(n_chan)]
@@ -410,11 +435,11 @@
         joined = (keep[e] + got[e].astype(F32)).astype(BF16)
         pattern = pattern + rotate(joined, "chan", 2 * e, n_chan).astype(F32)
 
-    scaled, recip = join(row_total, shares[0], arrived)
+    scaled, recip = join(row_total, own_share, arrived)
     residual = (pattern * (float(NIMG) * recip[:, :1]) - scaled).astype(BF16)
-    others = [rotate(residual, "scan", -d, n_scan) for d in range(1, n_scan)]
-    tile, col_recip, partial = prepare(all_rays, residual, image, first_row, angles)
-    return back_project(others, tile, col_recip, partial)
+    others = [rotate(residual, "scan", -d, n_scan) for d in order]
+    tile, col_recip, partial = prepare(all_rays, [residual, others[0]], image, first_row, angles)
+    return back_project(others[1:], tile, col_recip, partial)
 
 
 def solution(mesh):

time: 74.4 us -> 73.1 us (0.983)
  the two profiles are of different devices: /device:TPU:30 before, /device:TPU:0 now
where the time goes in v5:
time: 73.1 us; the launch traced here: 73 us
  Pallas kernels  27.7 us (38%)
  waiting for transfers between devices  22.2 us (30%)
  starting transfers between devices  21.7 us (30%)
  local copies, waits for them, and re-layouts  0.77 us (1%)
    ppermute x10, starting transfers between devices, rotate(): return lax.ppermute(x, axis, [(i, (i + shift) % n) for i in range(n)])  21.6 us
    ppermute x10, waiting for transfers between devices, rotate(): return lax.ppermute(x, axis, [(i, (i + shift) % n) for i in range(n)])  20.9 us
    pallas_call x1, Pallas kernels, project(): pl.pallas_call(functools.partial(project_kernel, angles), in_specs=[pl.Bl...  7.31 us
    pallas_call x1, Pallas kernels, prepare(): pl.pallas_call(functools.partial(prepare_kernel, angles, len(residuals)),...  6.23 us
    pallas_call x1, Pallas kernels, integrate(): pl.pallas_call(functools.partial(integrate_kernel, nx, chans // tile_bins...  5.43 us
    pallas_call x1, Pallas kernels, row_totals(): pl.pallas_call(functools.partial(row_total_kernel, angles), in_specs=[vme...  4.06 us
    pallas_call x1, Pallas kernels, back_project(): pl.pallas_call(functools.partial(back_kernel, parts), in_specs=[vmem] * (...  3.81 us
  transfers between devices with their start and end apart: 11, of which 4 were waited for; matrix products, arithmetic and copies ran while one was open for 0% of the time, Pallas kernels for 23%

profile of v5, /device:TPU:0, one launch (start us, length us, event | category | flops | bytes accessed | tf_op | source)
XLA Modules:
  0.0 73.0 jit_solution(11239339846322044128)
XLA Ops:
  0.0 3.0 %collective-permute-start.2 = (s32[2,128]{1,0:T(2,128)}, s32[2,128]{1,0:T(2,128)S(1)}, u32[]{:S(2)}, u32[]{:S(2)}) collective-permute-start(s32[2,128]{1,0:T(2,128)} %bitcast.20), channel_id=1, source_target_pairs={{0,4},{4,8},{8,12},{12,0},{1,5},{5,9},{9,13},{13,1},{2,6},{6,10},{... | collective-permute-start | bytes 3080 | tf_op jit(solution)/shard_map/ppermute | solution.py:398
  3.0 2.0 %collective-permute-start.1 = (s32[2,128]{1,0:T(2,128)}, s32[2,128]{1,0:T(2,128)S(1)}, u32[]{:S(2)}, u32[]{:S(2)}) collective-permute-start(s32[2,128]{1,0:T(2,128)} %bitcast.21), channel_id=1, source_target_pairs={{0,12},{4,0},{8,4},{12,8},{1,13},{5,1},{9,5},{13,9},{2,14},{6,2},{... | collective-permute-start | bytes 3080 | tf_op jit(solution)/shard_map/ppermute | solution.py:398
  5.1 1.0 %collective-permute-start = (s32[2,128]{1,0:T(2,128)}, s32[2,128]{1,0:T(2,128)S(1)}, u32[]{:S(2)}, u32[]{:S(2)}) collective-permute-start(s32[2,128]{1,0:T(2,128)} %bitcast.22), channel_id=1, source_target_pairs={{0,8},{4,12},{8,0},{12,4},{1,9},{5,13},{9,1},{13,5},{2,10},{6,14},... | collective-permute-start | bytes 3080 | tf_op jit(solution)/shard_map/ppermute | solution.py:398
  6.1 0.7 copy-done.5
  6.8 4.1 %row_totals.1.after.row_total = f32[256,128]{1,0:T(8,128)S(1)} custom-call(s32[2,128]{1,0:T(2,128)S(1)} %bitcast.23), custom_call_target="tpu_custom_call" | custom-call | flops 99999997952 | bytes 100000000 | tf_op jit(solution)/shard_map/row_totals/pallas_call | solution.py:251
  10.9 0.1 pad_add_fusion.1.place
  11.0 7.3 %project.1 = (f32[256,512]{1,0:T(8,128)S(1)}, bf16[256,512]{1,0:T(8,128)(2,1)S(1)}, bf16[256,512]{1,0:T(8,128)(2,1)S(1)}, bf16[256,512]{1,0:T(8,128)(2,1)S(1)}) custom-call(s32[1]{0:T(128)} %bitcast.4.first_row, f32[256,128]{1,0:T(8,128)S(1)} %row_totals.1.after.row_total, s32[8,128]{1,0:T(8,128)S(1)} %pad_add_fusion.rays, f32[4096,512]{1,0:T(8,128)} %refs_2_.1), custom_call_target="tpu_custom_call" | custom-call | flops 8589934592 | bytes 8388608 | tf_op jit(solution)/shard_map/project/pallas_call | solution.py:208
  18.4 2.0 %collective-permute-start.5 = (bf16[256,512]{1,0:T(8,128)(2,1)S(1)}, bf16[256,512]{1,0:T(8,128)(2,1)S(1)}, u32[]{:S(2)}, u32[]{:S(2)}) collective-permute-start(bf16[256,512]{1,0:T(8,128)(2,1)S(1)} %get-tuple-element.23), channel_id=1, source_target_pairs={{0,8},{4,12},{8,0},{12,4},{1,9},{5,13},{9,1},{13,5},{2,10},{6,14},... | collective-permute-start | bytes 786440 | tf_op jit(solution)/shard_map/ppermute | solution.py:398
  20.4 3.8 %collective-permute-start.7 = (bf16[256,512]{1,0:T(8,128)(2,1)S(1)}, bf16[256,512]{1,0:T(8,128)(2,1)S(1)}, u32[]{:S(2)}, u32[]{:S(2)}) collective-permute-start(bf16[256,512]{1,0:T(8,128)(2,1)S(1)} %get-tuple-element.25), channel_id=1, source_target_pairs={{0,12},{4,0},{8,4},{12,8},{1,13},{5,1},{9,5},{13,9},{2,14},{6,2},{... | collective-permute-start | bytes 786440 | tf_op jit(solution)/shard_map/ppermute | solution.py:398
  24.2 5.4 %integrate.1 = (bf16[2,256,512]{2,1,0:T(8,128)(2,1)S(1)}, f32[16,256,128]{2,1,0:T(8,128)S(1)}) custom-call(s32[48]{0:T(128)S(1)} %copy-done.7, s32[4]{0:T(128)S(1)} %pad_add_fusion.1.place, f32[256,512]{1,0:T(8,128)S(1)} %get-tuple-element.18.after.own, s32[1,256]{1,0:T(1,128)S(1)} %bitcast.19, bf16[384,6144]{1,0:T(8,128)(2,1)S(1)} %copy-done, ...), custom_call_target="tpu_custom_call" | custom-call | flops 1 | bytes 1 | tf_op jit(solution)/shard_map/integrate/pallas_call | solution.py:89
  29.7 0.7 select.11
  30.4 1.2 %collective-permute-done.3 = bf16[2,256,512]{2,1,0:T(8,128)(2,1)S(1)} collective-permute-done((bf16[2,256,512]{2,1,0:T(8,128)(2,1)S(1)}, bf16[2,256,512]{2,1,0:T(8,128)(2,1)S(1)}, u32[]{:S(2)}, u32[]{:S(2)}) %collective-permute-start.3) | collective-permute-done | bytes 524320 | tf_op jit(solution)/shard_map/ppermute | solution.py:432
  31.7 1.8 %collective-permute-start.4 = (bf16[256,512]{1,0:T(8,128)(2,1)S(1)}, bf16[256,512]{1,0:T(8,128)(2,1)S(1)}, u32[]{:S(2)}, u32[]{:S(2)}) collective-permute-start(bf16[256,512]{1,0:T(8,128)(2,1)S(1)} %fusion), channel_id=1, source_target_pairs={{0,2},{1,3},{2,0},{3,1},{4,6},{5,7},{6,4},{7,5},{8,10},{9,11},{10,... | collective-permute-start | bytes 786440 | tf_op jit(solution)/shard_map/ppermute | solution.py:398
  33.5 5.5 %collective-permute-done.5.refs_0_ = bf16[256,512]{1,0:T(8,128)(2,1)S(1)} collective-permute-done((bf16[256,512]{1,0:T(8,128)(2,1)S(1)}, bf16[256,512]{1,0:T(8,128)(2,1)S(1)}, u32[]{:S(2)}, u32[]{:S(2)}) %collective-permute-start.5) | collective-permute-done | bytes 262176 | tf_op jit(solution)/shard_map/ppermute | solution.py:398
  39.0 0.2 join.1
  39.2 0.1 multiply_reduce_fusion
  39.3 0.8 %collective-permute-done.4 = bf16[256,512]{1,0:T(8,128)(2,1)S(1)} collective-permute-done((bf16[256,512]{1,0:T(8,128)(2,1)S(1)}, bf16[256,512]{1,0:T(8,128)(2,1)S(1)}, u32[]{:S(2)}, u32[]{:S(2)}) %collective-permute-start.4) | collective-permute-done | bytes 262176 | tf_op jit(solution)/shard_map/ppermute | solution.py:398
  40.1 0.1 fusion.4.refs_0_
  40.3 4.2 %collective-permute-start.10 = (bf16[256,512]{1,0:T(8,128)(2,1)S(1)}, bf16[256,512]{1,0:T(8,128)(2,1)S(1)}, u32[]{:S(2)}, u32[]{:S(2)}) collective-permute-start(bf16[256,512]{1,0:T(8,128)(2,1)S(1)} %fusion.4.refs_0_), channel_id=1, source_target_pairs={{0,8},{4,12},{8,0},{12,4},{1,9},{5,13},{9,1},{13,5},{2,10},{6,14},... | collective-permute-start | bytes 786440 | tf_op jit(solution)/shard_map/ppermute | solution.py:398
  44.4 0.2 collective-permute-start.9
  44.6 3.7 %collective-permute-start.8 = (bf16[256,512]{1,0:T(8,128)(2,1)S(1)}, bf16[256,512]{1,0:T(8,128)(2,1)S(1)}, u32[]{:S(2)}, u32[]{:S(2)}) collective-permute-start(bf16[256,512]{1,0:T(8,128)(2,1)S(1)} %fusion.4.refs_0_), channel_id=1, source_target_pairs={{0,12},{4,0},{8,4},{12,8},{1,13},{5,1},{9,5},{13,9},{2,14},{6,2},{... | collective-permute-start | bytes 786440 | tf_op jit(solution)/shard_map/ppermute | solution.py:398
  48.3 14.6 %collective-permute-done.10.refs_1_ = bf16[256,512]{1,0:T(8,128)(2,1)S(1)} collective-permute-done((bf16[256,512]{1,0:T(8,128)(2,1)S(1)}, bf16[256,512]{1,0:T(8,128)(2,1)S(1)}, u32[]{:S(2)}, u32[]{:S(2)}) %collective-permute-start.10) | collective-permute-done | bytes 262176 | tf_op jit(solution)/shard_map/ppermute | solution.py:398
  62.9 6.2 %prepare.1 = (bf16[4096,1024]{1,0:T(8,128)(2,1)S(1)}, f32[4096,128]{1,0:T(8,128)S(1)}, f32[4096,512]{1,0:T(8,128)S(1)}) custom-call(s32[1]{0:T(128)} %bitcast.4.first_row, s32[8,128]{1,0:T(8,128)S(1)} %copy-done.3, bf16[256,512]{1,0:T(8,128)(2,1)S(1)} %fusion.4.refs_0_, bf16[256,512]{1,0:T(8,128)(2,1)S(1)} %collective-permute-done.10.refs_1_, ...), custom_call_target="tpu_custom_call" | custom-call | flops 1 | bytes 1 | tf_op jit(solution)/shard_map/prepare/pallas_call | solution.py:328
  69.2 3.8 %back_project.1 = f32[4096,512]{1,0:T(8,128)} custom-call(bf16[256,512]{1,0:T(8,128)(2,1)S(1)} %collective-permute-done.8.refs_0_, bf16[256,512]{1,0:T(8,128)(2,1)S(1)} %collective-permute-done.9.refs_1_, bf16[4096,1024]{1,0:T(8,128)(2,1)S(1)} %get-tuple-element.28.refs_2_, f32[4096,128]{1,0:T(8,128)S(1)} %get-tuple-element.29.refs_3_, ...), custom_call_target="tpu_custom_call" | custom-call | flops 1 | bytes 1 | tf_op jit(solution)/shard_map/back_project/pallas_call | solution.py:381
  (31 shorter events, 0.2 us)
Async XLA Ops:
  0.0 10.9 %collective-permute-start.2 = (s32[2,128]{1,0:T(2,128)}, s32[2,128]{1,0:T(2,128)S(1)}, u32[]{:S(2)}, u32[]{:S(2)}) collective-permute-start(s32[2,128]{1,0:T(2,128)} %bitcast.20), channel_id=1, source_target_pairs={{0,4},{4,8},{8,12},{12,0},{1,5},{5,9},{9,13},{13,1},{2,6},{6,10},{... | collective-permute-start | bytes 3080 | tf_op jit(solution)/shard_map/ppermute | solution.py:398
  3.0 7.9 %collective-permute-start.1 = (s32[2,128]{1,0:T(2,128)}, s32[2,128]{1,0:T(2,128)S(1)}, u32[]{:S(2)}, u32[]{:S(2)}) collective-permute-start(s32[2,128]{1,0:T(2,128)} %bitcast.21), channel_id=1, source_target_pairs={{0,12},{4,0},{8,4},{12,8},{1,13},{5,1},{9,5},{13,9},{2,14},{6,2},{... | collective-permute-start | bytes 3080 | tf_op jit(solution)/shard_map/ppermute | solution.py:398
  5.1 5.9 %collective-permute-start = (s32[2,128]{1,0:T(2,128)}, s32[2,128]{1,0:T(2,128)S(1)}, u32[]{:S(2)}, u32[]{:S(2)}) collective-permute-start(s32[2,128]{1,0:T(2,128)} %bitcast.22), channel_id=1, source_target_pairs={{0,8},{4,12},{8,0},{12,4},{1,9},{5,13},{9,1},{13,5},{2,10},{6,14},... | collective-permute-start | bytes 3080 | tf_op jit(solution)/shard_map/ppermute | solution.py:398
  6.1 0.7 copy-start.5
  6.8 4.2 %copy-start.6 = (s32[256]{0:T(256)S(1)}, s32[256]{0:T(256)}, u32[]{:S(2)}) copy-start(s32[256]{0:T(256)} %param.8) | copy-start | bytes 3076
  11.0 7.4 %copy-start.2 = (s32[8,128]{1,0:T(8,128)}, s32[8,128]{1,0:T(8,128)S(1)}, u32[]{:S(2)}) copy-start(s32[8,128]{1,0:T(8,128)S(1)} %pad_add_fusion.rays) | copy-start | bytes 12292
  11.0 13.2 %copy-start = (bf16[384,6144]{1,0:T(8,128)(2,1)S(1)}, bf16[384,6144]{1,0:T(8,128)(2,1)}, u32[]{:S(2)}) copy-start(bf16[384,6144]{1,0:T(8,128)(2,1)} %frames.1) | copy-start | bytes 14155780
  11.0 13.2 %copy-start.1 = (bf16[48,128,256]{2,1,0:T(8,128)(2,1)S(1)}, bf16[48,128,256]{2,1,0:T(8,128)(2,1)}, u32[]{:S(2)}) copy-start(bf16[48,128,256]{2,1,0:T(8,128)(2,1)} %weights.1) | copy-start | bytes 9437188
  11.0 13.2 %copy-start.4 = (s32[256]{0:T(256)S(1)}, s32[256]{0:T(256)}, u32[]{:S(2)}) copy-start(s32[256]{0:T(256)} %param.7) | copy-start | bytes 3076
  11.0 13.2 %copy-start.7 = (s32[48]{0:T(128)S(1)}, s32[48]{0:T(128)}, u32[]{:S(2)}) copy-start(s32[48]{0:T(128)} %tile_bin.1) | copy-start | bytes 580
  18.4 20.6 %collective-permute-start.5 = (bf16[256,512]{1,0:T(8,128)(2,1)S(1)}, bf16[256,512]{1,0:T(8,128)(2,1)S(1)}, u32[]{:S(2)}, u32[]{:S(2)}) collective-permute-start(bf16[256,512]{1,0:T(8,128)(2,1)S(1)} %get-tuple-element.23), channel_id=1, source_target_pairs={{0,8},{4,12},{8,0},{12,4},{1,9},{5,13},{9,1},{13,5},{2,10},{6,14},... | collective-permute-start | bytes 786440 | tf_op jit(solution)/shard_map/ppermute | solution.py:398
  20.4 18.6 %collective-permute-start.6 = (bf16[256,512]{1,0:T(8,128)(2,1)S(1)}, bf16[256,512]{1,0:T(8,128)(2,1)S(1)}, u32[]{:S(2)}, u32[]{:S(2)}) collective-permute-start(bf16[256,512]{1,0:T(8,128)(2,1)S(1)} %get-tuple-element.24), channel_id=1, source_target_pairs={{0,4},{4,8},{8,12},{12,0},{1,5},{5,9},{9,13},{13,1},{2,6},{6,10},{... | collective-permute-start | bytes 786440 | tf_op jit(solution)/shard_map/ppermute | solution.py:398
  20.4 18.6 %collective-permute-start.7 = (bf16[256,512]{1,0:T(8,128)(2,1)S(1)}, bf16[256,512]{1,0:T(8,128)(2,1)S(1)}, u32[]{:S(2)}, u32[]{:S(2)}) collective-permute-start(bf16[256,512]{1,0:T(8,128)(2,1)S(1)} %get-tuple-element.25), channel_id=1, source_target_pairs={{0,12},{4,0},{8,4},{12,8},{1,13},{5,1},{9,5},{13,9},{2,14},{6,2},{... | collective-permute-start | bytes 786440 | tf_op jit(solution)/shard_map/ppermute | solution.py:398
  29.6 2.0 %collective-permute-start.3 = (bf16[2,256,512]{2,1,0:T(8,128)(2,1)S(1)}, bf16[2,256,512]{2,1,0:T(8,128)(2,1)S(1)}, u32[]{:S(2)}, u32[]{:S(2)}) collective-permute-start(bf16[2,256,512]{2,1,0:T(8,128)(2,1)S(1)} %get-tuple-element.21), channel_id=1, source_target_pairs={{0,1},{1,0},{2,3},{3,2},{4,5},{5,4},{6,7},{7,6},{8,9},{9,8},{10,11... | collective-permute-start | bytes 1572872 | tf_op jit(solution)/shard_map/ppermute | solution.py:432
  31.6 31.3 %slice-start = ((s8[8388608]{0:T(1024)(128)(4,1)}), s8[4194304]{0:T(1024)(128)(4,1)S(1)}, s32[]{:S(2)}) async-start(s8[8388608]{0:T(1024)(128)(4,1)} %bitcast.17), calls=%async_computation | async-start | bytes 8388608
  31.7 31.2 %slice-start.1 = ((s8[8388608]{0:T(1024)(128)(4,1)}), s8[4194304]{0:T(1024)(128)(4,1)S(1)}, s32[]{:S(2)}) async-start(s8[8388608]{0:T(1024)(128)(4,1)} %bitcast.17), calls=%async_computation.1 | async-start | bytes 8388608
  31.7 31.2 %copy-start.3 = (s32[8,128]{1,0:T(8,128)S(1)}, s32[8,128]{1,0:T(8,128)}, u32[]{:S(2)}) copy-start(s32[8,128]{1,0:T(8,128)} %copy-done.2) | copy-start | bytes 12292
  31.7 8.4 %collective-permute-start.4 = (bf16[256,512]{1,0:T(8,128)(2,1)S(1)}, bf16[256,512]{1,0:T(8,128)(2,1)S(1)}, u32[]{:S(2)}, u32[]{:S(2)}) collective-permute-start(bf16[256,512]{1,0:T(8,128)(2,1)S(1)} %fusion), channel_id=1, source_target_pairs={{0,2},{1,3},{2,0},{3,1},{4,6},{5,7},{6,4},{7,5},{8,10},{9,11},{10,... | collective-permute-start | bytes 786440 | tf_op jit(solution)/shard_map/ppermute | solution.py:398
  40.3 22.6 %collective-permute-start.10 = (bf16[256,512]{1,0:T(8,128)(2,1)S(1)}, bf16[256,512]{1,0:T(8,128)(2,1)S(1)}, u32[]{:S(2)}, u32[]{:S(2)}) collective-permute-start(bf16[256,512]{1,0:T(8,128)(2,1)S(1)} %fusion.4.refs_0_), channel_id=1, source_target_pairs={{0,8},{4,12},{8,0},{12,4},{1,9},{5,13},{9,1},{13,5},{2,10},{6,14},... | collective-permute-start | bytes 786440 | tf_op jit(solution)/shard_map/ppermute | solution.py:398
  44.4 24.7 %collective-permute-start.9 = (bf16[256,512]{1,0:T(8,128)(2,1)S(1)}, bf16[256,512]{1,0:T(8,128)(2,1)S(1)}, u32[]{:S(2)}, u32[]{:S(2)}) collective-permute-start(bf16[256,512]{1,0:T(8,128)(2,1)S(1)} %fusion.4.refs_0_), channel_id=1, source_target_pairs={{0,4},{4,8},{8,12},{12,0},{1,5},{5,9},{9,13},{13,1},{2,6},{6,10},{... | collective-permute-start | bytes 786440 | tf_op jit(solution)/shard_map/ppermute | solution.py:398
  44.6 24.6 %collective-permute-start.8 = (bf16[256,512]{1,0:T(8,128)(2,1)S(1)}, bf16[256,512]{1,0:T(8,128)(2,1)S(1)}, u32[]{:S(2)}, u32[]{:S(2)}) collective-permute-start(bf16[256,512]{1,0:T(8,128)(2,1)S(1)} %fusion.4.refs_0_), channel_id=1, source_target_pairs={{0,12},{4,0},{8,4},{12,8},{1,13},{5,1},{9,5},{13,9},{2,14},{6,2},{... | collective-permute-start | bytes 786440 | tf_op jit(solution)/shard_map/ppermute | solution.py:398

commit v6 on v5

--- a/solution.py
+++ b/solution.py
@@ -143,10 +143,8 @@
     return sizes
 
 
-def project_kernel(angles, first_row, after, rays, image, *refs):
-    outs, (staged, cosine, base, tile_a, tile_b, total, arrived) = refs[:-7], refs[-7:]
-    parts = len(outs)
-    points = total.shape[0] // parts
+def project_kernel(angles, first_row, image, out, staged, base, tile_a, tile_b, total, arrived):
+    cos_tab, sin_tab = angle_tables(angles)
     tiles = (tile_a, tile_b)
     sizes = row_groups(image.shape[0] // LANES)
 
@@ -163,17 +161,17 @@
         first = first_row[0] + sum(sizes[:group])
         for i in range(sizes[group]):
             upos = (first + i).astype(F32) - HALF
-            tiles[group % 2][:, i * LANES : (i + 1) * LANES] = hat(base[...] + cosine[...] * upos)
+            lanes = slice(i * LANES, (i + 1) * LANES)
+            for a in range(angles):
+                here = slice(a * NIMG, (a + 1) * NIMG)
+                tiles[group % 2][here, lanes] = hat(base[here, :] + upos * cos_tab[a])
 
     for group in range(min(2, len(sizes))):
         load(group).start()
-    cos_c, sin_c, off_c = ray_geometry(rays[...], angles)
-    vpos = lax.broadcasted_iota(jnp.int32, (LANES, LANES), 1).astype(F32) - HALF
-    for k in range(rays.shape[0]):
-        here = slice(k * LANES, (k + 1) * LANES)
-        column = lambda x: jnp.transpose(jnp.broadcast_to(x[k : k + 1, :], (LANES, LANES)))
-        cosine[here, :] = column(cos_c)
-        base[here, :] = column(sin_c) * vpos - column(off_c)
+    vpos = lax.broadcasted_iota(jnp.int32, (NIMG, LANES), 1).astype(F32) - HALF
+    offset = lax.broadcasted_iota(jnp.int32, (NIMG, LANES), 0).astype(F32) - HALF
+    for a in range(angles):
+        base[a * NIMG : (a + 1) * NIMG, :] = sin_tab[a] * vpos - offset
     fill(0)
     for group, size in enumerate(sizes):
         if group + 1 < len(sizes):
@@ -191,77 +189,108 @@
         elif group + 1 < len(sizes):
             total[...] += product
         else:
-            product += total[...]
-            for d in range(parts):
-                here = slice(d * points, (d + 1) * points)
-                outs[d][...] = product[here, :].astype(outs[d].dtype)
-
-
-def project(rays, image, first_row, after, angles, kinds):
+            out[...] = (total[...] + product).astype(out.dtype)
+
+
+def project(image, first_row, angles):
     cells, chans = image.shape
-    all_points = rays.shape[0] * LANES
-    points = all_points // len(kinds)
+    rays = angles * NIMG
     sizes = row_groups(cells // LANES)
     widest = max(sizes) * LANES
     vmem = pl.BlockSpec(memory_space=pltpu.VMEM)
     anywhere = pl.BlockSpec(memory_space=pl.ANY)
     return pl.pallas_call(
         functools.partial(project_kernel, angles),
-        in_specs=[pl.BlockSpec(memory_space=pltpu.SMEM), anywhere, vmem, anywhere],
-        out_specs=[vmem] * len(kinds),
+        in_specs=[pl.BlockSpec(memory_space=pltpu.SMEM), anywhere],
+        out_specs=vmem,
         scratch_shapes=[
             pltpu.VMEM((cells, chans), F32),
-            pltpu.VMEM((all_points, LANES), F32),
-            pltpu.VMEM((all_points, LANES), F32),
-            pltpu.VMEM((all_points, widest), BF16),
-            pltpu.VMEM((all_points, widest), BF16),
-            pltpu.VMEM((all_points, chans), F32),
+            pltpu.VMEM((rays, LANES), F32),
+            pltpu.VMEM((rays, widest), BF16),
+            pltpu.VMEM((rays, widest), BF16),
+            pltpu.VMEM((rays, chans), F32),
             pltpu.SemaphoreType.DMA((len(sizes),)),
         ],
-        out_shape=[jax.ShapeDtypeStruct((points, chans), kind) for kind in kinds],
+        out_shape=jax.ShapeDtypeStruct((rays, chans), BF16),
         compiler_params=pltpu.CompilerParams(vmem_limit_bytes=40 * MIB),
         cost_estimate=pl.CostEstimate(
-            flops=4 * all_points * cells * chans, bytes_accessed=4 * cells * chans, transcendentals=0
+            flops=4 * rays * cells * chans, bytes_accessed=4 * cells * chans, transcendentals=0
         ),
         name="project",
-    )(first_row, after, rays, pltpu.with_memory_space_constraint(image, pltpu.HBM))
-
-
-def row_total_kernel(angles, rays, row_total):
+    )(first_row, pltpu.with_memory_space_constraint(image, pltpu.HBM))
+
+
+def reorder_kernel(rays, rows, *refs):
+    outs, hot = refs[:-1], refs[-1]
+    all_rays = rows.shape[0]
+    points = outs[0].shape[0]
+    together = hot.shape[0]
+    number = lax.broadcasted_iota(jnp.int32, (LANES, all_rays), 1)
+    for start in range(0, len(outs) * points, together):
+        for k in range(together // LANES):
+            row = start // LANES + k
+            wanted = jnp.transpose(jnp.broadcast_to(rays[row : row + 1, :], (LANES, LANES)))
+            hot[k * LANES : (k + 1) * LANES, :] = (number == wanted[:, :1]).astype(F32).astype(BF16)
+        picked = jnp.dot(hot[...], rows[...], preferred_element_type=F32).astype(BF16)
+        for k in range(0, together, points):
+            outs[(start + k) // points][...] = picked[k : k + points, :]
+
+
+def reorder(rays, rows, parts):
+    all_rays, chans = rows.shape
+    points = rays.shape[0] * LANES // parts
+    together = max(points, min(all_rays, MIB // all_rays))
+    vmem = pl.BlockSpec(memory_space=pltpu.VMEM)
+    return pl.pallas_call(
+        reorder_kernel,
+        in_specs=[vmem, vmem],
+        out_specs=[vmem] * parts,
+        scratch_shapes=[pltpu.VMEM((together, all_rays), BF16)],
+        out_shape=[jax.ShapeDtypeStruct((points, chans), BF16)] * parts,
+        compiler_params=pltpu.CompilerParams(vmem_limit_bytes=16 * MIB),
+        cost_estimate=SMALL,
+        name="reorder",
+    )(rays, rows)
+
+
+def row_total_kernel(angles, after, rays, row_total):
     cos_r, sin_r, off_r = ray_geometry(rays[...], angles)
-    vpos = lax.broadcasted_iota(jnp.int32, (LANES, LANES), 0).astype(F32) - HALF
+    line = lax.broadcasted_iota(jnp.int32, (LANES, LANES), 0).astype(F32) - HALF
     for k in range(rays.shape[0]):
-        base = sin_r[k : k + 1, :] * vpos - off_r[k : k + 1, :]
-        slope = cos_r[k : k + 1, :]
-
-        def add_row(i, sums):
-            upos = i.astype(F32) - HALF
-            return sums + hat(base + slope * upos).astype(F32)
-
-        sums = lax.fori_loop(0, NIMG, add_row, jnp.zeros((LANES, LANES), F32), unroll=4)
+        cosine, sine, offset = (x[k : k + 1, :] for x in (cos_r, sin_r, off_r))
+        along_u = jnp.abs(cosine) >= jnp.abs(sine)
+        steep = jnp.where(along_u, cosine, sine)
+        flat = jnp.where(along_u, sine, cosine)
+        crossing = jnp.floor((offset - flat * line) / steep + HALF)
+        sums = jnp.zeros((LANES, LANES), F32)
+        for near in range(-1, 3):
+            cell = crossing + float(near)
+            weight = hat(flat * line + steep * (cell - HALF) - offset).astype(F32)
+            inside = jnp.logical_and(cell >= 0.0, cell <= NIMG - 1.0)
+            sums += jnp.where(inside, weight, 0.0)
         total = jnp.sum(sums, axis=0, keepdims=True)
         row_total[k * LANES : (k + 1) * LANES, :] = jnp.transpose(
             jnp.broadcast_to(total, (LANES, LANES))
         )
 
 
-def row_totals(rays, angles):
+def row_totals(rays, after, angles):
     points = rays.shape[0] * LANES
     vmem = pl.BlockSpec(memory_space=pltpu.VMEM)
     return pl.pallas_call(
         functools.partial(row_total_kernel, angles),
-        in_specs=[vmem],
+        in_specs=[pl.BlockSpec(memory_space=pl.ANY), vmem],
         out_specs=vmem,
         out_shape=jax.ShapeDtypeStruct((points, LANES), F32),
         compiler_params=pltpu.CompilerParams(vmem_limit_bytes=8 * MIB),
-        cost_estimate=LARGE,
+        cost_estimate=SMALL,
         name="row_totals",
-    )(rays)
+    )(after, rays)
 
 
 def join_kernel(row_total, own, *refs):
     arrived, (scaled, recip) = refs[:-2], refs[-2:]
-    total = own[...]
+    total = own[...].astype(F32)
     for part in arrived:
         total += part[...].astype(F32)
     recip[...] = 1.0 / row_total[...]
@@ -414,9 +443,8 @@
     rays = [own_rays] + [rotate(own_rays, "scan", -d, n_scan) for d in order]
     all_rays = jnp.concatenate(rays, axis=0)
 
-    row_total = row_totals(own_rays, angles)
-    kinds = [F32] + [BF16] * (n_scan - 1)
-    own_share, *shares = project(all_rays, image, first_row, row_total, angles, kinds)
+    projected = project(image, first_row, angles)
+    own_share, *shares = reorder(all_rays, projected, n_scan)
     arrived = [rotate(share, "scan", d, n_scan) for d, share in zip(order, shares)]
 
     place = []
@@ -435,11 +463,12 @@
         joined = (keep[e] + got[e].astype(F32)).astype(BF16)
         pattern = pattern + rotate(joined, "chan", 2 * e, n_chan).astype(F32)
 
+    row_total = row_totals(own_rays, sums, angles)
     scaled, recip = join(row_total, own_share, arrived)
     residual = (pattern * (float(NIMG) * recip[:, :1]) - scaled).astype(BF16)
     others = [rotate(residual, "scan", -d, n_scan) for d in order]
-    tile, col_recip, partial = prepare(all_rays, [residual, others[0]], image, first_row, angles)
-    return back_project(others[1:], tile, col_recip, partial)
+    tile, col_recip, partial = prepare(all_rays, [residual], image, first_row, angles)
+    return back_project(others, tile, col_recip, partial)
 
 
 def solution(mesh):

time: 73.1 us -> 71.6 us (0.979)
  starting transfers between devices: 21.7 us -> 17.6 us
  local copies, waits for them, and re-layouts: 0.77 us -> 4.56 us
  Pallas kernels: 27.7 us -> 25.5 us
  waiting for transfers between devices: 22.2 us -> 23 us
    ppermute x10, starting transfers between devices: 21.6 us -> 17.6 us  [rotate(): return lax.ppermute(x, axis, [(i, (i + shift) % n) for i in range(n)])]
    unnamed x20 -> x22, local copies, waits for them, and re-layouts: 0.77 us -> 4.56 us
    pallas_call x1 -> x2, Pallas kernels: 4.06 us -> 2.11 us  [the longest x1 1.69 us: reorder(): pl.pallas_call(reorder_kernel, in_specs=[vmem, vmem], out_specs=[vmem] *...]
    ppermute x10, waiting for transfers between devices: 20.9 us -> 22.2 us  [rotate(): return lax.ppermute(x, axis, [(i, (i + shift) % n) for i in range(n)])]
  transfers between devices with their start and end apart: 11 -> 11, of which waited for: 4 -> 6; matrix products, arithmetic and copies ran while one was open for 0% -> 0% of each run, Pallas kernels for 23% -> 27%
where the time goes in v6:
time: 71.6 us; the launch traced here: 71.4 us
  Pallas kernels  25.5 us (36%)
  waiting for transfers between devices  23 us (32%)
  starting transfers between devices  17.6 us (25%)
  local copies, waits for them, and re-layouts  4.56 us (6%)
    ppermute x10, waiting for transfers between devices, rotate(): return lax.ppermute(x, axis, [(i, (i + shift) % n) for i in range(n)])  22.2 us
    ppermute x10, starting transfers between devices, rotate(): return lax.ppermute(x, axis, [(i, (i + shift) % n) for i in range(n)])  17.6 us
    pallas_call x1, Pallas kernels, project(): pl.pallas_call(functools.partial(project_kernel, angles), in_specs=[pl.Bl...  6.79 us
    pallas_call x1, Pallas kernels, prepare(): pl.pallas_call(functools.partial(prepare_kernel, angles, len(residuals)),...  5.82 us
    pallas_call x1, Pallas kernels, integrate(): pl.pallas_call(functools.partial(integrate_kernel, nx, chans // tile_bins...  5.36 us
    unnamed x22, local copies, waits for them, and re-layouts  4.56 us
    pallas_call x1, Pallas kernels, back_project(): pl.pallas_call(functools.partial(back_kernel, parts), in_specs=[vmem] * (...  4.51 us
    pallas_call x1, Pallas kernels, reorder(): pl.pallas_call(reorder_kernel, in_specs=[vmem, vmem], out_specs=[vmem] *...  1.69 us
  transfers between devices with their start and end apart: 11, of which 6 were waited for; matrix products, arithmetic and copies ran while one was open for 0% of the time, Pallas kernels for 27%

profile of v6, /device:TPU:0, one launch (start us, length us, event | category | flops | bytes accessed | tf_op | source)
XLA Modules:
  0.0 71.4 jit_solution(11717650962653011460)
XLA Ops:
  0.0 3.0 %collective-permute-start.2 = (s32[2,128]{1,0:T(2,128)}, s32[2,128]{1,0:T(2,128)S(1)}, u32[]{:S(2)}, u32[]{:S(2)}) collective-permute-start(s32[2,128]{1,0:T(2,128)} %bitcast.19), channel_id=1, source_target_pairs={{0,4},{4,8},{8,12},{12,0},{1,5},{5,9},{9,13},{13,1},{2,6},{6,10},{... | collective-permute-start | bytes 3080 | tf_op jit(solution)/shard_map/ppermute | solution.py:427
  3.0 2.0 %collective-permute-start.1 = (s32[2,128]{1,0:T(2,128)}, s32[2,128]{1,0:T(2,128)S(1)}, u32[]{:S(2)}, u32[]{:S(2)}) collective-permute-start(s32[2,128]{1,0:T(2,128)} %bitcast.20), channel_id=1, source_target_pairs={{0,12},{4,0},{8,4},{12,8},{1,13},{5,1},{9,5},{13,9},{2,14},{6,2},{... | collective-permute-start | bytes 3080 | tf_op jit(solution)/shard_map/ppermute | solution.py:427
  5.1 1.0 %collective-permute-start = (s32[2,128]{1,0:T(2,128)}, s32[2,128]{1,0:T(2,128)S(1)}, u32[]{:S(2)}, u32[]{:S(2)}) collective-permute-start(s32[2,128]{1,0:T(2,128)} %bitcast.21), channel_id=1, source_target_pairs={{0,8},{4,12},{8,0},{12,4},{1,9},{5,13},{9,1},{13,5},{2,10},{6,14},... | collective-permute-start | bytes 3080 | tf_op jit(solution)/shard_map/ppermute | solution.py:427
  6.1 6.8 %project.1.rows = bf16[1024,512]{1,0:T(8,128)(2,1)S(1)} custom-call(s32[1]{0:T(128)} %bitcast.5.first_row, f32[4096,512]{1,0:T(8,128)} %refs_1_.1), custom_call_target="tpu_custom_call" | custom-call | flops 8589934592 | bytes 8388608 | tf_op jit(solution)/shard_map/project/pallas_call | solution.py:202
  12.9 1.0 %copy-done.2 = bf16[1024,512]{1,0:T(8,128)(2,1)} copy-done((bf16[1024,512]{1,0:T(8,128)(2,1)}, bf16[1024,512]{1,0:T(8,128)(2,1)S(1)}, u32[]{:S(2)}) %copy-start.2) | copy-done | bytes 1048600
  14.0 1.2 %copy-done.3 = bf16[1024,512]{1,0:T(8,128)(2,1)S(1)} copy-done((bf16[1024,512]{1,0:T(8,128)(2,1)S(1)}, bf16[1024,512]{1,0:T(8,128)(2,1)}, u32[]{:S(2)}) %copy-start.3) | copy-done | bytes 1048600
  15.2 1.7 %reorder.1 = (bf16[256,512]{1,0:T(8,128)(2,1)S(1)}, bf16[256,512]{1,0:T(8,128)(2,1)S(1)}, bf16[256,512]{1,0:T(8,128)(2,1)S(1)}, bf16[256,512]{1,0:T(8,128)(2,1)S(1)}) custom-call(s32[8,128]{1,0:T(8,128)S(1)} %pad_add_fusion.rays, bf16[1024,512]{1,0:T(8,128)(2,1)S(1)} %copy-done.3), custom_call_target="tpu_custom_call" | custom-call | flops 1 | bytes 1 | tf_op jit(solution)/shard_map/reorder/pallas_call | solution.py:244
  16.9 2.0 %collective-permute-start.5 = (bf16[256,512]{1,0:T(8,128)(2,1)S(1)}, bf16[256,512]{1,0:T(8,128)(2,1)S(1)}, u32[]{:S(2)}, u32[]{:S(2)}) collective-permute-start(bf16[256,512]{1,0:T(8,128)(2,1)S(1)} %get-tuple-element.23), channel_id=1, source_target_pairs={{0,8},{4,12},{8,0},{12,4},{1,9},{5,13},{9,1},{13,5},{2,10},{6,14},... | collective-permute-start | bytes 786440 | tf_op jit(solution)/shard_map/ppermute | solution.py:427
  18.9 3.8 %collective-permute-start.7 = (bf16[256,512]{1,0:T(8,128)(2,1)S(1)}, bf16[256,512]{1,0:T(8,128)(2,1)S(1)}, u32[]{:S(2)}, u32[]{:S(2)}) collective-permute-start(bf16[256,512]{1,0:T(8,128)(2,1)S(1)} %get-tuple-element.25), channel_id=1, source_target_pairs={{0,12},{4,0},{8,4},{12,8},{1,13},{5,1},{9,5},{13,9},{2,14},{6,2},{... | collective-permute-start | bytes 786440 | tf_op jit(solution)/shard_map/ppermute | solution.py:427
  22.7 2.3 %copy-done = bf16[384,6144]{1,0:T(8,128)(2,1)S(1)} copy-done((bf16[384,6144]{1,0:T(8,128)(2,1)S(1)}, bf16[384,6144]{1,0:T(8,128)(2,1)}, u32[]{:S(2)}) %copy-start) | copy-done | bytes 4718616
  25.1 5.4 %integrate.1 = (bf16[2,256,512]{2,1,0:T(8,128)(2,1)S(1)}, f32[16,256,128]{2,1,0:T(8,128)S(1)}) custom-call(s32[48]{0:T(128)S(1)} %copy-done.8, s32[4]{0:T(128)S(1)} %pad_add_fusion.1.place, bf16[256,512]{1,0:T(8,128)(2,1)S(1)} %get-tuple-element.18.after.own, s32[1,256]{1,0:T(1,128)S(1)} %bitcast.24, bf16[384,6144]{1,0:T(8,128)(2,1)S(1)} %copy-done, ...), custom_call_target="tpu_custom_call" | custom-call | flops 1 | bytes 1 | tf_op jit(solution)/shard_map/integrate/pallas_call | solution.py:89
  30.5 0.7 select.11
  31.2 0.4 row_totals.1.row_total
  31.6 0.8 %collective-permute-done.3 = bf16[2,256,512]{2,1,0:T(8,128)(2,1)S(1)} collective-permute-done((bf16[2,256,512]{2,1,0:T(8,128)(2,1)S(1)}, bf16[2,256,512]{2,1,0:T(8,128)(2,1)S(1)}, u32[]{:S(2)}, u32[]{:S(2)}) %collective-permute-start.3) | collective-permute-done | bytes 524320 | tf_op jit(solution)/shard_map/ppermute | solution.py:460
  32.5 1.8 %collective-permute-start.4 = (bf16[256,512]{1,0:T(8,128)(2,1)S(1)}, bf16[256,512]{1,0:T(8,128)(2,1)S(1)}, u32[]{:S(2)}, u32[]{:S(2)}) collective-permute-start(bf16[256,512]{1,0:T(8,128)(2,1)S(1)} %fusion), channel_id=1, source_target_pairs={{0,2},{1,3},{2,0},{3,1},{4,6},{5,7},{6,4},{7,5},{8,10},{9,11},{10,... | collective-permute-start | bytes 786440 | tf_op jit(solution)/shard_map/ppermute | solution.py:427
  34.3 3.2 %collective-permute-done.5.refs_0_ = bf16[256,512]{1,0:T(8,128)(2,1)S(1)} collective-permute-done((bf16[256,512]{1,0:T(8,128)(2,1)S(1)}, bf16[256,512]{1,0:T(8,128)(2,1)S(1)}, u32[]{:S(2)}, u32[]{:S(2)}) %collective-permute-start.5) | collective-permute-done | bytes 262176 | tf_op jit(solution)/shard_map/ppermute | solution.py:427
  37.9 3.1 %collective-permute-done.4 = bf16[256,512]{1,0:T(8,128)(2,1)S(1)} collective-permute-done((bf16[256,512]{1,0:T(8,128)(2,1)S(1)}, bf16[256,512]{1,0:T(8,128)(2,1)S(1)}, u32[]{:S(2)}, u32[]{:S(2)}) %collective-permute-start.4) | collective-permute-done | bytes 262176 | tf_op jit(solution)/shard_map/ppermute | solution.py:427
  41.0 2.0 %collective-permute-start.10 = (bf16[256,512]{1,0:T(8,128)(2,1)S(1)}, bf16[256,512]{1,0:T(8,128)(2,1)S(1)}, u32[]{:S(2)}, u32[]{:S(2)}) collective-permute-start(bf16[256,512]{1,0:T(8,128)(2,1)S(1)} %fusion.4.refs_0_), channel_id=1, source_target_pairs={{0,4},{4,8},{8,12},{12,0},{1,5},{5,9},{9,13},{13,1},{2,6},{6,10},{... | collective-permute-start | bytes 786440 | tf_op jit(solution)/shard_map/ppermute | solution.py:427
  43.1 1.9 %collective-permute-start.9 = (bf16[256,512]{1,0:T(8,128)(2,1)S(1)}, bf16[256,512]{1,0:T(8,128)(2,1)S(1)}, u32[]{:S(2)}, u32[]{:S(2)}) collective-permute-start(bf16[256,512]{1,0:T(8,128)(2,1)S(1)} %fusion.4.refs_0_), channel_id=1, source_target_pairs={{0,12},{4,0},{8,4},{12,8},{1,13},{5,1},{9,5},{13,9},{2,14},{6,2},{... | collective-permute-start | bytes 786440 | tf_op jit(solution)/shard_map/ppermute | solution.py:427
  45.0 5.8 %prepare.1 = (bf16[4096,1024]{1,0:T(8,128)(2,1)S(1)}, f32[4096,128]{1,0:T(8,128)S(1)}, f32[4096,512]{1,0:T(8,128)S(1)}) custom-call(s32[1]{0:T(128)} %bitcast.5.first_row, s32[8,128]{1,0:T(8,128)S(1)} %copy-done.5, bf16[256,512]{1,0:T(8,128)(2,1)S(1)} %fusion.4.refs_0_, f32[4096,512]{1,0:T(8,128)S(1)} %bitcast.18), custom_call_target="tpu_custom_call" | custom-call | flops 1 | bytes 1 | tf_op jit(solution)/shard_map/prepare/pallas_call | solution.py:357
  50.8 1.3 %collective-permute-done.10.refs_2_ = bf16[256,512]{1,0:T(8,128)(2,1)S(1)} collective-permute-done((bf16[256,512]{1,0:T(8,128)(2,1)S(1)}, bf16[256,512]{1,0:T(8,128)(2,1)S(1)}, u32[]{:S(2)}, u32[]{:S(2)}) %collective-permute-start.10) | collective-permute-done | bytes 262176 | tf_op jit(solution)/shard_map/ppermute | solution.py:427
  52.2 3.5 %collective-permute-done.9.refs_1_ = bf16[256,512]{1,0:T(8,128)(2,1)S(1)} collective-permute-done((bf16[256,512]{1,0:T(8,128)(2,1)S(1)}, bf16[256,512]{1,0:T(8,128)(2,1)S(1)}, u32[]{:S(2)}, u32[]{:S(2)}) %collective-permute-start.9) | collective-permute-done | bytes 262176 | tf_op jit(solution)/shard_map/ppermute | solution.py:427
  55.7 11.1 %collective-permute-done.8.refs_0_ = bf16[256,512]{1,0:T(8,128)(2,1)S(1)} collective-permute-done((bf16[256,512]{1,0:T(8,128)(2,1)S(1)}, bf16[256,512]{1,0:T(8,128)(2,1)S(1)}, u32[]{:S(2)}, u32[]{:S(2)}) %collective-permute-start.8) | collective-permute-done | bytes 262176 | tf_op jit(solution)/shard_map/ppermute | solution.py:427
  66.7 4.5 %back_project.1 = f32[4096,512]{1,0:T(8,128)} custom-call(bf16[256,512]{1,0:T(8,128)(2,1)S(1)} %collective-permute-done.8.refs_0_, bf16[256,512]{1,0:T(8,128)(2,1)S(1)} %collective-permute-done.9.refs_1_, bf16[256,512]{1,0:T(8,128)(2,1)S(1)} %collective-permute-done.10.refs_2_, bf16[4096,1024]{1,0:T(8,128)(2,1)S(1)} %get-tuple-element.28.refs_3_, ...), custom_call_target="tpu_custom_call" | custom-call | flops 1 | bytes 1 | tf_op jit(solution)/shard_map/back_project/pallas_call | solution.py:410
  (34 shorter events, 0.8 us)
Async XLA Ops:
  0.0 13.8 %collective-permute-start.2 = (s32[2,128]{1,0:T(2,128)}, s32[2,128]{1,0:T(2,128)S(1)}, u32[]{:S(2)}, u32[]{:S(2)}) collective-permute-start(s32[2,128]{1,0:T(2,128)} %bitcast.19), channel_id=1, source_target_pairs={{0,4},{4,8},{8,12},{12,0},{1,5},{5,9},{9,13},{13,1},{2,6},{6,10},{... | collective-permute-start | bytes 3080 | tf_op jit(solution)/shard_map/ppermute | solution.py:427
  3.0 10.8 %collective-permute-start.1 = (s32[2,128]{1,0:T(2,128)}, s32[2,128]{1,0:T(2,128)S(1)}, u32[]{:S(2)}, u32[]{:S(2)}) collective-permute-start(s32[2,128]{1,0:T(2,128)} %bitcast.20), channel_id=1, source_target_pairs={{0,12},{4,0},{8,4},{12,8},{1,13},{5,1},{9,5},{13,9},{2,14},{6,2},{... | collective-permute-start | bytes 3080 | tf_op jit(solution)/shard_map/ppermute | solution.py:427
  5.1 8.8 %collective-permute-start = (s32[2,128]{1,0:T(2,128)}, s32[2,128]{1,0:T(2,128)S(1)}, u32[]{:S(2)}, u32[]{:S(2)}) collective-permute-start(s32[2,128]{1,0:T(2,128)} %bitcast.21), channel_id=1, source_target_pairs={{0,8},{4,12},{8,0},{12,4},{1,9},{5,13},{9,1},{13,5},{2,10},{6,14},... | collective-permute-start | bytes 3080 | tf_op jit(solution)/shard_map/ppermute | solution.py:427
  6.1 7.8 %copy-start.6 = (s32[256]{0:T(256)S(1)}, s32[256]{0:T(256)}, u32[]{:S(2)}) copy-start(s32[256]{0:T(256)} %param.8) | copy-start | bytes 3076
  6.1 16.6 %copy-start.1 = (bf16[48,128,256]{2,1,0:T(8,128)(2,1)S(1)}, bf16[48,128,256]{2,1,0:T(8,128)(2,1)}, u32[]{:S(2)}) copy-start(bf16[48,128,256]{2,1,0:T(8,128)(2,1)} %weights.1) | copy-start | bytes 9437188
  6.1 16.6 %copy-start.7 = (s32[256]{0:T(256)S(1)}, s32[256]{0:T(256)}, u32[]{:S(2)}) copy-start(s32[256]{0:T(256)} %param.7) | copy-start | bytes 3076
  6.1 16.6 %copy-start.8 = (s32[48]{0:T(128)S(1)}, s32[48]{0:T(128)}, u32[]{:S(2)}) copy-start(s32[48]{0:T(128)} %tile_bin.1) | copy-start | bytes 580
  12.9 1.0 %copy-start.2 = (bf16[1024,512]{1,0:T(8,128)(2,1)}, bf16[1024,512]{1,0:T(8,128)(2,1)S(1)}, u32[]{:S(2)}) copy-start(bf16[1024,512]{1,0:T(8,128)(2,1)S(1)} %project.1.rows) | copy-start | bytes 3145732
  13.9 8.8 %copy-start.4 = (s32[8,128]{1,0:T(8,128)}, s32[8,128]{1,0:T(8,128)S(1)}, u32[]{:S(2)}) copy-start(s32[8,128]{1,0:T(8,128)S(1)} %pad_add_fusion.rays) | copy-start | bytes 12292
  14.0 1.2 %copy-start.3 = (bf16[1024,512]{1,0:T(8,128)(2,1)S(1)}, bf16[1024,512]{1,0:T(8,128)(2,1)}, u32[]{:S(2)}) copy-start(bf16[1024,512]{1,0:T(8,128)(2,1)} %copy-done.2) | copy-start | bytes 3145732
  16.9 20.6 %collective-permute-start.5 = (bf16[256,512]{1,0:T(8,128)(2,1)S(1)}, bf16[256,512]{1,0:T(8,128)(2,1)S(1)}, u32[]{:S(2)}, u32[]{:S(2)}) collective-permute-start(bf16[256,512]{1,0:T(8,128)(2,1)S(1)} %get-tuple-element.23), channel_id=1, source_target_pairs={{0,8},{4,12},{8,0},{12,4},{1,9},{5,13},{9,1},{13,5},{2,10},{6,14},... | collective-permute-start | bytes 786440 | tf_op jit(solution)/shard_map/ppermute | solution.py:427
  18.9 18.6 %collective-permute-start.6 = (bf16[256,512]{1,0:T(8,128)(2,1)S(1)}, bf16[256,512]{1,0:T(8,128)(2,1)S(1)}, u32[]{:S(2)}, u32[]{:S(2)}) collective-permute-start(bf16[256,512]{1,0:T(8,128)(2,1)S(1)} %get-tuple-element.24), channel_id=1, source_target_pairs={{0,4},{4,8},{8,12},{12,0},{1,5},{5,9},{9,13},{13,1},{2,6},{6,10},{... | collective-permute-start | bytes 786440 | tf_op jit(solution)/shard_map/ppermute | solution.py:427
  18.9 18.6 %collective-permute-start.7 = (bf16[256,512]{1,0:T(8,128)(2,1)S(1)}, bf16[256,512]{1,0:T(8,128)(2,1)S(1)}, u32[]{:S(2)}, u32[]{:S(2)}) collective-permute-start(bf16[256,512]{1,0:T(8,128)(2,1)S(1)} %get-tuple-element.25), channel_id=1, source_target_pairs={{0,12},{4,0},{8,4},{12,8},{1,13},{5,1},{9,5},{13,9},{2,14},{6,2},{... | collective-permute-start | bytes 786440 | tf_op jit(solution)/shard_map/ppermute | solution.py:427
  22.7 2.3 %copy-start = (bf16[384,6144]{1,0:T(8,128)(2,1)S(1)}, bf16[384,6144]{1,0:T(8,128)(2,1)}, u32[]{:S(2)}) copy-start(bf16[384,6144]{1,0:T(8,128)(2,1)} %frames.1) | copy-start | bytes 14155780
  30.4 2.0 %collective-permute-start.3 = (bf16[2,256,512]{2,1,0:T(8,128)(2,1)S(1)}, bf16[2,256,512]{2,1,0:T(8,128)(2,1)S(1)}, u32[]{:S(2)}, u32[]{:S(2)}) collective-permute-start(bf16[2,256,512]{2,1,0:T(8,128)(2,1)S(1)} %get-tuple-element.21), channel_id=1, source_target_pairs={{0,1},{1,0},{2,3},{3,2},{4,5},{5,4},{6,7},{7,6},{8,9},{9,8},{10,11... | collective-permute-start | bytes 1572872 | tf_op jit(solution)/shard_map/ppermute | solution.py:460
  32.4 12.6 %slice-start = ((s8[8388608]{0:T(1024)(128)(4,1)}), s8[4194304]{0:T(1024)(128)(4,1)S(1)}, s32[]{:S(2)}) async-start(s8[8388608]{0:T(1024)(128)(4,1)} %bitcast.17), calls=%async_computation | async-start | bytes 8388608
  32.5 12.5 %slice-start.1 = ((s8[8388608]{0:T(1024)(128)(4,1)}), s8[4194304]{0:T(1024)(128)(4,1)S(1)}, s32[]{:S(2)}) async-start(s8[8388608]{0:T(1024)(128)(4,1)} %bitcast.17), calls=%async_computation.1 | async-start | bytes 8388608
  32.5 12.5 %copy-start.5 = (s32[8,128]{1,0:T(8,128)S(1)}, s32[8,128]{1,0:T(8,128)}, u32[]{:S(2)}) copy-start(s32[8,128]{1,0:T(8,128)} %copy-done.4) | copy-start | bytes 12292
  32.5 8.4 %collective-permute-start.4 = (bf16[256,512]{1,0:T(8,128)(2,1)S(1)}, bf16[256,512]{1,0:T(8,128)(2,1)S(1)}, u32[]{:S(2)}, u32[]{:S(2)}) collective-permute-start(bf16[256,512]{1,0:T(8,128)(2,1)S(1)} %fusion), channel_id=1, source_target_pairs={{0,2},{1,3},{2,0},{3,1},{4,6},{5,7},{6,4},{7,5},{8,10},{9,11},{10,... | collective-permute-start | bytes 786440 | tf_op jit(solution)/shard_map/ppermute | solution.py:427
  41.0 11.1 %collective-permute-start.10 = (bf16[256,512]{1,0:T(8,128)(2,1)S(1)}, bf16[256,512]{1,0:T(8,128)(2,1)S(1)}, u32[]{:S(2)}, u32[]{:S(2)}) collective-permute-start(bf16[256,512]{1,0:T(8,128)(2,1)S(1)} %fusion.4.refs_0_), channel_id=1, source_target_pairs={{0,4},{4,8},{8,12},{12,0},{1,5},{5,9},{9,13},{13,1},{2,6},{6,10},{... | collective-permute-start | bytes 786440 | tf_op jit(solution)/shard_map/ppermute | solution.py:427
  43.1 12.6 %collective-permute-start.9 = (bf16[256,512]{1,0:T(8,128)(2,1)S(1)}, bf16[256,512]{1,0:T(8,128)(2,1)S(1)}, u32[]{:S(2)}, u32[]{:S(2)}) collective-permute-start(bf16[256,512]{1,0:T(8,128)(2,1)S(1)} %fusion.4.refs_0_), channel_id=1, source_target_pairs={{0,12},{4,0},{8,4},{12,8},{1,13},{5,1},{9,5},{13,9},{2,14},{6,2},{... | collective-permute-start | bytes 786440 | tf_op jit(solution)/shard_map/ppermute | solution.py:427
  44.9 21.8 %collective-permute-start.8 = (bf16[256,512]{1,0:T(8,128)(2,1)S(1)}, bf16[256,512]{1,0:T(8,128)(2,1)S(1)}, u32[]{:S(2)}, u32[]{:S(2)}) collective-permute-start(bf16[256,512]{1,0:T(8,128)(2,1)S(1)} %fusion.4.refs_0_), channel_id=1, source_target_pairs={{0,8},{4,12},{8,0},{12,4},{1,9},{5,13},{9,1},{13,5},{2,10},{6,14},... | collective-permute-start | bytes 786440 | tf_op jit(solution)/shard_map/ppermute | solution.py:427

commit v7 on v6

--- a/solution.py
+++ b/solution.py
@@ -110,7 +110,14 @@
         compiler_params=pltpu.CompilerParams(vmem_limit_bytes=24 * MIB),
         cost_estimate=SMALL,
         name="integrate",
-    )(tile_bin, place, after, counts.reshape(1, points), frames, weights)
+    )(
+        tile_bin,
+        place,
+        after,
+        counts.reshape(1, points),
+        pltpu.with_memory_space_constraint(frames, pltpu.HBM),
+        pltpu.with_memory_space_constraint(weights, pltpu.HBM),
+    )
 
 
 def select_kernel(place, acc, own, *rest):
@@ -427,6 +434,10 @@
     return lax.ppermute(x, axis, [(i, (i + shift) % n) for i in range(n)])
 
 
+def swap(x, axis, mask, n):
+    return lax.ppermute(x, axis, [(i, i ^ mask) for i in range(n)])
+
+
 def body(frames, counts, point_ray, channel_pair_weights, tile_bin, image):
     n_scan = lax.axis_size("scan")
     n_chan = lax.axis_size("chan")
@@ -438,14 +449,14 @@
     x_me, core_me = chan_me // 2, chan_me % 2
     first_row = (lax.axis_index("scan") * (cells // NIMG)).astype(jnp.int32).reshape(1)
 
-    order = sorted(range(1, n_scan), key=lambda d: (2 * d != n_scan, d))
+    order = sorted(range(n_scan), key=lambda r: (r != 0, 2 * r != n_scan, r))
     own_rays = point_ray.reshape(points // LANES, LANES)
-    rays = [own_rays] + [rotate(own_rays, "scan", -d, n_scan) for d in order]
+    rays = [own_rays] + [swap(own_rays, "scan", r, n_scan) for r in order[1:]]
     all_rays = jnp.concatenate(rays, axis=0)
 
     projected = project(image, first_row, angles)
     own_share, *shares = reorder(all_rays, projected, n_scan)
-    arrived = [rotate(share, "scan", d, n_scan) for d, share in zip(order, shares)]
+    arrived = [swap(share, "scan", r, n_scan) for r, share in zip(order[1:], shares)]
 
     place = []
     for e in range(nx):
@@ -456,8 +467,7 @@
         frames, counts, channel_pair_weights, tile_bin, place, own_share, nx, chans
     )
     keep = select(place, sums, nx, chans)
-    partner = [(i, i ^ 1) for i in range(n_chan)]
-    got = lax.ppermute(send, "chan", partner)
+    got = swap(send, "chan", 1, n_chan)
     pattern = keep[0] + got[0].astype(F32)
     for e in range(1, nx):
         joined = (keep[e] + got[e].astype(F32)).astype(BF16)
@@ -466,9 +476,14 @@
     row_total = row_totals(own_rays, sums, angles)
     scaled, recip = join(row_total, own_share, arrived)
     residual = (pattern * (float(NIMG) * recip[:, :1]) - scaled).astype(BF16)
-    others = [rotate(residual, "scan", -d, n_scan) for d in order]
-    tile, col_recip, partial = prepare(all_rays, [residual], image, first_row, angles)
-    return back_project(others, tile, col_recip, partial)
+    gathered = {0: residual}
+    bit = n_scan // 2
+    while bit:
+        gathered |= {r ^ bit: swap(x, "scan", bit, n_scan) for r, x in gathered.items()}
+        bit //= 2
+    blocks = [gathered[r] for r in order]
+    tile, col_recip, partial = prepare(all_rays, blocks[:2], image, first_row, angles)
+    return back_project(blocks[2:], tile, col_recip, partial)
 
 
 def solution(mesh):

time: 71.6 us -> 66.5 us (0.929)
  local copies, waits for them, and re-layouts: 4.56 us -> 0.04 us
  waiting for transfers between devices: 23 us -> 21 us
  Pallas kernels: 25.5 us -> 26.6 us
    ppermute x10 -> x1, waiting for transfers between devices: 22.2 us -> 1 us  [rotate(): return lax.ppermute(x, axis, [(i, (i + shift) % n) for i in range(n)])]
    ppermute x1 -> x10, waiting for transfers between devices: 0.8 us -> 20 us  [swap(): return lax.ppermute(x, axis, [(i, i ^ mask) for i in range(n)])]
    ppermute x1 -> x10, starting transfers between devices: 0.07 us -> 16.1 us  [swap(): return lax.ppermute(x, axis, [(i, i ^ mask) for i in range(n)])]
    ppermute x10 -> x1, starting transfers between devices: 17.6 us -> 1.77 us  [rotate(): return lax.ppermute(x, axis, [(i, (i + shift) % n) for i in range(n)])]
    unnamed x22 -> x14, local copies, waits for them, and re-layouts: 4.56 us -> 0.04 us
    pallas_call x1, Pallas kernels: 5.36 us -> 7.2 us  [integrate(): pl.pallas_call(functools.partial(integrate_kernel, nx, chans // tile_bins...]
  transfers between devices with their start and end apart: 11 -> 11, of which waited for: 6 -> 5; matrix products, arithmetic and copies ran while one was open for 0% -> 0% of each run, Pallas kernels for 27% -> 32%
where the time goes in v7:
time: 66.5 us; the launch traced here: 66.3 us
  Pallas kernels  26.6 us (40%)
  waiting for transfers between devices  21 us (32%)
  starting transfers between devices  17.8 us (27%)
    ppermute x10, waiting for transfers between devices, swap(): return lax.ppermute(x, axis, [(i, i ^ mask) for i in range(n)])  20 us
    ppermute x10, starting transfers between devices, swap(): return lax.ppermute(x, axis, [(i, i ^ mask) for i in range(n)])  16.1 us
    pallas_call x1, Pallas kernels, integrate(): pl.pallas_call(functools.partial(integrate_kernel, nx, chans // tile_bins...  7.2 us
    pallas_call x1, Pallas kernels, project(): pl.pallas_call(functools.partial(project_kernel, angles), in_specs=[pl.Bl...  6.32 us
    pallas_call x1, Pallas kernels, prepare(): pl.pallas_call(functools.partial(prepare_kernel, angles, len(residuals)),...  6.22 us
    pallas_call x1, Pallas kernels, back_project(): pl.pallas_call(functools.partial(back_kernel, parts), in_specs=[vmem] * (...  3.81 us
    ppermute x1, starting transfers between devices, rotate(): return lax.ppermute(x, axis, [(i, (i + shift) % n) for i in range(n)])  1.77 us
    pallas_call x1, Pallas kernels, reorder(): pl.pallas_call(reorder_kernel, in_specs=[vmem, vmem], out_specs=[vmem] *...  1.69 us
  transfers between devices with their start and end apart: 11, of which 5 were waited for; matrix products, arithmetic and copies ran while one was open for 0% of the time, Pallas kernels for 32%

profile of v7, /device:TPU:0, one launch (start us, length us, event | category | flops | bytes accessed | tf_op | source)
XLA Modules:
  0.0 66.3 jit_solution(10629995273815309526)
XLA Ops:
  0.0 5.0 %collective-permute-start.2 = (s32[2,128]{1,0:T(2,128)}, s32[2,128]{1,0:T(2,128)S(1)}, u32[]{:S(2)}, u32[]{:S(2)}) collective-permute-start(s32[2,128]{1,0:T(2,128)} %bitcast.19), channel_id=1, source_target_pairs={{0,12},{4,8},{8,4},{12,0},{1,13},{5,9},{9,5},{13,1},{2,14},{6,10},... | collective-permute-start | bytes 3080 | tf_op jit(solution)/shard_map/ppermute | solution.py:438
  5.1 0.6 collective-permute-start
  5.6 6.3 %project.1.rows = bf16[1024,512]{1,0:T(8,128)(2,1)S(1)} custom-call(s32[1]{0:T(128)} %bitcast.5.first_row, f32[4096,512]{1,0:T(8,128)} %refs_2_.1), custom_call_target="tpu_custom_call" | custom-call | flops 8589934592 | bytes 8388608 | tf_op jit(solution)/shard_map/project/pallas_call | solution.py:209
  12.1 0.1 pad_add_fusion.1.place
  12.1 1.7 %reorder.1 = (bf16[256,512]{1,0:T(8,128)(2,1)S(1)}, bf16[256,512]{1,0:T(8,128)(2,1)S(1)}, bf16[256,512]{1,0:T(8,128)(2,1)S(1)}, bf16[256,512]{1,0:T(8,128)(2,1)S(1)}) custom-call(s32[8,128]{1,0:T(8,128)S(1)} %pad_add_fusion.rays, bf16[1024,512]{1,0:T(8,128)(2,1)S(1)} %project.1.rows), custom_call_target="tpu_custom_call" | custom-call | flops 1 | bytes 1 | tf_op jit(solution)/shard_map/reorder/pallas_call | solution.py:251
  13.8 2.4 %collective-permute-start.5 = (bf16[256,512]{1,0:T(8,128)(2,1)S(1)}, bf16[256,512]{1,0:T(8,128)(2,1)S(1)}, u32[]{:S(2)}, u32[]{:S(2)}) collective-permute-start(bf16[256,512]{1,0:T(8,128)(2,1)S(1)} %get-tuple-element.23), channel_id=1, source_target_pairs={{0,8},{4,12},{8,0},{12,4},{1,9},{5,13},{9,1},{13,5},{2,10},{6,14},... | collective-permute-start | bytes 786440 | tf_op jit(solution)/shard_map/ppermute | solution.py:438
  16.3 2.0 %collective-permute-start.6 = (bf16[256,512]{1,0:T(8,128)(2,1)S(1)}, bf16[256,512]{1,0:T(8,128)(2,1)S(1)}, u32[]{:S(2)}, u32[]{:S(2)}) collective-permute-start(bf16[256,512]{1,0:T(8,128)(2,1)S(1)} %get-tuple-element.24), channel_id=1, source_target_pairs={{0,4},{4,0},{8,12},{12,8},{1,5},{5,1},{9,13},{13,9},{2,6},{6,2},{1... | collective-permute-start | bytes 786440 | tf_op jit(solution)/shard_map/ppermute | solution.py:438
  18.3 7.2 %integrate.1 = (bf16[2,256,512]{2,1,0:T(8,128)(2,1)S(1)}, f32[16,256,128]{2,1,0:T(8,128)S(1)}) custom-call(s32[48]{0:T(128)S(1)} %copy-done.4, s32[4]{0:T(128)S(1)} %pad_add_fusion.1.place, bf16[256,512]{1,0:T(8,128)(2,1)S(1)} %get-tuple-element.18.after.own, s32[1,256]{1,0:T(1,128)S(1)} %bitcast.24, bf16[384,6144]{1,0:T(8,128)(2,1)} %frames.1, ...), custom_call_target="tpu_custom_call" | custom-call | flops 1 | bytes 1 | tf_op jit(solution)/shard_map/integrate/pallas_call | solution.py:89
  25.5 0.1 collective-permute-start.3
  25.6 0.7 %select.11 = (f32[256,512]{1,0:T(8,128)S(1)}, f32[256,512]{1,0:T(8,128)S(1)}) custom-call(s32[4]{0:T(128)S(1)} %pad_add_fusion.1.place, f32[16,256,128]{2,1,0:T(8,128)S(1)} %get-tuple-element.19.acc.after), custom_call_target="tpu_custom_call" | custom-call | flops 99999997952 | bytes 100000000 | tf_op jit(solution)/shard_map/select/pallas_call | solution.py:135
  26.3 0.4 row_totals.1.row_total
  26.7 0.8 %collective-permute-done.3 = bf16[2,256,512]{2,1,0:T(8,128)(2,1)S(1)} collective-permute-done((bf16[2,256,512]{2,1,0:T(8,128)(2,1)S(1)}, bf16[2,256,512]{2,1,0:T(8,128)(2,1)S(1)}, u32[]{:S(2)}, u32[]{:S(2)}) %collective-permute-start.3) | collective-permute-done | bytes 524320 | tf_op jit(solution)/shard_map/ppermute | solution.py:438
  27.5 0.1 fusion
  27.6 1.8 %collective-permute-start.4 = (bf16[256,512]{1,0:T(8,128)(2,1)S(1)}, bf16[256,512]{1,0:T(8,128)(2,1)S(1)}, u32[]{:S(2)}, u32[]{:S(2)}) collective-permute-start(bf16[256,512]{1,0:T(8,128)(2,1)S(1)} %fusion), channel_id=1, source_target_pairs={{0,2},{1,3},{2,0},{3,1},{4,6},{5,7},{6,4},{7,5},{8,10},{9,11},{10,... | collective-permute-start | bytes 786440 | tf_op jit(solution)/shard_map/ppermute | solution.py:434
  29.4 5.3 %collective-permute-done.5.refs_0_ = bf16[256,512]{1,0:T(8,128)(2,1)S(1)} collective-permute-done((bf16[256,512]{1,0:T(8,128)(2,1)S(1)}, bf16[256,512]{1,0:T(8,128)(2,1)S(1)}, u32[]{:S(2)}, u32[]{:S(2)}) %collective-permute-start.5) | collective-permute-done | bytes 262176 | tf_op jit(solution)/shard_map/ppermute | solution.py:438
  34.6 0.3 join.1
  34.9 0.1 multiply_reduce_fusion
  35.0 1.0 %collective-permute-done.4 = bf16[256,512]{1,0:T(8,128)(2,1)S(1)} collective-permute-done((bf16[256,512]{1,0:T(8,128)(2,1)S(1)}, bf16[256,512]{1,0:T(8,128)(2,1)S(1)}, u32[]{:S(2)}, u32[]{:S(2)}) %collective-permute-start.4) | collective-permute-done | bytes 262176 | tf_op jit(solution)/shard_map/ppermute | solution.py:434
  36.0 0.1 fusion.4.refs_0_
  36.2 5.9 %collective-permute-start.9 = (bf16[256,512]{1,0:T(8,128)(2,1)S(1)}, bf16[256,512]{1,0:T(8,128)(2,1)S(1)}, u32[]{:S(2)}, u32[]{:S(2)}) collective-permute-start(bf16[256,512]{1,0:T(8,128)(2,1)S(1)} %fusion.4.refs_0_), channel_id=1, source_target_pairs={{0,8},{4,12},{8,0},{12,4},{1,9},{5,13},{9,1},{13,5},{2,10},{6,14},... | collective-permute-start | bytes 786440 | tf_op jit(solution)/shard_map/ppermute | solution.py:438
  42.1 12.2 %collective-permute-done.9.refs_1_ = bf16[256,512]{1,0:T(8,128)(2,1)S(1)} collective-permute-done((bf16[256,512]{1,0:T(8,128)(2,1)S(1)}, bf16[256,512]{1,0:T(8,128)(2,1)S(1)}, u32[]{:S(2)}, u32[]{:S(2)}) %collective-permute-start.9) | collective-permute-done | bytes 262176 | tf_op jit(solution)/shard_map/ppermute | solution.py:438
  54.3 6.2 %prepare.1 = (bf16[4096,1024]{1,0:T(8,128)(2,1)S(1)}, f32[4096,128]{1,0:T(8,128)S(1)}, f32[4096,512]{1,0:T(8,128)S(1)}) custom-call(s32[1]{0:T(128)} %bitcast.5.first_row, s32[8,128]{1,0:T(8,128)S(1)} %copy-done.1, bf16[256,512]{1,0:T(8,128)(2,1)S(1)} %fusion.4.refs_0_, bf16[256,512]{1,0:T(8,128)(2,1)S(1)} %collective-permute-done.9.refs_1_, ...), custom_call_target="tpu_custom_call" | custom-call | flops 1 | bytes 1 | tf_op jit(solution)/shard_map/prepare/pallas_call | solution.py:364
  60.6 1.7 %collective-permute-done.10.refs_1_ = bf16[256,512]{1,0:T(8,128)(2,1)S(1)} collective-permute-done((bf16[256,512]{1,0:T(8,128)(2,1)S(1)}, bf16[256,512]{1,0:T(8,128)(2,1)S(1)}, u32[]{:S(2)}, u32[]{:S(2)}) %collective-permute-start.10) | collective-permute-done | bytes 262176 | tf_op jit(solution)/shard_map/ppermute | solution.py:438
  62.3 3.8 %back_project.1 = f32[4096,512]{1,0:T(8,128)} custom-call(bf16[256,512]{1,0:T(8,128)(2,1)S(1)} %collective-permute-done.8.refs_0_, bf16[256,512]{1,0:T(8,128)(2,1)S(1)} %collective-permute-done.10.refs_1_, bf16[4096,1024]{1,0:T(8,128)(2,1)S(1)} %get-tuple-element.28.refs_2_, f32[4096,128]{1,0:T(8,128)S(1)} %get-tuple-element.29.refs_3_, ...), custom_call_target="tpu_custom_call" | custom-call | flops 1 | bytes 1 | tf_op jit(solution)/shard_map/back_project/pallas_call | solution.py:417
  (26 shorter events, 0.1 us)
Async XLA Ops:
  0.0 12.0 %collective-permute-start.2 = (s32[2,128]{1,0:T(2,128)}, s32[2,128]{1,0:T(2,128)S(1)}, u32[]{:S(2)}, u32[]{:S(2)}) collective-permute-start(s32[2,128]{1,0:T(2,128)} %bitcast.19), channel_id=1, source_target_pairs={{0,12},{4,8},{8,4},{12,0},{1,13},{5,9},{9,5},{13,1},{2,14},{6,10},... | collective-permute-start | bytes 3080 | tf_op jit(solution)/shard_map/ppermute | solution.py:438
  5.0 7.0 %collective-permute-start.1 = (s32[2,128]{1,0:T(2,128)}, s32[2,128]{1,0:T(2,128)S(1)}, u32[]{:S(2)}, u32[]{:S(2)}) collective-permute-start(s32[2,128]{1,0:T(2,128)} %bitcast.20), channel_id=1, source_target_pairs={{0,4},{4,0},{8,12},{12,8},{1,5},{5,1},{9,13},{13,9},{2,6},{6,2},{1... | collective-permute-start | bytes 3080 | tf_op jit(solution)/shard_map/ppermute | solution.py:438
  5.1 7.0 %collective-permute-start = (s32[2,128]{1,0:T(2,128)}, s32[2,128]{1,0:T(2,128)S(1)}, u32[]{:S(2)}, u32[]{:S(2)}) collective-permute-start(s32[2,128]{1,0:T(2,128)} %bitcast.21), channel_id=1, source_target_pairs={{0,8},{4,12},{8,0},{12,4},{1,9},{5,13},{9,1},{13,5},{2,10},{6,14},... | collective-permute-start | bytes 3080 | tf_op jit(solution)/shard_map/ppermute | solution.py:438
  5.6 6.4 %copy-start.2 = (s32[256]{0:T(256)S(1)}, s32[256]{0:T(256)}, u32[]{:S(2)}) copy-start(s32[256]{0:T(256)} %param.8) | copy-start | bytes 3076
  5.6 12.7 %copy-start.3 = (s32[256]{0:T(256)S(1)}, s32[256]{0:T(256)}, u32[]{:S(2)}) copy-start(s32[256]{0:T(256)} %param.7) | copy-start | bytes 3076
  5.6 12.7 %copy-start.4 = (s32[48]{0:T(128)S(1)}, s32[48]{0:T(128)}, u32[]{:S(2)}) copy-start(s32[48]{0:T(128)} %tile_bin.1) | copy-start | bytes 580
  12.0 6.2 %copy-start = (s32[8,128]{1,0:T(8,128)}, s32[8,128]{1,0:T(8,128)S(1)}, u32[]{:S(2)}) copy-start(s32[8,128]{1,0:T(8,128)S(1)} %pad_add_fusion.rays) | copy-start | bytes 12292
  13.8 20.8 %collective-permute-start.5 = (bf16[256,512]{1,0:T(8,128)(2,1)S(1)}, bf16[256,512]{1,0:T(8,128)(2,1)S(1)}, u32[]{:S(2)}, u32[]{:S(2)}) collective-permute-start(bf16[256,512]{1,0:T(8,128)(2,1)S(1)} %get-tuple-element.23), channel_id=1, source_target_pairs={{0,8},{4,12},{8,0},{12,4},{1,9},{5,13},{9,1},{13,5},{2,10},{6,14},... | collective-permute-start | bytes 786440 | tf_op jit(solution)/shard_map/ppermute | solution.py:438
  16.3 18.4 %collective-permute-start.6 = (bf16[256,512]{1,0:T(8,128)(2,1)S(1)}, bf16[256,512]{1,0:T(8,128)(2,1)S(1)}, u32[]{:S(2)}, u32[]{:S(2)}) collective-permute-start(bf16[256,512]{1,0:T(8,128)(2,1)S(1)} %get-tuple-element.24), channel_id=1, source_target_pairs={{0,4},{4,0},{8,12},{12,8},{1,5},{5,1},{9,13},{13,9},{2,6},{6,2},{1... | collective-permute-start | bytes 786440 | tf_op jit(solution)/shard_map/ppermute | solution.py:438
  18.3 16.4 %collective-permute-start.7 = (bf16[256,512]{1,0:T(8,128)(2,1)S(1)}, bf16[256,512]{1,0:T(8,128)(2,1)S(1)}, u32[]{:S(2)}, u32[]{:S(2)}) collective-permute-start(bf16[256,512]{1,0:T(8,128)(2,1)S(1)} %get-tuple-element.25), channel_id=1, source_target_pairs={{0,12},{4,8},{8,4},{12,0},{1,13},{5,9},{9,5},{13,1},{2,14},{6,10},... | collective-permute-start | bytes 786440 | tf_op jit(solution)/shard_map/ppermute | solution.py:438
  25.5 2.0 %collective-permute-start.3 = (bf16[2,256,512]{2,1,0:T(8,128)(2,1)S(1)}, bf16[2,256,512]{2,1,0:T(8,128)(2,1)S(1)}, u32[]{:S(2)}, u32[]{:S(2)}) collective-permute-start(bf16[2,256,512]{2,1,0:T(8,128)(2,1)S(1)} %get-tuple-element.21), channel_id=1, source_target_pairs={{0,1},{1,0},{2,3},{3,2},{4,5},{5,4},{6,7},{7,6},{8,9},{9,8},{10,11... | collective-permute-start | bytes 1572872 | tf_op jit(solution)/shard_map/ppermute | solution.py:438
  27.5 26.8 %slice-start = ((s8[8388608]{0:T(1024)(128)(4,1)}), s8[4194304]{0:T(1024)(128)(4,1)S(1)}, s32[]{:S(2)}) async-start(s8[8388608]{0:T(1024)(128)(4,1)} %bitcast.17), calls=%async_computation | async-start | bytes 8388608
  27.6 26.7 %slice-start.1 = ((s8[8388608]{0:T(1024)(128)(4,1)}), s8[4194304]{0:T(1024)(128)(4,1)S(1)}, s32[]{:S(2)}) async-start(s8[8388608]{0:T(1024)(128)(4,1)} %bitcast.17), calls=%async_computation.1 | async-start | bytes 8388608
  27.6 26.7 %copy-start.1 = (s32[8,128]{1,0:T(8,128)S(1)}, s32[8,128]{1,0:T(8,128)}, u32[]{:S(2)}) copy-start(s32[8,128]{1,0:T(8,128)} %copy-done) | copy-start | bytes 12292
  27.6 8.4 %collective-permute-start.4 = (bf16[256,512]{1,0:T(8,128)(2,1)S(1)}, bf16[256,512]{1,0:T(8,128)(2,1)S(1)}, u32[]{:S(2)}, u32[]{:S(2)}) collective-permute-start(bf16[256,512]{1,0:T(8,128)(2,1)S(1)} %fusion), channel_id=1, source_target_pairs={{0,2},{1,3},{2,0},{3,1},{4,6},{5,7},{6,4},{7,5},{8,10},{9,11},{10,... | collective-permute-start | bytes 786440 | tf_op jit(solution)/shard_map/ppermute | solution.py:434
  36.2 18.1 %collective-permute-start.9 = (bf16[256,512]{1,0:T(8,128)(2,1)S(1)}, bf16[256,512]{1,0:T(8,128)(2,1)S(1)}, u32[]{:S(2)}, u32[]{:S(2)}) collective-permute-start(bf16[256,512]{1,0:T(8,128)(2,1)S(1)} %fusion.4.refs_0_), channel_id=1, source_target_pairs={{0,8},{4,12},{8,0},{12,4},{1,9},{5,13},{9,1},{13,5},{2,10},{6,14},... | collective-permute-start | bytes 786440 | tf_op jit(solution)/shard_map/ppermute | solution.py:438
  42.1 18.5 %collective-permute-start.8 = (bf16[256,512]{1,0:T(8,128)(2,1)S(1)}, bf16[256,512]{1,0:T(8,128)(2,1)S(1)}, u32[]{:S(2)}, u32[]{:S(2)}) collective-permute-start(bf16[256,512]{1,0:T(8,128)(2,1)S(1)} %fusion.4.refs_0_), channel_id=1, source_target_pairs={{0,4},{4,0},{8,12},{12,8},{1,5},{5,1},{9,13},{13,9},{2,6},{6,2},{1... | collective-permute-start | bytes 786440 | tf_op jit(solution)/shard_map/ppermute | solution.py:438
  54.3 8.0 %collective-permute-start.10 = (bf16[256,512]{1,0:T(8,128)(2,1)S(1)}, bf16[256,512]{1,0:T(8,128)(2,1)S(1)}, u32[]{:S(2)}, u32[]{:S(2)}) collective-permute-start(bf16[256,512]{1,0:T(8,128)(2,1)S(1)} %collective-permute-done.9.refs_1_), channel_id=1, source_target_pairs={{0,4},{4,0},{8,12},{12,8},{1,5},{5,1},{9,13},{13,9},{2,6},{6,2},{1... | collective-permute-start | bytes 786440 | tf_op jit(solution)/shard_map/ppermute | solution.py:438

commit v8 on v7

--- a/solution.py
+++ b/solution.py
@@ -326,7 +326,7 @@
     residuals, (image, tile, recip, partial, base, cosine) = refs[:early], refs[early:]
     step = pl.program_id(0)
     chunks = rays.shape[0]
-    points, chans = residuals[0].shape
+    chans = image.shape[1]
     rows = tile.shape[0] // LANES
 
     @pl.when(step == 0)
@@ -349,7 +349,7 @@
         total = jnp.sum(sums, axis=1, keepdims=True)
         recip[here, :] = jnp.broadcast_to(1.0 / total, (LANES, LANES))
     joined = jnp.concatenate([r[...] for r in residuals], axis=0)
-    back = jnp.dot(tile[:, : early * points], joined, preferred_element_type=F32)
+    back = jnp.dot(tile[:, : joined.shape[0]], joined, preferred_element_type=F32)
     for j in range(chans // LANES):
         lanes = slice(j * LANES, (j + 1) * LANES)
         partial[:, lanes] = image[:, lanes] + back[:, lanes] * recip[...]
@@ -383,23 +383,54 @@
     )(first_row, rays, *residuals, image)
 
 
-def back_kernel(parts, *refs):
-    residuals, (tile, recip, partial, out, joined, staged, sent) = refs[:parts], refs[parts:]
-    points, chans = residuals[0].shape
-    skip = tile.shape[1] - parts * points
+def gather_rows(pieces, joined):
+    start = 0
+    for piece in pieces:
+        joined[start : start + piece.shape[0], :] = piece[...]
+        start += piece.shape[0]
+
+
+def add_share(here, first, tile, recip, partial, joined, out):
+    columns = slice(first, first + joined.shape[0])
+    back = jnp.dot(tile[here, columns], joined[...], preferred_element_type=F32)
+    scale = recip[here, :]
+    for j in range(out.shape[1] // LANES):
+        lanes = slice(j * LANES, (j + 1) * LANES)
+        out[here, lanes] = partial[here, lanes] + back[:, lanes] * scale
+
+
+def add_kernel(first, count, *refs):
+    pieces, (tile, recip, partial, out, joined) = refs[:count], refs[count:]
+    gather_rows(pieces, joined)
+    rows = min(512, out.shape[0])
+    for start in range(0, out.shape[0], rows):
+        add_share(slice(start, start + rows), first, tile, recip, partial, joined, out)
+
+
+def add_back(pieces, first, tile, recip, partial):
+    cells, chans = partial.shape
+    vmem = pl.BlockSpec(memory_space=pltpu.VMEM)
+    return pl.pallas_call(
+        functools.partial(add_kernel, first, len(pieces)),
+        in_specs=[vmem] * (len(pieces) + 3),
+        out_specs=vmem,
+        scratch_shapes=[pltpu.VMEM((sum(x.shape[0] for x in pieces), chans), BF16)],
+        out_shape=jax.ShapeDtypeStruct((cells, chans), F32),
+        compiler_params=pltpu.CompilerParams(vmem_limit_bytes=8 * MIB),
+        cost_estimate=LARGE,
+        name="add_back",
+    )(*pieces, tile, recip, partial)
+
+
+def back_kernel(first, count, *refs):
+    pieces, (tile, recip, partial, out, joined, staged, sent) = refs[:count], refs[count:]
     chunks = sent.shape[0]
     rows = out.shape[0] // chunks
-
-    for d in range(parts):
-        joined[d * points : (d + 1) * points, :] = residuals[d][...]
+    gather_rows(pieces, joined)
     copies = []
     for chunk in range(chunks):
         here = slice(chunk * rows, (chunk + 1) * rows)
-        back = jnp.dot(tile[here, skip:], joined[...], preferred_element_type=F32)
-        scale = recip[here, :]
-        for j in range(chans // LANES):
-            lanes = slice(j * LANES, (j + 1) * LANES)
-            staged[here, lanes] = partial[here, lanes] + back[:, lanes] * scale
+        add_share(here, first, tile, recip, partial, joined, staged)
         copies.append(
             pltpu.make_async_copy(staged.at[here, :], out.at[here, :], sent.at[chunk])
         )
@@ -408,18 +439,16 @@
         copy.wait()
 
 
-def back_project(residuals, tile, recip, partial):
+def back_project(pieces, first, tile, recip, partial):
     cells, chans = partial.shape
-    parts = len(residuals)
-    points = residuals[0].shape[0]
     chunks = max(1, cells // 512)
     vmem = pl.BlockSpec(memory_space=pltpu.VMEM)
     return pl.pallas_call(
-        functools.partial(back_kernel, parts),
-        in_specs=[vmem] * (parts + 3),
+        functools.partial(back_kernel, first, len(pieces)),
+        in_specs=[vmem] * (len(pieces) + 3),
         out_specs=pl.BlockSpec(memory_space=pl.ANY),
         scratch_shapes=[
-            pltpu.VMEM((parts * points, chans), BF16),
+            pltpu.VMEM((sum(x.shape[0] for x in pieces), chans), BF16),
             pltpu.VMEM((cells, chans), F32),
             pltpu.SemaphoreType.DMA((chunks,)),
         ],
@@ -427,7 +456,7 @@
         compiler_params=pltpu.CompilerParams(vmem_limit_bytes=16 * MIB),
         cost_estimate=SMALL,
         name="back_project",
-    )(*residuals, tile, recip, partial)
+    )(*pieces, tile, recip, partial)
 
 
 def rotate(x, axis, shift, n):
@@ -449,14 +478,18 @@
     x_me, core_me = chan_me // 2, chan_me % 2
     first_row = (lax.axis_index("scan") * (cells // NIMG)).astype(jnp.int32).reshape(1)
 
-    order = sorted(range(n_scan), key=lambda r: (r != 0, 2 * r != n_scan, r))
+    middle = [r for r in range(1, n_scan) if r % 2 == 0] + [1]
+    late = [r for r in range(3, n_scan, 2)]
+    order = [0] + middle + late
     own_rays = point_ray.reshape(points // LANES, LANES)
     rays = [own_rays] + [swap(own_rays, "scan", r, n_scan) for r in order[1:]]
     all_rays = jnp.concatenate(rays, axis=0)
 
     projected = project(image, first_row, angles)
     own_share, *shares = reorder(all_rays, projected, n_scan)
-    arrived = [swap(share, "scan", r, n_scan) for r, share in zip(order[1:], shares)]
+    share_of = dict(zip(order[1:], shares))
+    sending = sorted(share_of, key=lambda r: (2 * r != n_scan, -r))
+    arrived = [swap(share_of[r], "scan", r, n_scan) for r in sending]
 
     place = []
     for e in range(nx):
@@ -475,15 +508,19 @@
 
     row_total = row_totals(own_rays, sums, angles)
     scaled, recip = join(row_total, own_share, arrived)
-    residual = (pattern * (float(NIMG) * recip[:, :1]) - scaled).astype(BF16)
-    gathered = {0: residual}
+    residual = (-scaled + pattern * (float(NIMG) * recip[:, :1])).astype(BF16)
+    half = points // 2
+    gathered = {0: [residual[:half], residual[half:]]}
     bit = n_scan // 2
     while bit:
-        gathered |= {r ^ bit: swap(x, "scan", bit, n_scan) for r, x in gathered.items()}
+        for r, pieces in list(gathered.items()):
+            gathered[r ^ bit] = [swap(x, "scan", bit, n_scan) for x in pieces]
         bit //= 2
-    blocks = [gathered[r] for r in order]
-    tile, col_recip, partial = prepare(all_rays, blocks[:2], image, first_row, angles)
-    return back_project(blocks[2:], tile, col_recip, partial)
+    tile, col_recip, partial = prepare(all_rays, gathered[0], image, first_row, angles)
+    pieces = [x for r in middle for x in gathered[r]]
+    partial = add_back(pieces, points, tile, col_recip, partial)
+    pieces = [x for r in late for x in gathered[r]]
+    return back_project(pieces, points * (1 + len(middle)), tile, col_recip, partial)
 
 
 def solution(mesh):

time: 66.5 us -> 64.5 us (0.970)
  waiting for transfers between devices: 21 us -> 15.8 us
  Pallas kernels: 26.6 us -> 28.4 us
  starting transfers between devices: 17.8 us -> 19.2 us
    ppermute x10 -> x13, waiting for transfers between devices: 20 us -> 15.1 us  [swap(): return lax.ppermute(x, axis, [(i, i ^ mask) for i in range(n)])]
    pallas_call x1 -> x2, Pallas kernels: 3.81 us -> 6.07 us  [the longest x1 3.67 us: back_project(): pl.pallas_call(functools.partial(back_kernel, first, len(pieces)), in_spe...]
    ppermute x10 -> x13, starting transfers between devices: 16.1 us -> 17.7 us  [swap(): return lax.ppermute(x, axis, [(i, i ^ mask) for i in range(n)])]
  transfers between devices with their start and end apart: 11 -> 14, of which waited for: 5 -> 9; matrix products, arithmetic and copies ran while one was open for 0% -> 0% of each run, Pallas kernels for 32% -> 36%
where the time goes in v8:
time: 64.5 us; the launch traced here: 64.3 us
  Pallas kernels  28.4 us (44%)
  starting transfers between devices  19.2 us (30%)
  waiting for transfers between devices  15.8 us (24%)
    ppermute x13, starting transfers between devices, swap(): return lax.ppermute(x, axis, [(i, i ^ mask) for i in range(n)])  17.7 us
    ppermute x13, waiting for transfers between devices, swap(): return lax.ppermute(x, axis, [(i, i ^ mask) for i in range(n)])  15.1 us
    pallas_call x1, Pallas kernels, integrate(): pl.pallas_call(functools.partial(integrate_kernel, nx, chans // tile_bins...  7.21 us
    pallas_call x1, Pallas kernels, project(): pl.pallas_call(functools.partial(project_kernel, angles), in_specs=[pl.Bl...  6.31 us
    pallas_call x1, Pallas kernels, prepare(): pl.pallas_call(functools.partial(prepare_kernel, angles, len(residuals)),...  5.82 us
    pallas_call x1, Pallas kernels, back_project(): pl.pallas_call(functools.partial(back_kernel, first, len(pieces)), in_spe...  3.67 us
    pallas_call x1, Pallas kernels, add_back(): pl.pallas_call(functools.partial(add_kernel, first, len(pieces)), in_spec...  2.4 us
    pallas_call x1, Pallas kernels, reorder(): pl.pallas_call(reorder_kernel, in_specs=[vmem, vmem], out_specs=[vmem] *...  1.69 us
  transfers between devices with their start and end apart: 14, of which 9 were waited for; matrix products, arithmetic and copies ran while one was open for 0% of the time, Pallas kernels for 36%

profile of v8, /device:TPU:0, one launch (start us, length us, event | category | flops | bytes accessed | tf_op | source)
XLA Modules:
  0.0 64.3 jit_solution(8320447574373867942)
XLA Ops:
  0.0 4.0 %collective-permute-start = (s32[2,128]{1,0:T(2,128)}, s32[2,128]{1,0:T(2,128)S(1)}, u32[]{:S(2)}, u32[]{:S(2)}) collective-permute-start(s32[2,128]{1,0:T(2,128)} %bitcast.19), channel_id=1, source_target_pairs={{0,8},{4,12},{8,0},{12,4},{1,9},{5,13},{9,1},{13,5},{2,10},{6,14},... | collective-permute-start | bytes 3080 | tf_op jit(solution)/shard_map/ppermute | solution.py:467
  4.0 1.6 %collective-permute-start.1 = (s32[2,128]{1,0:T(2,128)}, s32[2,128]{1,0:T(2,128)S(1)}, u32[]{:S(2)}, u32[]{:S(2)}) collective-permute-start(s32[2,128]{1,0:T(2,128)} %bitcast.20), channel_id=1, source_target_pairs={{0,4},{4,0},{8,12},{12,8},{1,5},{5,1},{9,13},{13,9},{2,6},{6,2},{1... | collective-permute-start | bytes 3080 | tf_op jit(solution)/shard_map/ppermute | solution.py:467
  5.6 6.3 %project.1.rows = bf16[1024,512]{1,0:T(8,128)(2,1)S(1)} custom-call(s32[1]{0:T(128)} %bitcast.5.first_row, f32[4096,512]{1,0:T(8,128)} %refs_2_.1), custom_call_target="tpu_custom_call" | custom-call | flops 8589934592 | bytes 8388608 | tf_op jit(solution)/shard_map/project/pallas_call | solution.py:209
  12.1 1.7 %reorder.1 = (bf16[256,512]{1,0:T(8,128)(2,1)S(1)}, bf16[256,512]{1,0:T(8,128)(2,1)S(1)}, bf16[256,512]{1,0:T(8,128)(2,1)S(1)}, bf16[256,512]{1,0:T(8,128)(2,1)S(1)}) custom-call(s32[8,128]{1,0:T(8,128)S(1)} %pad_add_fusion.rays, bf16[1024,512]{1,0:T(8,128)(2,1)S(1)} %project.1.rows), custom_call_target="tpu_custom_call" | custom-call | flops 1 | bytes 1 | tf_op jit(solution)/shard_map/reorder/pallas_call | solution.py:251
  13.8 2.0 %collective-permute-start.3 = (bf16[256,512]{1,0:T(8,128)(2,1)S(1)}, bf16[256,512]{1,0:T(8,128)(2,1)S(1)}, u32[]{:S(2)}, u32[]{:S(2)}) collective-permute-start(bf16[256,512]{1,0:T(8,128)(2,1)S(1)} %get-tuple-element.20), channel_id=1, source_target_pairs={{0,8},{4,12},{8,0},{12,4},{1,9},{5,13},{9,1},{13,5},{2,10},{6,14},... | collective-permute-start | bytes 786440 | tf_op jit(solution)/shard_map/ppermute | solution.py:467
  15.8 2.0 %collective-permute-start.4 = (bf16[256,512]{1,0:T(8,128)(2,1)S(1)}, bf16[256,512]{1,0:T(8,128)(2,1)S(1)}, u32[]{:S(2)}, u32[]{:S(2)}) collective-permute-start(bf16[256,512]{1,0:T(8,128)(2,1)S(1)} %get-tuple-element.21), channel_id=1, source_target_pairs={{0,12},{4,8},{8,4},{12,0},{1,13},{5,9},{9,5},{13,1},{2,14},{6,10},... | collective-permute-start | bytes 786440 | tf_op jit(solution)/shard_map/ppermute | solution.py:467
  17.8 0.5 collective-permute-start.5
  18.3 7.2 %integrate.1 = (bf16[2,256,512]{2,1,0:T(8,128)(2,1)S(1)}, f32[16,256,128]{2,1,0:T(8,128)S(1)}) custom-call(s32[48]{0:T(128)S(1)} %copy-done.4, s32[4]{0:T(128)S(1)} %pad_add_fusion.1.place, bf16[256,512]{1,0:T(8,128)(2,1)S(1)} %get-tuple-element.18.after.own, s32[1,256]{1,0:T(1,128)S(1)} %bitcast.24, bf16[384,6144]{1,0:T(8,128)(2,1)} %frames.1, ...), custom_call_target="tpu_custom_call" | custom-call | flops 1 | bytes 1 | tf_op jit(solution)/shard_map/integrate/pallas_call | solution.py:89
  25.6 0.7 %select.11 = (f32[256,512]{1,0:T(8,128)S(1)}, f32[256,512]{1,0:T(8,128)S(1)}) custom-call(s32[4]{0:T(128)S(1)} %pad_add_fusion.1.place, f32[16,256,128]{2,1,0:T(8,128)S(1)} %get-tuple-element.19.after.acc), custom_call_target="tpu_custom_call" | custom-call | flops 99999997952 | bytes 100000000 | tf_op jit(solution)/shard_map/select/pallas_call | solution.py:135
  26.3 0.4 row_totals.1.row_total
  26.7 0.8 %collective-permute-done.6 = bf16[2,256,512]{2,1,0:T(8,128)(2,1)S(1)} collective-permute-done((bf16[2,256,512]{2,1,0:T(8,128)(2,1)S(1)}, bf16[2,256,512]{2,1,0:T(8,128)(2,1)S(1)}, u32[]{:S(2)}, u32[]{:S(2)}) %collective-permute-start.6) | collective-permute-done | bytes 524320 | tf_op jit(solution)/shard_map/ppermute | solution.py:467
  27.6 1.5 %collective-permute-start.7 = (bf16[256,512]{1,0:T(8,128)(2,1)S(1)}, bf16[256,512]{1,0:T(8,128)(2,1)S(1)}, u32[]{:S(2)}, u32[]{:S(2)}) collective-permute-start(bf16[256,512]{1,0:T(8,128)(2,1)S(1)} %fusion), channel_id=1, source_target_pairs={{0,2},{1,3},{2,0},{3,1},{4,6},{5,7},{6,4},{7,5},{8,10},{9,11},{10,... | collective-permute-start | bytes 786440 | tf_op jit(solution)/shard_map/ppermute | solution.py:463
  29.2 5.5 %collective-permute-done.3.refs_0_ = bf16[256,512]{1,0:T(8,128)(2,1)S(1)} collective-permute-done((bf16[256,512]{1,0:T(8,128)(2,1)S(1)}, bf16[256,512]{1,0:T(8,128)(2,1)S(1)}, u32[]{:S(2)}, u32[]{:S(2)}) %collective-permute-start.3) | collective-permute-done | bytes 262176 | tf_op jit(solution)/shard_map/ppermute | solution.py:467
  35.3 0.7 %collective-permute-done.7 = bf16[256,512]{1,0:T(8,128)(2,1)S(1)} collective-permute-done((bf16[256,512]{1,0:T(8,128)(2,1)S(1)}, bf16[256,512]{1,0:T(8,128)(2,1)S(1)}, u32[]{:S(2)}, u32[]{:S(2)}) %collective-permute-start.7) | collective-permute-done | bytes 262176 | tf_op jit(solution)/shard_map/ppermute | solution.py:463
  36.2 5.2 %collective-permute-start.10 = (bf16[128,512]{1,0:T(8,128)(2,1)S(1)}, bf16[128,512]{1,0:T(8,128)(2,1)S(1)}, u32[]{:S(2)}, u32[]{:S(2)}) collective-permute-start(bf16[128,512]{1,0:T(8,128)(2,1)S(1)} %get-tuple-element.31.refs_1_), channel_id=1, source_target_pairs={{0,8},{4,12},{8,0},{12,4},{1,9},{5,13},{9,1},{13,5},{2,10},{6,14},... | collective-permute-start | bytes 393224 | tf_op jit(solution)/shard_map/ppermute | solution.py:467
  41.5 1.8 %collective-permute-start.12 = (bf16[128,512]{1,0:T(8,128)(2,1)S(1)}, bf16[128,512]{1,0:T(8,128)(2,1)S(1)}, u32[]{:S(2)}, u32[]{:S(2)}) collective-permute-start(bf16[128,512]{1,0:T(8,128)(2,1)S(1)} %get-tuple-element.32.refs_0_), channel_id=1, source_target_pairs={{0,4},{4,0},{8,12},{12,8},{1,5},{5,1},{9,13},{13,9},{2,6},{6,2},{1... | collective-permute-start | bytes 393224 | tf_op jit(solution)/shard_map/ppermute | solution.py:467
  43.6 5.8 %prepare.1 = (bf16[4096,1024]{1,0:T(8,128)(2,1)S(1)}, f32[4096,128]{1,0:T(8,128)S(1)}, f32[4096,512]{1,0:T(8,128)S(1)}) custom-call(s32[1]{0:T(128)} %bitcast.5.first_row, s32[8,128]{1,0:T(8,128)S(1)} %copy-done.1, bf16[128,512]{1,0:T(8,128)(2,1)S(1)} %get-tuple-element.32.refs_0_, bf16[128,512]{1,0:T(8,128)(2,1)S(1)} %get-tuple-element.31.refs_1_, ...), custom_call_target="tpu_custom_call" | custom-call | flops 1 | bytes 1 | tf_op jit(solution)/shard_map/prepare/pallas_call | solution.py:364
  49.4 1.7 %collective-permute-done.10.refs_1_ = bf16[128,512]{1,0:T(8,128)(2,1)S(1)} collective-permute-done((bf16[128,512]{1,0:T(8,128)(2,1)S(1)}, bf16[128,512]{1,0:T(8,128)(2,1)S(1)}, u32[]{:S(2)}, u32[]{:S(2)}) %collective-permute-start.10) | collective-permute-done | bytes 131104 | tf_op jit(solution)/shard_map/ppermute | solution.py:467
  51.3 2.4 %collective-permute-done.8.refs_0_ = bf16[128,512]{1,0:T(8,128)(2,1)S(1)} collective-permute-done((bf16[128,512]{1,0:T(8,128)(2,1)S(1)}, bf16[128,512]{1,0:T(8,128)(2,1)S(1)}, u32[]{:S(2)}, u32[]{:S(2)}) %collective-permute-start.8) | collective-permute-done | bytes 131104 | tf_op jit(solution)/shard_map/ppermute | solution.py:467
  53.7 2.3 %collective-permute-done.13.refs_3_ = bf16[128,512]{1,0:T(8,128)(2,1)S(1)} collective-permute-done((bf16[128,512]{1,0:T(8,128)(2,1)S(1)}, bf16[128,512]{1,0:T(8,128)(2,1)S(1)}, u32[]{:S(2)}, u32[]{:S(2)}) %collective-permute-start.13) | collective-permute-done | bytes 131104 | tf_op jit(solution)/shard_map/ppermute | solution.py:467
  56.0 2.4 %add_back.1.refs_4_ = f32[4096,512]{1,0:T(8,128)S(1)} custom-call(bf16[128,512]{1,0:T(8,128)(2,1)S(1)} %collective-permute-done.8.refs_0_, bf16[128,512]{1,0:T(8,128)(2,1)S(1)} %collective-permute-done.10.refs_1_, bf16[128,512]{1,0:T(8,128)(2,1)S(1)} %collective-permute-done.12.refs_2_, bf16[128,512]{1,0:T(8,128)(2,1)S(1)} %collective-permute-done.13.refs_3_, ...), custom_call_target="tpu_custom_call" | custom-call | flops 99999997952 | bytes 100000000 | tf_op jit(solution)/shard_map/add_back/pallas_call | solution.py:413
  58.4 0.4 collective-permute-done.11.refs_1_
  58.8 1.7 %collective-permute-done.9.refs_0_ = bf16[128,512]{1,0:T(8,128)(2,1)S(1)} collective-permute-done((bf16[128,512]{1,0:T(8,128)(2,1)S(1)}, bf16[128,512]{1,0:T(8,128)(2,1)S(1)}, u32[]{:S(2)}, u32[]{:S(2)}) %collective-permute-start.9) | collective-permute-done | bytes 131104 | tf_op jit(solution)/shard_map/ppermute | solution.py:467
  60.5 3.7 %back_project.1 = f32[4096,512]{1,0:T(8,128)} custom-call(bf16[128,512]{1,0:T(8,128)(2,1)S(1)} %collective-permute-done.9.refs_0_, bf16[128,512]{1,0:T(8,128)(2,1)S(1)} %collective-permute-done.11.refs_1_, bf16[4096,1024]{1,0:T(8,128)(2,1)S(1)} %get-tuple-element.28.refs_4_.refs_2_, f32[4096,128]{1,0:T(8,128)S(1)} %get-tuple-element.29.refs_5_.refs_3_, ...), custom_call_target="tpu_custom_call" | custom-call | flops 1 | bytes 1 | tf_op jit(solution)/shard_map/back_project/pallas_call | solution.py:446
  (34 shorter events, 1.6 us)
Async XLA Ops:
  0.0 12.0 %collective-permute-start = (s32[2,128]{1,0:T(2,128)}, s32[2,128]{1,0:T(2,128)S(1)}, u32[]{:S(2)}, u32[]{:S(2)}) collective-permute-start(s32[2,128]{1,0:T(2,128)} %bitcast.19), channel_id=1, source_target_pairs={{0,8},{4,12},{8,0},{12,4},{1,9},{5,13},{9,1},{13,5},{2,10},{6,14},... | collective-permute-start | bytes 3080 | tf_op jit(solution)/shard_map/ppermute | solution.py:467
  4.0 8.0 %collective-permute-start.1 = (s32[2,128]{1,0:T(2,128)}, s32[2,128]{1,0:T(2,128)S(1)}, u32[]{:S(2)}, u32[]{:S(2)}) collective-permute-start(s32[2,128]{1,0:T(2,128)} %bitcast.20), channel_id=1, source_target_pairs={{0,4},{4,0},{8,12},{12,8},{1,5},{5,1},{9,13},{13,9},{2,6},{6,2},{1... | collective-permute-start | bytes 3080 | tf_op jit(solution)/shard_map/ppermute | solution.py:467
  5.6 6.4 %collective-permute-start.2 = (s32[2,128]{1,0:T(2,128)}, s32[2,128]{1,0:T(2,128)S(1)}, u32[]{:S(2)}, u32[]{:S(2)}) collective-permute-start(s32[2,128]{1,0:T(2,128)} %bitcast.21), channel_id=1, source_target_pairs={{0,12},{4,8},{8,4},{12,0},{1,13},{5,9},{9,5},{13,1},{2,14},{6,10},... | collective-permute-start | bytes 3080 | tf_op jit(solution)/shard_map/ppermute | solution.py:467
  5.6 6.4 %copy-start.2 = (s32[256]{0:T(256)S(1)}, s32[256]{0:T(256)}, u32[]{:S(2)}) copy-start(s32[256]{0:T(256)} %param.8) | copy-start | bytes 3076
  5.6 12.7 %copy-start.3 = (s32[256]{0:T(256)S(1)}, s32[256]{0:T(256)}, u32[]{:S(2)}) copy-start(s32[256]{0:T(256)} %param.7) | copy-start | bytes 3076
  5.6 12.7 %copy-start.4 = (s32[48]{0:T(128)S(1)}, s32[48]{0:T(128)}, u32[]{:S(2)}) copy-start(s32[48]{0:T(128)} %tile_bin.1) | copy-start | bytes 580
  12.0 6.3 %copy-start = (s32[8,128]{1,0:T(8,128)}, s32[8,128]{1,0:T(8,128)S(1)}, u32[]{:S(2)}) copy-start(s32[8,128]{1,0:T(8,128)S(1)} %pad_add_fusion.rays) | copy-start | bytes 12292
  13.8 20.8 %collective-permute-start.3 = (bf16[256,512]{1,0:T(8,128)(2,1)S(1)}, bf16[256,512]{1,0:T(8,128)(2,1)S(1)}, u32[]{:S(2)}, u32[]{:S(2)}) collective-permute-start(bf16[256,512]{1,0:T(8,128)(2,1)S(1)} %get-tuple-element.20), channel_id=1, source_target_pairs={{0,8},{4,12},{8,0},{12,4},{1,9},{5,13},{9,1},{13,5},{2,10},{6,14},... | collective-permute-start | bytes 786440 | tf_op jit(solution)/shard_map/ppermute | solution.py:467
  15.8 18.8 %collective-permute-start.4 = (bf16[256,512]{1,0:T(8,128)(2,1)S(1)}, bf16[256,512]{1,0:T(8,128)(2,1)S(1)}, u32[]{:S(2)}, u32[]{:S(2)}) collective-permute-start(bf16[256,512]{1,0:T(8,128)(2,1)S(1)} %get-tuple-element.21), channel_id=1, source_target_pairs={{0,12},{4,8},{8,4},{12,0},{1,13},{5,9},{9,5},{13,1},{2,14},{6,10},... | collective-permute-start | bytes 786440 | tf_op jit(solution)/shard_map/ppermute | solution.py:467
  17.8 17.2 %collective-permute-start.5 = (bf16[256,512]{1,0:T(8,128)(2,1)S(1)}, bf16[256,512]{1,0:T(8,128)(2,1)S(1)}, u32[]{:S(2)}, u32[]{:S(2)}) collective-permute-start(bf16[256,512]{1,0:T(8,128)(2,1)S(1)} %get-tuple-element.22), channel_id=1, source_target_pairs={{0,4},{4,0},{8,12},{12,8},{1,5},{5,1},{9,13},{13,9},{2,6},{6,2},{1... | collective-permute-start | bytes 786440 | tf_op jit(solution)/shard_map/ppermute | solution.py:467
  25.5 2.0 %collective-permute-start.6 = (bf16[2,256,512]{2,1,0:T(8,128)(2,1)S(1)}, bf16[2,256,512]{2,1,0:T(8,128)(2,1)S(1)}, u32[]{:S(2)}, u32[]{:S(2)}) collective-permute-start(bf16[2,256,512]{2,1,0:T(8,128)(2,1)S(1)} %get-tuple-element.25), channel_id=1, source_target_pairs={{0,1},{1,0},{2,3},{3,2},{4,5},{5,4},{6,7},{7,6},{8,9},{9,8},{10,11... | collective-permute-start | bytes 1572872 | tf_op jit(solution)/shard_map/ppermute | solution.py:467
  27.5 16.1 %slice-start = ((s8[8388608]{0:T(1024)(128)(4,1)}), s8[4194304]{0:T(1024)(128)(4,1)S(1)}, s32[]{:S(2)}) async-start(s8[8388608]{0:T(1024)(128)(4,1)} %bitcast.17), calls=%async_computation | async-start | bytes 8388608
  27.6 16.0 %slice-start.1 = ((s8[8388608]{0:T(1024)(128)(4,1)}), s8[4194304]{0:T(1024)(128)(4,1)S(1)}, s32[]{:S(2)}) async-start(s8[8388608]{0:T(1024)(128)(4,1)} %bitcast.17), calls=%async_computation.1 | async-start | bytes 8388608
  27.6 16.0 %copy-start.1 = (s32[8,128]{1,0:T(8,128)S(1)}, s32[8,128]{1,0:T(8,128)}, u32[]{:S(2)}) copy-start(s32[8,128]{1,0:T(8,128)} %copy-done) | copy-start | bytes 12292
  27.6 8.4 %collective-permute-start.7 = (bf16[256,512]{1,0:T(8,128)(2,1)S(1)}, bf16[256,512]{1,0:T(8,128)(2,1)S(1)}, u32[]{:S(2)}, u32[]{:S(2)}) collective-permute-start(bf16[256,512]{1,0:T(8,128)(2,1)S(1)} %fusion), channel_id=1, source_target_pairs={{0,2},{1,3},{2,0},{3,1},{4,6},{5,7},{6,4},{7,5},{8,10},{9,11},{10,... | collective-permute-start | bytes 786440 | tf_op jit(solution)/shard_map/ppermute | solution.py:463
  36.2 14.9 %collective-permute-start.10 = (bf16[128,512]{1,0:T(8,128)(2,1)S(1)}, bf16[128,512]{1,0:T(8,128)(2,1)S(1)}, u32[]{:S(2)}, u32[]{:S(2)}) collective-permute-start(bf16[128,512]{1,0:T(8,128)(2,1)S(1)} %get-tuple-element.31.refs_1_), channel_id=1, source_target_pairs={{0,8},{4,12},{8,0},{12,4},{1,9},{5,13},{9,1},{13,5},{2,10},{6,14},... | collective-permute-start | bytes 393224 | tf_op jit(solution)/shard_map/ppermute | solution.py:467
  41.5 12.2 %collective-permute-start.8 = (bf16[128,512]{1,0:T(8,128)(2,1)S(1)}, bf16[128,512]{1,0:T(8,128)(2,1)S(1)}, u32[]{:S(2)}, u32[]{:S(2)}) collective-permute-start(bf16[128,512]{1,0:T(8,128)(2,1)S(1)} %get-tuple-element.32.refs_0_), channel_id=1, source_target_pairs={{0,8},{4,12},{8,0},{12,4},{1,9},{5,13},{9,1},{13,5},{2,10},{6,14},... | collective-permute-start | bytes 393224 | tf_op jit(solution)/shard_map/ppermute | solution.py:467
  41.5 12.1 %collective-permute-start.12 = (bf16[128,512]{1,0:T(8,128)(2,1)S(1)}, bf16[128,512]{1,0:T(8,128)(2,1)S(1)}, u32[]{:S(2)}, u32[]{:S(2)}) collective-permute-start(bf16[128,512]{1,0:T(8,128)(2,1)S(1)} %get-tuple-element.32.refs_0_), channel_id=1, source_target_pairs={{0,4},{4,0},{8,12},{12,8},{1,5},{5,1},{9,13},{13,9},{2,6},{6,2},{1... | collective-permute-start | bytes 393224 | tf_op jit(solution)/shard_map/ppermute | solution.py:467
  43.3 12.6 %collective-permute-start.13 = (bf16[128,512]{1,0:T(8,128)(2,1)S(1)}, bf16[128,512]{1,0:T(8,128)(2,1)S(1)}, u32[]{:S(2)}, u32[]{:S(2)}) collective-permute-start(bf16[128,512]{1,0:T(8,128)(2,1)S(1)} %get-tuple-element.31.refs_1_), channel_id=1, source_target_pairs={{0,4},{4,0},{8,12},{12,8},{1,5},{5,1},{9,13},{13,9},{2,6},{6,2},{1... | collective-permute-start | bytes 393224 | tf_op jit(solution)/shard_map/ppermute | solution.py:467
  51.1 7.7 %collective-permute-start.11 = (bf16[128,512]{1,0:T(8,128)(2,1)S(1)}, bf16[128,512]{1,0:T(8,128)(2,1)S(1)}, u32[]{:S(2)}, u32[]{:S(2)}) collective-permute-start(bf16[128,512]{1,0:T(8,128)(2,1)S(1)} %collective-permute-done.10.refs_1_), channel_id=1, source_target_pairs={{0,4},{4,0},{8,12},{12,8},{1,5},{5,1},{9,13},{13,9},{2,6},{6,2},{1... | collective-permute-start | bytes 393224 | tf_op jit(solution)/shard_map/ppermute | solution.py:467
  53.7 6.8 %collective-permute-start.9 = (bf16[128,512]{1,0:T(8,128)(2,1)S(1)}, bf16[128,512]{1,0:T(8,128)(2,1)S(1)}, u32[]{:S(2)}, u32[]{:S(2)}) collective-permute-start(bf16[128,512]{1,0:T(8,128)(2,1)S(1)} %collective-permute-done.8.refs_0_), channel_id=1, source_target_pairs={{0,4},{4,0},{8,12},{12,8},{1,5},{5,1},{9,13},{13,9},{2,6},{6,2},{1... | collective-permute-start | bytes 393224 | tf_op jit(solution)/shard_map/ppermute | solution.py:467

commit v9 on v8

--- a/solution.py
+++ b/solution.py
@@ -42,40 +42,57 @@
 
 
 def integrate_kernel(
-    nx, per_chunk, tile_bin, place, after, counts, frames, weights, send, acc, member
+    nx, per_chunk, tile_bin, place, after, counts, frames, weights, send, acc, *scratch
 ):
-    step = pl.program_id(0)
+    member, frame_buf, weight_buf, frame_sem, weight_sem = scratch
     points, slots = member.shape
-    blocks = weights.shape[0]
     tile_bins = acc.shape[2]
-
-    @pl.when(step == 0)
-    def _():
-        acc[...] = jnp.zeros_like(acc)
-        count_row = counts[...].astype(F32)
-        row = lax.broadcasted_iota(jnp.int32, (points, points), 0)
-        col = lax.broadcasted_iota(jnp.int32, (points, points), 1)
-        ends = jnp.sum(jnp.where(col <= row, count_row, 0.0), axis=1, keepdims=True)
-        count = jnp.sum(jnp.where(col == row, count_row, 0.0), axis=1, keepdims=True)
-        slot = lax.broadcasted_iota(jnp.int32, (points, slots), 1).astype(F32)
-        inside = jnp.logical_and(slot >= ends - count, slot < ends)
-        member[...] = jnp.where(inside, 1.0 / count, 0.0).astype(BF16)
-
-    means = jnp.dot(member[...], frames[...], preferred_element_type=F32).astype(BF16)
-    for b in range(blocks):
-        value = jnp.dot(
-            means[:, b * LANES : (b + 1) * LANES], weights[b], preferred_element_type=F32
+    chunks = frame_sem.shape[0]
+    width = frame_buf.shape[1] // chunks
+    blocks = width // LANES
+
+    def loads(chunk):
+        here = slice(chunk * width, (chunk + 1) * width)
+        return (
+            pltpu.make_async_copy(frames.at[:, here], frame_buf.at[:, here], frame_sem.at[chunk]),
+            pltpu.make_async_copy(weights.at[here, :], weight_buf.at[here, :], weight_sem.at[chunk]),
         )
-        k = tile_bin[step * blocks + b]
+
+    def add(mean, block, k):
+        rows = slice(block * LANES, (block + 1) * LANES)
+        lanes = slice(block % blocks * LANES, (block % blocks + 1) * LANES)
+        value = jnp.dot(mean[:, lanes], weight_buf[rows, :], preferred_element_type=F32)
         acc[k] += value[:, :tile_bins]
         acc[k + 1] += value[:, tile_bins:]
 
-    @pl.when(step == pl.num_programs(0) - 1)
-    def _():
-        for e in range(nx):
-            for j in range(per_chunk):
-                lanes = slice(j * tile_bins, (j + 1) * tile_bins)
-                send[e, :, lanes] = acc[place[2 * e] * per_chunk + j].astype(BF16)
+    for chunk in range(min(2, chunks)):
+        for load in loads(chunk):
+            load.start()
+    acc[...] = jnp.zeros_like(acc)
+    count_row = counts[...].astype(F32)
+    row = lax.broadcasted_iota(jnp.int32, (points, points), 0)
+    col = lax.broadcasted_iota(jnp.int32, (points, points), 1)
+    ends = jnp.sum(jnp.where(col <= row, count_row, 0.0), axis=1, keepdims=True)
+    count = jnp.sum(jnp.where(col == row, count_row, 0.0), axis=1, keepdims=True)
+    slot = lax.broadcasted_iota(jnp.int32, (points, slots), 1).astype(F32)
+    inside = jnp.logical_and(slot >= ends - count, slot < ends)
+    member[...] = jnp.where(inside, 1.0 / count, 0.0).astype(BF16)
+
+    for chunk in range(chunks):
+        for load in loads(chunk):
+            load.wait()
+        if chunk + 2 < chunks:
+            for load in loads(chunk + 2):
+                load.start()
+        here = slice(chunk * width, (chunk + 1) * width)
+        mean = jnp.dot(member[...], frame_buf[:, here], preferred_element_type=F32).astype(BF16)
+        for block in range(chunk * blocks, (chunk + 1) * blocks):
+            add(mean, block, tile_bin[block])
+
+    for e in range(nx):
+        for j in range(per_chunk):
+            lanes = slice(j * tile_bins, (j + 1) * tile_bins)
+            send[e, :, lanes] = acc[place[2 * e] * per_chunk + j].astype(BF16)
 
 
 def integrate(frames, counts, weights, tile_bin, place, after, nx, chans):
@@ -83,26 +100,22 @@
     points = counts.shape[0]
     nblocks, tile_pix, pair = weights.shape
     tile_bins = pair // 2
-    blocks = 16 if nblocks % 16 == 0 else 1
+    chunks = nblocks // 16 if nblocks % 16 == 0 else nblocks
     channel_blocks = 2 * nx * chans // tile_bins
-    whole = lambda shape: pl.BlockSpec(shape, lambda i, *_: (0,) * len(shape))
+    vmem = pl.BlockSpec(memory_space=pltpu.VMEM)
+    smem = pl.BlockSpec(memory_space=pltpu.SMEM)
+    anywhere = pl.BlockSpec(memory_space=pl.ANY)
     return pl.pallas_call(
         functools.partial(integrate_kernel, nx, chans // tile_bins),
-        grid_spec=pltpu.PrefetchScalarGridSpec(
-            num_scalar_prefetch=2,
-            grid=(nblocks // blocks,),
-            in_specs=[
-                pl.BlockSpec(memory_space=pl.ANY),
-                whole((1, points)),
-                pl.BlockSpec((slots, blocks * tile_pix), lambda i, *_: (0, i)),
-                pl.BlockSpec((blocks, tile_pix, pair), lambda i, *_: (i, 0, 0)),
-            ],
-            out_specs=[
-                whole((nx, points, chans)),
-                whole((channel_blocks, points, tile_bins)),
-            ],
-            scratch_shapes=[pltpu.VMEM((points, slots), BF16)],
-        ),
+        in_specs=[smem, smem, anywhere, vmem, anywhere, anywhere],
+        out_specs=[vmem, vmem],
+        scratch_shapes=[
+            pltpu.VMEM((points, slots), BF16),
+            pltpu.VMEM((slots, pixels), BF16),
+            pltpu.VMEM((pixels, pair), BF16),
+            pltpu.SemaphoreType.DMA((chunks,)),
+            pltpu.SemaphoreType.DMA((chunks,)),
+        ],
         out_shape=[
             jax.ShapeDtypeStruct((nx, points, chans), BF16),
             jax.ShapeDtypeStruct((channel_blocks, points, tile_bins), F32),
@@ -116,7 +129,7 @@
         after,
         counts.reshape(1, points),
         pltpu.with_memory_space_constraint(frames, pltpu.HBM),
-        pltpu.with_memory_space_constraint(weights, pltpu.HBM),
+        pltpu.with_memory_space_constraint(weights.reshape(pixels, pair), pltpu.HBM),
     )
 
 
@@ -260,6 +273,25 @@
     )(rays, rows)
 
 
+def merge_kernel(count, after, *refs):
+    for own, other, out in zip(refs[:count], refs[count : 2 * count], refs[2 * count :]):
+        out[...] = (own[...].astype(F32) + other[...].astype(F32)).astype(BF16)
+
+
+def merge(after, shares, received):
+    count = len(shares)
+    vmem = pl.BlockSpec(memory_space=pltpu.VMEM)
+    return pl.pallas_call(
+        functools.partial(merge_kernel, count),
+        in_specs=[pl.BlockSpec(memory_space=pl.ANY)] + [vmem] * (2 * count),
+        out_specs=[vmem] * count,
+        out_shape=[jax.ShapeDtypeStruct(x.shape, BF16) for x in shares],
+        compiler_params=pltpu.CompilerParams(vmem_limit_bytes=8 * MIB),
+        cost_estimate=SMALL,
+        name="merge",
+    )(after, *shares, *received)
+
+
 def row_total_kernel(angles, after, rays, row_total):
     cos_r, sin_r, off_r = ray_geometry(rays[...], angles)
     line = lax.broadcasted_iota(jnp.int32, (LANES, LANES), 0).astype(F32) - HALF
@@ -488,8 +520,7 @@
     projected = project(image, first_row, angles)
     own_share, *shares = reorder(all_rays, projected, n_scan)
     share_of = dict(zip(order[1:], shares))
-    sending = sorted(share_of, key=lambda r: (2 * r != n_scan, -r))
-    arrived = [swap(share_of[r], "scan", r, n_scan) for r in sending]
+    relayed = {r ^ 1: swap(share_of[r], "scan", 1, n_scan) for r in late}
 
     place = []
     for e in range(nx):
@@ -500,6 +531,10 @@
         frames, counts, channel_pair_weights, tile_bin, place, own_share, nx, chans
     )
     keep = select(place, sums, nx, chans)
+    even = sorted(relayed)
+    merged = merge(sums, [share_of[r] for r in even], [relayed[r] for r in even])
+    arrived = [swap(x, "scan", r, n_scan) for r, x in zip(even, merged)]
+    arrived.append(swap(share_of[1], "scan", 1, n_scan))
     got = swap(send, "chan", 1, n_chan)
     pattern = keep[0] + got[0].astype(F32)
     for e in range(1, nx):

time: 64.5 us -> 62.5 us (0.969)
  starting transfers between devices: 19.2 us -> 17.4 us
    ppermute x13, starting transfers between devices: 17.7 us -> 15.9 us  [swap(): return lax.ppermute(x, axis, [(i, i ^ mask) for i in range(n)])]
    ppermute x13, waiting for transfers between devices: 15.1 us -> 16.1 us  [swap(): return lax.ppermute(x, axis, [(i, i ^ mask) for i in range(n)])]
    ppermute x1, waiting for transfers between devices: 0.69 us -> 0.01 us  [rotate(): return lax.ppermute(x, axis, [(i, (i + shift) % n) for i in range(n)])]
    pallas_call x1, Pallas kernels: 7.21 us -> 6.52 us  [integrate(): pl.pallas_call(functools.partial(integrate_kernel, nx, chans // tile_bins...]
  transfers between devices with their start and end apart: 14 -> 14, of which waited for: 9 -> 6; matrix products, arithmetic and copies ran while one was open for 0% -> 0% of each run, Pallas kernels for 36% -> 36%
where the time goes in v9:
time: 62.5 us; the launch traced here: 62.1 us
  Pallas kernels  27.8 us (44%)
  starting transfers between devices  17.4 us (28%)
  waiting for transfers between devices  16.1 us (26%)
    ppermute x13, waiting for transfers between devices, swap(): return lax.ppermute(x, axis, [(i, i ^ mask) for i in range(n)])  16.1 us
    ppermute x13, starting transfers between devices, swap(): return lax.ppermute(x, axis, [(i, i ^ mask) for i in range(n)])  15.9 us
    pallas_call x1, Pallas kernels, integrate(): pl.pallas_call(functools.partial(integrate_kernel, nx, chans // tile_bins...  6.52 us
    pallas_call x1, Pallas kernels, project(): pl.pallas_call(functools.partial(project_kernel, angles), in_specs=[pl.Bl...  6.31 us
    pallas_call x1, Pallas kernels, prepare(): pl.pallas_call(functools.partial(prepare_kernel, angles, len(residuals)),...  5.82 us
    pallas_call x1, Pallas kernels, back_project(): pl.pallas_call(functools.partial(back_kernel, first, len(pieces)), in_spe...  3.67 us
    pallas_call x1, Pallas kernels, add_back(): pl.pallas_call(functools.partial(add_kernel, first, len(pieces)), in_spec...  2.41 us
    pallas_call x1, Pallas kernels, reorder(): pl.pallas_call(reorder_kernel, in_specs=[vmem, vmem], out_specs=[vmem] *...  1.68 us
  transfers between devices with their start and end apart: 14, of which 6 were waited for; matrix products, arithmetic and copies ran while one was open for 0% of the time, Pallas kernels for 36%

profile of v9, /device:TPU:0, one launch (start us, length us, event | category | flops | bytes accessed | tf_op | source)
XLA Modules:
  0.0 62.1 jit_solution(16485846459839085717)
XLA Ops:
  0.0 4.0 %collective-permute-start = (s32[2,128]{1,0:T(2,128)}, s32[2,128]{1,0:T(2,128)S(1)}, u32[]{:S(2)}, u32[]{:S(2)}) collective-permute-start(s32[2,128]{1,0:T(2,128)} %bitcast.20), channel_id=1, source_target_pairs={{0,8},{4,12},{8,0},{12,4},{1,9},{5,13},{9,1},{13,5},{2,10},{6,14},... | collective-permute-start | bytes 3080 | tf_op jit(solution)/shard_map/ppermute | solution.py:499
  4.0 1.6 %collective-permute-start.1 = (s32[2,128]{1,0:T(2,128)}, s32[2,128]{1,0:T(2,128)S(1)}, u32[]{:S(2)}, u32[]{:S(2)}) collective-permute-start(s32[2,128]{1,0:T(2,128)} %bitcast.21), channel_id=1, source_target_pairs={{0,4},{4,0},{8,12},{12,8},{1,5},{5,1},{9,13},{13,9},{2,6},{6,2},{1... | collective-permute-start | bytes 3080 | tf_op jit(solution)/shard_map/ppermute | solution.py:499
  5.6 6.3 %project.1.rows = bf16[1024,512]{1,0:T(8,128)(2,1)S(1)} custom-call(s32[1]{0:T(128)} %bitcast.5.first_row, f32[4096,512]{1,0:T(8,128)} %refs_2_.1), custom_call_target="tpu_custom_call" | custom-call | flops 8589934592 | bytes 8388608 | tf_op jit(solution)/shard_map/project/pallas_call | solution.py:222
  12.0 1.7 %reorder.1 = (bf16[256,512]{1,0:T(8,128)(2,1)S(1)}, bf16[256,512]{1,0:T(8,128)(2,1)S(1)}, bf16[256,512]{1,0:T(8,128)(2,1)S(1)}, bf16[256,512]{1,0:T(8,128)(2,1)S(1)}) custom-call(s32[8,128]{1,0:T(8,128)S(1)} %pad_add_fusion.rays, bf16[1024,512]{1,0:T(8,128)(2,1)S(1)} %project.1.rows), custom_call_target="tpu_custom_call" | custom-call | flops 1 | bytes 1 | tf_op jit(solution)/shard_map/reorder/pallas_call | solution.py:264
  13.7 1.0 %collective-permute-start.3 = (bf16[256,512]{1,0:T(8,128)(2,1)S(1)}, bf16[256,512]{1,0:T(8,128)(2,1)S(1)}, u32[]{:S(2)}, u32[]{:S(2)}) collective-permute-start(bf16[256,512]{1,0:T(8,128)(2,1)S(1)} %get-tuple-element.21), channel_id=1, source_target_pairs={{0,4},{4,0},{8,12},{12,8},{1,5},{5,1},{9,13},{13,9},{2,6},{6,2},{1... | collective-permute-start | bytes 786440 | tf_op jit(solution)/shard_map/ppermute | solution.py:499
  14.8 1.1 %collective-permute-start.5 = (bf16[256,512]{1,0:T(8,128)(2,1)S(1)}, bf16[256,512]{1,0:T(8,128)(2,1)S(1)}, u32[]{:S(2)}, u32[]{:S(2)}) collective-permute-start(bf16[256,512]{1,0:T(8,128)(2,1)S(1)} %get-tuple-element.22), channel_id=1, source_target_pairs={{0,4},{4,0},{8,12},{12,8},{1,5},{5,1},{9,13},{13,9},{2,6},{6,2},{1... | collective-permute-start | bytes 786440 | tf_op jit(solution)/shard_map/ppermute | solution.py:499
  15.9 6.5 %integrate.1 = (bf16[2,256,512]{2,1,0:T(8,128)(2,1)S(1)}, f32[16,256,128]{2,1,0:T(8,128)S(1)}) custom-call(s32[48]{0:T(128)S(1)} %copy-done.4, s32[4]{0:T(128)S(1)} %pad_add_fusion.1.place, bf16[256,512]{1,0:T(8,128)(2,1)S(1)} %get-tuple-element.18.after.own, s32[1,256]{1,0:T(1,128)S(1)} %bitcast.25, bf16[384,6144]{1,0:T(8,128)(2,1)} %frames.1, ...), custom_call_target="tpu_custom_call" | custom-call | flops 1 | bytes 1 | tf_op jit(solution)/shard_map/integrate/pallas_call | solution.py:108
  22.5 0.5 collective-permute-done.3.refs_1_
  23.1 2.4 %collective-permute-start.4 = (bf16[256,512]{1,0:T(8,128)(2,1)S(1)}, bf16[256,512]{1,0:T(8,128)(2,1)S(1)}, u32[]{:S(2)}, u32[]{:S(2)}) collective-permute-start(bf16[256,512]{1,0:T(8,128)(2,1)S(1)} %merge.1), channel_id=1, source_target_pairs={{0,8},{4,12},{8,0},{12,4},{1,9},{5,13},{9,1},{13,5},{2,10},{6,14},... | collective-permute-start | bytes 786440 | tf_op jit(solution)/shard_map/ppermute | solution.py:499
  25.5 0.7 %select.11 = (f32[256,512]{1,0:T(8,128)S(1)}, f32[256,512]{1,0:T(8,128)S(1)}) custom-call(s32[4]{0:T(128)S(1)} %pad_add_fusion.1.place, f32[16,256,128]{2,1,0:T(8,128)S(1)} %get-tuple-element.19.after.acc), custom_call_target="tpu_custom_call" | custom-call | flops 99999997952 | bytes 100000000 | tf_op jit(solution)/shard_map/select/pallas_call | solution.py:148
  26.2 0.4 row_totals.1.row_total
  26.8 1.5 %collective-permute-start.7 = (bf16[256,512]{1,0:T(8,128)(2,1)S(1)}, bf16[256,512]{1,0:T(8,128)(2,1)S(1)}, u32[]{:S(2)}, u32[]{:S(2)}) collective-permute-start(bf16[256,512]{1,0:T(8,128)(2,1)S(1)} %fusion), channel_id=1, source_target_pairs={{0,2},{1,3},{2,0},{3,1},{4,6},{5,7},{6,4},{7,5},{8,10},{9,11},{10,... | collective-permute-start | bytes 786440 | tf_op jit(solution)/shard_map/ppermute | solution.py:495
  28.3 9.6 %collective-permute-done.4.refs_0_ = bf16[256,512]{1,0:T(8,128)(2,1)S(1)} collective-permute-done((bf16[256,512]{1,0:T(8,128)(2,1)S(1)}, bf16[256,512]{1,0:T(8,128)(2,1)S(1)}, u32[]{:S(2)}, u32[]{:S(2)}) %collective-permute-start.4) | collective-permute-done | bytes 262176 | tf_op jit(solution)/shard_map/ppermute | solution.py:499
  38.5 2.9 %collective-permute-start.8 = (bf16[128,512]{1,0:T(8,128)(2,1)S(1)}, bf16[128,512]{1,0:T(8,128)(2,1)S(1)}, u32[]{:S(2)}, u32[]{:S(2)}) collective-permute-start(bf16[128,512]{1,0:T(8,128)(2,1)S(1)} %get-tuple-element.32.refs_0_), channel_id=1, source_target_pairs={{0,8},{4,12},{8,0},{12,4},{1,9},{5,13},{9,1},{13,5},{2,10},{6,14},... | collective-permute-start | bytes 393224 | tf_op jit(solution)/shard_map/ppermute | solution.py:499
  41.4 1.0 %collective-permute-start.12 = (bf16[128,512]{1,0:T(8,128)(2,1)S(1)}, bf16[128,512]{1,0:T(8,128)(2,1)S(1)}, u32[]{:S(2)}, u32[]{:S(2)}) collective-permute-start(bf16[128,512]{1,0:T(8,128)(2,1)S(1)} %get-tuple-element.32.refs_0_), channel_id=1, source_target_pairs={{0,4},{4,0},{8,12},{12,8},{1,5},{5,1},{9,13},{13,9},{2,6},{6,2},{1... | collective-permute-start | bytes 393224 | tf_op jit(solution)/shard_map/ppermute | solution.py:499
  42.4 1.0 %collective-permute-start.13 = (bf16[128,512]{1,0:T(8,128)(2,1)S(1)}, bf16[128,512]{1,0:T(8,128)(2,1)S(1)}, u32[]{:S(2)}, u32[]{:S(2)}) collective-permute-start(bf16[128,512]{1,0:T(8,128)(2,1)S(1)} %get-tuple-element.31.refs_1_), channel_id=1, source_target_pairs={{0,4},{4,0},{8,12},{12,8},{1,5},{5,1},{9,13},{13,9},{2,6},{6,2},{1... | collective-permute-start | bytes 393224 | tf_op jit(solution)/shard_map/ppermute | solution.py:499
  43.5 5.8 %prepare.1 = (bf16[4096,1024]{1,0:T(8,128)(2,1)S(1)}, f32[4096,128]{1,0:T(8,128)S(1)}, f32[4096,512]{1,0:T(8,128)S(1)}) custom-call(s32[1]{0:T(128)} %bitcast.5.first_row, s32[8,128]{1,0:T(8,128)S(1)} %copy-done.1, bf16[128,512]{1,0:T(8,128)(2,1)S(1)} %get-tuple-element.32.refs_0_, bf16[128,512]{1,0:T(8,128)(2,1)S(1)} %get-tuple-element.31.refs_1_, ...), custom_call_target="tpu_custom_call" | custom-call | flops 1 | bytes 1 | tf_op jit(solution)/shard_map/prepare/pallas_call | solution.py:396
  49.3 1.8 %collective-permute-done.10.refs_1_ = bf16[128,512]{1,0:T(8,128)(2,1)S(1)} collective-permute-done((bf16[128,512]{1,0:T(8,128)(2,1)S(1)}, bf16[128,512]{1,0:T(8,128)(2,1)S(1)}, u32[]{:S(2)}, u32[]{:S(2)}) %collective-permute-start.10) | collective-permute-done | bytes 131104 | tf_op jit(solution)/shard_map/ppermute | solution.py:499
  51.1 1.4 %collective-permute-done.8.refs_0_ = bf16[128,512]{1,0:T(8,128)(2,1)S(1)} collective-permute-done((bf16[128,512]{1,0:T(8,128)(2,1)S(1)}, bf16[128,512]{1,0:T(8,128)(2,1)S(1)}, u32[]{:S(2)}, u32[]{:S(2)}) %collective-permute-start.8) | collective-permute-done | bytes 131104 | tf_op jit(solution)/shard_map/ppermute | solution.py:499
  52.5 0.6 collective-permute-start.9
  53.1 2.4 %add_back.1.refs_4_ = f32[4096,512]{1,0:T(8,128)S(1)} custom-call(bf16[128,512]{1,0:T(8,128)(2,1)S(1)} %collective-permute-done.8.refs_0_, bf16[128,512]{1,0:T(8,128)(2,1)S(1)} %collective-permute-done.10.refs_1_, bf16[128,512]{1,0:T(8,128)(2,1)S(1)} %collective-permute-done.12.refs_2_, bf16[128,512]{1,0:T(8,128)(2,1)S(1)} %collective-permute-done.13.refs_3_, ...), custom_call_target="tpu_custom_call" | custom-call | flops 99999997952 | bytes 100000000 | tf_op jit(solution)/shard_map/add_back/pallas_call | solution.py:445
  55.5 1.4 %collective-permute-done.11.refs_1_ = bf16[128,512]{1,0:T(8,128)(2,1)S(1)} collective-permute-done((bf16[128,512]{1,0:T(8,128)(2,1)S(1)}, bf16[128,512]{1,0:T(8,128)(2,1)S(1)}, u32[]{:S(2)}, u32[]{:S(2)}) %collective-permute-start.11) | collective-permute-done | bytes 131104 | tf_op jit(solution)/shard_map/ppermute | solution.py:499
  56.9 1.4 %collective-permute-done.9.refs_0_ = bf16[128,512]{1,0:T(8,128)(2,1)S(1)} collective-permute-done((bf16[128,512]{1,0:T(8,128)(2,1)S(1)}, bf16[128,512]{1,0:T(8,128)(2,1)S(1)}, u32[]{:S(2)}, u32[]{:S(2)}) %collective-permute-start.9) | collective-permute-done | bytes 131104 | tf_op jit(solution)/shard_map/ppermute | solution.py:499
  58.3 3.7 %back_project.1 = f32[4096,512]{1,0:T(8,128)} custom-call(bf16[128,512]{1,0:T(8,128)(2,1)S(1)} %collective-permute-done.9.refs_0_, bf16[128,512]{1,0:T(8,128)(2,1)S(1)} %collective-permute-done.11.refs_1_, bf16[4096,1024]{1,0:T(8,128)(2,1)S(1)} %get-tuple-element.28.refs_4_.refs_2_, f32[4096,128]{1,0:T(8,128)S(1)} %get-tuple-element.29.refs_5_.refs_3_, ...), custom_call_target="tpu_custom_call" | custom-call | flops 1 | bytes 1 | tf_op jit(solution)/shard_map/back_project/pallas_call | solution.py:478
  (35 shorter events, 0.9 us)
Async XLA Ops:
  0.0 11.9 %collective-permute-start = (s32[2,128]{1,0:T(2,128)}, s32[2,128]{1,0:T(2,128)S(1)}, u32[]{:S(2)}, u32[]{:S(2)}) collective-permute-start(s32[2,128]{1,0:T(2,128)} %bitcast.20), channel_id=1, source_target_pairs={{0,8},{4,12},{8,0},{12,4},{1,9},{5,13},{9,1},{13,5},{2,10},{6,14},... | collective-permute-start | bytes 3080 | tf_op jit(solution)/shard_map/ppermute | solution.py:499
  4.0 7.9 %collective-permute-start.1 = (s32[2,128]{1,0:T(2,128)}, s32[2,128]{1,0:T(2,128)S(1)}, u32[]{:S(2)}, u32[]{:S(2)}) collective-permute-start(s32[2,128]{1,0:T(2,128)} %bitcast.21), channel_id=1, source_target_pairs={{0,4},{4,0},{8,12},{12,8},{1,5},{5,1},{9,13},{13,9},{2,6},{6,2},{1... | collective-permute-start | bytes 3080 | tf_op jit(solution)/shard_map/ppermute | solution.py:499
  5.6 6.4 %collective-permute-start.2 = (s32[2,128]{1,0:T(2,128)}, s32[2,128]{1,0:T(2,128)S(1)}, u32[]{:S(2)}, u32[]{:S(2)}) collective-permute-start(s32[2,128]{1,0:T(2,128)} %bitcast.22), channel_id=1, source_target_pairs={{0,12},{4,8},{8,4},{12,0},{1,13},{5,9},{9,5},{13,1},{2,14},{6,10},... | collective-permute-start | bytes 3080 | tf_op jit(solution)/shard_map/ppermute | solution.py:499
  5.6 6.4 %copy-start.2 = (s32[256]{0:T(256)S(1)}, s32[256]{0:T(256)}, u32[]{:S(2)}) copy-start(s32[256]{0:T(256)} %param.8) | copy-start | bytes 3076
  5.6 10.3 %copy-start.3 = (s32[256]{0:T(256)S(1)}, s32[256]{0:T(256)}, u32[]{:S(2)}) copy-start(s32[256]{0:T(256)} %param.7) | copy-start | bytes 3076
  5.6 10.3 %copy-start.4 = (s32[48]{0:T(128)S(1)}, s32[48]{0:T(128)}, u32[]{:S(2)}) copy-start(s32[48]{0:T(128)} %tile_bin.1) | copy-start | bytes 580
  12.0 1.7 %copy-start = (s32[8,128]{1,0:T(8,128)}, s32[8,128]{1,0:T(8,128)S(1)}, u32[]{:S(2)}) copy-start(s32[8,128]{1,0:T(8,128)S(1)} %pad_add_fusion.rays) | copy-start | bytes 12292
  13.7 9.3 %collective-permute-start.3 = (bf16[256,512]{1,0:T(8,128)(2,1)S(1)}, bf16[256,512]{1,0:T(8,128)(2,1)S(1)}, u32[]{:S(2)}, u32[]{:S(2)}) collective-permute-start(bf16[256,512]{1,0:T(8,128)(2,1)S(1)} %get-tuple-element.21), channel_id=1, source_target_pairs={{0,4},{4,0},{8,12},{12,8},{1,5},{5,1},{9,13},{13,9},{2,6},{6,2},{1... | collective-permute-start | bytes 786440 | tf_op jit(solution)/shard_map/ppermute | solution.py:499
  14.8 13.6 %collective-permute-start.5 = (bf16[256,512]{1,0:T(8,128)(2,1)S(1)}, bf16[256,512]{1,0:T(8,128)(2,1)S(1)}, u32[]{:S(2)}, u32[]{:S(2)}) collective-permute-start(bf16[256,512]{1,0:T(8,128)(2,1)S(1)} %get-tuple-element.22), channel_id=1, source_target_pairs={{0,4},{4,0},{8,12},{12,8},{1,5},{5,1},{9,13},{13,9},{2,6},{6,2},{1... | collective-permute-start | bytes 786440 | tf_op jit(solution)/shard_map/ppermute | solution.py:499
  22.4 4.2 %collective-permute-start.6 = (bf16[2,256,512]{2,1,0:T(8,128)(2,1)S(1)}, bf16[2,256,512]{2,1,0:T(8,128)(2,1)S(1)}, u32[]{:S(2)}, u32[]{:S(2)}) collective-permute-start(bf16[2,256,512]{2,1,0:T(8,128)(2,1)S(1)} %get-tuple-element.25), channel_id=1, source_target_pairs={{0,1},{1,0},{2,3},{3,2},{4,5},{5,4},{6,7},{7,6},{8,9},{9,8},{10,11... | collective-permute-start | bytes 1572872 | tf_op jit(solution)/shard_map/ppermute | solution.py:499
  23.1 14.8 %collective-permute-start.4 = (bf16[256,512]{1,0:T(8,128)(2,1)S(1)}, bf16[256,512]{1,0:T(8,128)(2,1)S(1)}, u32[]{:S(2)}, u32[]{:S(2)}) collective-permute-start(bf16[256,512]{1,0:T(8,128)(2,1)S(1)} %merge.1), channel_id=1, source_target_pairs={{0,8},{4,12},{8,0},{12,4},{1,9},{5,13},{9,1},{13,5},{2,10},{6,14},... | collective-permute-start | bytes 786440 | tf_op jit(solution)/shard_map/ppermute | solution.py:499
  26.6 16.8 %slice-start = ((s8[8388608]{0:T(1024)(128)(4,1)}), s8[4194304]{0:T(1024)(128)(4,1)S(1)}, s32[]{:S(2)}) async-start(s8[8388608]{0:T(1024)(128)(4,1)} %bitcast.18), calls=%async_computation | async-start | bytes 8388608
  26.7 16.7 %slice-start.1 = ((s8[8388608]{0:T(1024)(128)(4,1)}), s8[4194304]{0:T(1024)(128)(4,1)S(1)}, s32[]{:S(2)}) async-start(s8[8388608]{0:T(1024)(128)(4,1)} %bitcast.18), calls=%async_computation.1 | async-start | bytes 8388608
  26.8 16.7 %copy-start.1 = (s32[8,128]{1,0:T(8,128)S(1)}, s32[8,128]{1,0:T(8,128)}, u32[]{:S(2)}) copy-start(s32[8,128]{1,0:T(8,128)} %copy-done) | copy-start | bytes 12292
  26.8 11.5 %collective-permute-start.7 = (bf16[256,512]{1,0:T(8,128)(2,1)S(1)}, bf16[256,512]{1,0:T(8,128)(2,1)S(1)}, u32[]{:S(2)}, u32[]{:S(2)}) collective-permute-start(bf16[256,512]{1,0:T(8,128)(2,1)S(1)} %fusion), channel_id=1, source_target_pairs={{0,2},{1,3},{2,0},{3,1},{4,6},{5,7},{6,4},{7,5},{8,10},{9,11},{10,... | collective-permute-start | bytes 786440 | tf_op jit(solution)/shard_map/ppermute | solution.py:495
  38.4 12.6 %collective-permute-start.10 = (bf16[128,512]{1,0:T(8,128)(2,1)S(1)}, bf16[128,512]{1,0:T(8,128)(2,1)S(1)}, u32[]{:S(2)}, u32[]{:S(2)}) collective-permute-start(bf16[128,512]{1,0:T(8,128)(2,1)S(1)} %get-tuple-element.31.refs_1_), channel_id=1, source_target_pairs={{0,8},{4,12},{8,0},{12,4},{1,9},{5,13},{9,1},{13,5},{2,10},{6,14},... | collective-permute-start | bytes 393224 | tf_op jit(solution)/shard_map/ppermute | solution.py:499
  38.5 14.0 %collective-permute-start.8 = (bf16[128,512]{1,0:T(8,128)(2,1)S(1)}, bf16[128,512]{1,0:T(8,128)(2,1)S(1)}, u32[]{:S(2)}, u32[]{:S(2)}) collective-permute-start(bf16[128,512]{1,0:T(8,128)(2,1)S(1)} %get-tuple-element.32.refs_0_), channel_id=1, source_target_pairs={{0,8},{4,12},{8,0},{12,4},{1,9},{5,13},{9,1},{13,5},{2,10},{6,14},... | collective-permute-start | bytes 393224 | tf_op jit(solution)/shard_map/ppermute | solution.py:499
  41.4 11.7 %collective-permute-start.12 = (bf16[128,512]{1,0:T(8,128)(2,1)S(1)}, bf16[128,512]{1,0:T(8,128)(2,1)S(1)}, u32[]{:S(2)}, u32[]{:S(2)}) collective-permute-start(bf16[128,512]{1,0:T(8,128)(2,1)S(1)} %get-tuple-element.32.refs_0_), channel_id=1, source_target_pairs={{0,4},{4,0},{8,12},{12,8},{1,5},{5,1},{9,13},{13,9},{2,6},{6,2},{1... | collective-permute-start | bytes 393224 | tf_op jit(solution)/shard_map/ppermute | solution.py:499
  42.4 10.7 %collective-permute-start.13 = (bf16[128,512]{1,0:T(8,128)(2,1)S(1)}, bf16[128,512]{1,0:T(8,128)(2,1)S(1)}, u32[]{:S(2)}, u32[]{:S(2)}) collective-permute-start(bf16[128,512]{1,0:T(8,128)(2,1)S(1)} %get-tuple-element.31.refs_1_), channel_id=1, source_target_pairs={{0,4},{4,0},{8,12},{12,8},{1,5},{5,1},{9,13},{13,9},{2,6},{6,2},{1... | collective-permute-start | bytes 393224 | tf_op jit(solution)/shard_map/ppermute | solution.py:499
  51.1 5.8 %collective-permute-start.11 = (bf16[128,512]{1,0:T(8,128)(2,1)S(1)}, bf16[128,512]{1,0:T(8,128)(2,1)S(1)}, u32[]{:S(2)}, u32[]{:S(2)}) collective-permute-start(bf16[128,512]{1,0:T(8,128)(2,1)S(1)} %collective-permute-done.10.refs_1_), channel_id=1, source_target_pairs={{0,4},{4,0},{8,12},{12,8},{1,5},{5,1},{9,13},{13,9},{2,6},{6,2},{1... | collective-permute-start | bytes 393224 | tf_op jit(solution)/shard_map/ppermute | solution.py:499
  52.5 5.8 %collective-permute-start.9 = (bf16[128,512]{1,0:T(8,128)(2,1)S(1)}, bf16[128,512]{1,0:T(8,128)(2,1)S(1)}, u32[]{:S(2)}, u32[]{:S(2)}) collective-permute-start(bf16[128,512]{1,0:T(8,128)(2,1)S(1)} %collective-permute-done.8.refs_0_), channel_id=1, source_target_pairs={{0,4},{4,0},{8,12},{12,8},{1,5},{5,1},{9,13},{13,9},{2,6},{6,2},{1... | collective-permute-start | bytes 393224 | tf_op jit(solution)/shard_map/ppermute | solution.py:499

commit v10 on v9

--- a/solution.py
+++ b/solution.py
@@ -250,7 +250,7 @@
         for k in range(together // LANES):
             row = start // LANES + k
             wanted = jnp.transpose(jnp.broadcast_to(rays[row : row + 1, :], (LANES, LANES)))
-            hot[k * LANES : (k + 1) * LANES, :] = (number == wanted[:, :1]).astype(F32).astype(BF16)
+            hot[k * LANES : (k + 1) * LANES, :] = jnp.where(number == jnp.tile(wanted, (1, all_rays // LANES)), 1.0, 0.0).astype(BF16)
         picked = jnp.dot(hot[...], rows[...], preferred_element_type=F32).astype(BF16)
         for k in range(0, together, points):
             outs[(start + k) // points][...] = picked[k : k + points, :]
@@ -259,7 +259,7 @@
 def reorder(rays, rows, parts):
     all_rays, chans = rows.shape
     points = rays.shape[0] * LANES // parts
-    together = max(points, min(all_rays, MIB // all_rays))
+    together = points
     vmem = pl.BlockSpec(memory_space=pltpu.VMEM)
     return pl.pallas_call(
         reorder_kernel,

time: 62.5 us -> 62.1 us (level)
  no operation moved by 1% of the time
where the time goes in v10:
time: 62.1 us; the launch traced here: 61.8 us
  Pallas kernels  27.4 us (44%)
  starting transfers between devices  17.4 us (28%)
  waiting for transfers between devices  16.1 us (26%)
    ppermute x13, waiting for transfers between devices, swap(): return lax.ppermute(x, axis, [(i, i ^ mask) for i in range(n)])  16.1 us
    ppermute x13, starting transfers between devices, swap(): return lax.ppermute(x, axis, [(i, i ^ mask) for i in range(n)])  15.8 us
    pallas_call x1, Pallas kernels, integrate(): pl.pallas_call(functools.partial(integrate_kernel, nx, chans // tile_bins...  6.52 us
    pallas_call x1, Pallas kernels, project(): pl.pallas_call(functools.partial(project_kernel, angles), in_specs=[pl.Bl...  6.31 us
    pallas_call x1, Pallas kernels, prepare(): pl.pallas_call(functools.partial(prepare_kernel, angles, len(residuals)),...  5.82 us
    pallas_call x1, Pallas kernels, back_project(): pl.pallas_call(functools.partial(back_kernel, first, len(pieces)), in_spe...  3.67 us
    pallas_call x1, Pallas kernels, add_back(): pl.pallas_call(functools.partial(add_kernel, first, len(pieces)), in_spec...  2.41 us
    ppermute x1, starting transfers between devices, rotate(): return lax.ppermute(x, axis, [(i, (i + shift) % n) for i in range(n)])  1.55 us
  transfers between devices with their start and end apart: 14, of which 6 were waited for; matrix products, arithmetic and copies ran while one was open for 0% of the time, Pallas kernels for 36%

profile of v10, /device:TPU:0, one launch (start us, length us, event | category | flops | bytes accessed | tf_op | source)
XLA Modules:
  0.0 61.8 jit_solution(14013897846904602332)
XLA Ops:
  0.0 4.0 %collective-permute-start = (s32[2,128]{1,0:T(2,128)}, s32[2,128]{1,0:T(2,128)S(1)}, u32[]{:S(2)}, u32[]{:S(2)}) collective-permute-start(s32[2,128]{1,0:T(2,128)} %bitcast.20), channel_id=1, source_target_pairs={{0,8},{4,12},{8,0},{12,4},{1,9},{5,13},{9,1},{13,5},{2,10},{6,14},... | collective-permute-start | bytes 3080 | tf_op jit(solution)/shard_map/ppermute | solution.py:499
  4.0 1.6 %collective-permute-start.1 = (s32[2,128]{1,0:T(2,128)}, s32[2,128]{1,0:T(2,128)S(1)}, u32[]{:S(2)}, u32[]{:S(2)}) collective-permute-start(s32[2,128]{1,0:T(2,128)} %bitcast.21), channel_id=1, source_target_pairs={{0,4},{4,0},{8,12},{12,8},{1,5},{5,1},{9,13},{13,9},{2,6},{6,2},{1... | collective-permute-start | bytes 3080 | tf_op jit(solution)/shard_map/ppermute | solution.py:499
  5.6 6.3 %project.1.rows = bf16[1024,512]{1,0:T(8,128)(2,1)S(1)} custom-call(s32[1]{0:T(128)} %bitcast.5.first_row, f32[4096,512]{1,0:T(8,128)} %refs_2_.1), custom_call_target="tpu_custom_call" | custom-call | flops 8589934592 | bytes 8388608 | tf_op jit(solution)/shard_map/project/pallas_call | solution.py:222
  12.0 1.3 %reorder.1 = (bf16[256,512]{1,0:T(8,128)(2,1)S(1)}, bf16[256,512]{1,0:T(8,128)(2,1)S(1)}, bf16[256,512]{1,0:T(8,128)(2,1)S(1)}, bf16[256,512]{1,0:T(8,128)(2,1)S(1)}) custom-call(s32[8,128]{1,0:T(8,128)S(1)} %pad_add_fusion.rays, bf16[1024,512]{1,0:T(8,128)(2,1)S(1)} %project.1.rows), custom_call_target="tpu_custom_call" | custom-call | flops 1 | bytes 1 | tf_op jit(solution)/shard_map/reorder/pallas_call | solution.py:264
  13.4 1.0 %collective-permute-start.3 = (bf16[256,512]{1,0:T(8,128)(2,1)S(1)}, bf16[256,512]{1,0:T(8,128)(2,1)S(1)}, u32[]{:S(2)}, u32[]{:S(2)}) collective-permute-start(bf16[256,512]{1,0:T(8,128)(2,1)S(1)} %get-tuple-element.21), channel_id=1, source_target_pairs={{0,4},{4,0},{8,12},{12,8},{1,5},{5,1},{9,13},{13,9},{2,6},{6,2},{1... | collective-permute-start | bytes 786440 | tf_op jit(solution)/shard_map/ppermute | solution.py:499
  14.4 1.1 %collective-permute-start.5 = (bf16[256,512]{1,0:T(8,128)(2,1)S(1)}, bf16[256,512]{1,0:T(8,128)(2,1)S(1)}, u32[]{:S(2)}, u32[]{:S(2)}) collective-permute-start(bf16[256,512]{1,0:T(8,128)(2,1)S(1)} %get-tuple-element.22), channel_id=1, source_target_pairs={{0,4},{4,0},{8,12},{12,8},{1,5},{5,1},{9,13},{13,9},{2,6},{6,2},{1... | collective-permute-start | bytes 786440 | tf_op jit(solution)/shard_map/ppermute | solution.py:499
  15.5 6.5 %integrate.1 = (bf16[2,256,512]{2,1,0:T(8,128)(2,1)S(1)}, f32[16,256,128]{2,1,0:T(8,128)S(1)}) custom-call(s32[48]{0:T(128)S(1)} %copy-done.4, s32[4]{0:T(128)S(1)} %pad_add_fusion.1.place, bf16[256,512]{1,0:T(8,128)(2,1)S(1)} %get-tuple-element.18.after.own, s32[1,256]{1,0:T(1,128)S(1)} %bitcast.25, bf16[384,6144]{1,0:T(8,128)(2,1)} %frames.1, ...), custom_call_target="tpu_custom_call" | custom-call | flops 1 | bytes 1 | tf_op jit(solution)/shard_map/integrate/pallas_call | solution.py:108
  22.2 0.5 collective-permute-done.3.refs_1_
  22.7 2.4 %collective-permute-start.4 = (bf16[256,512]{1,0:T(8,128)(2,1)S(1)}, bf16[256,512]{1,0:T(8,128)(2,1)S(1)}, u32[]{:S(2)}, u32[]{:S(2)}) collective-permute-start(bf16[256,512]{1,0:T(8,128)(2,1)S(1)} %merge.1), channel_id=1, source_target_pairs={{0,8},{4,12},{8,0},{12,4},{1,9},{5,13},{9,1},{13,5},{2,10},{6,14},... | collective-permute-start | bytes 786440 | tf_op jit(solution)/shard_map/ppermute | solution.py:499
  25.2 0.7 %select.11 = (f32[256,512]{1,0:T(8,128)S(1)}, f32[256,512]{1,0:T(8,128)S(1)}) custom-call(s32[4]{0:T(128)S(1)} %pad_add_fusion.1.place, f32[16,256,128]{2,1,0:T(8,128)S(1)} %get-tuple-element.19.after.acc), custom_call_target="tpu_custom_call" | custom-call | flops 99999997952 | bytes 100000000 | tf_op jit(solution)/shard_map/select/pallas_call | solution.py:148
  25.9 0.4 row_totals.1.row_total
  26.4 1.5 %collective-permute-start.7 = (bf16[256,512]{1,0:T(8,128)(2,1)S(1)}, bf16[256,512]{1,0:T(8,128)(2,1)S(1)}, u32[]{:S(2)}, u32[]{:S(2)}) collective-permute-start(bf16[256,512]{1,0:T(8,128)(2,1)S(1)} %fusion), channel_id=1, source_target_pairs={{0,2},{1,3},{2,0},{3,1},{4,6},{5,7},{6,4},{7,5},{8,10},{9,11},{10,... | collective-permute-start | bytes 786440 | tf_op jit(solution)/shard_map/ppermute | solution.py:495
  28.0 9.6 %collective-permute-done.4.refs_0_ = bf16[256,512]{1,0:T(8,128)(2,1)S(1)} collective-permute-done((bf16[256,512]{1,0:T(8,128)(2,1)S(1)}, bf16[256,512]{1,0:T(8,128)(2,1)S(1)}, u32[]{:S(2)}, u32[]{:S(2)}) %collective-permute-start.4) | collective-permute-done | bytes 262176 | tf_op jit(solution)/shard_map/ppermute | solution.py:499
  38.2 2.9 %collective-permute-start.8 = (bf16[128,512]{1,0:T(8,128)(2,1)S(1)}, bf16[128,512]{1,0:T(8,128)(2,1)S(1)}, u32[]{:S(2)}, u32[]{:S(2)}) collective-permute-start(bf16[128,512]{1,0:T(8,128)(2,1)S(1)} %get-tuple-element.32.refs_0_), channel_id=1, source_target_pairs={{0,8},{4,12},{8,0},{12,4},{1,9},{5,13},{9,1},{13,5},{2,10},{6,14},... | collective-permute-start | bytes 393224 | tf_op jit(solution)/shard_map/ppermute | solution.py:499
  41.1 1.0 %collective-permute-start.12 = (bf16[128,512]{1,0:T(8,128)(2,1)S(1)}, bf16[128,512]{1,0:T(8,128)(2,1)S(1)}, u32[]{:S(2)}, u32[]{:S(2)}) collective-permute-start(bf16[128,512]{1,0:T(8,128)(2,1)S(1)} %get-tuple-element.32.refs_0_), channel_id=1, source_target_pairs={{0,4},{4,0},{8,12},{12,8},{1,5},{5,1},{9,13},{13,9},{2,6},{6,2},{1... | collective-permute-start | bytes 393224 | tf_op jit(solution)/shard_map/ppermute | solution.py:499
  42.1 1.0 %collective-permute-start.13 = (bf16[128,512]{1,0:T(8,128)(2,1)S(1)}, bf16[128,512]{1,0:T(8,128)(2,1)S(1)}, u32[]{:S(2)}, u32[]{:S(2)}) collective-permute-start(bf16[128,512]{1,0:T(8,128)(2,1)S(1)} %get-tuple-element.31.refs_1_), channel_id=1, source_target_pairs={{0,4},{4,0},{8,12},{12,8},{1,5},{5,1},{9,13},{13,9},{2,6},{6,2},{1... | collective-permute-start | bytes 393224 | tf_op jit(solution)/shard_map/ppermute | solution.py:499
  43.1 5.8 %prepare.1 = (bf16[4096,1024]{1,0:T(8,128)(2,1)S(1)}, f32[4096,128]{1,0:T(8,128)S(1)}, f32[4096,512]{1,0:T(8,128)S(1)}) custom-call(s32[1]{0:T(128)} %bitcast.5.first_row, s32[8,128]{1,0:T(8,128)S(1)} %copy-done.1, bf16[128,512]{1,0:T(8,128)(2,1)S(1)} %get-tuple-element.32.refs_0_, bf16[128,512]{1,0:T(8,128)(2,1)S(1)} %get-tuple-element.31.refs_1_, ...), custom_call_target="tpu_custom_call" | custom-call | flops 1 | bytes 1 | tf_op jit(solution)/shard_map/prepare/pallas_call | solution.py:396
  48.9 1.8 %collective-permute-done.10.refs_1_ = bf16[128,512]{1,0:T(8,128)(2,1)S(1)} collective-permute-done((bf16[128,512]{1,0:T(8,128)(2,1)S(1)}, bf16[128,512]{1,0:T(8,128)(2,1)S(1)}, u32[]{:S(2)}, u32[]{:S(2)}) %collective-permute-start.10) | collective-permute-done | bytes 131104 | tf_op jit(solution)/shard_map/ppermute | solution.py:499
  50.7 1.4 %collective-permute-done.8.refs_0_ = bf16[128,512]{1,0:T(8,128)(2,1)S(1)} collective-permute-done((bf16[128,512]{1,0:T(8,128)(2,1)S(1)}, bf16[128,512]{1,0:T(8,128)(2,1)S(1)}, u32[]{:S(2)}, u32[]{:S(2)}) %collective-permute-start.8) | collective-permute-done | bytes 131104 | tf_op jit(solution)/shard_map/ppermute | solution.py:499
  52.1 0.6 %collective-permute-start.9 = (bf16[128,512]{1,0:T(8,128)(2,1)S(1)}, bf16[128,512]{1,0:T(8,128)(2,1)S(1)}, u32[]{:S(2)}, u32[]{:S(2)}) collective-permute-start(bf16[128,512]{1,0:T(8,128)(2,1)S(1)} %collective-permute-done.8.refs_0_), channel_id=1, source_target_pairs={{0,4},{4,0},{8,12},{12,8},{1,5},{5,1},{9,13},{13,9},{2,6},{6,2},{1... | collective-permute-start | bytes 393224 | tf_op jit(solution)/shard_map/ppermute | solution.py:499
  52.8 2.4 %add_back.1.refs_4_ = f32[4096,512]{1,0:T(8,128)S(1)} custom-call(bf16[128,512]{1,0:T(8,128)(2,1)S(1)} %collective-permute-done.8.refs_0_, bf16[128,512]{1,0:T(8,128)(2,1)S(1)} %collective-permute-done.10.refs_1_, bf16[128,512]{1,0:T(8,128)(2,1)S(1)} %collective-permute-done.12.refs_2_, bf16[128,512]{1,0:T(8,128)(2,1)S(1)} %collective-permute-done.13.refs_3_, ...), custom_call_target="tpu_custom_call" | custom-call | flops 99999997952 | bytes 100000000 | tf_op jit(solution)/shard_map/add_back/pallas_call | solution.py:445
  55.2 1.4 %collective-permute-done.11.refs_1_ = bf16[128,512]{1,0:T(8,128)(2,1)S(1)} collective-permute-done((bf16[128,512]{1,0:T(8,128)(2,1)S(1)}, bf16[128,512]{1,0:T(8,128)(2,1)S(1)}, u32[]{:S(2)}, u32[]{:S(2)}) %collective-permute-start.11) | collective-permute-done | bytes 131104 | tf_op jit(solution)/shard_map/ppermute | solution.py:499
  56.6 1.4 %collective-permute-done.9.refs_0_ = bf16[128,512]{1,0:T(8,128)(2,1)S(1)} collective-permute-done((bf16[128,512]{1,0:T(8,128)(2,1)S(1)}, bf16[128,512]{1,0:T(8,128)(2,1)S(1)}, u32[]{:S(2)}, u32[]{:S(2)}) %collective-permute-start.9) | collective-permute-done | bytes 131104 | tf_op jit(solution)/shard_map/ppermute | solution.py:499
  58.0 3.7 %back_project.1 = f32[4096,512]{1,0:T(8,128)} custom-call(bf16[128,512]{1,0:T(8,128)(2,1)S(1)} %collective-permute-done.9.refs_0_, bf16[128,512]{1,0:T(8,128)(2,1)S(1)} %collective-permute-done.11.refs_1_, bf16[4096,1024]{1,0:T(8,128)(2,1)S(1)} %get-tuple-element.28.refs_4_.refs_2_, f32[4096,128]{1,0:T(8,128)S(1)} %get-tuple-element.29.refs_5_.refs_3_, ...), custom_call_target="tpu_custom_call" | custom-call | flops 1 | bytes 1 | tf_op jit(solution)/shard_map/back_project/pallas_call | solution.py:478
  (35 shorter events, 0.9 us)
Async XLA Ops:
  0.0 11.9 %collective-permute-start = (s32[2,128]{1,0:T(2,128)}, s32[2,128]{1,0:T(2,128)S(1)}, u32[]{:S(2)}, u32[]{:S(2)}) collective-permute-start(s32[2,128]{1,0:T(2,128)} %bitcast.20), channel_id=1, source_target_pairs={{0,8},{4,12},{8,0},{12,4},{1,9},{5,13},{9,1},{13,5},{2,10},{6,14},... | collective-permute-start | bytes 3080 | tf_op jit(solution)/shard_map/ppermute | solution.py:499
  4.0 7.9 %collective-permute-start.1 = (s32[2,128]{1,0:T(2,128)}, s32[2,128]{1,0:T(2,128)S(1)}, u32[]{:S(2)}, u32[]{:S(2)}) collective-permute-start(s32[2,128]{1,0:T(2,128)} %bitcast.21), channel_id=1, source_target_pairs={{0,4},{4,0},{8,12},{12,8},{1,5},{5,1},{9,13},{13,9},{2,6},{6,2},{1... | collective-permute-start | bytes 3080 | tf_op jit(solution)/shard_map/ppermute | solution.py:499
  5.6 6.4 %collective-permute-start.2 = (s32[2,128]{1,0:T(2,128)}, s32[2,128]{1,0:T(2,128)S(1)}, u32[]{:S(2)}, u32[]{:S(2)}) collective-permute-start(s32[2,128]{1,0:T(2,128)} %bitcast.22), channel_id=1, source_target_pairs={{0,12},{4,8},{8,4},{12,0},{1,13},{5,9},{9,5},{13,1},{2,14},{6,10},... | collective-permute-start | bytes 3080 | tf_op jit(solution)/shard_map/ppermute | solution.py:499
  5.6 6.4 %copy-start.2 = (s32[256]{0:T(256)S(1)}, s32[256]{0:T(256)}, u32[]{:S(2)}) copy-start(s32[256]{0:T(256)} %param.8) | copy-start | bytes 3076
  5.6 9.9 %copy-start.3 = (s32[256]{0:T(256)S(1)}, s32[256]{0:T(256)}, u32[]{:S(2)}) copy-start(s32[256]{0:T(256)} %param.7) | copy-start | bytes 3076
  5.6 9.9 %copy-start.4 = (s32[48]{0:T(128)S(1)}, s32[48]{0:T(128)}, u32[]{:S(2)}) copy-start(s32[48]{0:T(128)} %tile_bin.1) | copy-start | bytes 580
  12.0 1.4 %copy-start = (s32[8,128]{1,0:T(8,128)}, s32[8,128]{1,0:T(8,128)S(1)}, u32[]{:S(2)}) copy-start(s32[8,128]{1,0:T(8,128)S(1)} %pad_add_fusion.rays) | copy-start | bytes 12292
  13.4 9.3 %collective-permute-start.3 = (bf16[256,512]{1,0:T(8,128)(2,1)S(1)}, bf16[256,512]{1,0:T(8,128)(2,1)S(1)}, u32[]{:S(2)}, u32[]{:S(2)}) collective-permute-start(bf16[256,512]{1,0:T(8,128)(2,1)S(1)} %get-tuple-element.21), channel_id=1, source_target_pairs={{0,4},{4,0},{8,12},{12,8},{1,5},{5,1},{9,13},{13,9},{2,6},{6,2},{1... | collective-permute-start | bytes 786440 | tf_op jit(solution)/shard_map/ppermute | solution.py:499
  14.4 13.6 %collective-permute-start.5 = (bf16[256,512]{1,0:T(8,128)(2,1)S(1)}, bf16[256,512]{1,0:T(8,128)(2,1)S(1)}, u32[]{:S(2)}, u32[]{:S(2)}) collective-permute-start(bf16[256,512]{1,0:T(8,128)(2,1)S(1)} %get-tuple-element.22), channel_id=1, source_target_pairs={{0,4},{4,0},{8,12},{12,8},{1,5},{5,1},{9,13},{13,9},{2,6},{6,2},{1... | collective-permute-start | bytes 786440 | tf_op jit(solution)/shard_map/ppermute | solution.py:499
  22.1 4.2 %collective-permute-start.6 = (bf16[2,256,512]{2,1,0:T(8,128)(2,1)S(1)}, bf16[2,256,512]{2,1,0:T(8,128)(2,1)S(1)}, u32[]{:S(2)}, u32[]{:S(2)}) collective-permute-start(bf16[2,256,512]{2,1,0:T(8,128)(2,1)S(1)} %get-tuple-element.25), channel_id=1, source_target_pairs={{0,1},{1,0},{2,3},{3,2},{4,5},{5,4},{6,7},{7,6},{8,9},{9,8},{10,11... | collective-permute-start | bytes 1572872 | tf_op jit(solution)/shard_map/ppermute | solution.py:499
  22.7 14.8 %collective-permute-start.4 = (bf16[256,512]{1,0:T(8,128)(2,1)S(1)}, bf16[256,512]{1,0:T(8,128)(2,1)S(1)}, u32[]{:S(2)}, u32[]{:S(2)}) collective-permute-start(bf16[256,512]{1,0:T(8,128)(2,1)S(1)} %merge.1), channel_id=1, source_target_pairs={{0,8},{4,12},{8,0},{12,4},{1,9},{5,13},{9,1},{13,5},{2,10},{6,14},... | collective-permute-start | bytes 786440 | tf_op jit(solution)/shard_map/ppermute | solution.py:499
  26.3 16.8 %slice-start = ((s8[8388608]{0:T(1024)(128)(4,1)}), s8[4194304]{0:T(1024)(128)(4,1)S(1)}, s32[]{:S(2)}) async-start(s8[8388608]{0:T(1024)(128)(4,1)} %bitcast.18), calls=%async_computation | async-start | bytes 8388608
  26.4 16.7 %slice-start.1 = ((s8[8388608]{0:T(1024)(128)(4,1)}), s8[4194304]{0:T(1024)(128)(4,1)S(1)}, s32[]{:S(2)}) async-start(s8[8388608]{0:T(1024)(128)(4,1)} %bitcast.18), calls=%async_computation.1 | async-start | bytes 8388608
  26.4 16.7 %copy-start.1 = (s32[8,128]{1,0:T(8,128)S(1)}, s32[8,128]{1,0:T(8,128)}, u32[]{:S(2)}) copy-start(s32[8,128]{1,0:T(8,128)} %copy-done) | copy-start | bytes 12292
  26.4 11.5 %collective-permute-start.7 = (bf16[256,512]{1,0:T(8,128)(2,1)S(1)}, bf16[256,512]{1,0:T(8,128)(2,1)S(1)}, u32[]{:S(2)}, u32[]{:S(2)}) collective-permute-start(bf16[256,512]{1,0:T(8,128)(2,1)S(1)} %fusion), channel_id=1, source_target_pairs={{0,2},{1,3},{2,0},{3,1},{4,6},{5,7},{6,4},{7,5},{8,10},{9,11},{10,... | collective-permute-start | bytes 786440 | tf_op jit(solution)/shard_map/ppermute | solution.py:495
  38.1 12.6 %collective-permute-start.10 = (bf16[128,512]{1,0:T(8,128)(2,1)S(1)}, bf16[128,512]{1,0:T(8,128)(2,1)S(1)}, u32[]{:S(2)}, u32[]{:S(2)}) collective-permute-start(bf16[128,512]{1,0:T(8,128)(2,1)S(1)} %get-tuple-element.31.refs_1_), channel_id=1, source_target_pairs={{0,8},{4,12},{8,0},{12,4},{1,9},{5,13},{9,1},{13,5},{2,10},{6,14},... | collective-permute-start | bytes 393224 | tf_op jit(solution)/shard_map/ppermute | solution.py:499
  38.2 14.0 %collective-permute-start.8 = (bf16[128,512]{1,0:T(8,128)(2,1)S(1)}, bf16[128,512]{1,0:T(8,128)(2,1)S(1)}, u32[]{:S(2)}, u32[]{:S(2)}) collective-permute-start(bf16[128,512]{1,0:T(8,128)(2,1)S(1)} %get-tuple-element.32.refs_0_), channel_id=1, source_target_pairs={{0,8},{4,12},{8,0},{12,4},{1,9},{5,13},{9,1},{13,5},{2,10},{6,14},... | collective-permute-start | bytes 393224 | tf_op jit(solution)/shard_map/ppermute | solution.py:499
  41.1 11.7 %collective-permute-start.12 = (bf16[128,512]{1,0:T(8,128)(2,1)S(1)}, bf16[128,512]{1,0:T(8,128)(2,1)S(1)}, u32[]{:S(2)}, u32[]{:S(2)}) collective-permute-start(bf16[128,512]{1,0:T(8,128)(2,1)S(1)} %get-tuple-element.32.refs_0_), channel_id=1, source_target_pairs={{0,4},{4,0},{8,12},{12,8},{1,5},{5,1},{9,13},{13,9},{2,6},{6,2},{1... | collective-permute-start | bytes 393224 | tf_op jit(solution)/shard_map/ppermute | solution.py:499
  42.1 10.7 %collective-permute-start.13 = (bf16[128,512]{1,0:T(8,128)(2,1)S(1)}, bf16[128,512]{1,0:T(8,128)(2,1)S(1)}, u32[]{:S(2)}, u32[]{:S(2)}) collective-permute-start(bf16[128,512]{1,0:T(8,128)(2,1)S(1)} %get-tuple-element.31.refs_1_), channel_id=1, source_target_pairs={{0,4},{4,0},{8,12},{12,8},{1,5},{5,1},{9,13},{13,9},{2,6},{6,2},{1... | collective-permute-start | bytes 393224 | tf_op jit(solution)/shard_map/ppermute | solution.py:499
  50.7 5.8 %collective-permute-start.11 = (bf16[128,512]{1,0:T(8,128)(2,1)S(1)}, bf16[128,512]{1,0:T(8,128)(2,1)S(1)}, u32[]{:S(2)}, u32[]{:S(2)}) collective-permute-start(bf16[128,512]{1,0:T(8,128)(2,1)S(1)} %collective-permute-done.10.refs_1_), channel_id=1, source_target_pairs={{0,4},{4,0},{8,12},{12,8},{1,5},{5,1},{9,13},{13,9},{2,6},{6,2},{1... | collective-permute-start | bytes 393224 | tf_op jit(solution)/shard_map/ppermute | solution.py:499
  52.1 5.8 %collective-permute-start.9 = (bf16[128,512]{1,0:T(8,128)(2,1)S(1)}, bf16[128,512]{1,0:T(8,128)(2,1)S(1)}, u32[]{:S(2)}, u32[]{:S(2)}) collective-permute-start(bf16[128,512]{1,0:T(8,128)(2,1)S(1)} %collective-permute-done.8.refs_0_), channel_id=1, source_target_pairs={{0,4},{4,0},{8,12},{12,8},{1,5},{5,1},{9,13},{13,9},{2,6},{6,2},{1... | collective-permute-start | bytes 393224 | tf_op jit(solution)/shard_map/ppermute | solution.py:499

commit v11 on v10

--- a/solution.py
+++ b/solution.py
@@ -499,6 +499,37 @@
     return lax.ppermute(x, axis, [(i, i ^ mask) for i in range(n)])
 
 
+def onward(i):
+    return i - i % 4 + (1, 3, 0, 2)[i % 4]
+
+
+def backward(i):
+    return i - i % 4 + (2, 0, 3, 1)[i % 4]
+
+
+def pick_kernel(start, flag, first, second, out):
+    @pl.when(flag[0] == 1)
+    def _():
+        out[...] = first[start : start + out.shape[0], :]
+
+    @pl.when(flag[0] != 1)
+    def _():
+        out[...] = second[...]
+
+
+def pick(flag, first, second, start):
+    vmem = pl.BlockSpec(memory_space=pltpu.VMEM)
+    return pl.pallas_call(
+        functools.partial(pick_kernel, start),
+        in_specs=[pl.BlockSpec(memory_space=pltpu.SMEM), vmem, vmem],
+        out_specs=vmem,
+        out_shape=jax.ShapeDtypeStruct(second.shape, second.dtype),
+        compiler_params=pltpu.CompilerParams(vmem_limit_bytes=8 * MIB),
+        cost_estimate=SMALL,
+        name="pick",
+    )(flag, first, second)
+
+
 def body(frames, counts, point_ray, channel_pair_weights, tile_bin, image):
     n_scan = lax.axis_size("scan")
     n_chan = lax.axis_size("chan")
@@ -514,8 +545,8 @@
     late = [r for r in range(3, n_scan, 2)]
     order = [0] + middle + late
     own_rays = point_ray.reshape(points // LANES, LANES)
-    rays = [own_rays] + [swap(own_rays, "scan", r, n_scan) for r in order[1:]]
-    all_rays = jnp.concatenate(rays, axis=0)
+    rays = {r: own_rays if r == 0 else swap(own_rays, "scan", r, n_scan) for r in order}
+    all_rays = jnp.concatenate([rays[r] for r in order], axis=0)
 
     projected = project(image, first_row, angles)
     own_share, *shares = reorder(all_rays, projected, n_scan)
@@ -545,17 +576,33 @@
     scaled, recip = join(row_total, own_share, arrived)
     residual = (-scaled + pattern * (float(NIMG) * recip[:, :1])).astype(BF16)
     half = points // 2
-    gathered = {0: [residual[:half], residual[half:]]}
+    masks = range(0, n_scan, 4)
+    gathered = {0: residual}
     bit = n_scan // 2
-    while bit:
-        for r, pieces in list(gathered.items()):
-            gathered[r ^ bit] = [swap(x, "scan", bit, n_scan) for x in pieces]
+    while bit >= 4:
+        gathered |= {mask ^ bit: swap(x, "scan", bit, n_scan) for mask, x in gathered.items()}
         bit //= 2
-    tile, col_recip, partial = prepare(all_rays, gathered[0], image, first_row, angles)
-    pieces = [x for r in middle for x in gathered[r]]
+    scan_low = lax.axis_index("scan") % 4
+    outer = jnp.logical_or(scan_low == 0, scan_low == 3)
+    flag = outer.astype(jnp.int32).reshape(1)
+    columns = [rays[mask] for mask in masks]
+    pieces = [gathered[mask] for mask in masks if mask]
+    last = []
+    for mask in masks:
+        block = gathered[mask]
+        first = lax.ppermute(block, "scan", [(i, onward(i)) for i in range(n_scan)])
+        second = [
+            lax.ppermute(x, "scan", [(i, backward(i)) for i in range(n_scan)])
+            for x in (block[:half], block[half:])
+        ]
+        pieces += [first] + second
+        last += [swap(pick(flag, first, x, k * half), "scan", 1, n_scan) for k, x in enumerate(second)]
+        two, one = rays[mask ^ 2], rays[mask ^ 1]
+        columns += [jnp.where(outer, two, one), jnp.where(outer, one, two)]
+    columns = jnp.concatenate(columns + [rays[mask ^ 3] for mask in masks], axis=0)
+    tile, col_recip, partial = prepare(columns, [residual], image, first_row, angles)
     partial = add_back(pieces, points, tile, col_recip, partial)
-    pieces = [x for r in late for x in gathered[r]]
-    return back_project(pieces, points * (1 + len(middle)), tile, col_recip, partial)
+    return back_project(last, points * (n_scan - len(masks)), tile, col_recip, partial)
 
 
 def solution(mesh):

time: 62.1 us -> 63.4 us (1.021)
  local copies, waits for them, and re-layouts: 0.06 us -> 3.41 us
  waiting for transfers between devices: 16.1 us -> 12.8 us
  starting transfers between devices: 17.4 us -> 18.7 us
    ppermute x0 -> x3, starting transfers between devices: none -> 4.15 us  [the longest x2 3.45 us: body(): lax.ppermute(x, 'scan', [(i, backward(i)) for i in range(n_scan)])]
    unnamed x14 -> x8, local copies, waits for them, and re-layouts: 0.04 us -> 3.39 us
    ppermute x13 -> x9, waiting for transfers between devices: 16.1 us -> 12.8 us  [swap(): return lax.ppermute(x, axis, [(i, i ^ mask) for i in range(n)])]
    ppermute x13 -> x9, starting transfers between devices: 15.8 us -> 13 us  [swap(): return lax.ppermute(x, axis, [(i, i ^ mask) for i in range(n)])]
  transfers between devices with their start and end apart: 14 -> 13, of which waited for: 6 -> 4; matrix products, arithmetic and copies ran while one was open for 0% -> 0% of each run, Pallas kernels for 36% -> 35%
where the time goes in v11:
time: 63.4 us; the launch traced here: 63.2 us
  Pallas kernels  27.4 us (43%)
  starting transfers between devices  18.7 us (29%)
  waiting for transfers between devices  12.8 us (20%)
  local copies, waits for them, and re-layouts  3.41 us (5%)
    ppermute x9, starting transfers between devices, swap(): return lax.ppermute(x, axis, [(i, i ^ mask) for i in range(n)])  13 us
    ppermute x9, waiting for transfers between devices, swap(): return lax.ppermute(x, axis, [(i, i ^ mask) for i in range(n)])  12.8 us
    pallas_call x1, Pallas kernels, integrate(): pl.pallas_call(functools.partial(integrate_kernel, nx, chans // tile_bins...  6.54 us
    pallas_call x1, Pallas kernels, project(): pl.pallas_call(functools.partial(project_kernel, angles), in_specs=[pl.Bl...  6.31 us
    pallas_call x1, Pallas kernels, prepare(): pl.pallas_call(functools.partial(prepare_kernel, angles, len(residuals)),...  5.8 us
    pallas_call x1, Pallas kernels, back_project(): pl.pallas_call(functools.partial(back_kernel, first, len(pieces)), in_spe...  3.67 us
    ppermute x2, starting transfers between devices, body(): lax.ppermute(x, 'scan', [(i, backward(i)) for i in range(n_scan)])  3.45 us
    unnamed x8, local copies, waits for them, and re-layouts  3.39 us
  transfers between devices with their start and end apart: 13, of which 4 were waited for; matrix products, arithmetic and copies ran while one was open for 0% of the time, Pallas kernels for 35%

profile of v11, /device:TPU:0, one launch (start us, length us, event | category | flops | bytes accessed | tf_op | source)
XLA Modules:
  0.0 63.2 jit_solution(2416113022100847962)
XLA Ops:
  0.0 4.0 %collective-permute-start = (s32[2,128]{1,0:T(2,128)}, s32[2,128]{1,0:T(2,128)S(1)}, u32[]{:S(2)}, u32[]{:S(2)}) collective-permute-start(s32[2,128]{1,0:T(2,128)} %bitcast.19), channel_id=1, source_target_pairs={{0,8},{4,12},{8,0},{12,4},{1,9},{5,13},{9,1},{13,5},{2,10},{6,14},... | collective-permute-start | bytes 3080 | tf_op jit(solution)/shard_map/ppermute | solution.py:499
  4.0 1.6 %collective-permute-start.1 = (s32[2,128]{1,0:T(2,128)}, s32[2,128]{1,0:T(2,128)S(1)}, u32[]{:S(2)}, u32[]{:S(2)}) collective-permute-start(s32[2,128]{1,0:T(2,128)} %bitcast.20), channel_id=1, source_target_pairs={{0,4},{4,0},{8,12},{12,8},{1,5},{5,1},{9,13},{13,9},{2,6},{6,2},{1... | collective-permute-start | bytes 3080 | tf_op jit(solution)/shard_map/ppermute | solution.py:499
  5.6 6.3 %project.1.rows = bf16[1024,512]{1,0:T(8,128)(2,1)S(1)} custom-call(s32[1]{0:T(128)} %bitcast.6.first_row, f32[4096,512]{1,0:T(8,128)} %refs_1_.1), custom_call_target="tpu_custom_call" | custom-call | flops 8589934592 | bytes 8388608 | tf_op jit(solution)/shard_map/project/pallas_call | solution.py:222
  12.0 1.3 %reorder.1 = (bf16[256,512]{1,0:T(8,128)(2,1)S(1)}, bf16[256,512]{1,0:T(8,128)(2,1)S(1)}, bf16[256,512]{1,0:T(8,128)(2,1)S(1)}, bf16[256,512]{1,0:T(8,128)(2,1)S(1)}) custom-call(s32[8,128]{1,0:T(8,128)S(1)} %get-tuple-element.34.rays, bf16[1024,512]{1,0:T(8,128)(2,1)S(1)} %project.1.rows), custom_call_target="tpu_custom_call" | custom-call | flops 1 | bytes 1 | tf_op jit(solution)/shard_map/reorder/pallas_call | solution.py:264
  13.4 1.0 %collective-permute-start.3 = (bf16[256,512]{1,0:T(8,128)(2,1)S(1)}, bf16[256,512]{1,0:T(8,128)(2,1)S(1)}, u32[]{:S(2)}, u32[]{:S(2)}) collective-permute-start(bf16[256,512]{1,0:T(8,128)(2,1)S(1)} %get-tuple-element.21), channel_id=1, source_target_pairs={{0,4},{4,0},{8,12},{12,8},{1,5},{5,1},{9,13},{13,9},{2,6},{6,2},{1... | collective-permute-start | bytes 786440 | tf_op jit(solution)/shard_map/ppermute | solution.py:499
  14.4 1.1 %collective-permute-start.5 = (bf16[256,512]{1,0:T(8,128)(2,1)S(1)}, bf16[256,512]{1,0:T(8,128)(2,1)S(1)}, u32[]{:S(2)}, u32[]{:S(2)}) collective-permute-start(bf16[256,512]{1,0:T(8,128)(2,1)S(1)} %get-tuple-element.22), channel_id=1, source_target_pairs={{0,4},{4,0},{8,12},{12,8},{1,5},{5,1},{9,13},{13,9},{2,6},{6,2},{1... | collective-permute-start | bytes 786440 | tf_op jit(solution)/shard_map/ppermute | solution.py:499
  15.6 6.5 %integrate.1 = (bf16[2,256,512]{2,1,0:T(8,128)(2,1)S(1)}, f32[16,256,128]{2,1,0:T(8,128)S(1)}) custom-call(s32[48]{0:T(128)S(1)} %copy-done.3, s32[4]{0:T(128)S(1)} %pad_add_fusion.4.place, bf16[256,512]{1,0:T(8,128)(2,1)S(1)} %get-tuple-element.18.after.own, s32[1,256]{1,0:T(1,128)S(1)} %bitcast.24, bf16[384,6144]{1,0:T(8,128)(2,1)} %frames.1, ...), custom_call_target="tpu_custom_call" | custom-call | flops 1 | bytes 1 | tf_op jit(solution)/shard_map/integrate/pallas_call | solution.py:108
  22.2 0.5 collective-permute-done.3.refs_1_
  22.8 2.4 %collective-permute-start.4 = (bf16[256,512]{1,0:T(8,128)(2,1)S(1)}, bf16[256,512]{1,0:T(8,128)(2,1)S(1)}, u32[]{:S(2)}, u32[]{:S(2)}) collective-permute-start(bf16[256,512]{1,0:T(8,128)(2,1)S(1)} %merge.1), channel_id=1, source_target_pairs={{0,8},{4,12},{8,0},{12,4},{1,9},{5,13},{9,1},{13,5},{2,10},{6,14},... | collective-permute-start | bytes 786440 | tf_op jit(solution)/shard_map/ppermute | solution.py:499
  25.2 0.7 %select.13 = (f32[256,512]{1,0:T(8,128)S(1)}, f32[256,512]{1,0:T(8,128)S(1)}) custom-call(s32[4]{0:T(128)S(1)} %pad_add_fusion.4.place, f32[16,256,128]{2,1,0:T(8,128)S(1)} %get-tuple-element.19.after.acc), custom_call_target="tpu_custom_call" | custom-call | flops 99999997952 | bytes 100000000 | tf_op jit(solution)/shard_map/select/pallas_call | solution.py:148
  25.9 0.4 row_totals.1.row_total
  26.4 1.5 %collective-permute-start.7 = (bf16[256,512]{1,0:T(8,128)(2,1)S(1)}, bf16[256,512]{1,0:T(8,128)(2,1)S(1)}, u32[]{:S(2)}, u32[]{:S(2)}) collective-permute-start(bf16[256,512]{1,0:T(8,128)(2,1)S(1)} %fusion), channel_id=1, source_target_pairs={{0,2},{1,3},{2,0},{3,1},{4,6},{5,7},{6,4},{7,5},{8,10},{9,11},{10,... | collective-permute-start | bytes 786440 | tf_op jit(solution)/shard_map/ppermute | solution.py:495
  28.0 9.6 %collective-permute-done.4.refs_0_ = bf16[256,512]{1,0:T(8,128)(2,1)S(1)} collective-permute-done((bf16[256,512]{1,0:T(8,128)(2,1)S(1)}, bf16[256,512]{1,0:T(8,128)(2,1)S(1)}, u32[]{:S(2)}, u32[]{:S(2)}) %collective-permute-start.4) | collective-permute-done | bytes 262176 | tf_op jit(solution)/shard_map/ppermute | solution.py:499
  38.0 0.7 %collective-permute-start.8 = (bf16[256,512]{1,0:T(8,128)(2,1)S(1)}, bf16[256,512]{1,0:T(8,128)(2,1)S(1)}, u32[]{:S(2)}, u32[]{:S(2)}) collective-permute-start(bf16[256,512]{1,0:T(8,128)(2,1)S(1)} %fusion.4.refs_0_), channel_id=1, source_target_pairs={{0,4},{4,12},{8,0},{12,8},{1,5},{5,13},{9,1},{13,9},{2,6},{6,14},{... | collective-permute-start | bytes 786440 | tf_op jit(solution)/shard_map/ppermute | solution.py:593
  38.8 2.5 %collective-permute-start.11 = (bf16[128,512]{1,0:T(8,128)(2,1)S(1)}, bf16[128,512]{1,0:T(8,128)(2,1)S(1)}, u32[]{:S(2)}, u32[]{:S(2)}) collective-permute-start(bf16[128,512]{1,0:T(8,128)(2,1)S(1)} %get-tuple-element.31), channel_id=1, source_target_pairs={{0,8},{4,0},{8,12},{12,4},{1,9},{5,1},{9,13},{13,5},{2,10},{6,2},{... | collective-permute-start | bytes 393224 | tf_op jit(solution)/shard_map/ppermute | solution.py:595
  41.3 0.9 %collective-permute-start.9 = (bf16[128,512]{1,0:T(8,128)(2,1)S(1)}, bf16[128,512]{1,0:T(8,128)(2,1)S(1)}, u32[]{:S(2)}, u32[]{:S(2)}) collective-permute-start(bf16[128,512]{1,0:T(8,128)(2,1)S(1)} %get-tuple-element.32), channel_id=1, source_target_pairs={{0,8},{4,0},{8,12},{12,4},{1,9},{5,1},{9,13},{13,5},{2,10},{6,2},{... | collective-permute-start | bytes 393224 | tf_op jit(solution)/shard_map/ppermute | solution.py:595
  42.2 3.4 %copy-done = f32[4096,512]{1,0:T(8,128)S(1)} copy-done((f32[4096,512]{1,0:T(8,128)S(1)}, f32[4096,512]{1,0:T(8,128)}, u32[]{:S(2)}) %copy-start) | copy-done | bytes 8388632
  45.6 5.8 %prepare.1 = (bf16[4096,1024]{1,0:T(8,128)(2,1)S(1)}, f32[4096,128]{1,0:T(8,128)S(1)}, f32[4096,512]{1,0:T(8,128)S(1)}) custom-call(s32[1]{0:T(128)} %bitcast.6.first_row, s32[8,128]{1,0:T(8,128)S(1)} %get-tuple-element.33.rays, bf16[256,512]{1,0:T(8,128)(2,1)S(1)} %fusion.4.refs_0_, f32[4096,512]{1,0:T(8,128)S(1)} %copy-done), custom_call_target="tpu_custom_call" | custom-call | flops 1 | bytes 1 | tf_op jit(solution)/shard_map/prepare/pallas_call | solution.py:396
  51.5 2.2 %collective-permute-start.12 = (bf16[128,512]{1,0:T(8,128)(2,1)S(1)}, bf16[128,512]{1,0:T(8,128)(2,1)S(1)}, u32[]{:S(2)}, u32[]{:S(2)}) collective-permute-start(bf16[128,512]{1,0:T(8,128)(2,1)S(1)} %pick.3), channel_id=1, source_target_pairs={{0,4},{4,0},{8,12},{12,8},{1,5},{5,1},{9,13},{13,9},{2,6},{6,2},{1... | collective-permute-start | bytes 393224 | tf_op jit(solution)/shard_map/ppermute | solution.py:499
  53.6 0.7 %collective-permute-start.10 = (bf16[128,512]{1,0:T(8,128)(2,1)S(1)}, bf16[128,512]{1,0:T(8,128)(2,1)S(1)}, u32[]{:S(2)}, u32[]{:S(2)}) collective-permute-start(bf16[128,512]{1,0:T(8,128)(2,1)S(1)} %pick.2), channel_id=1, source_target_pairs={{0,4},{4,0},{8,12},{12,8},{1,5},{5,1},{9,13},{13,9},{2,6},{6,2},{1... | collective-permute-start | bytes 393224 | tf_op jit(solution)/shard_map/ppermute | solution.py:499
  54.3 2.4 %add_back.1.refs_4_ = f32[4096,512]{1,0:T(8,128)S(1)} custom-call(bf16[256,512]{1,0:T(8,128)(2,1)S(1)} %collective-permute-done.8.first.refs_0_, bf16[128,512]{1,0:T(8,128)(2,1)S(1)} %collective-permute-done.9.second.refs_1_, bf16[128,512]{1,0:T(8,128)(2,1)S(1)} %collective-permute-done.11.second.refs_2_, ...), custom_call_target="tpu_custom_call" | custom-call | flops 99999997952 | bytes 100000000 | tf_op jit(solution)/shard_map/add_back/pallas_call | solution.py:445
  56.7 1.2 %collective-permute-done.12.refs_1_ = bf16[128,512]{1,0:T(8,128)(2,1)S(1)} collective-permute-done((bf16[128,512]{1,0:T(8,128)(2,1)S(1)}, bf16[128,512]{1,0:T(8,128)(2,1)S(1)}, u32[]{:S(2)}, u32[]{:S(2)}) %collective-permute-start.12) | collective-permute-done | bytes 131104 | tf_op jit(solution)/shard_map/ppermute | solution.py:499
  57.9 1.4 %collective-permute-done.10.refs_0_ = bf16[128,512]{1,0:T(8,128)(2,1)S(1)} collective-permute-done((bf16[128,512]{1,0:T(8,128)(2,1)S(1)}, bf16[128,512]{1,0:T(8,128)(2,1)S(1)}, u32[]{:S(2)}, u32[]{:S(2)}) %collective-permute-start.10) | collective-permute-done | bytes 131104 | tf_op jit(solution)/shard_map/ppermute | solution.py:499
  59.4 3.7 %back_project.1 = f32[4096,512]{1,0:T(8,128)} custom-call(bf16[128,512]{1,0:T(8,128)(2,1)S(1)} %collective-permute-done.10.refs_0_, bf16[128,512]{1,0:T(8,128)(2,1)S(1)} %collective-permute-done.12.refs_1_, bf16[4096,1024]{1,0:T(8,128)(2,1)S(1)} %get-tuple-element.28.refs_3_.refs_2_, f32[4096,128]{1,0:T(8,128)S(1)} %get-tuple-element.29.refs_4_.refs_3_, ...), custom_call_target="tpu_custom_call" | custom-call | flops 1 | bytes 1 | tf_op jit(solution)/shard_map/back_project/pallas_call | solution.py:478
  (29 shorter events, 0.9 us)
Async XLA Ops:
  0.0 12.0 %collective-permute-start = (s32[2,128]{1,0:T(2,128)}, s32[2,128]{1,0:T(2,128)S(1)}, u32[]{:S(2)}, u32[]{:S(2)}) collective-permute-start(s32[2,128]{1,0:T(2,128)} %bitcast.19), channel_id=1, source_target_pairs={{0,8},{4,12},{8,0},{12,4},{1,9},{5,13},{9,1},{13,5},{2,10},{6,14},... | collective-permute-start | bytes 3080 | tf_op jit(solution)/shard_map/ppermute | solution.py:499
  4.0 7.9 %collective-permute-start.1 = (s32[2,128]{1,0:T(2,128)}, s32[2,128]{1,0:T(2,128)S(1)}, u32[]{:S(2)}, u32[]{:S(2)}) collective-permute-start(s32[2,128]{1,0:T(2,128)} %bitcast.20), channel_id=1, source_target_pairs={{0,4},{4,0},{8,12},{12,8},{1,5},{5,1},{9,13},{13,9},{2,6},{6,2},{1... | collective-permute-start | bytes 3080 | tf_op jit(solution)/shard_map/ppermute | solution.py:499
  5.6 6.4 %collective-permute-start.2 = (s32[2,128]{1,0:T(2,128)}, s32[2,128]{1,0:T(2,128)S(1)}, u32[]{:S(2)}, u32[]{:S(2)}) collective-permute-start(s32[2,128]{1,0:T(2,128)} %bitcast.21), channel_id=1, source_target_pairs={{0,12},{4,8},{8,4},{12,0},{1,13},{5,9},{9,5},{13,1},{2,14},{6,10},... | collective-permute-start | bytes 3080 | tf_op jit(solution)/shard_map/ppermute | solution.py:499
  5.6 6.4 %copy-start.1 = (s32[256]{0:T(256)S(1)}, s32[256]{0:T(256)}, u32[]{:S(2)}) copy-start(s32[256]{0:T(256)} %param.8) | copy-start | bytes 3076
  5.6 9.9 %copy-start.2 = (s32[256]{0:T(256)S(1)}, s32[256]{0:T(256)}, u32[]{:S(2)}) copy-start(s32[256]{0:T(256)} %param.7) | copy-start | bytes 3076
  5.6 9.9 %copy-start.3 = (s32[48]{0:T(128)S(1)}, s32[48]{0:T(128)}, u32[]{:S(2)}) copy-start(s32[48]{0:T(128)} %tile_bin.1) | copy-start | bytes 580
  13.4 9.3 %collective-permute-start.3 = (bf16[256,512]{1,0:T(8,128)(2,1)S(1)}, bf16[256,512]{1,0:T(8,128)(2,1)S(1)}, u32[]{:S(2)}, u32[]{:S(2)}) collective-permute-start(bf16[256,512]{1,0:T(8,128)(2,1)S(1)} %get-tuple-element.21), channel_id=1, source_target_pairs={{0,4},{4,0},{8,12},{12,8},{1,5},{5,1},{9,13},{13,9},{2,6},{6,2},{1... | collective-permute-start | bytes 786440 | tf_op jit(solution)/shard_map/ppermute | solution.py:499
  14.4 13.5 %collective-permute-start.5 = (bf16[256,512]{1,0:T(8,128)(2,1)S(1)}, bf16[256,512]{1,0:T(8,128)(2,1)S(1)}, u32[]{:S(2)}, u32[]{:S(2)}) collective-permute-start(bf16[256,512]{1,0:T(8,128)(2,1)S(1)} %get-tuple-element.22), channel_id=1, source_target_pairs={{0,4},{4,0},{8,12},{12,8},{1,5},{5,1},{9,13},{13,9},{2,6},{6,2},{1... | collective-permute-start | bytes 786440 | tf_op jit(solution)/shard_map/ppermute | solution.py:499
  22.1 4.2 %collective-permute-start.6 = (bf16[2,256,512]{2,1,0:T(8,128)(2,1)S(1)}, bf16[2,256,512]{2,1,0:T(8,128)(2,1)S(1)}, u32[]{:S(2)}, u32[]{:S(2)}) collective-permute-start(bf16[2,256,512]{2,1,0:T(8,128)(2,1)S(1)} %get-tuple-element.25), channel_id=1, source_target_pairs={{0,1},{1,0},{2,3},{3,2},{4,5},{5,4},{6,7},{7,6},{8,9},{9,8},{10,11... | collective-permute-start | bytes 1572872 | tf_op jit(solution)/shard_map/ppermute | solution.py:499
  22.8 14.8 %collective-permute-start.4 = (bf16[256,512]{1,0:T(8,128)(2,1)S(1)}, bf16[256,512]{1,0:T(8,128)(2,1)S(1)}, u32[]{:S(2)}, u32[]{:S(2)}) collective-permute-start(bf16[256,512]{1,0:T(8,128)(2,1)S(1)} %merge.1), channel_id=1, source_target_pairs={{0,8},{4,12},{8,0},{12,4},{1,9},{5,13},{9,1},{13,5},{2,10},{6,14},... | collective-permute-start | bytes 786440 | tf_op jit(solution)/shard_map/ppermute | solution.py:499
  26.4 11.5 %collective-permute-start.7 = (bf16[256,512]{1,0:T(8,128)(2,1)S(1)}, bf16[256,512]{1,0:T(8,128)(2,1)S(1)}, u32[]{:S(2)}, u32[]{:S(2)}) collective-permute-start(bf16[256,512]{1,0:T(8,128)(2,1)S(1)} %fusion), channel_id=1, source_target_pairs={{0,2},{1,3},{2,0},{3,1},{4,6},{5,7},{6,4},{7,5},{8,10},{9,11},{10,... | collective-permute-start | bytes 786440 | tf_op jit(solution)/shard_map/ppermute | solution.py:495
  38.0 13.4 %collective-permute-start.8 = (bf16[256,512]{1,0:T(8,128)(2,1)S(1)}, bf16[256,512]{1,0:T(8,128)(2,1)S(1)}, u32[]{:S(2)}, u32[]{:S(2)}) collective-permute-start(bf16[256,512]{1,0:T(8,128)(2,1)S(1)} %fusion.4.refs_0_), channel_id=1, source_target_pairs={{0,4},{4,12},{8,0},{12,8},{1,5},{5,13},{9,1},{13,9},{2,6},{6,14},{... | collective-permute-start | bytes 786440 | tf_op jit(solution)/shard_map/ppermute | solution.py:593
  38.8 12.6 %collective-permute-start.11 = (bf16[128,512]{1,0:T(8,128)(2,1)S(1)}, bf16[128,512]{1,0:T(8,128)(2,1)S(1)}, u32[]{:S(2)}, u32[]{:S(2)}) collective-permute-start(bf16[128,512]{1,0:T(8,128)(2,1)S(1)} %get-tuple-element.31), channel_id=1, source_target_pairs={{0,8},{4,0},{8,12},{12,4},{1,9},{5,1},{9,13},{13,5},{2,10},{6,2},{... | collective-permute-start | bytes 393224 | tf_op jit(solution)/shard_map/ppermute | solution.py:595
  41.3 12.3 %collective-permute-start.9 = (bf16[128,512]{1,0:T(8,128)(2,1)S(1)}, bf16[128,512]{1,0:T(8,128)(2,1)S(1)}, u32[]{:S(2)}, u32[]{:S(2)}) collective-permute-start(bf16[128,512]{1,0:T(8,128)(2,1)S(1)} %get-tuple-element.32), channel_id=1, source_target_pairs={{0,8},{4,0},{8,12},{12,4},{1,9},{5,1},{9,13},{13,5},{2,10},{6,2},{... | collective-permute-start | bytes 393224 | tf_op jit(solution)/shard_map/ppermute | solution.py:595
  42.2 3.4 %copy-start = (f32[4096,512]{1,0:T(8,128)S(1)}, f32[4096,512]{1,0:T(8,128)}, u32[]{:S(2)}) copy-start(f32[4096,512]{1,0:T(8,128)} %refs_1_.1) | copy-start | bytes 25165828
  51.5 6.5 %collective-permute-start.12 = (bf16[128,512]{1,0:T(8,128)(2,1)S(1)}, bf16[128,512]{1,0:T(8,128)(2,1)S(1)}, u32[]{:S(2)}, u32[]{:S(2)}) collective-permute-start(bf16[128,512]{1,0:T(8,128)(2,1)S(1)} %pick.3), channel_id=1, source_target_pairs={{0,4},{4,0},{8,12},{12,8},{1,5},{5,1},{9,13},{13,9},{2,6},{6,2},{1... | collective-permute-start | bytes 393224 | tf_op jit(solution)/shard_map/ppermute | solution.py:499
  53.6 5.7 %collective-permute-start.10 = (bf16[128,512]{1,0:T(8,128)(2,1)S(1)}, bf16[128,512]{1,0:T(8,128)(2,1)S(1)}, u32[]{:S(2)}, u32[]{:S(2)}) collective-permute-start(bf16[128,512]{1,0:T(8,128)(2,1)S(1)} %pick.2), channel_id=1, source_target_pairs={{0,4},{4,0},{8,12},{12,8},{1,5},{5,1},{9,13},{13,9},{2,6},{6,2},{1... | collective-permute-start | bytes 393224 | tf_op jit(solution)/shard_map/ppermute | solution.py:499

commit v12 on v11

--- a/solution.py
+++ b/solution.py
@@ -412,7 +412,7 @@
         compiler_params=pltpu.CompilerParams(vmem_limit_bytes=16 * MIB),
         cost_estimate=SMALL,
         name="prepare",
-    )(first_row, rays, *residuals, image)
+    )(first_row, rays, *residuals, pltpu.with_memory_space_constraint(image, pltpu.HBM))
 
 
 def gather_rows(pieces, joined):

time: 63.4 us -> 63.5 us (level)
  local copies, waits for them, and re-layouts: 3.41 us -> 0.03 us
  Pallas kernels: 27.4 us -> 30.3 us
    unnamed x8 -> x6, local copies, waits for them, and re-layouts: 3.39 us -> 0.01 us
    pallas_call x1, Pallas kernels: 5.8 us -> 8.69 us  [prepare(): pl.pallas_call(functools.partial(prepare_kernel, angles, len(residuals)),...]
  transfers between devices with their start and end apart: 13 -> 13, of which waited for: 4 -> 4; matrix products, arithmetic and copies ran while one was open for 0% -> 0% of each run, Pallas kernels for 35% -> 40%
where the time goes in v12:
time: 63.5 us; the launch traced here: 63.2 us
  Pallas kernels  30.3 us (48%)
  starting transfers between devices  19.2 us (30%)
  waiting for transfers between devices  12.8 us (20%)
    ppermute x9, starting transfers between devices, swap(): return lax.ppermute(x, axis, [(i, i ^ mask) for i in range(n)])  13.5 us
    ppermute x9, waiting for transfers between devices, swap(): return lax.ppermute(x, axis, [(i, i ^ mask) for i in range(n)])  12.8 us
    pallas_call x1, Pallas kernels, prepare(): pl.pallas_call(functools.partial(prepare_kernel, angles, len(residuals)),...  8.69 us
    pallas_call x1, Pallas kernels, integrate(): pl.pallas_call(functools.partial(integrate_kernel, nx, chans // tile_bins...  6.54 us
    pallas_call x1, Pallas kernels, project(): pl.pallas_call(functools.partial(project_kernel, angles), in_specs=[pl.Bl...  6.31 us
    pallas_call x1, Pallas kernels, back_project(): pl.pallas_call(functools.partial(back_kernel, first, len(pieces)), in_spe...  3.67 us
    ppermute x2, starting transfers between devices, body(): lax.ppermute(x, 'scan', [(i, backward(i)) for i in range(n_scan)])  3.45 us
    pallas_call x1, Pallas kernels, add_back(): pl.pallas_call(functools.partial(add_kernel, first, len(pieces)), in_spec...  2.39 us
  transfers between devices with their start and end apart: 13, of which 4 were waited for; matrix products, arithmetic and copies ran while one was open for 0% of the time, Pallas kernels for 40%

profile of v12, /device:TPU:0, one launch (start us, length us, event | category | flops | bytes accessed | tf_op | source)
XLA Modules:
  0.0 63.2 jit_solution(4819180527986272669)
XLA Ops:
  0.0 4.0 %collective-permute-start = (s32[2,128]{1,0:T(2,128)}, s32[2,128]{1,0:T(2,128)S(1)}, u32[]{:S(2)}, u32[]{:S(2)}) collective-permute-start(s32[2,128]{1,0:T(2,128)} %bitcast.19), channel_id=1, source_target_pairs={{0,8},{4,12},{8,0},{12,4},{1,9},{5,13},{9,1},{13,5},{2,10},{6,14},... | collective-permute-start | bytes 3080 | tf_op jit(solution)/shard_map/ppermute | solution.py:499
  4.0 1.6 %collective-permute-start.1 = (s32[2,128]{1,0:T(2,128)}, s32[2,128]{1,0:T(2,128)S(1)}, u32[]{:S(2)}, u32[]{:S(2)}) collective-permute-start(s32[2,128]{1,0:T(2,128)} %bitcast.20), channel_id=1, source_target_pairs={{0,4},{4,0},{8,12},{12,8},{1,5},{5,1},{9,13},{13,9},{2,6},{6,2},{1... | collective-permute-start | bytes 3080 | tf_op jit(solution)/shard_map/ppermute | solution.py:499
  5.6 6.3 %project.1.rows = bf16[1024,512]{1,0:T(8,128)(2,1)S(1)} custom-call(s32[1]{0:T(128)} %bitcast.6.first_row, f32[4096,512]{1,0:T(8,128)} %refs_1_.1), custom_call_target="tpu_custom_call" | custom-call | flops 8589934592 | bytes 8388608 | tf_op jit(solution)/shard_map/project/pallas_call | solution.py:222
  12.0 1.3 %reorder.1 = (bf16[256,512]{1,0:T(8,128)(2,1)S(1)}, bf16[256,512]{1,0:T(8,128)(2,1)S(1)}, bf16[256,512]{1,0:T(8,128)(2,1)S(1)}, bf16[256,512]{1,0:T(8,128)(2,1)S(1)}) custom-call(s32[8,128]{1,0:T(8,128)S(1)} %get-tuple-element.34.rays, bf16[1024,512]{1,0:T(8,128)(2,1)S(1)} %project.1.rows), custom_call_target="tpu_custom_call" | custom-call | flops 1 | bytes 1 | tf_op jit(solution)/shard_map/reorder/pallas_call | solution.py:264
  13.4 1.0 %collective-permute-start.3 = (bf16[256,512]{1,0:T(8,128)(2,1)S(1)}, bf16[256,512]{1,0:T(8,128)(2,1)S(1)}, u32[]{:S(2)}, u32[]{:S(2)}) collective-permute-start(bf16[256,512]{1,0:T(8,128)(2,1)S(1)} %get-tuple-element.21), channel_id=1, source_target_pairs={{0,4},{4,0},{8,12},{12,8},{1,5},{5,1},{9,13},{13,9},{2,6},{6,2},{1... | collective-permute-start | bytes 786440 | tf_op jit(solution)/shard_map/ppermute | solution.py:499
  14.4 1.1 %collective-permute-start.5 = (bf16[256,512]{1,0:T(8,128)(2,1)S(1)}, bf16[256,512]{1,0:T(8,128)(2,1)S(1)}, u32[]{:S(2)}, u32[]{:S(2)}) collective-permute-start(bf16[256,512]{1,0:T(8,128)(2,1)S(1)} %get-tuple-element.22), channel_id=1, source_target_pairs={{0,4},{4,0},{8,12},{12,8},{1,5},{5,1},{9,13},{13,9},{2,6},{6,2},{1... | collective-permute-start | bytes 786440 | tf_op jit(solution)/shard_map/ppermute | solution.py:499
  15.6 6.5 %integrate.1 = (bf16[2,256,512]{2,1,0:T(8,128)(2,1)S(1)}, f32[16,256,128]{2,1,0:T(8,128)S(1)}) custom-call(s32[48]{0:T(128)S(1)} %copy-done.2, s32[4]{0:T(128)S(1)} %pad_add_fusion.4.place, bf16[256,512]{1,0:T(8,128)(2,1)S(1)} %get-tuple-element.18.after.own, s32[1,256]{1,0:T(1,128)S(1)} %bitcast.24, bf16[384,6144]{1,0:T(8,128)(2,1)} %frames.1, ...), custom_call_target="tpu_custom_call" | custom-call | flops 1 | bytes 1 | tf_op jit(solution)/shard_map/integrate/pallas_call | solution.py:108
  22.2 0.5 collective-permute-done.3.refs_1_
  22.8 2.4 %collective-permute-start.4 = (bf16[256,512]{1,0:T(8,128)(2,1)S(1)}, bf16[256,512]{1,0:T(8,128)(2,1)S(1)}, u32[]{:S(2)}, u32[]{:S(2)}) collective-permute-start(bf16[256,512]{1,0:T(8,128)(2,1)S(1)} %merge.1), channel_id=1, source_target_pairs={{0,8},{4,12},{8,0},{12,4},{1,9},{5,13},{9,1},{13,5},{2,10},{6,14},... | collective-permute-start | bytes 786440 | tf_op jit(solution)/shard_map/ppermute | solution.py:499
  25.2 0.7 %select.13 = (f32[256,512]{1,0:T(8,128)S(1)}, f32[256,512]{1,0:T(8,128)S(1)}) custom-call(s32[4]{0:T(128)S(1)} %pad_add_fusion.4.place, f32[16,256,128]{2,1,0:T(8,128)S(1)} %get-tuple-element.19.after.acc), custom_call_target="tpu_custom_call" | custom-call | flops 99999997952 | bytes 100000000 | tf_op jit(solution)/shard_map/select/pallas_call | solution.py:148
  25.9 0.4 row_totals.1.row_total
  26.4 1.5 %collective-permute-start.7 = (bf16[256,512]{1,0:T(8,128)(2,1)S(1)}, bf16[256,512]{1,0:T(8,128)(2,1)S(1)}, u32[]{:S(2)}, u32[]{:S(2)}) collective-permute-start(bf16[256,512]{1,0:T(8,128)(2,1)S(1)} %fusion), channel_id=1, source_target_pairs={{0,2},{1,3},{2,0},{3,1},{4,6},{5,7},{6,4},{7,5},{8,10},{9,11},{10,... | collective-permute-start | bytes 786440 | tf_op jit(solution)/shard_map/ppermute | solution.py:495
  28.0 9.6 %collective-permute-done.4.refs_0_ = bf16[256,512]{1,0:T(8,128)(2,1)S(1)} collective-permute-done((bf16[256,512]{1,0:T(8,128)(2,1)S(1)}, bf16[256,512]{1,0:T(8,128)(2,1)S(1)}, u32[]{:S(2)}, u32[]{:S(2)}) %collective-permute-start.4) | collective-permute-done | bytes 262176 | tf_op jit(solution)/shard_map/ppermute | solution.py:499
  37.6 0.2 join.1
  38.0 0.7 %collective-permute-start.8 = (bf16[256,512]{1,0:T(8,128)(2,1)S(1)}, bf16[256,512]{1,0:T(8,128)(2,1)S(1)}, u32[]{:S(2)}, u32[]{:S(2)}) collective-permute-start(bf16[256,512]{1,0:T(8,128)(2,1)S(1)} %fusion.4.refs_0_), channel_id=1, source_target_pairs={{0,4},{4,12},{8,0},{12,8},{1,5},{5,13},{9,1},{13,9},{2,6},{6,14},{... | collective-permute-start | bytes 786440 | tf_op jit(solution)/shard_map/ppermute | solution.py:593
  38.8 2.5 %collective-permute-start.11 = (bf16[128,512]{1,0:T(8,128)(2,1)S(1)}, bf16[128,512]{1,0:T(8,128)(2,1)S(1)}, u32[]{:S(2)}, u32[]{:S(2)}) collective-permute-start(bf16[128,512]{1,0:T(8,128)(2,1)S(1)} %get-tuple-element.31), channel_id=1, source_target_pairs={{0,8},{4,0},{8,12},{12,4},{1,9},{5,1},{9,13},{13,5},{2,10},{6,2},{... | collective-permute-start | bytes 393224 | tf_op jit(solution)/shard_map/ppermute | solution.py:595
  41.3 0.9 %collective-permute-start.9 = (bf16[128,512]{1,0:T(8,128)(2,1)S(1)}, bf16[128,512]{1,0:T(8,128)(2,1)S(1)}, u32[]{:S(2)}, u32[]{:S(2)}) collective-permute-start(bf16[128,512]{1,0:T(8,128)(2,1)S(1)} %get-tuple-element.32), channel_id=1, source_target_pairs={{0,8},{4,0},{8,12},{12,4},{1,9},{5,1},{9,13},{13,5},{2,10},{6,2},{... | collective-permute-start | bytes 393224 | tf_op jit(solution)/shard_map/ppermute | solution.py:595
  42.2 8.7 %prepare.1 = (bf16[4096,1024]{1,0:T(8,128)(2,1)S(1)}, f32[4096,128]{1,0:T(8,128)S(1)}, f32[4096,512]{1,0:T(8,128)S(1)}) custom-call(s32[1]{0:T(128)} %bitcast.6.first_row, s32[8,128]{1,0:T(8,128)S(1)} %get-tuple-element.33.rays, bf16[256,512]{1,0:T(8,128)(2,1)S(1)} %fusion.4.refs_0_, f32[4096,512]{1,0:T(8,128)} %refs_1_.1), custom_call_target="tpu_custom_call" | custom-call | flops 1 | bytes 1 | tf_op jit(solution)/shard_map/prepare/pallas_call | solution.py:396
  51.0 2.7 %collective-permute-start.12 = (bf16[128,512]{1,0:T(8,128)(2,1)S(1)}, bf16[128,512]{1,0:T(8,128)(2,1)S(1)}, u32[]{:S(2)}, u32[]{:S(2)}) collective-permute-start(bf16[128,512]{1,0:T(8,128)(2,1)S(1)} %pick.3), channel_id=1, source_target_pairs={{0,4},{4,0},{8,12},{12,8},{1,5},{5,1},{9,13},{13,9},{2,6},{6,2},{1... | collective-permute-start | bytes 393224 | tf_op jit(solution)/shard_map/ppermute | solution.py:499
  53.6 0.7 %collective-permute-start.10 = (bf16[128,512]{1,0:T(8,128)(2,1)S(1)}, bf16[128,512]{1,0:T(8,128)(2,1)S(1)}, u32[]{:S(2)}, u32[]{:S(2)}) collective-permute-start(bf16[128,512]{1,0:T(8,128)(2,1)S(1)} %pick.2), channel_id=1, source_target_pairs={{0,4},{4,0},{8,12},{12,8},{1,5},{5,1},{9,13},{13,9},{2,6},{6,2},{1... | collective-permute-start | bytes 393224 | tf_op jit(solution)/shard_map/ppermute | solution.py:499
  54.3 2.4 %add_back.1.refs_4_ = f32[4096,512]{1,0:T(8,128)S(1)} custom-call(bf16[256,512]{1,0:T(8,128)(2,1)S(1)} %collective-permute-done.8.first.refs_0_, bf16[128,512]{1,0:T(8,128)(2,1)S(1)} %collective-permute-done.9.second.refs_1_, bf16[128,512]{1,0:T(8,128)(2,1)S(1)} %collective-permute-done.11.second.refs_2_, ...), custom_call_target="tpu_custom_call" | custom-call | flops 99999997952 | bytes 100000000 | tf_op jit(solution)/shard_map/add_back/pallas_call | solution.py:445
  56.7 1.2 %collective-permute-done.12.refs_1_ = bf16[128,512]{1,0:T(8,128)(2,1)S(1)} collective-permute-done((bf16[128,512]{1,0:T(8,128)(2,1)S(1)}, bf16[128,512]{1,0:T(8,128)(2,1)S(1)}, u32[]{:S(2)}, u32[]{:S(2)}) %collective-permute-start.12) | collective-permute-done | bytes 131104 | tf_op jit(solution)/shard_map/ppermute | solution.py:499
  57.9 1.4 %collective-permute-done.10.refs_0_ = bf16[128,512]{1,0:T(8,128)(2,1)S(1)} collective-permute-done((bf16[128,512]{1,0:T(8,128)(2,1)S(1)}, bf16[128,512]{1,0:T(8,128)(2,1)S(1)}, u32[]{:S(2)}, u32[]{:S(2)}) %collective-permute-start.10) | collective-permute-done | bytes 131104 | tf_op jit(solution)/shard_map/ppermute | solution.py:499
  59.4 3.7 %back_project.1 = f32[4096,512]{1,0:T(8,128)} custom-call(bf16[128,512]{1,0:T(8,128)(2,1)S(1)} %collective-permute-done.10.refs_0_, bf16[128,512]{1,0:T(8,128)(2,1)S(1)} %collective-permute-done.12.refs_1_, bf16[4096,1024]{1,0:T(8,128)(2,1)S(1)} %get-tuple-element.28.refs_3_.refs_2_, f32[4096,128]{1,0:T(8,128)S(1)} %get-tuple-element.29.refs_4_.refs_3_, ...), custom_call_target="tpu_custom_call" | custom-call | flops 1 | bytes 1 | tf_op jit(solution)/shard_map/back_project/pallas_call | solution.py:478
  (27 shorter events, 0.7 us)
Async XLA Ops:
  0.0 12.0 %collective-permute-start = (s32[2,128]{1,0:T(2,128)}, s32[2,128]{1,0:T(2,128)S(1)}, u32[]{:S(2)}, u32[]{:S(2)}) collective-permute-start(s32[2,128]{1,0:T(2,128)} %bitcast.19), channel_id=1, source_target_pairs={{0,8},{4,12},{8,0},{12,4},{1,9},{5,13},{9,1},{13,5},{2,10},{6,14},... | collective-permute-start | bytes 3080 | tf_op jit(solution)/shard_map/ppermute | solution.py:499
  4.0 7.9 %collective-permute-start.1 = (s32[2,128]{1,0:T(2,128)}, s32[2,128]{1,0:T(2,128)S(1)}, u32[]{:S(2)}, u32[]{:S(2)}) collective-permute-start(s32[2,128]{1,0:T(2,128)} %bitcast.20), channel_id=1, source_target_pairs={{0,4},{4,0},{8,12},{12,8},{1,5},{5,1},{9,13},{13,9},{2,6},{6,2},{1... | collective-permute-start | bytes 3080 | tf_op jit(solution)/shard_map/ppermute | solution.py:499
  5.6 6.4 %collective-permute-start.2 = (s32[2,128]{1,0:T(2,128)}, s32[2,128]{1,0:T(2,128)S(1)}, u32[]{:S(2)}, u32[]{:S(2)}) collective-permute-start(s32[2,128]{1,0:T(2,128)} %bitcast.21), channel_id=1, source_target_pairs={{0,12},{4,8},{8,4},{12,0},{1,13},{5,9},{9,5},{13,1},{2,14},{6,10},... | collective-permute-start | bytes 3080 | tf_op jit(solution)/shard_map/ppermute | solution.py:499
  5.6 6.4 %copy-start = (s32[256]{0:T(256)S(1)}, s32[256]{0:T(256)}, u32[]{:S(2)}) copy-start(s32[256]{0:T(256)} %param.8) | copy-start | bytes 3076
  5.6 9.9 %copy-start.1 = (s32[256]{0:T(256)S(1)}, s32[256]{0:T(256)}, u32[]{:S(2)}) copy-start(s32[256]{0:T(256)} %param.7) | copy-start | bytes 3076
  5.6 9.9 %copy-start.2 = (s32[48]{0:T(128)S(1)}, s32[48]{0:T(128)}, u32[]{:S(2)}) copy-start(s32[48]{0:T(128)} %tile_bin.1) | copy-start | bytes 580
  13.4 9.3 %collective-permute-start.3 = (bf16[256,512]{1,0:T(8,128)(2,1)S(1)}, bf16[256,512]{1,0:T(8,128)(2,1)S(1)}, u32[]{:S(2)}, u32[]{:S(2)}) collective-permute-start(bf16[256,512]{1,0:T(8,128)(2,1)S(1)} %get-tuple-element.21), channel_id=1, source_target_pairs={{0,4},{4,0},{8,12},{12,8},{1,5},{5,1},{9,13},{13,9},{2,6},{6,2},{1... | collective-permute-start | bytes 786440 | tf_op jit(solution)/shard_map/ppermute | solution.py:499
  14.4 13.5 %collective-permute-start.5 = (bf16[256,512]{1,0:T(8,128)(2,1)S(1)}, bf16[256,512]{1,0:T(8,128)(2,1)S(1)}, u32[]{:S(2)}, u32[]{:S(2)}) collective-permute-start(bf16[256,512]{1,0:T(8,128)(2,1)S(1)} %get-tuple-element.22), channel_id=1, source_target_pairs={{0,4},{4,0},{8,12},{12,8},{1,5},{5,1},{9,13},{13,9},{2,6},{6,2},{1... | collective-permute-start | bytes 786440 | tf_op jit(solution)/shard_map/ppermute | solution.py:499
  22.1 4.2 %collective-permute-start.6 = (bf16[2,256,512]{2,1,0:T(8,128)(2,1)S(1)}, bf16[2,256,512]{2,1,0:T(8,128)(2,1)S(1)}, u32[]{:S(2)}, u32[]{:S(2)}) collective-permute-start(bf16[2,256,512]{2,1,0:T(8,128)(2,1)S(1)} %get-tuple-element.25), channel_id=1, source_target_pairs={{0,1},{1,0},{2,3},{3,2},{4,5},{5,4},{6,7},{7,6},{8,9},{9,8},{10,11... | collective-permute-start | bytes 1572872 | tf_op jit(solution)/shard_map/ppermute | solution.py:499
  22.8 14.8 %collective-permute-start.4 = (bf16[256,512]{1,0:T(8,128)(2,1)S(1)}, bf16[256,512]{1,0:T(8,128)(2,1)S(1)}, u32[]{:S(2)}, u32[]{:S(2)}) collective-permute-start(bf16[256,512]{1,0:T(8,128)(2,1)S(1)} %merge.1), channel_id=1, source_target_pairs={{0,8},{4,12},{8,0},{12,4},{1,9},{5,13},{9,1},{13,5},{2,10},{6,14},... | collective-permute-start | bytes 786440 | tf_op jit(solution)/shard_map/ppermute | solution.py:499
  26.4 11.5 %collective-permute-start.7 = (bf16[256,512]{1,0:T(8,128)(2,1)S(1)}, bf16[256,512]{1,0:T(8,128)(2,1)S(1)}, u32[]{:S(2)}, u32[]{:S(2)}) collective-permute-start(bf16[256,512]{1,0:T(8,128)(2,1)S(1)} %fusion), channel_id=1, source_target_pairs={{0,2},{1,3},{2,0},{3,1},{4,6},{5,7},{6,4},{7,5},{8,10},{9,11},{10,... | collective-permute-start | bytes 786440 | tf_op jit(solution)/shard_map/ppermute | solution.py:495
  38.0 12.9 %collective-permute-start.8 = (bf16[256,512]{1,0:T(8,128)(2,1)S(1)}, bf16[256,512]{1,0:T(8,128)(2,1)S(1)}, u32[]{:S(2)}, u32[]{:S(2)}) collective-permute-start(bf16[256,512]{1,0:T(8,128)(2,1)S(1)} %fusion.4.refs_0_), channel_id=1, source_target_pairs={{0,4},{4,12},{8,0},{12,8},{1,5},{5,13},{9,1},{13,9},{2,6},{6,14},{... | collective-permute-start | bytes 786440 | tf_op jit(solution)/shard_map/ppermute | solution.py:593
  38.8 12.2 %collective-permute-start.11 = (bf16[128,512]{1,0:T(8,128)(2,1)S(1)}, bf16[128,512]{1,0:T(8,128)(2,1)S(1)}, u32[]{:S(2)}, u32[]{:S(2)}) collective-permute-start(bf16[128,512]{1,0:T(8,128)(2,1)S(1)} %get-tuple-element.31), channel_id=1, source_target_pairs={{0,8},{4,0},{8,12},{12,4},{1,9},{5,1},{9,13},{13,5},{2,10},{6,2},{... | collective-permute-start | bytes 393224 | tf_op jit(solution)/shard_map/ppermute | solution.py:595
  41.3 12.3 %collective-permute-start.9 = (bf16[128,512]{1,0:T(8,128)(2,1)S(1)}, bf16[128,512]{1,0:T(8,128)(2,1)S(1)}, u32[]{:S(2)}, u32[]{:S(2)}) collective-permute-start(bf16[128,512]{1,0:T(8,128)(2,1)S(1)} %get-tuple-element.32), channel_id=1, source_target_pairs={{0,8},{4,0},{8,12},{12,4},{1,9},{5,1},{9,13},{13,5},{2,10},{6,2},{... | collective-permute-start | bytes 393224 | tf_op jit(solution)/shard_map/ppermute | solution.py:595
  51.0 7.0 %collective-permute-start.12 = (bf16[128,512]{1,0:T(8,128)(2,1)S(1)}, bf16[128,512]{1,0:T(8,128)(2,1)S(1)}, u32[]{:S(2)}, u32[]{:S(2)}) collective-permute-start(bf16[128,512]{1,0:T(8,128)(2,1)S(1)} %pick.3), channel_id=1, source_target_pairs={{0,4},{4,0},{8,12},{12,8},{1,5},{5,1},{9,13},{13,9},{2,6},{6,2},{1... | collective-permute-start | bytes 393224 | tf_op jit(solution)/shard_map/ppermute | solution.py:499
  53.6 5.7 %collective-permute-start.10 = (bf16[128,512]{1,0:T(8,128)(2,1)S(1)}, bf16[128,512]{1,0:T(8,128)(2,1)S(1)}, u32[]{:S(2)}, u32[]{:S(2)}) collective-permute-start(bf16[128,512]{1,0:T(8,128)(2,1)S(1)} %pick.2), channel_id=1, source_target_pairs={{0,4},{4,0},{8,12},{12,8},{1,5},{5,1},{9,13},{13,9},{2,6},{6,2},{1... | collective-permute-start | bytes 393224 | tf_op jit(solution)/shard_map/ppermute | solution.py:499

commit v13 on v11

--- a/solution.py
+++ b/solution.py
@@ -222,17 +222,19 @@
     return pl.pallas_call(
         functools.partial(project_kernel, angles),
         in_specs=[pl.BlockSpec(memory_space=pltpu.SMEM), anywhere],
-        out_specs=vmem,
+        out_specs=[vmem, vmem],
         scratch_shapes=[
-            pltpu.VMEM((cells, chans), F32),
             pltpu.VMEM((rays, LANES), F32),
             pltpu.VMEM((rays, widest), BF16),
             pltpu.VMEM((rays, widest), BF16),
             pltpu.VMEM((rays, chans), F32),
             pltpu.SemaphoreType.DMA((len(sizes),)),
         ],
-        out_shape=jax.ShapeDtypeStruct((rays, chans), BF16),
-        compiler_params=pltpu.CompilerParams(vmem_limit_bytes=40 * MIB),
+        out_shape=[
+            jax.ShapeDtypeStruct((rays, chans), BF16),
+            jax.ShapeDtypeStruct((cells, chans), F32),
+        ],
+        compiler_params=pltpu.CompilerParams(vmem_limit_bytes=32 * MIB),
         cost_estimate=pl.CostEstimate(
             flops=4 * rays * cells * chans, bytes_accessed=4 * cells * chans, transcendentals=0
         ),
@@ -548,7 +550,7 @@
     rays = {r: own_rays if r == 0 else swap(own_rays, "scan", r, n_scan) for r in order}
     all_rays = jnp.concatenate([rays[r] for r in order], axis=0)
 
-    projected = project(image, first_row, angles)
+    projected, near_image = project(image, first_row, angles)
     own_share, *shares = reorder(all_rays, projected, n_scan)
     share_of = dict(zip(order[1:], shares))
     relayed = {r ^ 1: swap(share_of[r], "scan", 1, n_scan) for r in late}
@@ -600,7 +602,7 @@
         two, one = rays[mask ^ 2], rays[mask ^ 1]
         columns += [jnp.where(outer, two, one), jnp.where(outer, one, two)]
     columns = jnp.concatenate(columns + [rays[mask ^ 3] for mask in masks], axis=0)
-    tile, col_recip, partial = prepare(columns, [residual], image, first_row, angles)
+    tile, col_recip, partial = prepare(columns, [residual], near_image, first_row, angles)
     partial = add_back(pieces, points, tile, col_recip, partial)
     return back_project(last, points * (n_scan - len(masks)), tile, col_recip, partial)
 

time: 63.4 us -> 66.8 us (1.054)
  local copies, waits for them, and re-layouts: 3.41 us -> 6.8 us
    unnamed x8 -> x10, local copies, waits for them, and re-layouts: 3.39 us -> 6.78 us
  transfers between devices with their start and end apart: 13 -> 13, of which waited for: 4 -> 4; matrix products, arithmetic and copies ran while one was open for 0% -> 0% of each run, Pallas kernels for 35% -> 34%
where the time goes in v13:
time: 66.8 us; the launch traced here: 66.6 us
  Pallas kernels  27.5 us (41%)
  starting transfers between devices  18.7 us (28%)
  waiting for transfers between devices  12.9 us (19%)
  local copies, waits for them, and re-layouts  6.8 us (10%)
    ppermute x9, starting transfers between devices, swap(): return lax.ppermute(x, axis, [(i, i ^ mask) for i in range(n)])  13 us
    ppermute x9, waiting for transfers between devices, swap(): return lax.ppermute(x, axis, [(i, i ^ mask) for i in range(n)])  12.9 us
    unnamed x10, local copies, waits for them, and re-layouts  6.78 us
    pallas_call x1, Pallas kernels, integrate(): pl.pallas_call(functools.partial(integrate_kernel, nx, chans // tile_bins...  6.52 us
    pallas_call x1, Pallas kernels, project(): pl.pallas_call(functools.partial(project_kernel, angles), in_specs=[pl.Bl...  6.42 us
    pallas_call x1, Pallas kernels, prepare(): pl.pallas_call(functools.partial(prepare_kernel, angles, len(residuals)),...  5.8 us
    pallas_call x1, Pallas kernels, back_project(): pl.pallas_call(functools.partial(back_kernel, first, len(pieces)), in_spe...  3.67 us
    ppermute x2, starting transfers between devices, body(): lax.ppermute(x, 'scan', [(i, backward(i)) for i in range(n_scan)])  3.45 us
  transfers between devices with their start and end apart: 13, of which 4 were waited for; matrix products, arithmetic and copies ran while one was open for 0% of the time, Pallas kernels for 34%

profile of v13, /device:TPU:0, one launch (start us, length us, event | category | flops | bytes accessed | tf_op | source)
XLA Modules:
  0.0 66.6 jit_solution(2121758320673655021)
XLA Ops:
  0.0 4.0 %collective-permute-start = (s32[2,128]{1,0:T(2,128)}, s32[2,128]{1,0:T(2,128)S(1)}, u32[]{:S(2)}, u32[]{:S(2)}) collective-permute-start(s32[2,128]{1,0:T(2,128)} %bitcast.19), channel_id=1, source_target_pairs={{0,8},{4,12},{8,0},{12,4},{1,9},{5,13},{9,1},{13,5},{2,10},{6,14},... | collective-permute-start | bytes 3080 | tf_op jit(solution)/shard_map/ppermute | solution.py:501
  4.0 1.6 %collective-permute-start.1 = (s32[2,128]{1,0:T(2,128)}, s32[2,128]{1,0:T(2,128)S(1)}, u32[]{:S(2)}, u32[]{:S(2)}) collective-permute-start(s32[2,128]{1,0:T(2,128)} %bitcast.20), channel_id=1, source_target_pairs={{0,4},{4,0},{8,12},{12,8},{1,5},{5,1},{9,13},{13,9},{2,6},{6,2},{1... | collective-permute-start | bytes 3080 | tf_op jit(solution)/shard_map/ppermute | solution.py:501
  5.6 6.4 %project.1 = (bf16[1024,512]{1,0:T(8,128)(2,1)S(1)}, f32[4096,512]{1,0:T(8,128)S(1)}) custom-call(s32[1]{0:T(128)} %bitcast.6.first_row, f32[4096,512]{1,0:T(8,128)} %image.1), custom_call_target="tpu_custom_call" | custom-call | flops 8589934592 | bytes 8388608 | tf_op jit(solution)/shard_map/project/pallas_call | solution.py:222
  12.1 3.4 %copy-done = f32[4096,512]{1,0:T(8,128)} copy-done((f32[4096,512]{1,0:T(8,128)}, f32[4096,512]{1,0:T(8,128)S(1)}, u32[]{:S(2)}) %copy-start) | copy-done | bytes 8388632
  15.5 1.3 %reorder.1 = (bf16[256,512]{1,0:T(8,128)(2,1)S(1)}, bf16[256,512]{1,0:T(8,128)(2,1)S(1)}, bf16[256,512]{1,0:T(8,128)(2,1)S(1)}, bf16[256,512]{1,0:T(8,128)(2,1)S(1)}) custom-call(s32[8,128]{1,0:T(8,128)S(1)} %get-tuple-element.38.rays, bf16[1024,512]{1,0:T(8,128)(2,1)S(1)} %get-tuple-element.20.rows), custom_call_target="tpu_custom_call" | custom-call | flops 1 | bytes 1 | tf_op jit(solution)/shard_map/reorder/pallas_call | solution.py:266
  16.8 1.0 %collective-permute-start.3 = (bf16[256,512]{1,0:T(8,128)(2,1)S(1)}, bf16[256,512]{1,0:T(8,128)(2,1)S(1)}, u32[]{:S(2)}, u32[]{:S(2)}) collective-permute-start(bf16[256,512]{1,0:T(8,128)(2,1)S(1)} %get-tuple-element.24), channel_id=1, source_target_pairs={{0,4},{4,0},{8,12},{12,8},{1,5},{5,1},{9,13},{13,9},{2,6},{6,2},{1... | collective-permute-start | bytes 786440 | tf_op jit(solution)/shard_map/ppermute | solution.py:501
  17.9 1.1 %collective-permute-start.5 = (bf16[256,512]{1,0:T(8,128)(2,1)S(1)}, bf16[256,512]{1,0:T(8,128)(2,1)S(1)}, u32[]{:S(2)}, u32[]{:S(2)}) collective-permute-start(bf16[256,512]{1,0:T(8,128)(2,1)S(1)} %get-tuple-element.25), channel_id=1, source_target_pairs={{0,4},{4,0},{8,12},{12,8},{1,5},{5,1},{9,13},{13,9},{2,6},{6,2},{1... | collective-permute-start | bytes 786440 | tf_op jit(solution)/shard_map/ppermute | solution.py:501
  19.0 6.5 %integrate.1 = (bf16[2,256,512]{2,1,0:T(8,128)(2,1)S(1)}, f32[16,256,128]{2,1,0:T(8,128)S(1)}) custom-call(s32[48]{0:T(128)S(1)} %copy-done.4, s32[4]{0:T(128)S(1)} %pad_add_fusion.4.place, bf16[256,512]{1,0:T(8,128)(2,1)S(1)} %get-tuple-element.21.after.own, s32[1,256]{1,0:T(1,128)S(1)} %bitcast.24, bf16[384,6144]{1,0:T(8,128)(2,1)} %frames.1, ...), custom_call_target="tpu_custom_call" | custom-call | flops 1 | bytes 1 | tf_op jit(solution)/shard_map/integrate/pallas_call | solution.py:108
  25.6 0.5 collective-permute-done.3.refs_1_
  26.2 2.4 %collective-permute-start.4 = (bf16[256,512]{1,0:T(8,128)(2,1)S(1)}, bf16[256,512]{1,0:T(8,128)(2,1)S(1)}, u32[]{:S(2)}, u32[]{:S(2)}) collective-permute-start(bf16[256,512]{1,0:T(8,128)(2,1)S(1)} %merge.1), channel_id=1, source_target_pairs={{0,8},{4,12},{8,0},{12,4},{1,9},{5,13},{9,1},{13,5},{2,10},{6,14},... | collective-permute-start | bytes 786440 | tf_op jit(solution)/shard_map/ppermute | solution.py:501
  28.6 0.7 select.13
  29.8 1.6 %collective-permute-start.7 = (bf16[256,512]{1,0:T(8,128)(2,1)S(1)}, bf16[256,512]{1,0:T(8,128)(2,1)S(1)}, u32[]{:S(2)}, u32[]{:S(2)}) collective-permute-start(bf16[256,512]{1,0:T(8,128)(2,1)S(1)} %fusion), channel_id=1, source_target_pairs={{0,2},{1,3},{2,0},{3,1},{4,6},{5,7},{6,4},{7,5},{8,10},{9,11},{10,... | collective-permute-start | bytes 786440 | tf_op jit(solution)/shard_map/ppermute | solution.py:497
  31.4 9.6 %collective-permute-done.4.refs_0_ = bf16[256,512]{1,0:T(8,128)(2,1)S(1)} collective-permute-done((bf16[256,512]{1,0:T(8,128)(2,1)S(1)}, bf16[256,512]{1,0:T(8,128)(2,1)S(1)}, u32[]{:S(2)}, u32[]{:S(2)}) %collective-permute-start.4) | collective-permute-done | bytes 262176 | tf_op jit(solution)/shard_map/ppermute | solution.py:501
  41.5 0.7 %collective-permute-start.8 = (bf16[256,512]{1,0:T(8,128)(2,1)S(1)}, bf16[256,512]{1,0:T(8,128)(2,1)S(1)}, u32[]{:S(2)}, u32[]{:S(2)}) collective-permute-start(bf16[256,512]{1,0:T(8,128)(2,1)S(1)} %fusion.4.refs_0_), channel_id=1, source_target_pairs={{0,4},{4,12},{8,0},{12,8},{1,5},{5,13},{9,1},{13,9},{2,6},{6,14},{... | collective-permute-start | bytes 786440 | tf_op jit(solution)/shard_map/ppermute | solution.py:595
  42.2 2.5 %collective-permute-start.11 = (bf16[128,512]{1,0:T(8,128)(2,1)S(1)}, bf16[128,512]{1,0:T(8,128)(2,1)S(1)}, u32[]{:S(2)}, u32[]{:S(2)}) collective-permute-start(bf16[128,512]{1,0:T(8,128)(2,1)S(1)} %get-tuple-element.35), channel_id=1, source_target_pairs={{0,8},{4,0},{8,12},{12,4},{1,9},{5,1},{9,13},{13,5},{2,10},{6,2},{... | collective-permute-start | bytes 393224 | tf_op jit(solution)/shard_map/ppermute | solution.py:597
  44.7 0.9 %collective-permute-start.9 = (bf16[128,512]{1,0:T(8,128)(2,1)S(1)}, bf16[128,512]{1,0:T(8,128)(2,1)S(1)}, u32[]{:S(2)}, u32[]{:S(2)}) collective-permute-start(bf16[128,512]{1,0:T(8,128)(2,1)S(1)} %get-tuple-element.36), channel_id=1, source_target_pairs={{0,8},{4,0},{8,12},{12,4},{1,9},{5,1},{9,13},{13,5},{2,10},{6,2},{... | collective-permute-start | bytes 393224 | tf_op jit(solution)/shard_map/ppermute | solution.py:597
  45.7 3.4 %copy-done.1 = f32[4096,512]{1,0:T(8,128)S(1)} copy-done((f32[4096,512]{1,0:T(8,128)S(1)}, f32[4096,512]{1,0:T(8,128)}, u32[]{:S(2)}) %copy-start.1) | copy-done | bytes 8388632
  49.0 5.8 %prepare.1 = (bf16[4096,1024]{1,0:T(8,128)(2,1)S(1)}, f32[4096,128]{1,0:T(8,128)S(1)}, f32[4096,512]{1,0:T(8,128)S(1)}) custom-call(s32[1]{0:T(128)} %bitcast.6.first_row, s32[8,128]{1,0:T(8,128)S(1)} %get-tuple-element.37.rays, bf16[256,512]{1,0:T(8,128)(2,1)S(1)} %fusion.4.refs_0_, f32[4096,512]{1,0:T(8,128)S(1)} %copy-done.1), custom_call_target="tpu_custom_call" | custom-call | flops 1 | bytes 1 | tf_op jit(solution)/shard_map/prepare/pallas_call | solution.py:398
  54.9 2.2 %collective-permute-start.12 = (bf16[128,512]{1,0:T(8,128)(2,1)S(1)}, bf16[128,512]{1,0:T(8,128)(2,1)S(1)}, u32[]{:S(2)}, u32[]{:S(2)}) collective-permute-start(bf16[128,512]{1,0:T(8,128)(2,1)S(1)} %pick.3), channel_id=1, source_target_pairs={{0,4},{4,0},{8,12},{12,8},{1,5},{5,1},{9,13},{13,9},{2,6},{6,2},{1... | collective-permute-start | bytes 393224 | tf_op jit(solution)/shard_map/ppermute | solution.py:501
  57.1 0.7 %collective-permute-start.10 = (bf16[128,512]{1,0:T(8,128)(2,1)S(1)}, bf16[128,512]{1,0:T(8,128)(2,1)S(1)}, u32[]{:S(2)}, u32[]{:S(2)}) collective-permute-start(bf16[128,512]{1,0:T(8,128)(2,1)S(1)} %pick.2), channel_id=1, source_target_pairs={{0,4},{4,0},{8,12},{12,8},{1,5},{5,1},{9,13},{13,9},{2,6},{6,2},{1... | collective-permute-start | bytes 393224 | tf_op jit(solution)/shard_map/ppermute | solution.py:501
  57.8 2.4 %add_back.1.refs_4_ = f32[4096,512]{1,0:T(8,128)S(1)} custom-call(bf16[256,512]{1,0:T(8,128)(2,1)S(1)} %collective-permute-done.8.first.refs_0_, bf16[128,512]{1,0:T(8,128)(2,1)S(1)} %collective-permute-done.9.second.refs_1_, bf16[128,512]{1,0:T(8,128)(2,1)S(1)} %collective-permute-done.11.second.refs_2_, ...), custom_call_target="tpu_custom_call" | custom-call | flops 99999997952 | bytes 100000000 | tf_op jit(solution)/shard_map/add_back/pallas_call | solution.py:447
  60.2 1.2 %collective-permute-done.12.refs_1_ = bf16[128,512]{1,0:T(8,128)(2,1)S(1)} collective-permute-done((bf16[128,512]{1,0:T(8,128)(2,1)S(1)}, bf16[128,512]{1,0:T(8,128)(2,1)S(1)}, u32[]{:S(2)}, u32[]{:S(2)}) %collective-permute-start.12) | collective-permute-done | bytes 131104 | tf_op jit(solution)/shard_map/ppermute | solution.py:501
  61.4 1.4 %collective-permute-done.10.refs_0_ = bf16[128,512]{1,0:T(8,128)(2,1)S(1)} collective-permute-done((bf16[128,512]{1,0:T(8,128)(2,1)S(1)}, bf16[128,512]{1,0:T(8,128)(2,1)S(1)}, u32[]{:S(2)}, u32[]{:S(2)}) %collective-permute-start.10) | collective-permute-done | bytes 131104 | tf_op jit(solution)/shard_map/ppermute | solution.py:501
  62.8 3.7 %back_project.1 = f32[4096,512]{1,0:T(8,128)} custom-call(bf16[128,512]{1,0:T(8,128)(2,1)S(1)} %collective-permute-done.10.refs_0_, bf16[128,512]{1,0:T(8,128)(2,1)S(1)} %collective-permute-done.12.refs_1_, bf16[4096,1024]{1,0:T(8,128)(2,1)S(1)} %get-tuple-element.32.refs_3_.refs_2_, f32[4096,128]{1,0:T(8,128)S(1)} %get-tuple-element.33.refs_4_.refs_3_, ...), custom_call_target="tpu_custom_call" | custom-call | flops 1 | bytes 1 | tf_op jit(solution)/shard_map/back_project/pallas_call | solution.py:480
  (31 shorter events, 1.3 us)
Async XLA Ops:
  0.0 15.5 %collective-permute-start = (s32[2,128]{1,0:T(2,128)}, s32[2,128]{1,0:T(2,128)S(1)}, u32[]{:S(2)}, u32[]{:S(2)}) collective-permute-start(s32[2,128]{1,0:T(2,128)} %bitcast.19), channel_id=1, source_target_pairs={{0,8},{4,12},{8,0},{12,4},{1,9},{5,13},{9,1},{13,5},{2,10},{6,14},... | collective-permute-start | bytes 3080 | tf_op jit(solution)/shard_map/ppermute | solution.py:501
  4.0 11.4 %collective-permute-start.1 = (s32[2,128]{1,0:T(2,128)}, s32[2,128]{1,0:T(2,128)S(1)}, u32[]{:S(2)}, u32[]{:S(2)}) collective-permute-start(s32[2,128]{1,0:T(2,128)} %bitcast.20), channel_id=1, source_target_pairs={{0,4},{4,0},{8,12},{12,8},{1,5},{5,1},{9,13},{13,9},{2,6},{6,2},{1... | collective-permute-start | bytes 3080 | tf_op jit(solution)/shard_map/ppermute | solution.py:501
  5.6 9.9 %collective-permute-start.2 = (s32[2,128]{1,0:T(2,128)}, s32[2,128]{1,0:T(2,128)S(1)}, u32[]{:S(2)}, u32[]{:S(2)}) collective-permute-start(s32[2,128]{1,0:T(2,128)} %bitcast.21), channel_id=1, source_target_pairs={{0,12},{4,8},{8,4},{12,0},{1,13},{5,9},{9,5},{13,1},{2,14},{6,10},... | collective-permute-start | bytes 3080 | tf_op jit(solution)/shard_map/ppermute | solution.py:501
  5.6 9.9 %copy-start.2 = (s32[256]{0:T(256)S(1)}, s32[256]{0:T(256)}, u32[]{:S(2)}) copy-start(s32[256]{0:T(256)} %param.8) | copy-start | bytes 3076
  5.6 13.4 %copy-start.3 = (s32[256]{0:T(256)S(1)}, s32[256]{0:T(256)}, u32[]{:S(2)}) copy-start(s32[256]{0:T(256)} %param.7) | copy-start | bytes 3076
  5.6 13.4 %copy-start.4 = (s32[48]{0:T(128)S(1)}, s32[48]{0:T(128)}, u32[]{:S(2)}) copy-start(s32[48]{0:T(128)} %tile_bin.1) | copy-start | bytes 580
  12.1 3.4 %copy-start = (f32[4096,512]{1,0:T(8,128)}, f32[4096,512]{1,0:T(8,128)S(1)}, u32[]{:S(2)}) copy-start(f32[4096,512]{1,0:T(8,128)S(1)} %get-tuple-element.31.refs_1_) | copy-start | bytes 25165828
  16.8 9.3 %collective-permute-start.3 = (bf16[256,512]{1,0:T(8,128)(2,1)S(1)}, bf16[256,512]{1,0:T(8,128)(2,1)S(1)}, u32[]{:S(2)}, u32[]{:S(2)}) collective-permute-start(bf16[256,512]{1,0:T(8,128)(2,1)S(1)} %get-tuple-element.24), channel_id=1, source_target_pairs={{0,4},{4,0},{8,12},{12,8},{1,5},{5,1},{9,13},{13,9},{2,6},{6,2},{1... | collective-permute-start | bytes 786440 | tf_op jit(solution)/shard_map/ppermute | solution.py:501
  17.9 13.5 %collective-permute-start.5 = (bf16[256,512]{1,0:T(8,128)(2,1)S(1)}, bf16[256,512]{1,0:T(8,128)(2,1)S(1)}, u32[]{:S(2)}, u32[]{:S(2)}) collective-permute-start(bf16[256,512]{1,0:T(8,128)(2,1)S(1)} %get-tuple-element.25), channel_id=1, source_target_pairs={{0,4},{4,0},{8,12},{12,8},{1,5},{5,1},{9,13},{13,9},{2,6},{6,2},{1... | collective-permute-start | bytes 786440 | tf_op jit(solution)/shard_map/ppermute | solution.py:501
  25.6 4.2 %collective-permute-start.6 = (bf16[2,256,512]{2,1,0:T(8,128)(2,1)S(1)}, bf16[2,256,512]{2,1,0:T(8,128)(2,1)S(1)}, u32[]{:S(2)}, u32[]{:S(2)}) collective-permute-start(bf16[2,256,512]{2,1,0:T(8,128)(2,1)S(1)} %get-tuple-element.28), channel_id=1, source_target_pairs={{0,1},{1,0},{2,3},{3,2},{4,5},{5,4},{6,7},{7,6},{8,9},{9,8},{10,11... | collective-permute-start | bytes 1572872 | tf_op jit(solution)/shard_map/ppermute | solution.py:501
  26.2 14.8 %collective-permute-start.4 = (bf16[256,512]{1,0:T(8,128)(2,1)S(1)}, bf16[256,512]{1,0:T(8,128)(2,1)S(1)}, u32[]{:S(2)}, u32[]{:S(2)}) collective-permute-start(bf16[256,512]{1,0:T(8,128)(2,1)S(1)} %merge.1), channel_id=1, source_target_pairs={{0,8},{4,12},{8,0},{12,4},{1,9},{5,13},{9,1},{13,5},{2,10},{6,14},... | collective-permute-start | bytes 786440 | tf_op jit(solution)/shard_map/ppermute | solution.py:501
  29.8 11.5 %collective-permute-start.7 = (bf16[256,512]{1,0:T(8,128)(2,1)S(1)}, bf16[256,512]{1,0:T(8,128)(2,1)S(1)}, u32[]{:S(2)}, u32[]{:S(2)}) collective-permute-start(bf16[256,512]{1,0:T(8,128)(2,1)S(1)} %fusion), channel_id=1, source_target_pairs={{0,2},{1,3},{2,0},{3,1},{4,6},{5,7},{6,4},{7,5},{8,10},{9,11},{10,... | collective-permute-start | bytes 786440 | tf_op jit(solution)/shard_map/ppermute | solution.py:497
  41.5 13.4 %collective-permute-start.8 = (bf16[256,512]{1,0:T(8,128)(2,1)S(1)}, bf16[256,512]{1,0:T(8,128)(2,1)S(1)}, u32[]{:S(2)}, u32[]{:S(2)}) collective-permute-start(bf16[256,512]{1,0:T(8,128)(2,1)S(1)} %fusion.4.refs_0_), channel_id=1, source_target_pairs={{0,4},{4,12},{8,0},{12,8},{1,5},{5,13},{9,1},{13,9},{2,6},{6,14},{... | collective-permute-start | bytes 786440 | tf_op jit(solution)/shard_map/ppermute | solution.py:595
  42.2 12.6 %collective-permute-start.11 = (bf16[128,512]{1,0:T(8,128)(2,1)S(1)}, bf16[128,512]{1,0:T(8,128)(2,1)S(1)}, u32[]{:S(2)}, u32[]{:S(2)}) collective-permute-start(bf16[128,512]{1,0:T(8,128)(2,1)S(1)} %get-tuple-element.35), channel_id=1, source_target_pairs={{0,8},{4,0},{8,12},{12,4},{1,9},{5,1},{9,13},{13,5},{2,10},{6,2},{... | collective-permute-start | bytes 393224 | tf_op jit(solution)/shard_map/ppermute | solution.py:597
  44.7 12.3 %collective-permute-start.9 = (bf16[128,512]{1,0:T(8,128)(2,1)S(1)}, bf16[128,512]{1,0:T(8,128)(2,1)S(1)}, u32[]{:S(2)}, u32[]{:S(2)}) collective-permute-start(bf16[128,512]{1,0:T(8,128)(2,1)S(1)} %get-tuple-element.36), channel_id=1, source_target_pairs={{0,8},{4,0},{8,12},{12,4},{1,9},{5,1},{9,13},{13,5},{2,10},{6,2},{... | collective-permute-start | bytes 393224 | tf_op jit(solution)/shard_map/ppermute | solution.py:597
  45.7 3.4 %copy-start.1 = (f32[4096,512]{1,0:T(8,128)S(1)}, f32[4096,512]{1,0:T(8,128)}, u32[]{:S(2)}) copy-start(f32[4096,512]{1,0:T(8,128)} %copy-done) | copy-start | bytes 25165828
  54.9 6.5 %collective-permute-start.12 = (bf16[128,512]{1,0:T(8,128)(2,1)S(1)}, bf16[128,512]{1,0:T(8,128)(2,1)S(1)}, u32[]{:S(2)}, u32[]{:S(2)}) collective-permute-start(bf16[128,512]{1,0:T(8,128)(2,1)S(1)} %pick.3), channel_id=1, source_target_pairs={{0,4},{4,0},{8,12},{12,8},{1,5},{5,1},{9,13},{13,9},{2,6},{6,2},{1... | collective-permute-start | bytes 393224 | tf_op jit(solution)/shard_map/ppermute | solution.py:501
  57.1 5.7 %collective-permute-start.10 = (bf16[128,512]{1,0:T(8,128)(2,1)S(1)}, bf16[128,512]{1,0:T(8,128)(2,1)S(1)}, u32[]{:S(2)}, u32[]{:S(2)}) collective-permute-start(bf16[128,512]{1,0:T(8,128)(2,1)S(1)} %pick.2), channel_id=1, source_target_pairs={{0,4},{4,0},{8,12},{12,8},{1,5},{5,1},{9,13},{13,9},{2,6},{6,2},{1... | collective-permute-start | bytes 393224 | tf_op jit(solution)/shard_map/ppermute | solution.py:501
